TPU v7x, 32 devices: a whole 2x2x4 slice. The times are simulated.
32 devices in a mesh: table: 4 (over z), rep: 8 (over y, x, core).
Axes of the slice: x: 2, y: 2, z: 4, core: 2. Of those that a mesh axis runs over, the one named last changes fastest.
Arguments:
- activations: bfloat16 [4096, 3456], P(('table', 'rep')), may hold values from -6 to 6
- cotangent: bfloat16 [4096, 3456], P(('table', 'rep')), may hold values from -6 to 6
- down_weight: bfloat16 [256, 3456], replicated, may hold values from -0.109375 to 0.109375
- up_weight: bfloat16 [256, 3456], replicated, may hold values from -0.375 to 0.375
- bias: float32 [3456], replicated, may hold values from -3 to 3
- bag_ids: int32 [4096, 26, 4], P(('table', 'rep')), may hold values from 0 to 511
- bag_lengths: int32 [4096, 26], P(('table', 'rep')), may hold values from 1 to 4
- feature_table_slot: int32 [26], replicated, may hold values from 0 to 27, as said below
Outputs:
- dense_grad: bfloat16 [4096, 128], P(('table', 'rep'))
- up_grad: float32 [256, 3456], P('rep', 'table')
- down_grad: float32 [256, 3456], P('rep', 'table')
- bias_grad: float32 [3456], replicated
- row_grad: float32 [8, 28, 512, 128], P('rep', 'table')
Inputs may be any that keep to these rules, and one draw needn't show every extreme that they name: `feature_table_slot`: distinct slots, one for each feature; slot s belongs to the table owner s // 7.
All inputs are finite; a program needn't handle non-finite values.
Results may differ from a plain program's by a relative error of at most 0.0051.
Values may be sent and summed in bfloat16 or wider, within the bound.
No kernel may reach another device: no remote copies, remote signals or barrier semaphores. Data moves between devices by JAX's collectives and lax.ppermute only.
A program may use at most 64 MiB of HBM per device.

v0:
```python
import math

import jax
import jax.numpy as jnp
from jax import lax
from jax.sharding import PartitionSpec as P

EMBED_WIDTH = 128
SPARSE_FEATURES = 26
BAG = 4
TABLE_REACH_ROWS = 512


def body(
    activations, cotangent, down_weight, up_weight, bias, bag_ids, bag_lengths, feature_table_slot
):
    tokens = activations.shape[0]
    n_table = lax.axis_size("table")
    n_rep = lax.axis_size("rep")
    slots = (SPARSE_FEATURES + n_table - 1) // n_table
    n_slot = n_table * slots
    scale = 1.0 / math.sqrt(tokens * n_table * n_rep)
    hidden = jnp.einsum(
        "td,rd->tr", activations, down_weight, preferred_element_type=jnp.float32
    ).astype(jnp.bfloat16)
    mixed = jnp.dot(hidden, up_weight, preferred_element_type=jnp.float32) + bias
    grad_f = cotangent.astype(jnp.float32)
    scaled = grad_f * activations.astype(jnp.float32)
    scaled_b = scaled.astype(jnp.bfloat16)
    back_hidden = jnp.einsum(
        "td,rd->tr", scaled_b, up_weight, preferred_element_type=jnp.float32
    ).astype(jnp.bfloat16)
    input_grad = grad_f * (1.0 + mixed) + jnp.dot(
        back_hidden, down_weight, preferred_element_type=jnp.float32
    )
    dense_grad = input_grad[:, :EMBED_WIDTH].astype(jnp.bfloat16)
    pooled = (
        input_grad[:, EMBED_WIDTH:]
        .reshape(tokens, SPARSE_FEATURES, EMBED_WIDTH)
        .astype(jnp.bfloat16)
    )
    slot_ids = jnp.arange(n_slot, dtype=jnp.int32)
    matches = feature_table_slot[None, :] == slot_ids[:, None]
    slotted = jnp.einsum(
        "sf,tfc->stc", matches.astype(jnp.bfloat16), pooled, preferred_element_type=jnp.float32
    ).astype(jnp.bfloat16)
    grads = slotted.reshape(n_table, slots, tokens, EMBED_WIDTH)
    entries = jnp.arange(BAG, dtype=jnp.int32)
    masked = jnp.where(entries[None, None, :] < bag_lengths[:, :, None], bag_ids, -1)
    feature_of = jnp.sum(
        matches.astype(jnp.int32) * jnp.arange(SPARSE_FEATURES, dtype=jnp.int32)[None, :], axis=1
    )
    filled = jnp.any(matches, axis=1)
    taken = jnp.take(masked, feature_of, axis=1)
    taken = jnp.where(filled[None, :, None], taken, -1)
    row_ids = jnp.transpose(taken, (1, 0, 2)).reshape(n_table, slots, tokens, BAG)
    table_rows = jnp.arange(TABLE_REACH_ROWS, dtype=jnp.int32)
    grad_part = lax.all_to_all(grads, "table", split_axis=0, concat_axis=2, tiled=True)
    id_part = lax.all_to_all(row_ids, "table", split_axis=0, concat_axis=2, tiled=True)
    grad_items = grad_part.reshape((-1,) + grad_part.shape[2:])
    id_items = id_part.reshape((-1,) + id_part.shape[2:])
    count = jnp.zeros(id_items.shape[:2] + (TABLE_REACH_ROWS,), jnp.bfloat16)
    for entry in range(BAG):
        count = count + (id_items[:, :, entry, None] == table_rows).astype(jnp.bfloat16)
    received = jnp.einsum("ksr,ksc->krc", count, grad_items, preferred_element_type=jnp.float32)
    row_grad = received[None]
    columns = lax.all_to_all(
        jnp.stack([scaled_b, activations]), "table", split_axis=2, concat_axis=1, tiled=True
    )
    factors = jnp.stack([hidden, back_hidden])
    piece = lax.all_gather(factors, "table", axis=1, tiled=True)
    up_part = jnp.einsum("tr,tc->rc", piece[0], columns[0], preferred_element_type=jnp.float32)
    down_part = jnp.einsum("tr,tc->rc", piece[1], columns[1], preferred_element_type=jnp.float32)
    partial_terms = jnp.stack([up_part, down_part], axis=1)
    totals = lax.psum_scatter(partial_terms * scale, "rep", scatter_dimension=0, tiled=True)
    up_grad = totals[:, 0, :]
    down_grad = totals[:, 1, :]
    bias_grad = lax.psum(jnp.sum(scaled, axis=0) * scale, ("table", "rep"))
    return (dense_grad, up_grad, down_grad, bias_grad, row_grad)


def solution(mesh):
    placed = (
        P(("table", "rep"), None),
        P(("table", "rep"), None),
        P(),
        P(),
        P(),
        P(("table", "rep"), None, None),
        P(("table", "rep"), None),
        P(),
    )
    return jax.shard_map(
        body,
        mesh=mesh,
        in_specs=placed,
        out_specs=(
            P(("table", "rep"), None),
            P("rep", "table"),
            P("rep", "table"),
            P(),
            P("rep", "table", None, None),
        ),
        check_vma=False,
    )
```

profile of v0, /device:TPU:0, one launch (start us, length us, event | category | flops | bytes accessed | tf_op | source)
XLA Modules:
  0.0 194.7 jit_solution(18329929425954995187)
XLA Ops:
  7.2 0.9 select_reduce_fusion
  8.1 0.8 fusion.28
  8.9 0.8 fusion.26
  10.3 0.8 select_select_fusion
  11.1 6.3 %all-to-all-start.1 = ((s32[4,7,128,4]{2,3,1,0:T(4,128)}), s32[4,7,128,4]{2,3,1,0:T(4,128)S(1)}, u32[]{:S(2)}, u32[]{:S(2)}) async-start(s32[4,7,128,4]{2,3,1,0:T(4,128)} %bitcast.15), calls=%async_computation.1 | async-start | bytes 114688 | tf_op jit(solution)/shard_map/all_to_all | solution.py:59
  17.4 1.5 fusion.19
  18.9 1.4 pad_maximum_fusion
  20.3 5.5 %copy.26 = bf16[2,128,3456]{1,0,2:T(2,128)(2,1)} copy(bf16[2,128,3456]{2,1,0:T(8,128)(2,1)} %pad_maximum_fusion) | data formatting | bytes 3538944 | tf_op jit(solution)/shard_map/stack | solution.py:68
  25.7 5.1 %all-to-all-start = ((bf16[2,128,3456]{1,0,2:T(2,128)(2,1)}), bf16[2,128,3456]{1,0,2:T(2,128)(2,1)}, u32[]{:S(2)}, u32[]{:S(2)}) async-start(bf16[2,128,3456]{1,0,2:T(2,128)(2,1)} %copy.26), calls=%async_computation | async-start | bytes 3538944 | tf_op jit(solution)/shard_map/all_to_all | solution.py:67
  30.8 2.2 %convolution_convert_fusion.2 = bf16[128,256]{1,0:T(8,128)(2,1)S(1)} fusion(bf16[128,3456]{1,0:T(8,128)(2,1)S(1)} %copy-done.1, bf16[256,3456]{1,0:T(8,128)(2,1)} %param.10), kind=kOutput, calls=%fused_computation.32 | convolution fusion | flops 226525184 | bytes 2719744 | tf_op jit(solution)/shard_map/td,rd->tr/dot_general | solution.py:23
  33.1 0.7 convolution_convert_fusion.1
  34.3 1.0 copy-done.3
  37.8 1.3 copy.32
  39.0 1.9 copy.33
  41.4 1.3 copy.34
  42.7 49.1 %psum.7 = f32[3456]{0:T(1024)} all-reduce(f32[3456]{0:T(1024)S(1)} %broadcast_multiply_fusion), channel_id=1, replica_groups=mesh['table'=4,'rep'=8] {'table','rep'}, use_global_device_ids=true, to_apply=%region_2.3 | all-reduce | flops 3456 | bytes 27648 | tf_op jit(solution)/shard_map/psum | solution.py:78
  91.8 15.0 %all_gather.3 = bf16[2,512,256]{2,1,0:T(8,128)(2,1)S(1)} all-gather(bf16[2,128,256]{2,1,0:T(8,128)(2,1)S(1)} %pad_maximum_fusion.1), channel_id=1, replica_groups=mesh['table'=4,'rep'=8] {'table'}, dimensions={1}, use_global_device_ids=true | all-gather | bytes 655360 | tf_op jit(solution)/shard_map/all_gather | solution.py:71
  106.9 4.2 %all-to-all-start.2 = ((bf16[4,7,128,128]{3,2,1,0:T(8,128)(2,1)}), bf16[4,7,128,128]{3,2,1,0:T(8,128)(2,1)}, u32[]{:S(2)}, u32[]{:S(2)}) async-start(bf16[4,7,128,128]{3,2,1,0:T(8,128)(2,1)} %bitcast.20), calls=%async_computation.2 | async-start | bytes 1835008 | tf_op jit(solution)/shard_map/all_to_all | solution.py:58
  111.2 0.6 fusion.33
  111.8 1.7 copy.27
  113.5 1.3 fusion.32
  114.8 1.5 copy.29
  116.4 2.2 %copy.28 = bf16[1,4,128,864]{3,2,1,0:T(8,128)(2,1)} copy(bf16[1,4,128,864]{2,3,1,0:T(8,128)(2,1)} %get-tuple-element.19) | data formatting | bytes 1769472 | tf_op jit(solution)/shard_map/slice | solution.py:72
  119.1 0.7 copy-done.4
  120.4 2.4 %copy.30 = f32[256,2,864]{2,1,0:T(2,128)} copy(f32[256,2,864]{0,2,1:T(8,128)S(1)} %maximum_multiply_fusion) | data formatting | bytes 3538944 | tf_op jit(solution)/shard_map/mul | solution.py:75
  122.9 0.7 copy-done.6
  123.6 8.7 %all-to-all-done.2 = bf16[4,7,128,128]{3,2,1,0:T(8,128)(2,1)} async-done(((bf16[4,7,128,128]{3,2,1,0:T(8,128)(2,1)}), bf16[4,7,128,128]{3,2,1,0:T(8,128)(2,1)}, u32[]{:S(2)}, u32[]{:S(2)}) %all-to-all-start.2) | async-done | bytes 917536 | tf_op jit(solution)/shard_map/all_to_all | solution.py:58
  132.3 1.3 copy.35
  133.6 4.9 %fusion.21 = f32[1,7,512,128]{3,2,1,0:T(8,128)} fusion(bf16[7,512,128]{2,1,0:T(8,128)(2,1)S(1)} %bitcast.70, s32[7,512]{1,0:T(8,128)S(1)} %get-tuple-element.27, s32[7,512]{1,0:T(8,128)S(1)} %get-tuple-element.28, s32[7,512]{1,0:T(8,128)S(1)} %get-tuple-element.29, s32[7,512]{1,0:T(8,128)S(1)} %get-tuple-element.30), kind=kOutput, calls=%fused_computation.27 | convolution fusion | flops 499122176 | bytes 2809856 | tf_op jit(solution)/shard_map/ksr,ksc->krc/dot_general | solution.py:65
  138.5 47.5 %all-reduce.3.cloned.1.call-done = f32[256,2,864]{2,1,0:T(2,128)} async-done(((f32[256,2,864]{2,1,0:T(2,128)}), f32[256,2,864]{2,1,0:T(2,128)}) %all-reduce.3.cloned.1.call-update) | async-done | bytes 1769488
  185.9 1.2 constant_dynamic-slice_fusion.1
  187.2 0.7 copy_bitcast_fusion
  (42 shorter events, 4.5 us)
Async XLA Ops:
  7.2 25.9 %copy-start = (bf16[256,3456]{1,0:T(8,128)(2,1)S(1)}, bf16[256,3456]{1,0:T(8,128)(2,1)}, u32[]{:S(2)}) copy-start(bf16[256,3456]{1,0:T(8,128)(2,1)} %param.11) | copy-start | bytes 5308420
  9.7 7.7 %copy-start.1 = (bf16[128,3456]{1,0:T(8,128)(2,1)S(1)}, bf16[128,3456]{1,0:T(8,128)(2,1)}, u32[]{:S(2)}) copy-start(bf16[128,3456]{1,0:T(8,128)(2,1)} %param.8) | copy-start | bytes 2654212
  11.1 14.6 %all-to-all-start.1 = ((s32[4,7,128,4]{2,3,1,0:T(4,128)}), s32[4,7,128,4]{2,3,1,0:T(4,128)S(1)}, u32[]{:S(2)}, u32[]{:S(2)}) async-start(s32[4,7,128,4]{2,3,1,0:T(4,128)} %bitcast.15), calls=%async_computation.1 | async-start | bytes 114688 | tf_op jit(solution)/shard_map/all_to_all | solution.py:59
  25.7 81.1 %all-to-all-start = ((bf16[2,128,3456]{1,0,2:T(2,128)(2,1)}), bf16[2,128,3456]{1,0,2:T(2,128)(2,1)}, u32[]{:S(2)}, u32[]{:S(2)}) async-start(bf16[2,128,3456]{1,0,2:T(2,128)(2,1)} %copy.26), calls=%async_computation | async-start | bytes 3538944 | tf_op jit(solution)/shard_map/all_to_all | solution.py:67
  30.8 2.3 %copy-start.2 = (bf16[128,3456]{1,0:T(8,128)(2,1)S(1)}, bf16[128,3456]{1,0:T(8,128)(2,1)}, u32[]{:S(2)}) copy-start(bf16[128,3456]{1,0:T(8,128)(2,1)} %param.9) | copy-start | bytes 2654212
  33.1 0.8 copy-start.8
  33.9 1.5 copy-start.3
  35.8 0.7 copy-start.10
  37.7 3.2 %copy-start.9 = (s32[26]{0:T(128)S(1)}, s32[26]{0:T(128)}, u32[]{:S(2)}) copy-start(s32[26]{0:T(128)} %param.15) | copy-start | bytes 316
  106.9 25.4 %all-to-all-start.2 = ((bf16[4,7,128,128]{3,2,1,0:T(8,128)(2,1)}), bf16[4,7,128,128]{3,2,1,0:T(8,128)(2,1)}, u32[]{:S(2)}, u32[]{:S(2)}) async-start(bf16[4,7,128,128]{3,2,1,0:T(8,128)(2,1)} %bitcast.20), calls=%async_computation.2 | async-start | bytes 1835008 | tf_op jit(solution)/shard_map/all_to_all | solution.py:58
  111.1 74.8 %all-reduce.3.cloned.1.call-start = ((), (), s32[]{:S(2)}) async-start(), calls=%async_computation.3 | async-start | bytes 3670016
  118.6 1.2 copy-start.4
  122.8 0.7 copy-start.6
  122.9 0.7 copy-start.7
  122.9 0.7 copy-start.5
Sparse Core Ops, SparseCore 0:
  123.0 62.8 all-reduce.2
where the time goes:
time: 196 us; the launch traced here: 195 us
  blocking collectives  64.1 us (33%)
  waiting for transfers between devices  56.2 us (29%)
  local copies, waits for them, and re-layouts  27.4 us (14%)
  starting transfers between devices  15.7 us (8%)
  between operations  14.9 us (8%)
  matrix products  10.2 us (5%)
  other arithmetic  6.25 us (3%)
    psum x1, blocking collectives, body(): bias_grad = lax.psum(jnp.sum(scaled, axis=0) * scale, ('table', 'rep'))  49.1 us
    unnamed x2, waiting for transfers between devices  47.5 us
    all_gather x1, blocking collectives, body(): piece = lax.all_gather(factors, 'table', axis=1, tiled=True)  15 us
    all_to_all x1, waiting for transfers between devices, body(): lax.all_to_all(grads, 'table', split_axis=0, concat_axis=2, tiled=True)  8.72 us
    all_to_all x1, starting transfers between devices, body(): lax.all_to_all(row_ids, 'table', split_axis=0, concat_axis=2, tiled=True)  6.32 us
    another operation x1, local copies, waits for them, and re-layouts, body(): jnp.stack([scaled_b, activations])  5.48 us
    all_to_all x1, starting transfers between devices, body(): lax.all_to_all(jnp.stack([scaled_b, activations]), 'table', split_axis=2,...  5.09 us
    dot_general x1, matrix products, body(): jnp.einsum('ksr,ksc->krc', count, grad_items, preferred_element_type=jnp....  4.87 us
  transfers between devices with their start and end apart: 4, of which 2 were waited for; matrix products, arithmetic and copies ran while one was open for 18% of the time, Pallas kernels for 0%

commit v1 on v0

v1 whole, which is shorter than its diff:
```python
import functools
import math

import jax
import jax.numpy as jnp
from jax import lax
from jax.experimental import pallas as pl
from jax.experimental.pallas import tpu as pltpu
from jax.sharding import PartitionSpec as P

EMBED_WIDTH = 128
SPARSE_FEATURES = 26
BAG = 4
TABLE_REACH_ROWS = 512
F32 = jnp.float32
BF16 = jnp.bfloat16
VMEM_LIMIT = 48 * 1024 * 1024


def column_chunk(width):
    blocks = width // EMBED_WIDTH
    for parts in (3, 2, 1):
        if blocks % parts == 0:
            return width // parts


def params(*semantics):
    return pltpu.CompilerParams(
        dimension_semantics=semantics or None, vmem_limit_bytes=VMEM_LIMIT
    )


def order_matrix(rep_index, size, block, bits):
    out_row = lax.broadcasted_iota(jnp.int32, (size, size), 0)
    in_row = lax.broadcasted_iota(jnp.int32, (size, size), 1)
    source = out_row % block
    position = out_row // block
    for place, bit in enumerate(bits):
        flag = (position // (1 << (len(bits) - 1 - place))) % 2
        own = (rep_index // bit) % 2
        source = source + jnp.where(flag == own, 0, bit) * block
    return (source == in_row).astype(F32).astype(BF16)


def hidden_kernel(
    up_bits, down_bits, rep_ref, act_ref, cot_ref, dw_ref, uw_ref,
    hidden_ref, back_ref, keep_ref, send_ref, hidden_acc, back_acc,
):
    step = pl.program_id(0)

    @pl.when(step == 0)
    def _():
        hidden_acc[...] = jnp.zeros_like(hidden_acc)
        back_acc[...] = jnp.zeros_like(back_acc)

    act = act_ref[...]
    scaled_b = (cot_ref[...].astype(F32) * act.astype(F32)).astype(BF16)
    dims = (((1,), (1,)), ((), ()))
    hidden_acc[...] += lax.dot_general(act, dw_ref[...], dims, preferred_element_type=F32)
    back_acc[...] += lax.dot_general(scaled_b, uw_ref[...], dims, preferred_element_type=F32)

    @pl.when(step == pl.num_programs(0) - 1)
    def _():
        hidden = hidden_acc[...].astype(BF16)
        back = back_acc[...].astype(BF16)
        hidden_ref[...] = hidden
        back_ref[...] = back
        rank = hidden.shape[1]
        half = rank // 2
        block = rank >> len(up_bits)
        for which, (value, bits) in enumerate(((hidden, up_bits), (back, down_bits))):
            order = order_matrix(rep_ref[0], rank, block, bits)
            rows = lax.dot_general(order, value, dims, preferred_element_type=F32).astype(BF16)
            keep_ref[which] = rows[:half]
            send_ref[which] = rows[half:]


def hidden_call(act, cot, dw, uw, rep_index, up_bits, down_bits):
    tokens, width = act.shape
    rank = dw.shape[0]
    chunk = column_chunk(width)
    wide = pl.BlockSpec((tokens, chunk), lambda i: (0, i))
    weight = pl.BlockSpec((rank, chunk), lambda i: (0, i))
    factor = pl.BlockSpec((tokens, rank), lambda i: (0, 0))
    rows = pl.BlockSpec((2, rank // 2, tokens), lambda i: (0, 0, 0))
    return pl.pallas_call(
        functools.partial(hidden_kernel, up_bits, down_bits),
        grid=(width // chunk,),
        in_specs=[pl.BlockSpec(memory_space=pltpu.SMEM), wide, wide, weight, weight],
        out_specs=[factor, factor, rows, rows],
        out_shape=[
            jax.ShapeDtypeStruct((tokens, rank), BF16),
            jax.ShapeDtypeStruct((tokens, rank), BF16),
            jax.ShapeDtypeStruct((2, rank // 2, tokens), BF16),
            jax.ShapeDtypeStruct((2, rank // 2, tokens), BF16),
        ],
        scratch_shapes=[pltpu.VMEM((tokens, rank), F32), pltpu.VMEM((tokens, rank), F32)],
        compiler_params=params("arbitrary"),
        cost_estimate=pl.CostEstimate(
            flops=4 * tokens * rank * width, bytes_accessed=4 * (tokens + rank) * width, transcendentals=0
        ),
    )(rep_index, act, cot, dw, uw)


def grad_kernel(
    n_table, slots, feature_ref, hidden_ref, back_ref, cot_ref, dw_ref, uw_ref, bias_ref, dense_ref, *rest
):
    outs, store = rest[:n_table], rest[n_table]
    step = pl.program_id(0)
    blocks = cot_ref.shape[1] // EMBED_WIDTH
    mixed = jnp.dot(hidden_ref[...], uw_ref[...], preferred_element_type=F32) + bias_ref[...]
    grad = cot_ref[...].astype(F32) * (1.0 + mixed) + jnp.dot(
        back_ref[...], dw_ref[...], preferred_element_type=F32
    )
    grad = grad.astype(BF16)
    for block in range(blocks):
        store[step * blocks + block] = grad[:, block * EMBED_WIDTH : (block + 1) * EMBED_WIDTH]

    @pl.when(step == pl.num_programs(0) - 1)
    def _():
        store[SPARSE_FEATURES + 1] = jnp.zeros(store.shape[1:], BF16)
        dense_ref[...] = store[0]
        for shift in range(n_table):
            for slot in range(slots):
                outs[shift][slot] = store[feature_ref[shift * slots + slot] + 1]


def grad_call(features, hidden, back, cot, dw, uw, bias, n_table, slots):
    tokens, width = cot.shape
    rank = dw.shape[0]
    chunk = column_chunk(width)
    factor = pl.BlockSpec((tokens, rank), lambda i: (0, 0))
    weight = pl.BlockSpec((rank, chunk), lambda i: (0, i))
    part = pl.BlockSpec((slots, tokens, EMBED_WIDTH), lambda i: (0, 0, 0))
    return pl.pallas_call(
        functools.partial(grad_kernel, n_table, slots),
        grid=(width // chunk,),
        in_specs=[
            pl.BlockSpec(memory_space=pltpu.SMEM),
            factor,
            factor,
            pl.BlockSpec((tokens, chunk), lambda i: (0, i)),
            weight,
            weight,
            pl.BlockSpec((1, chunk), lambda i: (0, i)),
        ],
        out_specs=[pl.BlockSpec((tokens, EMBED_WIDTH), lambda i: (0, 0))] + [part] * n_table,
        out_shape=[jax.ShapeDtypeStruct((tokens, EMBED_WIDTH), BF16)]
        + [jax.ShapeDtypeStruct((slots, tokens, EMBED_WIDTH), BF16)] * n_table,
        scratch_shapes=[pltpu.VMEM((SPARSE_FEATURES + 2, tokens, EMBED_WIDTH), BF16)],
        compiler_params=params("arbitrary"),
        cost_estimate=pl.CostEstimate(
            flops=4 * tokens * rank * width, bytes_accessed=4 * (tokens + rank) * width, transcendentals=0
        ),
    )(features, hidden, back, cot, dw, uw, bias.reshape(1, width))


def ids_kernel(n_table, slots, feature_ref, ids_ref, length_ref, *outs):
    entries = lax.broadcasted_iota(jnp.int32, ids_ref.shape[1:], 0)
    for shift in range(n_table):
        for slot in range(slots):
            feature = feature_ref[shift * slots + slot]
            at = jnp.minimum(feature, SPARSE_FEATURES - 1)
            length = jnp.where(feature < SPARSE_FEATURES, length_ref[at], 0)
            outs[shift][slot] = jnp.where(entries < length, ids_ref[at], -1)


def ids_call(features, bag_ids, bag_lengths, n_table, slots):
    tokens = bag_ids.shape[0]
    ids = jnp.transpose(bag_ids, (1, 2, 0))
    lengths = jnp.transpose(bag_lengths, (1, 0))[:, None, :]
    vmem = pl.BlockSpec(memory_space=pltpu.VMEM)
    return pl.pallas_call(
        functools.partial(ids_kernel, n_table, slots),
        in_specs=[pl.BlockSpec(memory_space=pltpu.SMEM), vmem, vmem],
        out_specs=[vmem] * n_table,
        out_shape=[jax.ShapeDtypeStruct((slots, BAG, tokens), jnp.int32)] * n_table,
        compiler_params=params(),
    )(features, ids, lengths)


def terms_kernel(
    keep_ref, other_ref, act_ref, act_other_ref, cot_ref, cot_other_ref,
    up_keep_ref, up_send_ref, down_keep_ref, down_send_ref, bias_ref,
):
    act = jnp.concatenate([act_ref[...], act_other_ref[...]], axis=0)
    cot = jnp.concatenate([cot_ref[...], cot_other_ref[...]], axis=0)
    scaled = cot.astype(F32) * act.astype(F32)
    bias_ref[...] = jnp.sum(scaled, axis=0, keepdims=True)
    hidden = jnp.concatenate([keep_ref[0], other_ref[0]], axis=1)
    back = jnp.concatenate([keep_ref[1], other_ref[1]], axis=1)
    up = jnp.dot(hidden, scaled.astype(BF16), preferred_element_type=F32)
    down = jnp.dot(back, act, preferred_element_type=F32)
    half = up.shape[0] // 2
    up_keep_ref[...] = up[:half]
    up_send_ref[...] = up[half:].astype(BF16)
    down_keep_ref[...] = down[:half]
    down_send_ref[...] = down[half:].astype(BF16)


def terms_call(keep, other, act, act_other, cot, cot_other):
    tokens, width = act.shape
    rows = keep.shape[1]
    chunk = column_chunk(width)
    factor = pl.BlockSpec(keep.shape, lambda i: (0, 0, 0))
    wide = pl.BlockSpec((tokens, chunk), lambda i: (0, i))
    half = pl.BlockSpec((rows // 2, chunk), lambda i: (0, i))
    return pl.pallas_call(
        terms_kernel,
        grid=(width // chunk,),
        in_specs=[factor, factor, wide, wide, wide, wide],
        out_specs=[half, half, half, half, pl.BlockSpec((1, chunk), lambda i: (0, i))],
        out_shape=[
            jax.ShapeDtypeStruct((rows // 2, width), F32),
            jax.ShapeDtypeStruct((rows // 2, width), BF16),
            jax.ShapeDtypeStruct((rows // 2, width), F32),
            jax.ShapeDtypeStruct((rows // 2, width), BF16),
            jax.ShapeDtypeStruct((1, width), F32),
        ],
        compiler_params=params("arbitrary"),
        cost_estimate=pl.CostEstimate(
            flops=8 * tokens * rows * width, bytes_accessed=8 * tokens * width + 6 * rows * width, transcendentals=0
        ),
    )(keep, other, act, act_other, cot, cot_other)


def split_kernel(
    n_table, scale, table_ref, up_keep_ref, up_in_ref, down_keep_ref, down_in_ref, own_ref, *rest
):
    sends, store = rest[: n_table - 1], rest[n_table - 1]
    columns = own_ref.shape[2]
    pairs = ((up_keep_ref, up_in_ref), (down_keep_ref, down_in_ref))
    for which, (keep, arrived) in enumerate(pairs):
        total = (keep[...] + arrived[...].astype(F32)) * scale
        for table in range(n_table):
            store[table, which] = total[:, table * columns : (table + 1) * columns]
    own_ref[...] = store[table_ref[0]]
    for shift in range(1, n_table):
        sends[shift - 1][...] = store[(table_ref[0] + shift) % n_table].astype(BF16)


def split_call(table_index, up_keep, up_in, down_keep, down_in, n_table, scale):
    rows, width = up_keep.shape
    columns = width // n_table
    vmem = pl.BlockSpec(memory_space=pltpu.VMEM)
    return pl.pallas_call(
        functools.partial(split_kernel, n_table, scale),
        in_specs=[pl.BlockSpec(memory_space=pltpu.SMEM), vmem, vmem, vmem, vmem],
        out_specs=[vmem] * n_table,
        out_shape=[jax.ShapeDtypeStruct((2, rows, columns), F32)]
        + [jax.ShapeDtypeStruct((2, rows, columns), BF16)] * (n_table - 1),
        scratch_shapes=[pltpu.VMEM((n_table, 2, rows, columns), F32)],
        compiler_params=params(),
    )(table_index, up_keep, up_in, down_keep, down_in)


def rows_kernel(n_table, *refs):
    ids, grads, out_ref = refs[:n_table], refs[n_table : 2 * n_table], refs[2 * n_table]
    tokens = grads[0].shape[1]
    rows = lax.broadcasted_iota(jnp.int32, (TABLE_REACH_ROWS, tokens), 0)
    counts = []
    for source in range(n_table):
        count = jnp.zeros((TABLE_REACH_ROWS, tokens), F32)
        for entry in range(BAG):
            count = count + jnp.where(ids[source][0, entry : entry + 1, :] == rows, 1.0, 0.0)
        counts.append(count.astype(BF16))
    count = jnp.concatenate(counts, axis=1)
    grad = jnp.concatenate([grad_ref[0] for grad_ref in grads], axis=0)
    out_ref[0, 0] = jnp.dot(count, grad, preferred_element_type=F32)


def rows_call(ids, grads):
    n_table = len(ids)
    slots, _, tokens = ids[0].shape
    id_spec = pl.BlockSpec((1, BAG, tokens), lambda i: (i, 0, 0))
    grad_spec = pl.BlockSpec((1, tokens, EMBED_WIDTH), lambda i: (i, 0, 0))
    return pl.pallas_call(
        functools.partial(rows_kernel, n_table),
        grid=(slots,),
        in_specs=[id_spec] * n_table + [grad_spec] * n_table,
        out_specs=pl.BlockSpec((1, 1, TABLE_REACH_ROWS, EMBED_WIDTH), lambda i: (0, i, 0, 0)),
        out_shape=jax.ShapeDtypeStruct((1, slots, TABLE_REACH_ROWS, EMBED_WIDTH), F32),
        compiler_params=params("arbitrary"),
        cost_estimate=pl.CostEstimate(
            flops=2 * slots * n_table * tokens * TABLE_REACH_ROWS * EMBED_WIDTH,
            bytes_accessed=4 * slots * TABLE_REACH_ROWS * EMBED_WIDTH,
            transcendentals=0,
        ),
    )(*ids, *grads)


def body(
    activations, cotangent, down_weight, up_weight, bias, bag_ids, bag_lengths, feature_table_slot
):
    tokens = activations.shape[0]
    n_table = lax.axis_size("table")
    n_rep = lax.axis_size("rep")
    slots = (SPARSE_FEATURES + n_table - 1) // n_table
    scale = 1.0 / math.sqrt(tokens * n_table * n_rep)
    table_index = lax.axis_index("table").astype(jnp.int32)
    rep_index = lax.axis_index("rep").astype(jnp.int32)
    far_bits = [1 << k for k in range(1, n_rep.bit_length() - 1)]
    up_bits, down_bits = [1] + far_bits, [1] + far_bits[::-1]

    def swap(value, axis, bit):
        size = n_rep if axis == "rep" else n_table
        return lax.ppermute(value, axis, [(k, k ^ bit) for k in range(size)])

    def shifted(value, shift):
        return lax.ppermute(value, "table", [(k, (k + shift) % n_table) for k in range(n_table)])

    act_other = swap(activations, "rep", 1)
    cot_other = swap(cotangent, "rep", 1)

    owners = (table_index + jnp.arange(n_table, dtype=jnp.int32)) % n_table
    wanted = (owners[:, None] * slots + jnp.arange(slots, dtype=jnp.int32)[None, :]).reshape(-1)
    matches = feature_table_slot[None, :] == wanted[:, None]
    numbers = jnp.arange(SPARSE_FEATURES, dtype=jnp.int32)
    features = jnp.min(jnp.where(matches, numbers[None, :], SPARSE_FEATURES), axis=1)

    id_parts = ids_call(features, bag_ids, bag_lengths, n_table, slots)
    id_parts = [id_parts[0]] + [shifted(id_parts[k], k) for k in range(1, n_table)]

    hidden, back, keep, send = hidden_call(
        activations, cotangent, down_weight, up_weight, rep_index.reshape(1), up_bits, down_bits
    )
    other = swap(send, "rep", 1)
    dense_grad, *grad_parts = grad_call(
        features, hidden, back, cotangent, down_weight, up_weight, bias, n_table, slots
    )
    grad_parts = [grad_parts[0]] + [shifted(grad_parts[k], k) for k in range(1, n_table)]

    up_keep, up_send, down_keep, down_send, bias_sum = terms_call(
        keep, other, activations, act_other, cotangent, cot_other
    )
    for place, (up_bit, down_bit) in enumerate(zip(up_bits[1:], down_bits[1:])):
        up_in = swap(up_send, "rep", up_bit)
        down_in = swap(down_send, "rep", down_bit)
        bias_sum = bias_sum + swap(bias_sum, "rep", up_bit)
        if place < len(far_bits) - 1:
            half = up_keep.shape[0] // 2
            up = up_keep + up_in.astype(F32)
            down = down_keep + down_in.astype(F32)
            up_keep, up_send = up[:half], up[half:].astype(BF16)
            down_keep, down_send = down[:half], down[half:].astype(BF16)
    bit = 1
    while bit < n_table:
        bias_sum = bias_sum + swap(bias_sum, "table", bit)
        bit *= 2
    bias_grad = bias_sum.reshape(-1) * scale
    total, *sends = split_call(
        table_index.reshape(1), up_keep, up_in, down_keep, down_in, n_table, scale
    )
    arrived = [shifted(value, k + 1) for k, value in enumerate(sends)]
    total = functools.reduce(lambda a, b: a + b.astype(F32), arrived, total)
    up_grad, down_grad = total[0], total[1]
    row_grad = rows_call(id_parts, grad_parts)
    return (dense_grad, up_grad, down_grad, bias_grad, row_grad)


def solution(mesh):
    placed = (
        P(("table", "rep"), None),
        P(("table", "rep"), None),
        P(),
        P(),
        P(),
        P(("table", "rep"), None, None),
        P(("table", "rep"), None),
        P(),
    )
    return jax.shard_map(
        body,
        mesh=mesh,
        in_specs=placed,
        out_specs=(
            P(("table", "rep"), None),
            P("rep", "table"),
            P("rep", "table"),
            P(),
            P("rep", "table", None, None),
        ),
        check_vma=False,
    )
```

time: 196 us -> 85.9 us (0.44)
  blocking collectives: 64.1 us -> 0 us
  waiting for transfers between devices: 56.2 us -> 18.7 us
  Pallas kernels: 0 us -> 14.8 us
  starting transfers between devices: 15.7 us -> 30.1 us
  between operations: 14.9 us -> 0.86 us
  matrix products: 10.2 us -> 0 us
  local copies, waits for them, and re-layouts: 27.4 us -> 18.9 us
  other arithmetic: 6.25 us -> 1.85 us
    psum x1 -> x0, blocking collectives: 49.1 us -> none  [body(): bias_grad = lax.psum(jnp.sum(scaled, axis=0) * scale, ('table', 'rep'))]
    unnamed x2 -> x0, waiting for transfers between devices: 47.5 us -> none
    ppermute x0 -> x20, starting transfers between devices: none -> 30.1 us  [the longest x9 17.4 us: shifted(): lax.ppermute(value, 'table', [(k, (k + shift) % n_table) for k in range(n...]
    ppermute x0 -> x20, waiting for transfers between devices: none -> 18.7 us  [the longest x9 16.1 us: shifted(): lax.ppermute(value, 'table', [(k, (k + shift) % n_table) for k in range(n...]
    all_to_all x3 -> x0, starting transfers between devices: 15.6 us -> none  [the longest x1 6.32 us: body(): lax.all_to_all(row_ids, 'table', split_axis=0, concat_axis=2, tiled=True)]
    all_gather x1 -> x0, blocking collectives: 15 us -> none  [body(): piece = lax.all_gather(factors, 'table', axis=1, tiled=True)]
    pallas_call x0 -> x6, Pallas kernels: none -> 14.8 us  [the longest x1 5.03 us: rows_call(): pl.pallas_call(functools.partial(rows_kernel, n_table), grid=(slots,), in...]
    unnamed x26 -> x52, local copies, waits for them, and re-layouts: 3.72 us -> 17.3 us
  transfers between devices with their start and end apart: 4 -> 20, of which waited for: 2 -> 8; matrix products, arithmetic and copies ran while one was open for 18% -> 3% of each run, Pallas kernels for 0% -> 13%
where the time goes in v1:
time: 85.9 us; the launch traced here: 85.2 us
  starting transfers between devices  30.1 us (35%)
  local copies, waits for them, and re-layouts  18.9 us (22%)
  waiting for transfers between devices  18.7 us (22%)
  Pallas kernels  14.8 us (17%)
  other arithmetic  1.85 us (2%)
  between operations  0.86 us (1%)
    ppermute x9, starting transfers between devices, shifted(): lax.ppermute(value, 'table', [(k, (k + shift) % n_table) for k in range(n...  17.4 us
    unnamed x52, local copies, waits for them, and re-layouts  17.3 us
    ppermute x9, waiting for transfers between devices, shifted(): lax.ppermute(value, 'table', [(k, (k + shift) % n_table) for k in range(n...  16.1 us
    ppermute x11, starting transfers between devices, swap(): return lax.ppermute(value, axis, [(k, k ^ bit) for k in range(size)])  12.6 us
    pallas_call x1, Pallas kernels, rows_call(): pl.pallas_call(functools.partial(rows_kernel, n_table), grid=(slots,), in...  5.03 us
    pallas_call x1, Pallas kernels, terms_call(): pl.pallas_call(terms_kernel, grid=(width // chunk,), in_specs=[factor, fa...  3.86 us
    pallas_call x1, Pallas kernels, grad_call(): pl.pallas_call(functools.partial(grad_kernel, n_table, slots), grid=(widt...  2.61 us
    ppermute x11, waiting for transfers between devices, swap(): return lax.ppermute(value, axis, [(k, k ^ bit) for k in range(size)])  2.52 us
  transfers between devices with their start and end apart: 20, of which 8 were waited for; matrix products, arithmetic and copies ran while one was open for 3% of the time, Pallas kernels for 13%

profile of v1, /device:TPU:0, one launch (start us, length us, event | category | flops | bytes accessed | tf_op | source)
XLA Modules:
  0.0 85.2 jit_solution(7338803058416027207)
XLA Ops:
  1.2 1.2 %copy-done = bf16[128,3456]{1,0:T(8,128)(2,1)S(1)} copy-done((bf16[128,3456]{1,0:T(8,128)(2,1)S(1)}, bf16[128,3456]{1,0:T(8,128)(2,1)}, u32[]{:S(2)}) %copy-start) | copy-done | bytes 884760
  2.4 1.5 %copy-done.2 = bf16[256,3456]{1,0:T(8,128)(2,1)S(1)} copy-done((bf16[256,3456]{1,0:T(8,128)(2,1)S(1)}, bf16[256,3456]{1,0:T(8,128)(2,1)}, u32[]{:S(2)}) %copy-start.2) | copy-done | bytes 1769496
  3.9 1.5 %copy-done.4 = bf16[256,3456]{1,0:T(8,128)(2,1)S(1)} copy-done((bf16[256,3456]{1,0:T(8,128)(2,1)S(1)}, bf16[256,3456]{1,0:T(8,128)(2,1)}, u32[]{:S(2)}) %copy-start.4) | copy-done | bytes 1769496
  5.4 1.2 %copy-done.6 = bf16[128,3456]{1,0:T(8,128)(2,1)S(1)} copy-done((bf16[128,3456]{1,0:T(8,128)(2,1)S(1)}, bf16[128,3456]{1,0:T(8,128)(2,1)}, u32[]{:S(2)}) %copy-start.6) | copy-done | bytes 884760
  6.5 2.4 %shard_map.119 = (bf16[128,256]{1,0:T(8,128)(2,1)S(1)}, bf16[128,256]{1,0:T(8,128)(2,1)S(1)}, bf16[2,128,128]{2,1,0:T(8,128)(2,1)S(1)}, bf16[2,128,128]{2,1,0:T(8,128)(2,1)S(1)}) custom-call(s32[1]{0:T(128)} %bitcast.rep_ref, bf16[128,3456]{1,0:T(8,128)(2,1)S(1)} %copy-done.6, bf16[128,3456]{1,0:T(8,128)(2,1)S(1)} %copy-done, ...), custom_call_target="tpu_custom_call" | custom-call | flops 452984832 | bytes 5308416 | tf_op jit(solution)/shard_map/pallas_call | solution.py:86
  11.2 0.9 %collective-permute-done.other_ref = bf16[2,128,128]{2,1,0:T(8,128)(2,1)S(1)} collective-permute-done((bf16[2,128,128]{2,1,0:T(8,128)(2,1)S(1)}, bf16[2,128,128]{2,1,0:T(8,128)(2,1)S(1)}, u32[]{:S(2)}, u32[]{:S(2)}) %collective-permute-start) | collective-permute-done | bytes 65568 | tf_op jit(solution)/shard_map/ppermute | solution.py:307
  12.8 0.9 %copy-done.8 = bf16[128,3456]{1,0:T(8,128)(2,1)} copy-done((bf16[128,3456]{1,0:T(8,128)(2,1)}, bf16[128,3456]{1,0:T(8,128)(2,1)S(1)}, u32[]{:S(2)}) %copy-start.8) | copy-done | bytes 884760
  13.7 1.2 %copy-done.9 = bf16[128,3456]{1,0:T(8,128)(2,1)S(1)} copy-done((bf16[128,3456]{1,0:T(8,128)(2,1)S(1)}, bf16[128,3456]{1,0:T(8,128)(2,1)}, u32[]{:S(2)}) %copy-start.9) | copy-done | bytes 884760
  16.5 3.9 %shard_map.121 = (f32[64,3456]{1,0:T(8,128)S(1)}, bf16[64,3456]{1,0:T(8,128)(2,1)S(1)}, f32[64,3456]{1,0:T(8,128)S(1)}, bf16[64,3456]{1,0:T(8,128)(2,1)}, f32[1,3456]{1,0:T(1,128)S(1)}) custom-call(bf16[2,128,128]{2,1,0:T(8,128)(2,1)S(1)} %copy-done.19, bf16[2,128,128]{2,1,0:T(8,128)(2,1)S(1)} %copy-done.21, bf16[128,3456]{1,0:T(8,128)(2,1)S(1)} %copy-done.7, ...), custom_call_target="tpu_custom_call" | custom-call | flops 452984832 | bytes 6193152 | tf_op jit(solution)/shard_map/pallas_call | solution.py:208
  20.4 0.9 %copy-done.10 = f32[64,3456]{1,0:T(8,128)} copy-done((f32[64,3456]{1,0:T(8,128)}, f32[64,3456]{1,0:T(8,128)S(1)}, u32[]{:S(2)}) %copy-start.10) | copy-done | bytes 884760
  21.3 0.9 %copy-done.12 = f32[64,3456]{1,0:T(8,128)} copy-done((f32[64,3456]{1,0:T(8,128)}, f32[64,3456]{1,0:T(8,128)S(1)}, u32[]{:S(2)}) %copy-start.12) | copy-done | bytes 884760
  23.0 2.9 %collective-permute-start.5 = (bf16[64,3456]{1,0:T(8,128)(2,1)}, bf16[64,3456]{1,0:T(8,128)(2,1)S(1)}, u32[]{:S(2)}, u32[]{:S(2)}) collective-permute-start(bf16[64,3456]{1,0:T(8,128)(2,1)} %get-tuple-element.35), channel_id=1, source_target_pairs={{0,4},{1,5},{2,6},{3,7},{4,0},{5,1},{6,2},{7,3},{8,12},{9,13},{10,... | collective-permute-start | bytes 1327112 | tf_op jit(solution)/shard_map/ppermute | solution.py:307
  26.0 1.5 %collective-permute-start.10 = (f32[1,3456]{1,0:T(1,128)S(1)}, f32[1,3456]{1,0:T(1,128)S(1)}, u32[]{:S(2)}, u32[]{:S(2)}) collective-permute-start(f32[1,3456]{1,0:T(1,128)S(1)} %get-tuple-element.40), channel_id=1, source_target_pairs={{0,2},{1,3},{2,0},{3,1},{4,6},{5,7},{6,4},{7,5},{8,10},{9,11},{10,... | collective-permute-start | bytes 41480 | tf_op jit(solution)/shard_map/ppermute | solution.py:307
  29.9 1.5 %copy-done.5 = bf16[256,3456]{1,0:T(8,128)(2,1)S(1)} copy-done((bf16[256,3456]{1,0:T(8,128)(2,1)S(1)}, bf16[256,3456]{1,0:T(8,128)(2,1)}, u32[]{:S(2)}) %copy-start.5) | copy-done | bytes 1769496
  33.0 2.6 %shard_map.120 = (bf16[128,128]{1,0:T(8,128)(2,1)}, bf16[7,128,128]{2,1,0:T(8,128)(2,1)S(1)}, bf16[7,128,128]{2,1,0:T(8,128)(2,1)S(1)}, bf16[7,128,128]{2,1,0:T(8,128)(2,1)S(1)}, bf16[7,128,128]{2,1,0:T(8,128)(2,1)S(1)}) custom-call(s32[28]{0:T(128)S(1)} %select_reduce_fusion.feature_ref, bf16[128,256]{1,0:T(8,128)(2,1)S(1)} %copy-done.15, ...), custom_call_target="tpu_custom_call" | custom-call | flops 452984832 | bytes 5308416 | tf_op jit(solution)/shard_map/pallas_call | solution.py:135
  35.7 2.1 %collective-permute-start.17 = (bf16[7,128,128]{2,1,0:T(8,128)(2,1)S(1)}, bf16[7,128,128]{2,1,0:T(8,128)(2,1)S(1)}, u32[]{:S(2)}, u32[]{:S(2)}) collective-permute-start(bf16[7,128,128]{2,1,0:T(8,128)(2,1)S(1)} %get-tuple-element.46), channel_id=1, source_target_pairs={{0,8},{8,16},{16,24},{24,0},{1,9},{9,17},{17,25},{25,1},{2,10},{10... | collective-permute-start | bytes 688136 | tf_op jit(solution)/shard_map/ppermute | solution.py:310
  37.7 2.6 %collective-permute-start.18 = (bf16[7,128,128]{2,1,0:T(8,128)(2,1)S(1)}, bf16[7,128,128]{2,1,0:T(8,128)(2,1)S(1)}, u32[]{:S(2)}, u32[]{:S(2)}) collective-permute-start(bf16[7,128,128]{2,1,0:T(8,128)(2,1)S(1)} %get-tuple-element.47), channel_id=1, source_target_pairs={{0,16},{8,24},{16,0},{24,8},{1,17},{9,25},{17,1},{25,9},{2,18},{10... | collective-permute-start | bytes 688136 | tf_op jit(solution)/shard_map/ppermute | solution.py:310
  41.0 1.9 %collective-permute-start.15 = (s32[7,4,128]{2,1,0:T(4,128)S(1)}, s32[7,4,128]{2,1,0:T(4,128)S(1)}, u32[]{:S(2)}, u32[]{:S(2)}) collective-permute-start(s32[7,4,128]{2,1,0:T(4,128)S(1)} %get-tuple-element.43), channel_id=1, source_target_pairs={{0,16},{8,24},{16,0},{24,8},{1,17},{9,25},{17,1},{25,9},{2,18},{10... | collective-permute-start | bytes 43016 | tf_op jit(solution)/shard_map/ppermute | solution.py:310
  43.0 1.6 %collective-permute-start.3 = (bf16[64,3456]{1,0:T(8,128)(2,1)S(1)}, bf16[64,3456]{1,0:T(8,128)(2,1)S(1)}, u32[]{:S(2)}, u32[]{:S(2)}) collective-permute-start(bf16[64,3456]{1,0:T(8,128)(2,1)S(1)} %copy-done.24), channel_id=1, source_target_pairs={{0,2},{1,3},{2,0},{3,1},{4,6},{5,7},{6,4},{7,5},{8,10},{9,11},{10,... | collective-permute-start | bytes 1327112 | tf_op jit(solution)/shard_map/ppermute | solution.py:307
  44.6 5.0 %collective-permute-done.14.refs_1_ = s32[7,4,128]{2,1,0:T(4,128)S(1)} collective-permute-done((s32[7,4,128]{2,1,0:T(4,128)S(1)}, s32[7,4,128]{2,1,0:T(4,128)S(1)}, u32[]{:S(2)}, u32[]{:S(2)}) %collective-permute-start.14) | collective-permute-done | bytes 14368 | tf_op jit(solution)/shard_map/ppermute | solution.py:310
  49.7 5.3 %collective-permute-done.15.refs_2_ = s32[7,4,128]{2,1,0:T(4,128)S(1)} collective-permute-done((s32[7,4,128]{2,1,0:T(4,128)S(1)}, s32[7,4,128]{2,1,0:T(4,128)S(1)}, u32[]{:S(2)}, u32[]{:S(2)}) %collective-permute-start.15) | collective-permute-done | bytes 14368 | tf_op jit(solution)/shard_map/ppermute | solution.py:310
  54.9 7.0 %collective-permute-start.16 = (s32[7,4,128]{2,1,0:T(4,128)S(1)}, s32[7,4,128]{2,1,0:T(4,128)S(1)}, u32[]{:S(2)}, u32[]{:S(2)}) collective-permute-start(s32[7,4,128]{2,1,0:T(4,128)S(1)} %get-tuple-element.44), channel_id=1, source_target_pairs={{0,24},{8,0},{16,8},{24,16},{1,25},{9,1},{17,9},{25,17},{2,26},{10... | collective-permute-start | bytes 43016 | tf_op jit(solution)/shard_map/ppermute | solution.py:310
  62.1 1.2 %collective-permute-done.16.refs_3_ = s32[7,4,128]{2,1,0:T(4,128)S(1)} collective-permute-done((s32[7,4,128]{2,1,0:T(4,128)S(1)}, s32[7,4,128]{2,1,0:T(4,128)S(1)}, u32[]{:S(2)}, u32[]{:S(2)}) %collective-permute-start.16) | collective-permute-done | bytes 14368 | tf_op jit(solution)/shard_map/ppermute | solution.py:310
  63.3 1.3 %collective-permute-start.6 = (bf16[32,3456]{1,0:T(8,128)(2,1)S(1)}, bf16[32,3456]{1,0:T(8,128)(2,1)S(1)}, u32[]{:S(2)}, u32[]{:S(2)}) collective-permute-start(bf16[32,3456]{1,0:T(8,128)(2,1)S(1)} %slice.36), channel_id=1, source_target_pairs={{0,2},{1,3},{2,0},{3,1},{4,6},{5,7},{6,4},{7,5},{8,10},{9,11},{10,... | collective-permute-start | bytes 663560 | tf_op jit(solution)/shard_map/ppermute | solution.py:307
  64.7 0.9 %collective-permute-done.12 = f32[1,3456]{1,0:T(1,128)S(1)} collective-permute-done((f32[1,3456]{1,0:T(1,128)S(1)}, f32[1,3456]{1,0:T(1,128)S(1)}, u32[]{:S(2)}, u32[]{:S(2)}) %collective-permute-start.12) | collective-permute-done | bytes 13856 | tf_op jit(solution)/shard_map/ppermute | solution.py:307
  65.6 1.6 %collective-permute-start.4 = (bf16[32,3456]{1,0:T(8,128)(2,1)S(1)}, bf16[32,3456]{1,0:T(8,128)(2,1)S(1)}, u32[]{:S(2)}, u32[]{:S(2)}) collective-permute-start(bf16[32,3456]{1,0:T(8,128)(2,1)S(1)} %slice.37), channel_id=1, source_target_pairs={{0,4},{1,5},{2,6},{3,7},{4,0},{5,1},{6,2},{7,3},{8,12},{9,13},{10,... | collective-permute-start | bytes 663560 | tf_op jit(solution)/shard_map/ppermute | solution.py:307
  67.2 2.7 %collective-permute-start.13 = (f32[1,3456]{1,0:T(1,128)S(1)}, f32[1,3456]{1,0:T(1,128)S(1)}, u32[]{:S(2)}, u32[]{:S(2)}) collective-permute-start(f32[1,3456]{1,0:T(1,128)S(1)} %add.81), channel_id=1, source_target_pairs={{0,16},{8,24},{16,0},{24,8},{1,17},{9,25},{17,1},{25,9},{2,18},{10... | collective-permute-start | bytes 41480 | tf_op jit(solution)/shard_map/ppermute | solution.py:307
  69.9 5.0 %shard_map.124 = f32[1,7,512,128]{3,2,1,0:T(8,128)} custom-call(s32[7,4,128]{2,1,0:T(4,128)S(1)} %get-tuple-element.41.refs_0_, s32[7,4,128]{2,1,0:T(4,128)S(1)} %collective-permute-done.14.refs_1_, s32[7,4,128]{2,1,0:T(4,128)S(1)} %collective-permute-done.15.refs_2_, s32[7,4,128]{2,1,0:T(4,128)S(1)} %collective-permute-done.16.refs_3_, ...), custom_call_target="tpu_custom_call" | custom-call | flops 469762048 | bytes 1835008 | tf_op jit(solution)/shard_map/pallas_call | solution.py:277
  75.4 1.3 %collective-permute-start.7 = (bf16[2,32,864]{2,1,0:T(8,128)(2,1)S(1)}, bf16[2,32,864]{2,1,0:T(8,128)(2,1)S(1)}, u32[]{:S(2)}, u32[]{:S(2)}) collective-permute-start(bf16[2,32,864]{2,1,0:T(8,128)(2,1)S(1)} %get-tuple-element.37), channel_id=1, source_target_pairs={{0,8},{8,16},{16,24},{24,0},{1,9},{9,17},{17,25},{25,1},{2,10},{10... | collective-permute-start | bytes 331784 | tf_op jit(solution)/shard_map/ppermute | solution.py:310
  76.8 2.5 %collective-permute-start.9 = (bf16[2,32,864]{2,1,0:T(8,128)(2,1)S(1)}, bf16[2,32,864]{2,1,0:T(8,128)(2,1)S(1)}, u32[]{:S(2)}, u32[]{:S(2)}) collective-permute-start(bf16[2,32,864]{2,1,0:T(8,128)(2,1)S(1)} %get-tuple-element.39), channel_id=1, source_target_pairs={{0,24},{8,0},{16,8},{24,16},{1,25},{9,1},{17,9},{25,17},{2,26},{10... | collective-permute-start | bytes 331784 | tf_op jit(solution)/shard_map/ppermute | solution.py:310
  79.9 2.3 %collective-permute-done.7 = bf16[2,32,864]{2,1,0:T(8,128)(2,1)S(1)} collective-permute-done((bf16[2,32,864]{2,1,0:T(8,128)(2,1)S(1)}, bf16[2,32,864]{2,1,0:T(8,128)(2,1)S(1)}, u32[]{:S(2)}, u32[]{:S(2)}) %collective-permute-start.7) | collective-permute-done | bytes 110624 | tf_op jit(solution)/shard_map/ppermute | solution.py:310
  82.2 2.3 %collective-permute-done.8 = bf16[2,32,864]{2,1,0:T(8,128)(2,1)S(1)} collective-permute-done((bf16[2,32,864]{2,1,0:T(8,128)(2,1)S(1)}, bf16[2,32,864]{2,1,0:T(8,128)(2,1)S(1)}, u32[]{:S(2)}, u32[]{:S(2)}) %collective-permute-start.8) | collective-permute-done | bytes 110624 | tf_op jit(solution)/shard_map/ppermute | solution.py:310
  (84 shorter events, 13.0 us)
Async XLA Ops:
  0.6 12.1 %collective-permute-start.1 = (bf16[128,3456]{1,0:T(8,128)(2,1)}, bf16[128,3456]{1,0:T(8,128)(2,1)S(1)}, u32[]{:S(2)}, u32[]{:S(2)}) collective-permute-start(bf16[128,3456]{1,0:T(8,128)(2,1)} %act_ref.3), channel_id=1, source_target_pairs={{0,1},{1,0},{2,3},{3,2},{4,5},{5,4},{6,7},{7,6},{8,9},{9,8},{10,11... | collective-permute-start | bytes 2654216 | tf_op jit(solution)/shard_map/ppermute | solution.py:307
  1.1 12.5 %collective-permute-start.2 = (bf16[128,3456]{1,0:T(8,128)(2,1)}, bf16[128,3456]{1,0:T(8,128)(2,1)}, u32[]{:S(2)}, u32[]{:S(2)}) collective-permute-start(bf16[128,3456]{1,0:T(8,128)(2,1)} %cot_ref.5), channel_id=1, source_target_pairs={{0,1},{1,0},{2,3},{3,2},{4,5},{5,4},{6,7},{7,6},{8,9},{9,8},{10,11... | collective-permute-start | bytes 2654216 | tf_op jit(solution)/shard_map/ppermute | solution.py:307
  2.4 1.5 %copy-start.2 = (bf16[256,3456]{1,0:T(8,128)(2,1)S(1)}, bf16[256,3456]{1,0:T(8,128)(2,1)}, u32[]{:S(2)}) copy-start(bf16[256,3456]{1,0:T(8,128)(2,1)} %dw_ref.3) | copy-start | bytes 5308420
  3.9 1.5 %copy-start.4 = (bf16[256,3456]{1,0:T(8,128)(2,1)S(1)}, bf16[256,3456]{1,0:T(8,128)(2,1)}, u32[]{:S(2)}) copy-start(bf16[256,3456]{1,0:T(8,128)(2,1)} %uw_ref.3) | copy-start | bytes 5308420
  6.5 7.2 %copy-start.1 = (bf16[128,3456]{1,0:T(8,128)(2,1)S(1)}, bf16[128,3456]{1,0:T(8,128)(2,1)}, u32[]{:S(2)}) copy-start(bf16[128,3456]{1,0:T(8,128)(2,1)} %cot_ref.5) | copy-start | bytes 2654212
  6.5 7.2 %copy-start.7 = (bf16[128,3456]{1,0:T(8,128)(2,1)S(1)}, bf16[128,3456]{1,0:T(8,128)(2,1)}, u32[]{:S(2)}) copy-start(bf16[128,3456]{1,0:T(8,128)(2,1)} %act_ref.3) | copy-start | bytes 2654212
  10.8 1.3 %collective-permute-start = (bf16[2,128,128]{2,1,0:T(8,128)(2,1)S(1)}, bf16[2,128,128]{2,1,0:T(8,128)(2,1)S(1)}, u32[]{:S(2)}, u32[]{:S(2)}) collective-permute-start(bf16[2,128,128]{2,1,0:T(8,128)(2,1)S(1)} %get-tuple-element.31), channel_id=1, source_target_pairs={{0,1},{1,0},{2,3},{3,2},{4,5},{5,4},{6,7},{7,6},{8,9},{9,8},{10,11... | collective-permute-start | bytes 196616 | tf_op jit(solution)/shard_map/ppermute | solution.py:307
  13.7 1.2 %copy-start.9 = (bf16[128,3456]{1,0:T(8,128)(2,1)S(1)}, bf16[128,3456]{1,0:T(8,128)(2,1)}, u32[]{:S(2)}) copy-start(bf16[128,3456]{1,0:T(8,128)(2,1)} %copy-done.8) | copy-start | bytes 2654212
  16.5 13.3 %copy-start.3 = (bf16[256,3456]{1,0:T(8,128)(2,1)S(1)}, bf16[256,3456]{1,0:T(8,128)(2,1)}, u32[]{:S(2)}) copy-start(bf16[256,3456]{1,0:T(8,128)(2,1)} %dw_ref.3) | copy-start | bytes 5308420
  23.0 19.9 %collective-permute-start.5 = (bf16[64,3456]{1,0:T(8,128)(2,1)}, bf16[64,3456]{1,0:T(8,128)(2,1)S(1)}, u32[]{:S(2)}, u32[]{:S(2)}) collective-permute-start(bf16[64,3456]{1,0:T(8,128)(2,1)} %get-tuple-element.35), channel_id=1, source_target_pairs={{0,4},{1,5},{2,6},{3,7},{4,0},{5,1},{6,2},{7,3},{8,12},{9,13},{10,... | collective-permute-start | bytes 1327112 | tf_op jit(solution)/shard_map/ppermute | solution.py:307
  26.0 3.7 %collective-permute-start.10 = (f32[1,3456]{1,0:T(1,128)S(1)}, f32[1,3456]{1,0:T(1,128)S(1)}, u32[]{:S(2)}, u32[]{:S(2)}) collective-permute-start(f32[1,3456]{1,0:T(1,128)S(1)} %get-tuple-element.40), channel_id=1, source_target_pairs={{0,2},{1,3},{2,0},{3,1},{4,6},{5,7},{6,4},{7,5},{8,10},{9,11},{10,... | collective-permute-start | bytes 41480 | tf_op jit(solution)/shard_map/ppermute | solution.py:307
  29.8 11.2 %collective-permute-start.11 = (f32[1,3456]{1,0:T(1,128)S(1)}, f32[1,3456]{1,0:T(1,128)S(1)}, u32[]{:S(2)}, u32[]{:S(2)}) collective-permute-start(f32[1,3456]{1,0:T(1,128)S(1)} %add.79), channel_id=1, source_target_pairs={{0,4},{1,5},{2,6},{3,7},{4,0},{5,1},{6,2},{7,3},{8,12},{9,13},{10,... | collective-permute-start | bytes 41480 | tf_op jit(solution)/shard_map/ppermute | solution.py:307
  29.9 1.5 %copy-start.5 = (bf16[256,3456]{1,0:T(8,128)(2,1)S(1)}, bf16[256,3456]{1,0:T(8,128)(2,1)}, u32[]{:S(2)}) copy-start(bf16[256,3456]{1,0:T(8,128)(2,1)} %uw_ref.3) | copy-start | bytes 5308420
  33.0 7.3 %copy-start.25 = (s32[128,26]{0,1:T(8,128)S(1)}, s32[128,26]{0,1:T(8,128)}, u32[]{:S(2)}) copy-start(s32[128,26]{0,1:T(8,128)} %param.14) | copy-start | bytes 39940
  33.0 7.3 %copy-start.22 = (s32[128,26,4]{0,2,1:T(4,128)S(1)}, s32[128,26,4]{0,2,1:T(4,128)}, u32[]{:S(2)}) copy-start(s32[128,26,4]{0,2,1:T(4,128)} %param.13) | copy-start | bytes 159748
  33.0 9.9 %copy-start.24 = (bf16[64,3456]{1,0:T(8,128)(2,1)S(1)}, bf16[64,3456]{1,0:T(8,128)(2,1)}, u32[]{:S(2)}) copy-start(bf16[64,3456]{1,0:T(8,128)(2,1)} %copy-done.23) | copy-start | bytes 1327108
  33.0 11.5 %copy-start.13 = (f32[64,3456]{1,0:T(8,128)S(1)}, f32[64,3456]{1,0:T(8,128)}, u32[]{:S(2)}) copy-start(f32[64,3456]{1,0:T(8,128)} %copy-done.12) | copy-start | bytes 2654212
  35.7 26.3 %copy-start.11 = (f32[64,3456]{1,0:T(8,128)S(1)}, f32[64,3456]{1,0:T(8,128)}, u32[]{:S(2)}) copy-start(f32[64,3456]{1,0:T(8,128)} %copy-done.10) | copy-start | bytes 2654212
  35.7 31.6 %collective-permute-start.17 = (bf16[7,128,128]{2,1,0:T(8,128)(2,1)S(1)}, bf16[7,128,128]{2,1,0:T(8,128)(2,1)S(1)}, u32[]{:S(2)}, u32[]{:S(2)}) collective-permute-start(bf16[7,128,128]{2,1,0:T(8,128)(2,1)S(1)} %get-tuple-element.46), channel_id=1, source_target_pairs={{0,8},{8,16},{16,24},{24,0},{1,9},{9,17},{17,25},{25,1},{2,10},{10... | collective-permute-start | bytes 688136 | tf_op jit(solution)/shard_map/ppermute | solution.py:310
  37.7 32.2 %collective-permute-start.18 = (bf16[7,128,128]{2,1,0:T(8,128)(2,1)S(1)}, bf16[7,128,128]{2,1,0:T(8,128)(2,1)S(1)}, u32[]{:S(2)}, u32[]{:S(2)}) collective-permute-start(bf16[7,128,128]{2,1,0:T(8,128)(2,1)S(1)} %get-tuple-element.47), channel_id=1, source_target_pairs={{0,16},{8,24},{16,0},{24,8},{1,17},{9,25},{17,1},{25,9},{2,18},{10... | collective-permute-start | bytes 688136 | tf_op jit(solution)/shard_map/ppermute | solution.py:310
  40.9 8.7 %collective-permute-start.14 = (s32[7,4,128]{2,1,0:T(4,128)S(1)}, s32[7,4,128]{2,1,0:T(4,128)S(1)}, u32[]{:S(2)}, u32[]{:S(2)}) collective-permute-start(s32[7,4,128]{2,1,0:T(4,128)S(1)} %get-tuple-element.42), channel_id=1, source_target_pairs={{0,8},{8,16},{16,24},{24,0},{1,9},{9,17},{17,25},{25,1},{2,10},{10... | collective-permute-start | bytes 43016 | tf_op jit(solution)/shard_map/ppermute | solution.py:310
  41.0 13.9 %collective-permute-start.15 = (s32[7,4,128]{2,1,0:T(4,128)S(1)}, s32[7,4,128]{2,1,0:T(4,128)S(1)}, u32[]{:S(2)}, u32[]{:S(2)}) collective-permute-start(s32[7,4,128]{2,1,0:T(4,128)S(1)} %get-tuple-element.43), channel_id=1, source_target_pairs={{0,16},{8,24},{16,0},{24,8},{1,17},{9,25},{17,1},{25,9},{2,18},{10... | collective-permute-start | bytes 43016 | tf_op jit(solution)/shard_map/ppermute | solution.py:310
  43.0 18.9 %collective-permute-start.3 = (bf16[64,3456]{1,0:T(8,128)(2,1)S(1)}, bf16[64,3456]{1,0:T(8,128)(2,1)S(1)}, u32[]{:S(2)}, u32[]{:S(2)}) collective-permute-start(bf16[64,3456]{1,0:T(8,128)(2,1)S(1)} %copy-done.24), channel_id=1, source_target_pairs={{0,2},{1,3},{2,0},{3,1},{4,6},{5,7},{6,4},{7,5},{8,10},{9,11},{10,... | collective-permute-start | bytes 1327112 | tf_op jit(solution)/shard_map/ppermute | solution.py:307
  49.7 20.3 %collective-permute-start.19 = (bf16[7,128,128]{2,1,0:T(8,128)(2,1)S(1)}, bf16[7,128,128]{2,1,0:T(8,128)(2,1)S(1)}, u32[]{:S(2)}, u32[]{:S(2)}) collective-permute-start(bf16[7,128,128]{2,1,0:T(8,128)(2,1)S(1)} %get-tuple-element.48), channel_id=1, source_target_pairs={{0,24},{8,0},{16,8},{24,16},{1,25},{9,1},{17,9},{25,17},{2,26},{10... | collective-permute-start | bytes 688136 | tf_op jit(solution)/shard_map/ppermute | solution.py:310
  54.9 8.4 %collective-permute-start.16 = (s32[7,4,128]{2,1,0:T(4,128)S(1)}, s32[7,4,128]{2,1,0:T(4,128)S(1)}, u32[]{:S(2)}, u32[]{:S(2)}) collective-permute-start(s32[7,4,128]{2,1,0:T(4,128)S(1)} %get-tuple-element.44), channel_id=1, source_target_pairs={{0,24},{8,0},{16,8},{24,16},{1,25},{9,1},{17,9},{25,17},{2,26},{10... | collective-permute-start | bytes 43016 | tf_op jit(solution)/shard_map/ppermute | solution.py:310
  61.9 3.7 %collective-permute-start.12 = (f32[1,3456]{1,0:T(1,128)S(1)}, f32[1,3456]{1,0:T(1,128)S(1)}, u32[]{:S(2)}, u32[]{:S(2)}) collective-permute-start(f32[1,3456]{1,0:T(1,128)S(1)} %add.80), channel_id=1, source_target_pairs={{0,8},{8,0},{16,24},{24,16},{1,9},{9,1},{17,25},{25,17},{2,10},{10... | collective-permute-start | bytes 41480 | tf_op jit(solution)/shard_map/ppermute | solution.py:307
  63.3 11.7 %collective-permute-start.6 = (bf16[32,3456]{1,0:T(8,128)(2,1)S(1)}, bf16[32,3456]{1,0:T(8,128)(2,1)S(1)}, u32[]{:S(2)}, u32[]{:S(2)}) collective-permute-start(bf16[32,3456]{1,0:T(8,128)(2,1)S(1)} %slice.36), channel_id=1, source_target_pairs={{0,2},{1,3},{2,0},{3,1},{4,6},{5,7},{6,4},{7,5},{8,10},{9,11},{10,... | collective-permute-start | bytes 663560 | tf_op jit(solution)/shard_map/ppermute | solution.py:307
  65.6 9.4 %collective-permute-start.4 = (bf16[32,3456]{1,0:T(8,128)(2,1)S(1)}, bf16[32,3456]{1,0:T(8,128)(2,1)S(1)}, u32[]{:S(2)}, u32[]{:S(2)}) collective-permute-start(bf16[32,3456]{1,0:T(8,128)(2,1)S(1)} %slice.37), channel_id=1, source_target_pairs={{0,4},{1,5},{2,6},{3,7},{4,0},{5,1},{6,2},{7,3},{8,12},{9,13},{10,... | collective-permute-start | bytes 663560 | tf_op jit(solution)/shard_map/ppermute | solution.py:307
  67.2 12.0 %collective-permute-start.13 = (f32[1,3456]{1,0:T(1,128)S(1)}, f32[1,3456]{1,0:T(1,128)S(1)}, u32[]{:S(2)}, u32[]{:S(2)}) collective-permute-start(f32[1,3456]{1,0:T(1,128)S(1)} %add.81), channel_id=1, source_target_pairs={{0,16},{8,24},{16,0},{24,8},{1,17},{9,25},{17,1},{25,9},{2,18},{10... | collective-permute-start | bytes 41480 | tf_op jit(solution)/shard_map/ppermute | solution.py:307
  75.4 6.8 %collective-permute-start.7 = (bf16[2,32,864]{2,1,0:T(8,128)(2,1)S(1)}, bf16[2,32,864]{2,1,0:T(8,128)(2,1)S(1)}, u32[]{:S(2)}, u32[]{:S(2)}) collective-permute-start(bf16[2,32,864]{2,1,0:T(8,128)(2,1)S(1)} %get-tuple-element.37), channel_id=1, source_target_pairs={{0,8},{8,16},{16,24},{24,0},{1,9},{9,17},{17,25},{25,1},{2,10},{10... | collective-permute-start | bytes 331784 | tf_op jit(solution)/shard_map/ppermute | solution.py:310
  76.7 7.8 %collective-permute-start.8 = (bf16[2,32,864]{2,1,0:T(8,128)(2,1)S(1)}, bf16[2,32,864]{2,1,0:T(8,128)(2,1)S(1)}, u32[]{:S(2)}, u32[]{:S(2)}) collective-permute-start(bf16[2,32,864]{2,1,0:T(8,128)(2,1)S(1)} %get-tuple-element.38), channel_id=1, source_target_pairs={{0,16},{8,24},{16,0},{24,8},{1,17},{9,25},{17,1},{25,9},{2,18},{10... | collective-permute-start | bytes 331784 | tf_op jit(solution)/shard_map/ppermute | solution.py:310
  76.8 7.7 %collective-permute-start.9 = (bf16[2,32,864]{2,1,0:T(8,128)(2,1)S(1)}, bf16[2,32,864]{2,1,0:T(8,128)(2,1)S(1)}, u32[]{:S(2)}, u32[]{:S(2)}) collective-permute-start(bf16[2,32,864]{2,1,0:T(8,128)(2,1)S(1)} %get-tuple-element.39), channel_id=1, source_target_pairs={{0,24},{8,0},{16,8},{24,16},{1,25},{9,1},{17,9},{25,17},{2,26},{10... | collective-permute-start | bytes 331784 | tf_op jit(solution)/shard_map/ppermute | solution.py:310
  (14 other events, 11.7 us)

commit v2 on v0

v2 whole, which is shorter than its diff:
```python
import functools
import math

import jax
import jax.numpy as jnp
from jax import lax
from jax.experimental import pallas as pl
from jax.experimental.pallas import tpu as pltpu
from jax.sharding import PartitionSpec as P

EMBED_WIDTH = 128
SPARSE_FEATURES = 26
BAG = 4
TABLE_REACH_ROWS = 512
EMPTY = TABLE_REACH_ROWS // 2
BIAS_ROWS = 32
F32 = jnp.float32
BF16 = jnp.bfloat16
MIB = 1024 * 1024
NT = (((1,), (1,)), ((), ()))
ANY = pl.BlockSpec(memory_space=pl.ANY)
VMEM = pl.BlockSpec(memory_space=pltpu.VMEM)
SMEM = pl.BlockSpec(memory_space=pltpu.SMEM)


def params(mib):
    return pltpu.CompilerParams(vmem_limit_bytes=mib * MIB)


def pieces_of(width):
    blocks = width // EMBED_WIDTH
    parts = max(p for p in (3, 2, 1) if blocks % p == 0)
    step = width // parts
    return [(k * step, step) for k in range(parts)]


def fetch(pairs, width, sems):
    copies = {}
    for place, (start, size) in enumerate(pieces_of(width)):
        for which, (source, target) in enumerate(pairs):
            part = pl.ds(start, size)
            copy = pltpu.make_async_copy(
                source.at[:, part], target.at[:, part], sems.at[which, place]
            )
            copy.start()
            copies[which, place] = copy
    return lambda which, place: copies[which, place].wait()


def factors(act, cot, down, up, width, wait):
    hidden = back = None
    for place, (start, size) in enumerate(pieces_of(width)):
        part = slice(start, start + size)
        wait(0, place)
        wait(1, place)
        value = act[:, part]
        term = lax.dot_general(value, down[:, part], NT, preferred_element_type=F32)
        hidden = term if hidden is None else hidden + term
        wait(2, place)
        wait(3, place)
        scaled_b = (cot[:, part].astype(F32) * value.astype(F32)).astype(BF16)
        term = lax.dot_general(scaled_b, up[:, part], NT, preferred_element_type=F32)
        back = term if back is None else back + term
    return hidden.astype(BF16), back.astype(BF16)


def input_kernel(
    n_table, slots, table_ref, owner_ref, act_hbm, cot_hbm, down_hbm, up_hbm, bias_ref, ids_ref, length_ref,
    hidden_ref, back_ref, dense_ref, *rest,
):
    outs = rest[:n_table]
    act, cot, down, up, store, id_store, feature_ref, sems = rest[n_table:]
    tokens, width = act.shape
    wait = fetch(((act_hbm, act), (down_hbm, down), (cot_hbm, cot), (up_hbm, up)), width, sems)
    for place in range(n_table * slots):
        feature_ref[place] = SPARSE_FEATURES
    for feature in range(SPARSE_FEATURES):
        slot = owner_ref[feature]
        shift = lax.rem(lax.div(slot, slots) + n_table - table_ref[0], n_table)
        feature_ref[shift * slots + lax.rem(slot, slots)] = feature
    store[SPARSE_FEATURES + 1] = jnp.zeros(store.shape[1:], BF16)
    id_store[...] = jnp.full(id_store.shape, EMPTY, F32)
    entries = lax.broadcasted_iota(jnp.int32, (BAG, tokens), 0)
    for shift in range(n_table):
        for slot in range(slots):
            feature = feature_ref[shift * slots + slot]
            at = jnp.minimum(feature, SPARSE_FEATURES - 1)
            length = jnp.where(feature < SPARSE_FEATURES, length_ref[pl.ds(at, 1), :], 0)
            ids = jnp.where(entries < length, ids_ref[at] - EMPTY, EMPTY)
            id_store[shift, slot * BAG : (slot + 1) * BAG, :] = ids.astype(F32)
        outs[shift][slots * tokens :, :] = id_store[shift].astype(BF16)
    hidden, back = factors(act, cot, down, up, width, wait)
    hidden_ref[...] = hidden
    back_ref[...] = back
    blocks = 3
    for first in range(0, width // EMBED_WIDTH, blocks):
        part = slice(first * EMBED_WIDTH, (first + blocks) * EMBED_WIDTH)
        mixed = jnp.dot(hidden, up[:, part], preferred_element_type=F32)
        tail = jnp.dot(back, down[:, part], preferred_element_type=F32)
        for k in range(blocks):
            block = first + k
            mine = slice(k * EMBED_WIDTH, (k + 1) * EMBED_WIDTH)
            cols = slice(block * EMBED_WIDTH, (block + 1) * EMBED_WIDTH)
            bias = bias_ref[block : block + 1, :]
            grad = cot[:, cols].astype(F32) * (1.0 + (mixed[:, mine] + bias)) + tail[:, mine]
            store[block] = grad.astype(BF16)
    dense_ref[...] = store[0]
    for shift in range(n_table):
        for slot in range(slots):
            rows = slice(slot * tokens, (slot + 1) * tokens)
            outs[shift][rows, :] = store[feature_ref[shift * slots + slot] + 1]


def input_call(table_index, owners, act, cot, down, up, bias, ids, lengths, n_table, slots):
    tokens, width = act.shape
    rank = down.shape[0]
    id_rows = -(-slots * BAG // 16) * 16
    parts = len(pieces_of(width))
    return pl.pallas_call(
        functools.partial(input_kernel, n_table, slots),
        in_specs=[SMEM, SMEM, ANY, ANY, ANY, ANY, VMEM, VMEM, VMEM],
        out_specs=[VMEM] * (3 + n_table),
        out_shape=[
            jax.ShapeDtypeStruct((tokens, rank), BF16),
            jax.ShapeDtypeStruct((tokens, rank), BF16),
            jax.ShapeDtypeStruct((tokens, EMBED_WIDTH), BF16),
        ]
        + [jax.ShapeDtypeStruct((slots * tokens + id_rows, EMBED_WIDTH), BF16)] * n_table,
        scratch_shapes=[
            pltpu.VMEM((tokens, width), BF16),
            pltpu.VMEM((tokens, width), BF16),
            pltpu.VMEM((rank, width), BF16),
            pltpu.VMEM((rank, width), BF16),
            pltpu.VMEM((SPARSE_FEATURES + 2, tokens, EMBED_WIDTH), BF16),
            pltpu.VMEM((n_table, id_rows, EMBED_WIDTH), F32),
            pltpu.SMEM((n_table * slots,), jnp.int32),
            pltpu.SemaphoreType.DMA((4, parts)),
        ],
        compiler_params=params(60),
        cost_estimate=pl.CostEstimate(
            flops=8 * tokens * rank * width, bytes_accessed=4 * (tokens + rank) * width, transcendentals=0
        ),
    )(table_index, owners, act, cot, down, up, bias, ids, lengths)


def order_matrix(rep_index, rows, size, block, bits):
    out_row = lax.broadcasted_iota(jnp.int32, (rows, size), 0)
    in_row = lax.broadcasted_iota(jnp.int32, (rows, size), 1)
    source = lax.rem(out_row, block)
    position = lax.div(out_row, block)
    for place, bit in enumerate(bits):
        flag = lax.rem(lax.div(position, 1 << (len(bits) - 1 - place)), 2)
        own = lax.rem(lax.div(rep_index, bit), 2)
        source = source + jnp.where(flag == own, 0, bit) * block
    return (source == in_row).astype(F32).astype(BF16)


def bias_terms(value):
    high = value.astype(BF16).astype(F32)
    return high, (value - high).astype(BF16).astype(F32)


def put_bias(ref, width, high, low):
    if ref.shape[0] >= 2 * BIAS_ROWS:
        both = jnp.concatenate([high, low], axis=0).astype(BF16)
        ref[: 2 * BIAS_ROWS, width : width + EMBED_WIDTH] = both
    else:
        ref[:BIAS_ROWS, width : width + EMBED_WIDTH] = high.astype(BF16)
        ref[:BIAS_ROWS, width + EMBED_WIDTH : width + 2 * EMBED_WIDTH] = low.astype(BF16)


def get_bias(ref, width):
    if ref.shape[0] >= 2 * BIAS_ROWS:
        both = ref[: 2 * BIAS_ROWS, width : width + EMBED_WIDTH].astype(F32)
        return both[:BIAS_ROWS] + both[BIAS_ROWS:]
    high = ref[:BIAS_ROWS, width : width + EMBED_WIDTH].astype(F32)
    return high + ref[:BIAS_ROWS, width + EMBED_WIDTH : width + 2 * EMBED_WIDTH].astype(F32)


def extra_columns(rows):
    return EMBED_WIDTH if rows >= 2 * BIAS_ROWS else 2 * EMBED_WIDTH


def terms_kernel(
    ride, up_bits, down_bits, rep_ref, hidden_ref, back_ref, act_hbm, cot_hbm, act_other_hbm, cot_other_hbm,
    down_hbm, up_hbm, up_keep_ref, up_send_ref, down_keep_ref, down_send_ref, bias_ref,
    act, cot, act_other, cot_other, down, up, sems,
):
    tokens, width = act.shape
    rank = down.shape[0]
    wait = fetch(
        (
            (act_other_hbm, act_other), (down_hbm, down), (cot_other_hbm, cot_other), (up_hbm, up),
            (act_hbm, act), (cot_hbm, cot),
        ),
        width,
        sems,
    )
    half, block = rank // 2, rank >> len(up_bits)
    up_order = order_matrix(rep_ref[0], half, rank, block, up_bits)
    down_order = order_matrix(rep_ref[0], half, rank, block, down_bits)
    hidden_other, back_other = factors(act_other, cot_other, down, up, width, wait)
    hidden = jnp.concatenate([hidden_ref[...], hidden_other], axis=0)
    back = jnp.concatenate([back_ref[...], back_other], axis=0)
    hidden = lax.dot_general(up_order, hidden, NT, preferred_element_type=F32).astype(BF16)
    back = lax.dot_general(down_order, back, NT, preferred_element_type=F32).astype(BF16)
    for place in range(len(pieces_of(width))):
        wait(4, place)
        wait(5, place)
    blocks = 3
    keep = half // 2
    if width // EMBED_WIDTH < BIAS_ROWS:
        bias_ref[...] = jnp.zeros_like(bias_ref)
    for first in range(0, width // EMBED_WIDTH, blocks):
        part = slice(first * EMBED_WIDTH, (first + blocks) * EMBED_WIDTH)
        values = jnp.concatenate([act[:, part], act_other[:, part]], axis=0)
        grads = jnp.concatenate([cot[:, part], cot_other[:, part]], axis=0)
        scaled = grads.astype(F32) * values.astype(F32)
        sums = jnp.sum(scaled, axis=0, keepdims=True)
        for k in range(blocks):
            bias_ref[first + k : first + k + 1, :] = sums[:, k * EMBED_WIDTH : (k + 1) * EMBED_WIDTH]
        up_part = jnp.dot(hidden, scaled.astype(BF16), preferred_element_type=F32)
        up_keep_ref[:, part] = up_part[:keep]
        up_send_ref[:, part] = up_part[keep:].astype(BF16)
        down_part = jnp.dot(back, values, preferred_element_type=F32)
        down_keep_ref[:, part] = down_part[:keep]
        down_send_ref[:, part] = down_part[keep:].astype(BF16)
    if ride:
        high, low = bias_terms(bias_ref[...])
        put_bias(up_send_ref, width, high, low)
        bias_ref[...] = high + low


def terms_call(
    rep_index, hidden, back, act, cot, act_other, cot_other, down, up, ride, up_bits, down_bits
):
    tokens, width = act.shape
    rank = down.shape[0]
    rows = rank // 4
    extra = extra_columns(rows) if ride else 0
    parts = len(pieces_of(width))
    wide = pltpu.VMEM((tokens, width), BF16)
    return pl.pallas_call(
        functools.partial(terms_kernel, ride, up_bits, down_bits),
        in_specs=[SMEM, VMEM, VMEM] + [ANY] * 6,
        out_specs=[VMEM] * 5,
        out_shape=[
            jax.ShapeDtypeStruct((rows, width), F32),
            jax.ShapeDtypeStruct((rows, width + extra), BF16),
            jax.ShapeDtypeStruct((rows, width), F32),
            jax.ShapeDtypeStruct((rows, width), BF16),
            jax.ShapeDtypeStruct((BIAS_ROWS, EMBED_WIDTH), F32),
        ],
        scratch_shapes=[
            wide, wide, wide, wide,
            pltpu.VMEM((rank, width), BF16),
            pltpu.VMEM((rank, width), BF16),
            pltpu.SemaphoreType.DMA((6, parts)),
        ],
        compiler_params=params(60),
        cost_estimate=pl.CostEstimate(
            flops=8 * tokens * rank * width, bytes_accessed=8 * tokens * width + 4 * rank * width, transcendentals=0
        ),
    )(rep_index, hidden, back, act, cot, act_other, cot_other, down, up)


def halve_kernel(
    up_keep_ref, up_in_ref, down_keep_ref, down_in_ref, bias_ref,
    up_out_ref, up_send_ref, down_out_ref, down_send_ref, bias_out_ref,
):
    rows, width = up_keep_ref.shape
    half = rows // 2
    up = up_keep_ref[...] + up_in_ref[:, :width].astype(F32)
    up_out_ref[...] = up[:half]
    up_send_ref[:, :width] = up[half:].astype(BF16)
    down = down_keep_ref[...] + down_in_ref[...].astype(F32)
    down_out_ref[...] = down[:half]
    down_send_ref[...] = down[half:].astype(BF16)
    high, low = bias_terms(bias_ref[...] + get_bias(up_in_ref, width))
    put_bias(up_send_ref, width, high, low)
    bias_out_ref[...] = high + low


def halve_call(up_keep, up_in, down_keep, down_in, bias_sum):
    rows, width = up_keep.shape
    half = rows // 2
    return pl.pallas_call(
        halve_kernel,
        in_specs=[VMEM] * 5,
        out_specs=[VMEM] * 5,
        out_shape=[
            jax.ShapeDtypeStruct((half, width), F32),
            jax.ShapeDtypeStruct((half, width + extra_columns(half)), BF16),
            jax.ShapeDtypeStruct((half, width), F32),
            jax.ShapeDtypeStruct((half, width), BF16),
            jax.ShapeDtypeStruct(bias_sum.shape, F32),
        ],
        compiler_params=params(16),
    )(up_keep, up_in, down_keep, down_in, bias_sum)


def split_kernel(
    ride, n_table, scale, table_ref, up_keep_ref, up_in_ref, down_keep_ref, down_in_ref, bias_ref,
    own_ref, bias_out_ref, *rest,
):
    sends, store = rest[: n_table - 1], rest[n_table - 1]
    columns = own_ref.shape[2]
    width = up_keep_ref.shape[1]
    pairs = ((up_keep_ref, up_in_ref), (down_keep_ref, down_in_ref))
    for which, (keep, arrived) in enumerate(pairs):
        total = (keep[...] + arrived[:, :width].astype(F32)) * scale
        for table in range(n_table):
            store[table, which] = total[:, table * columns : (table + 1) * columns]
    own_ref[...] = store[table_ref[0]]
    start = -(-columns // EMBED_WIDTH) * EMBED_WIDTH
    bias = bias_ref[...]
    if ride:
        high, low = bias_terms(bias + get_bias(up_in_ref, width))
        bias = high + low
    bias_out_ref[...] = bias
    for shift in range(1, n_table):
        value = store[lax.rem(table_ref[0] + shift, n_table)].astype(BF16)
        sends[shift - 1][:, :, :columns] = value
        if ride:
            sends[shift - 1][0, :BIAS_ROWS, start:] = high.astype(BF16)
            sends[shift - 1][1, :BIAS_ROWS, start:] = low.astype(BF16)


def split_call(table_index, up_keep, up_in, down_keep, down_in, bias_sum, n_table, scale, ride):
    rows, width = up_keep.shape
    columns = width // n_table
    sent = -(-columns // EMBED_WIDTH) * EMBED_WIDTH + EMBED_WIDTH if ride else columns
    return pl.pallas_call(
        functools.partial(split_kernel, ride, n_table, scale),
        in_specs=[SMEM] + [VMEM] * 5,
        out_specs=[VMEM] * (n_table + 1),
        out_shape=[
            jax.ShapeDtypeStruct((2, rows, columns), F32),
            jax.ShapeDtypeStruct(bias_sum.shape, F32),
        ]
        + [jax.ShapeDtypeStruct((2, rows, sent), BF16)] * (n_table - 1),
        scratch_shapes=[pltpu.VMEM((n_table, 2, rows, columns), F32)],
        compiler_params=params(16),
    )(table_index, up_keep, up_in, down_keep, down_in, bias_sum)


def finish_kernel(ride, n_table, scale, table_ref, own_ref, bias_ref, *rest):
    arrived = rest[: n_table - 1]
    up_ref, down_ref, bias_out_ref, store = rest[n_table - 1 :]
    columns = own_ref.shape[2]
    start = -(-columns // EMBED_WIDTH) * EMBED_WIDTH
    up, down = own_ref[0], own_ref[1]
    store[table_ref[0]] = bias_ref[...]
    for shift in range(1, n_table):
        value = arrived[shift - 1]
        up = up + value[0, :, :columns].astype(F32)
        down = down + value[1, :, :columns].astype(F32)
        if ride:
            source = lax.rem(table_ref[0] + n_table - shift, n_table)
            high = value[0, :BIAS_ROWS, start:].astype(F32)
            store[source] = high + value[1, :BIAS_ROWS, start:].astype(F32)
    up_ref[...] = up
    down_ref[...] = down
    total = bias_ref[...]
    if ride:
        total = store[0]
        for table in range(1, n_table):
            total = total + store[table]
    bias_out_ref[...] = total * scale


def finish_call(table_index, own, bias_sum, arrived, scale, ride):
    n_table = len(arrived) + 1
    _, rows, columns = own.shape
    return pl.pallas_call(
        functools.partial(finish_kernel, ride, n_table, scale),
        in_specs=[SMEM] + [VMEM] * (n_table + 1),
        out_specs=[VMEM] * 3,
        out_shape=[
            jax.ShapeDtypeStruct((rows, columns), F32),
            jax.ShapeDtypeStruct((rows, columns), F32),
            jax.ShapeDtypeStruct(bias_sum.shape, F32),
        ],
        scratch_shapes=[pltpu.VMEM((n_table,) + bias_sum.shape, F32)],
        compiler_params=params(16),
    )(table_index, own, bias_sum, *arrived)


def rows_kernel(n_table, slots, *refs):
    parts, out_ref = refs[:n_table], refs[n_table]
    id_store = refs[n_table + 1]
    tokens = (parts[0].shape[0] - id_store.shape[1]) // slots
    slot = pl.program_id(0)

    @pl.when(slot == 0)
    def _():
        for source in range(n_table):
            ids = parts[source][slots * tokens :, :].astype(F32).astype(jnp.int32)
            id_store[source] = ids + EMPTY

    rows = lax.broadcasted_iota(jnp.int32, (TABLE_REACH_ROWS, tokens), 0)
    counts, grads = [], []
    for source in range(n_table):
        count = jnp.zeros((TABLE_REACH_ROWS, tokens), F32)
        for entry in range(BAG):
            ids = id_store[source, pl.ds(slot * BAG + entry, 1), :]
            count = count + jnp.where(ids == rows, 1.0, 0.0)
        counts.append(count.astype(BF16))
        grads.append(parts[source][pl.ds(pl.multiple_of(slot * tokens, tokens), tokens), :])
    count = jnp.concatenate(counts, axis=1)
    grad = jnp.concatenate(grads, axis=0)
    out_ref[0, 0] = jnp.dot(count, grad, preferred_element_type=F32)


def rows_call(parts, slots):
    n_table = len(parts)
    id_rows = -(-slots * BAG // 16) * 16
    tokens = (parts[0].shape[0] - id_rows) // slots
    whole = pl.BlockSpec(parts[0].shape, lambda i: (0, 0))
    return pl.pallas_call(
        functools.partial(rows_kernel, n_table, slots),
        grid=(slots,),
        in_specs=[whole] * n_table,
        out_specs=pl.BlockSpec((1, 1, TABLE_REACH_ROWS, EMBED_WIDTH), lambda i: (0, i, 0, 0)),
        out_shape=jax.ShapeDtypeStruct((1, slots, TABLE_REACH_ROWS, EMBED_WIDTH), F32),
        scratch_shapes=[pltpu.VMEM((n_table, id_rows, tokens), jnp.int32)],
        compiler_params=params(32),
        cost_estimate=pl.CostEstimate(
            flops=2 * slots * n_table * tokens * TABLE_REACH_ROWS * EMBED_WIDTH,
            bytes_accessed=4 * slots * TABLE_REACH_ROWS * EMBED_WIDTH,
            transcendentals=0,
        ),
    )(*parts)


def body(
    activations, cotangent, down_weight, up_weight, bias, bag_ids, bag_lengths, feature_table_slot
):
    tokens, width = activations.shape
    rank = down_weight.shape[0]
    n_table = lax.axis_size("table")
    n_rep = lax.axis_size("rep")
    slots = (SPARSE_FEATURES + n_table - 1) // n_table
    scale = 1.0 / math.sqrt(tokens * n_table * n_rep)
    table_index = lax.axis_index("table").astype(jnp.int32).reshape(1)
    rep_index = lax.axis_index("rep").astype(jnp.int32).reshape(1)
    far_bits = [1 << k for k in range(1, n_rep.bit_length() - 1)]
    up_bits, down_bits = [1] + far_bits, [1] + far_bits[::-1]
    ride = rank // n_rep >= BIAS_ROWS

    def swap(value, axis, bit):
        size = n_rep if axis == "rep" else n_table
        return lax.ppermute(value, axis, [(k, k ^ bit) for k in range(size)])

    def shifted(value, shift):
        return lax.ppermute(value, "table", [(k, (k + shift) % n_table) for k in range(n_table)])

    act_other = swap(activations, "rep", 1)
    cot_other = swap(cotangent, "rep", 1)
    hidden, back, dense_grad, *parts = input_call(
        table_index, feature_table_slot, activations, cotangent, down_weight, up_weight,
        bias.reshape(-1, EMBED_WIDTH), jnp.transpose(bag_ids, (1, 2, 0)), jnp.transpose(bag_lengths, (1, 0)),
        n_table, slots,
    )
    parts = [parts[0]] + [shifted(parts[k], k) for k in range(1, n_table)]
    up_keep, up_send, down_keep, down_send, bias_sum = terms_call(
        rep_index, hidden, back, activations, cotangent, act_other, cot_other, down_weight, up_weight,
        ride, up_bits, down_bits,
    )
    for place, (up_bit, down_bit) in enumerate(zip(up_bits[1:], down_bits[1:])):
        up_in = swap(up_send, "rep", up_bit)
        down_in = swap(down_send, "rep", down_bit)
        if not ride:
            bias_sum = bias_sum + swap(bias_sum, "rep", up_bit)
        if place == len(far_bits) - 1:
            break
        if ride:
            up_keep, up_send, down_keep, down_send, bias_sum = halve_call(
                up_keep, up_in, down_keep, down_in, bias_sum
            )
        else:
            half = up_keep.shape[0] // 2
            up = up_keep + up_in.astype(F32)
            down = down_keep + down_in.astype(F32)
            up_keep, up_send = up[:half], up[half:].astype(BF16)
            down_keep, down_send = down[:half], down[half:].astype(BF16)
    if not ride:
        for bit in [1 << k for k in range(n_table.bit_length() - 1)]:
            bias_sum = bias_sum + swap(bias_sum, "table", bit)
    own, bias_sum, *sends = split_call(
        table_index, up_keep, up_in, down_keep, down_in, bias_sum, n_table, scale, ride
    )
    arrived = [shifted(value, k + 1) for k, value in enumerate(sends)]
    up_grad, down_grad, bias_grad = finish_call(table_index, own, bias_sum, arrived, scale, ride)
    parts, _ = lax.optimization_barrier((parts, own))
    row_grad = rows_call(parts, slots)
    bias_grad = bias_grad[: width // EMBED_WIDTH].reshape(width)
    return (dense_grad, up_grad, down_grad, bias_grad, row_grad)


def solution(mesh):
    placed = (
        P(("table", "rep"), None),
        P(("table", "rep"), None),
        P(),
        P(),
        P(),
        P(("table", "rep"), None, None),
        P(("table", "rep"), None),
        P(),
    )
    return jax.shard_map(
        body,
        mesh=mesh,
        in_specs=placed,
        out_specs=(
            P(("table", "rep"), None),
            P("rep", "table"),
            P("rep", "table"),
            P(),
            P("rep", "table", None, None),
        ),
        check_vma=False,
    )
```

time: 196 us -> 71.2 us (0.36)
  blocking collectives: 64.1 us -> 0 us
  waiting for transfers between devices: 56.2 us -> 25.5 us
  local copies, waits for them, and re-layouts: 27.4 us -> 4.87 us
  Pallas kernels: 0 us -> 20.4 us
  between operations: 14.9 us -> 0.71 us
  matrix products: 10.2 us -> 0 us
  other arithmetic: 6.25 us -> 0 us
  starting transfers between devices: 15.7 us -> 18.4 us
    psum x1 -> x0, blocking collectives: 49.1 us -> none  [body(): bias_grad = lax.psum(jnp.sum(scaled, axis=0) * scale, ('table', 'rep'))]
    unnamed x2 -> x0, waiting for transfers between devices: 47.5 us -> none
    ppermute x0 -> x12, waiting for transfers between devices: none -> 25.5 us  [the longest x6 13.6 us: shifted(): lax.ppermute(value, 'table', [(k, (k + shift) % n_table) for k in range(n...]
    pallas_call x0 -> x6, Pallas kernels: none -> 20.4 us  [the longest x1 7.65 us: terms_call(): pl.pallas_call(functools.partial(terms_kernel, ride, up_bits, down_bits),...]
    ppermute x0 -> x12, starting transfers between devices: none -> 18.4 us  [the longest x6 11.1 us: shifted(): lax.ppermute(value, 'table', [(k, (k + shift) % n_table) for k in range(n...]
    all_to_all x3 -> x0, starting transfers between devices: 15.6 us -> none  [the longest x1 6.32 us: body(): lax.all_to_all(row_ids, 'table', split_axis=0, concat_axis=2, tiled=True)]
    all_gather x1 -> x0, blocking collectives: 15 us -> none  [body(): piece = lax.all_gather(factors, 'table', axis=1, tiled=True)]
    dot_general x8 -> x0, matrix products: 10.2 us -> none  [the longest x1 4.87 us: body(): jnp.einsum('ksr,ksc->krc', count, grad_items, preferred_element_type=jnp....]
  transfers between devices with their start and end apart: 4 -> 12, of which waited for: 2 -> 4; matrix products, arithmetic and copies ran while one was open for 18% -> 0% of each run, Pallas kernels for 0% -> 17%
where the time goes in v2:
time: 71.2 us; the launch traced here: 69.9 us
  waiting for transfers between devices  25.5 us (36%)
  Pallas kernels  20.4 us (29%)
  starting transfers between devices  18.4 us (26%)
  local copies, waits for them, and re-layouts  4.87 us (7%)
    ppermute x6, waiting for transfers between devices, shifted(): lax.ppermute(value, 'table', [(k, (k + shift) % n_table) for k in range(n...  13.6 us
    ppermute x6, waiting for transfers between devices, swap(): return lax.ppermute(value, axis, [(k, k ^ bit) for k in range(size)])  11.9 us
    ppermute x6, starting transfers between devices, shifted(): lax.ppermute(value, 'table', [(k, (k + shift) % n_table) for k in range(n...  11.1 us
    pallas_call x1, Pallas kernels, terms_call(): pl.pallas_call(functools.partial(terms_kernel, ride, up_bits, down_bits),...  7.65 us
    ppermute x6, starting transfers between devices, swap(): return lax.ppermute(value, axis, [(k, k ^ bit) for k in range(size)])  7.3 us
    pallas_call x1, Pallas kernels, input_call(): pl.pallas_call(functools.partial(input_kernel, n_table, slots), in_specs=...  6.53 us
    pallas_call x1, Pallas kernels, rows_call(): pl.pallas_call(functools.partial(rows_kernel, n_table, slots), grid=(slot...  4.97 us
    unnamed x18, local copies, waits for them, and re-layouts  4.26 us
  transfers between devices with their start and end apart: 12, of which 4 were waited for; matrix products, arithmetic and copies ran while one was open for 0% of the time, Pallas kernels for 17%

profile of v2, /device:TPU:0, one launch (start us, length us, event | category | flops | bytes accessed | tf_op | source)
XLA Modules:
  0.0 69.9 jit_solution(6861817168239444187)
XLA Ops:
  0.6 0.5 collective-permute-start
  1.1 0.1 collective-permute-start.1
  1.2 6.5 %shard_map.119 = (bf16[128,256]{1,0:T(8,128)(2,1)}, bf16[128,256]{1,0:T(8,128)(2,1)}, bf16[128,128]{1,0:T(8,128)(2,1)}, bf16[928,128]{1,0:T(8,128)(2,1)}, bf16[9...) custom-call(s32[1]{0:T(128)} %bitcast.table_ref, s32[26]{0:T(128)} %owner_ref.1, ...), custom_call_target="tpu_custom_call" | custom-call | flops 905969664 | bytes 5308416 | tf_op jit(solution)/shard_map/pallas_call | solution.py:119
  7.8 0.0 collective-permute-done.act_other_hbm
  7.8 0.0 copy-start.4
  7.8 0.9 %copy-done.4 = bf16[128,3456]{1,0:T(8,128)(2,1)} copy-done((bf16[128,3456]{1,0:T(8,128)(2,1)}, bf16[128,3456]{1,0:T(8,128)(2,1)S(1)}, u32[]{:S(2)}) %copy-start.4) | copy-done | bytes 884760
  8.7 0.3 copy-done.5
  9.0 7.6 %shard_map.120 = (f32[64,3456]{1,0:T(8,128)}, bf16[64,3584]{1,0:T(8,128)(2,1)}, f32[64,3456]{1,0:T(8,128)}, bf16[64,3456]{1,0:T(8,128)(2,1)}, f32[32,128]{1,0:T(8,128)}) custom-call(s32[1]{0:T(128)} %bitcast.4.rep_ref, bf16[128,256]{1,0:T(8,128)(2,1)} %get-tuple-element.35.hidden_ref, bf16[128,256]{1,0:T(8,128)(2,1)} %get-tuple-element.36.back_ref, ...), custom_call_target="tpu_custom_call" | custom-call | flops 905969664 | bytes 7077888 | tf_op jit(solution)/shard_map/pallas_call | solution.py:243
  16.7 3.0 %collective-permute-start.2 = (bf16[64,3584]{1,0:T(8,128)(2,1)}, bf16[64,3584]{1,0:T(8,128)(2,1)S(1)}, u32[]{:S(2)}, u32[]{:S(2)}) collective-permute-start(bf16[64,3584]{1,0:T(8,128)(2,1)} %get-tuple-element.38), channel_id=1, source_target_pairs={{0,2},{1,3},{2,0},{3,1},{4,6},{5,7},{6,4},{7,5},{8,10},{9,11},{10,... | collective-permute-start | bytes 1376264 | tf_op jit(solution)/shard_map/ppermute | solution.py:453
  19.6 1.5 %collective-permute-start.3 = (bf16[64,3456]{1,0:T(8,128)(2,1)}, bf16[64,3456]{1,0:T(8,128)(2,1)S(1)}, u32[]{:S(2)}, u32[]{:S(2)}) collective-permute-start(bf16[64,3456]{1,0:T(8,128)(2,1)} %get-tuple-element.40), channel_id=1, source_target_pairs={{0,4},{1,5},{2,6},{3,7},{4,0},{5,1},{6,2},{7,3},{8,12},{9,13},{10,... | collective-permute-start | bytes 1327112 | tf_op jit(solution)/shard_map/ppermute | solution.py:453
  21.2 10.6 %collective-permute-done.3.down_in_ref = bf16[64,3456]{1,0:T(8,128)(2,1)S(1)} collective-permute-done((bf16[64,3456]{1,0:T(8,128)(2,1)}, bf16[64,3456]{1,0:T(8,128)(2,1)S(1)}, u32[]{:S(2)}, u32[]{:S(2)}) %collective-permute-start.3) | collective-permute-done | bytes 442400 | tf_op jit(solution)/shard_map/ppermute | solution.py:453
  31.7 0.0 collective-permute-done.2.up_in_ref
  31.7 1.2 %copy-done = f32[64,3456]{1,0:T(8,128)S(1)} copy-done((f32[64,3456]{1,0:T(8,128)S(1)}, f32[64,3456]{1,0:T(8,128)}, u32[]{:S(2)}) %copy-start) | copy-done | bytes 884760
  32.9 1.2 %copy-done.1 = f32[64,3456]{1,0:T(8,128)S(1)} copy-done((f32[64,3456]{1,0:T(8,128)S(1)}, f32[64,3456]{1,0:T(8,128)}, u32[]{:S(2)}) %copy-start.1) | copy-done | bytes 884760
  34.1 0.7 %copy-done.3 = f32[32,128]{1,0:T(8,128)S(1)} copy-done((f32[32,128]{1,0:T(8,128)S(1)}, f32[32,128]{1,0:T(8,128)}, u32[]{:S(2)}) %copy-start.3) | copy-done | bytes 16408
  34.8 0.2 shard_map.121
  34.9 1.6 %collective-permute-start.4 = (bf16[32,3712]{1,0:T(8,128)(2,1)S(1)}, bf16[32,3712]{1,0:T(8,128)(2,1)S(1)}, u32[]{:S(2)}, u32[]{:S(2)}) collective-permute-start(bf16[32,3712]{1,0:T(8,128)(2,1)S(1)} %get-tuple-element.43), channel_id=1, source_target_pairs={{0,4},{1,5},{2,6},{3,7},{4,0},{5,1},{6,2},{7,3},{8,12},{9,13},{10,... | collective-permute-start | bytes 712712 | tf_op jit(solution)/shard_map/ppermute | solution.py:453
  36.5 1.6 %collective-permute-start.9 = (bf16[928,128]{1,0:T(8,128)(2,1)S(1)}, bf16[928,128]{1,0:T(8,128)(2,1)S(1)}, u32[]{:S(2)}, u32[]{:S(2)}) collective-permute-start(bf16[928,128]{1,0:T(8,128)(2,1)S(1)} %copy-done.8), channel_id=1, source_target_pairs={{0,8},{8,16},{16,24},{24,0},{1,9},{9,17},{17,25},{25,1},{2,10},{10... | collective-permute-start | bytes 712712 | tf_op jit(solution)/shard_map/ppermute | solution.py:456
  38.1 0.6 collective-permute-start.5
  38.7 2.6 %collective-permute-start.10 = (bf16[928,128]{1,0:T(8,128)(2,1)S(1)}, bf16[928,128]{1,0:T(8,128)(2,1)S(1)}, u32[]{:S(2)}, u32[]{:S(2)}) collective-permute-start(bf16[928,128]{1,0:T(8,128)(2,1)S(1)} %copy-done.7), channel_id=1, source_target_pairs={{0,16},{8,24},{16,0},{24,8},{1,17},{9,25},{17,1},{25,9},{2,18},{10... | collective-permute-start | bytes 712712 | tf_op jit(solution)/shard_map/ppermute | solution.py:456
  41.3 1.3 %collective-permute-start.11 = (bf16[928,128]{1,0:T(8,128)(2,1)S(1)}, bf16[928,128]{1,0:T(8,128)(2,1)S(1)}, u32[]{:S(2)}, u32[]{:S(2)}) collective-permute-start(bf16[928,128]{1,0:T(8,128)(2,1)S(1)} %copy-done.6), channel_id=1, source_target_pairs={{0,24},{8,0},{16,8},{24,16},{1,25},{9,1},{17,9},{25,17},{2,26},{10... | collective-permute-start | bytes 712712 | tf_op jit(solution)/shard_map/ppermute | solution.py:456
  42.7 1.4 %collective-permute-done.5.down_in_ref = bf16[32,3456]{1,0:T(8,128)(2,1)S(1)} collective-permute-done((bf16[32,3456]{1,0:T(8,128)(2,1)S(1)}, bf16[32,3456]{1,0:T(8,128)(2,1)S(1)}, u32[]{:S(2)}, u32[]{:S(2)}) %collective-permute-start.5) | collective-permute-done | bytes 221216 | tf_op jit(solution)/shard_map/ppermute | solution.py:453
  44.1 0.4 shard_map.122
  44.4 1.6 %collective-permute-start.6 = (bf16[2,32,1024]{2,1,0:T(8,128)(2,1)S(1)}, bf16[2,32,1024]{2,1,0:T(8,128)(2,1)S(1)}, u32[]{:S(2)}, u32[]{:S(2)}) collective-permute-start(bf16[2,32,1024]{2,1,0:T(8,128)(2,1)S(1)} %get-tuple-element.49), channel_id=1, source_target_pairs={{0,8},{8,16},{16,24},{24,0},{1,9},{9,17},{17,25},{25,1},{2,10},{10... | collective-permute-start | bytes 393224 | tf_op jit(solution)/shard_map/ppermute | solution.py:456
  46.0 1.2 %collective-permute-start.7 = (bf16[2,32,1024]{2,1,0:T(8,128)(2,1)S(1)}, bf16[2,32,1024]{2,1,0:T(8,128)(2,1)S(1)}, u32[]{:S(2)}, u32[]{:S(2)}) collective-permute-start(bf16[2,32,1024]{2,1,0:T(8,128)(2,1)S(1)} %get-tuple-element.50), channel_id=1, source_target_pairs={{0,16},{8,24},{16,0},{24,8},{1,17},{9,25},{17,1},{25,9},{2,18},{10... | collective-permute-start | bytes 393224 | tf_op jit(solution)/shard_map/ppermute | solution.py:456
  47.3 0.0 collective-permute-done.9.refs_1_
  47.3 2.7 %collective-permute-start.8 = (bf16[2,32,1024]{2,1,0:T(8,128)(2,1)S(1)}, bf16[2,32,1024]{2,1,0:T(8,128)(2,1)S(1)}, u32[]{:S(2)}, u32[]{:S(2)}) collective-permute-start(bf16[2,32,1024]{2,1,0:T(8,128)(2,1)S(1)} %get-tuple-element.51), channel_id=1, source_target_pairs={{0,24},{8,0},{16,8},{24,16},{1,25},{9,1},{17,9},{25,17},{2,26},{10... | collective-permute-start | bytes 393224 | tf_op jit(solution)/shard_map/ppermute | solution.py:456
  50.0 8.4 %collective-permute-done.10.refs_2_ = bf16[928,128]{1,0:T(8,128)(2,1)S(1)} collective-permute-done((bf16[928,128]{1,0:T(8,128)(2,1)S(1)}, bf16[928,128]{1,0:T(8,128)(2,1)S(1)}, u32[]{:S(2)}, u32[]{:S(2)}) %collective-permute-start.10) | collective-permute-done | bytes 237600 | tf_op jit(solution)/shard_map/ppermute | solution.py:456
  58.4 5.0 %shard_map.124 = f32[1,7,512,128]{3,2,1,0:T(8,128)} custom-call(bf16[928,128]{1,0:T(8,128)(2,1)S(1)} %copy-done.2, bf16[928,128]{1,0:T(8,128)(2,1)S(1)} %collective-permute-done.9.refs_1_, bf16[928,128]{1,0:T(8,128)(2,1)S(1)} %collective-permute-done.10.refs_2_, bf16[928,128]{1,0:T(8,128)(2,1)S(1)} %collective-permute-done.11.refs_3_), custom_call_target="tpu_custom_call" | custom-call | flops 469762048 | bytes 1835008 | tf_op jit(solution)/shard_map/pallas_call | solution.py:420
  63.4 5.2 %collective-permute-done.7.rest_1_ = bf16[2,32,1024]{2,1,0:T(8,128)(2,1)S(1)} collective-permute-done((bf16[2,32,1024]{2,1,0:T(8,128)(2,1)S(1)}, bf16[2,32,1024]{2,1,0:T(8,128)(2,1)S(1)}, u32[]{:S(2)}, u32[]{:S(2)}) %collective-permute-start.7) | collective-permute-done | bytes 131104 | tf_op jit(solution)/shard_map/ppermute | solution.py:456
  68.6 0.7 %shard_map.123 = (f32[32,864]{1,0:T(8,128)}, f32[32,864]{1,0:T(8,128)}, f32[32,128]{1,0:T(8,128)S(1)}) custom-call(s32[1]{0:T(128)} %bitcast.table_ref, f32[2,32,864]{2,1,0:T(8,128)S(1)} %get-tuple-element.47.own_ref, f32[32,128]{1,0:T(8,128)S(1)} %get-tuple-element.48.bias_ref, bf16[2,32,1024]{2,1,0:T(8,128)(2,1)S(1)} %collective-permute-done.6.rest_0_, ...), custom_call_target="tpu_custom_call" | custom-call | tf_op jit(solution)/shard_map/pallas_call | solution.py:375
  69.3 0.6 slice_bitcast_fusion
  (17 shorter events, 0.0 us)
Async XLA Ops:
  0.6 7.1 %collective-permute-start = (bf16[128,3456]{1,0:T(8,128)(2,1)}, bf16[128,3456]{1,0:T(8,128)(2,1)S(1)}, u32[]{:S(2)}, u32[]{:S(2)}) collective-permute-start(bf16[128,3456]{1,0:T(8,128)(2,1)} %act_hbm.3), channel_id=1, source_target_pairs={{0,1},{1,0},{2,3},{3,2},{4,5},{5,4},{6,7},{7,6},{8,9},{9,8},{10,11... | collective-permute-start | bytes 2654216 | tf_op jit(solution)/shard_map/ppermute | solution.py:453
  1.1 6.6 %collective-permute-start.1 = (bf16[128,3456]{1,0:T(8,128)(2,1)}, bf16[128,3456]{1,0:T(8,128)(2,1)S(1)}, u32[]{:S(2)}, u32[]{:S(2)}) collective-permute-start(bf16[128,3456]{1,0:T(8,128)(2,1)} %cot_hbm.3), channel_id=1, source_target_pairs={{0,1},{1,0},{2,3},{3,2},{4,5},{5,4},{6,7},{7,6},{8,9},{9,8},{10,11... | collective-permute-start | bytes 2654216 | tf_op jit(solution)/shard_map/ppermute | solution.py:453
  7.8 0.9 %copy-start.4 = (bf16[128,3456]{1,0:T(8,128)(2,1)}, bf16[128,3456]{1,0:T(8,128)(2,1)S(1)}, u32[]{:S(2)}) copy-start(bf16[128,3456]{1,0:T(8,128)(2,1)S(1)} %collective-permute-done.act_other_hbm) | copy-start | bytes 2654212
  7.8 1.2 %copy-start.5 = (bf16[128,3456]{1,0:T(8,128)(2,1)}, bf16[128,3456]{1,0:T(8,128)(2,1)S(1)}, u32[]{:S(2)}) copy-start(bf16[128,3456]{1,0:T(8,128)(2,1)S(1)} %collective-permute-done.1.cot_other_hbm) | copy-start | bytes 2654212
  9.0 27.5 %copy-start.8 = (bf16[928,128]{1,0:T(8,128)(2,1)S(1)}, bf16[928,128]{1,0:T(8,128)(2,1)}, u32[]{:S(2)}) copy-start(bf16[928,128]{1,0:T(8,128)(2,1)} %get-tuple-element.56) | copy-start | bytes 712708
  9.0 29.7 %copy-start.7 = (bf16[928,128]{1,0:T(8,128)(2,1)S(1)}, bf16[928,128]{1,0:T(8,128)(2,1)}, u32[]{:S(2)}) copy-start(bf16[928,128]{1,0:T(8,128)(2,1)} %get-tuple-element.57) | copy-start | bytes 712708
  9.0 32.3 %copy-start.6 = (bf16[928,128]{1,0:T(8,128)(2,1)S(1)}, bf16[928,128]{1,0:T(8,128)(2,1)}, u32[]{:S(2)}) copy-start(bf16[928,128]{1,0:T(8,128)(2,1)} %get-tuple-element.58) | copy-start | bytes 712708
  16.7 15.1 %collective-permute-start.2 = (bf16[64,3584]{1,0:T(8,128)(2,1)}, bf16[64,3584]{1,0:T(8,128)(2,1)S(1)}, u32[]{:S(2)}, u32[]{:S(2)}) collective-permute-start(bf16[64,3584]{1,0:T(8,128)(2,1)} %get-tuple-element.38), channel_id=1, source_target_pairs={{0,2},{1,3},{2,0},{3,1},{4,6},{5,7},{6,4},{7,5},{8,10},{9,11},{10,... | collective-permute-start | bytes 1376264 | tf_op jit(solution)/shard_map/ppermute | solution.py:453
  19.6 12.1 %collective-permute-start.3 = (bf16[64,3456]{1,0:T(8,128)(2,1)}, bf16[64,3456]{1,0:T(8,128)(2,1)S(1)}, u32[]{:S(2)}, u32[]{:S(2)}) collective-permute-start(bf16[64,3456]{1,0:T(8,128)(2,1)} %get-tuple-element.40), channel_id=1, source_target_pairs={{0,4},{1,5},{2,6},{3,7},{4,0},{5,1},{6,2},{7,3},{8,12},{9,13},{10,... | collective-permute-start | bytes 1327112 | tf_op jit(solution)/shard_map/ppermute | solution.py:453
  31.7 1.2 %copy-start = (f32[64,3456]{1,0:T(8,128)S(1)}, f32[64,3456]{1,0:T(8,128)}, u32[]{:S(2)}) copy-start(f32[64,3456]{1,0:T(8,128)} %get-tuple-element.37.up_keep_ref) | copy-start | bytes 2654212
  32.9 1.2 %copy-start.1 = (f32[64,3456]{1,0:T(8,128)S(1)}, f32[64,3456]{1,0:T(8,128)}, u32[]{:S(2)}) copy-start(f32[64,3456]{1,0:T(8,128)} %get-tuple-element.39.down_keep_ref) | copy-start | bytes 2654212
  34.1 0.7 %copy-start.3 = (f32[32,128]{1,0:T(8,128)S(1)}, f32[32,128]{1,0:T(8,128)}, u32[]{:S(2)}) copy-start(f32[32,128]{1,0:T(8,128)} %get-tuple-element.41.bias_ref) | copy-start | bytes 49156
  34.8 23.6 %copy-start.2 = (bf16[928,128]{1,0:T(8,128)(2,1)S(1)}, bf16[928,128]{1,0:T(8,128)(2,1)}, u32[]{:S(2)}) copy-start(bf16[928,128]{1,0:T(8,128)(2,1)} %get-tuple-element.59.refs_0_) | copy-start | bytes 712708
  34.9 9.1 %collective-permute-start.4 = (bf16[32,3712]{1,0:T(8,128)(2,1)S(1)}, bf16[32,3712]{1,0:T(8,128)(2,1)S(1)}, u32[]{:S(2)}, u32[]{:S(2)}) collective-permute-start(bf16[32,3712]{1,0:T(8,128)(2,1)S(1)} %get-tuple-element.43), channel_id=1, source_target_pairs={{0,4},{1,5},{2,6},{3,7},{4,0},{5,1},{6,2},{7,3},{8,12},{9,13},{10,... | collective-permute-start | bytes 712712 | tf_op jit(solution)/shard_map/ppermute | solution.py:453
  36.5 10.7 %collective-permute-start.9 = (bf16[928,128]{1,0:T(8,128)(2,1)S(1)}, bf16[928,128]{1,0:T(8,128)(2,1)S(1)}, u32[]{:S(2)}, u32[]{:S(2)}) collective-permute-start(bf16[928,128]{1,0:T(8,128)(2,1)S(1)} %copy-done.8), channel_id=1, source_target_pairs={{0,8},{8,16},{16,24},{24,0},{1,9},{9,17},{17,25},{25,1},{2,10},{10... | collective-permute-start | bytes 712712 | tf_op jit(solution)/shard_map/ppermute | solution.py:456
  38.1 5.9 %collective-permute-start.5 = (bf16[32,3456]{1,0:T(8,128)(2,1)S(1)}, bf16[32,3456]{1,0:T(8,128)(2,1)S(1)}, u32[]{:S(2)}, u32[]{:S(2)}) collective-permute-start(bf16[32,3456]{1,0:T(8,128)(2,1)S(1)} %get-tuple-element.45), channel_id=1, source_target_pairs={{0,2},{1,3},{2,0},{3,1},{4,6},{5,7},{6,4},{7,5},{8,10},{9,11},{10,... | collective-permute-start | bytes 663560 | tf_op jit(solution)/shard_map/ppermute | solution.py:453
  38.7 19.7 %collective-permute-start.10 = (bf16[928,128]{1,0:T(8,128)(2,1)S(1)}, bf16[928,128]{1,0:T(8,128)(2,1)S(1)}, u32[]{:S(2)}, u32[]{:S(2)}) collective-permute-start(bf16[928,128]{1,0:T(8,128)(2,1)S(1)} %copy-done.7), channel_id=1, source_target_pairs={{0,16},{8,24},{16,0},{24,8},{1,17},{9,25},{17,1},{25,9},{2,18},{10... | collective-permute-start | bytes 712712 | tf_op jit(solution)/shard_map/ppermute | solution.py:456
  41.3 17.1 %collective-permute-start.11 = (bf16[928,128]{1,0:T(8,128)(2,1)S(1)}, bf16[928,128]{1,0:T(8,128)(2,1)S(1)}, u32[]{:S(2)}, u32[]{:S(2)}) collective-permute-start(bf16[928,128]{1,0:T(8,128)(2,1)S(1)} %copy-done.6), channel_id=1, source_target_pairs={{0,24},{8,0},{16,8},{24,16},{1,25},{9,1},{17,9},{25,17},{2,26},{10... | collective-permute-start | bytes 712712 | tf_op jit(solution)/shard_map/ppermute | solution.py:456
  44.4 19.0 %collective-permute-start.6 = (bf16[2,32,1024]{2,1,0:T(8,128)(2,1)S(1)}, bf16[2,32,1024]{2,1,0:T(8,128)(2,1)S(1)}, u32[]{:S(2)}, u32[]{:S(2)}) collective-permute-start(bf16[2,32,1024]{2,1,0:T(8,128)(2,1)S(1)} %get-tuple-element.49), channel_id=1, source_target_pairs={{0,8},{8,16},{16,24},{24,0},{1,9},{9,17},{17,25},{25,1},{2,10},{10... | collective-permute-start | bytes 393224 | tf_op jit(solution)/shard_map/ppermute | solution.py:456
  46.0 22.5 %collective-permute-start.7 = (bf16[2,32,1024]{2,1,0:T(8,128)(2,1)S(1)}, bf16[2,32,1024]{2,1,0:T(8,128)(2,1)S(1)}, u32[]{:S(2)}, u32[]{:S(2)}) collective-permute-start(bf16[2,32,1024]{2,1,0:T(8,128)(2,1)S(1)} %get-tuple-element.50), channel_id=1, source_target_pairs={{0,16},{8,24},{16,0},{24,8},{1,17},{9,25},{17,1},{25,9},{2,18},{10... | collective-permute-start | bytes 393224 | tf_op jit(solution)/shard_map/ppermute | solution.py:456
  47.3 21.3 %collective-permute-start.8 = (bf16[2,32,1024]{2,1,0:T(8,128)(2,1)S(1)}, bf16[2,32,1024]{2,1,0:T(8,128)(2,1)S(1)}, u32[]{:S(2)}, u32[]{:S(2)}) collective-permute-start(bf16[2,32,1024]{2,1,0:T(8,128)(2,1)S(1)} %get-tuple-element.51), channel_id=1, source_target_pairs={{0,24},{8,0},{16,8},{24,16},{1,25},{9,1},{17,9},{25,17},{2,26},{10... | collective-permute-start | bytes 393224 | tf_op jit(solution)/shard_map/ppermute | solution.py:456

commit v3 on v2

--- a/solution.py
+++ b/solution.py
@@ -29,49 +29,49 @@
 
 def pieces_of(width):
     blocks = width // EMBED_WIDTH
-    parts = max(p for p in (3, 2, 1) if blocks % p == 0)
+    parts = max(p for p in (9, 3, 1) if blocks % p == 0)
     step = width // parts
     return [(k * step, step) for k in range(parts)]
 
 
-def fetch(pairs, width, sems):
-    copies = {}
-    for place, (start, size) in enumerate(pieces_of(width)):
-        for which, (source, target) in enumerate(pairs):
-            part = pl.ds(start, size)
-            copy = pltpu.make_async_copy(
-                source.at[:, part], target.at[:, part], sems.at[which, place]
-            )
-            copy.start()
-            copies[which, place] = copy
-    return lambda which, place: copies[which, place].wait()
-
-
-def factors(act, cot, down, up, width, wait):
-    hidden = back = None
-    for place, (start, size) in enumerate(pieces_of(width)):
-        part = slice(start, start + size)
-        wait(0, place)
-        wait(1, place)
-        value = act[:, part]
-        term = lax.dot_general(value, down[:, part], NT, preferred_element_type=F32)
-        hidden = term if hidden is None else hidden + term
-        wait(2, place)
-        wait(3, place)
-        scaled_b = (cot[:, part].astype(F32) * value.astype(F32)).astype(BF16)
-        term = lax.dot_general(scaled_b, up[:, part], NT, preferred_element_type=F32)
-        back = term if back is None else back + term
-    return hidden.astype(BF16), back.astype(BF16)
+def order_matrix(rep_index, size, block, bits):
+    out_row = lax.broadcasted_iota(jnp.int32, (size, size), 0)
+    in_row = lax.broadcasted_iota(jnp.int32, (size, size), 1)
+    source = lax.rem(out_row, block)
+    position = lax.div(out_row, block)
+    for place, bit in enumerate(bits):
+        flag = lax.rem(lax.div(position, 1 << (len(bits) - 1 - place)), 2)
+        own = lax.rem(lax.div(rep_index, bit), 2)
+        source = source + jnp.where(flag == own, 0, bit) * block
+    return (source == in_row).astype(F32).astype(BF16)
 
 
 def input_kernel(
-    n_table, slots, table_ref, owner_ref, act_hbm, cot_hbm, down_hbm, up_hbm, bias_ref, ids_ref, length_ref,
-    hidden_ref, back_ref, dense_ref, *rest,
+    n_table, slots, up_bits, down_bits, table_ref, rep_ref, owner_ref,
+    act_hbm, cot_hbm, down_hbm, up_hbm, bias_ref, ids_ref, length_ref,
+    keep_hbm, send_hbm, dense_hbm, *rest,
 ):
     outs = rest[:n_table]
-    act, cot, down, up, store, id_store, feature_ref, sems = rest[n_table:]
+    act, cot, down, up, keep, send, store, message, id_store, feature_ref, in_sems, out_sems = rest[n_table:]
     tokens, width = act.shape
-    wait = fetch(((act_hbm, act), (down_hbm, down), (cot_hbm, cot), (up_hbm, up)), width, sems)
+    rank = down.shape[0]
+    half = rank // 2
+    pieces = pieces_of(width)
+    arrays = ((act_hbm, act), (down_hbm, down), (cot_hbm, cot), (up_hbm, up))
+    fetched = []
+    for place, (start, size) in enumerate(pieces):
+        part = pl.ds(start, size)
+        fetched.append(
+            [
+                pltpu.make_async_copy(source.at[:, part], target.at[:, part], in_sems.at[which, place])
+                for which, (source, target) in enumerate(arrays)
+            ]
+        )
+        for copy in fetched[-1]:
+            copy.start()
+    block = rank >> len(up_bits)
+    up_order = order_matrix(rep_ref[0], rank, block, up_bits)
+    down_order = order_matrix(rep_ref[0], rank, block, down_bits)
     for place in range(n_table * slots):
         feature_ref[place] = SPARSE_FEATURES
     for feature in range(SPARSE_FEATURES):
@@ -88,71 +88,89 @@
             length = jnp.where(feature < SPARSE_FEATURES, length_ref[pl.ds(at, 1), :], 0)
             ids = jnp.where(entries < length, ids_ref[at] - EMPTY, EMPTY)
             id_store[shift, slot * BAG : (slot + 1) * BAG, :] = ids.astype(F32)
-        outs[shift][slots * tokens :, :] = id_store[shift].astype(BF16)
-    hidden, back = factors(act, cot, down, up, width, wait)
-    hidden_ref[...] = hidden
-    back_ref[...] = back
+        message[shift, slots * tokens :, :] = id_store[shift].astype(BF16)
+    hidden = back = None
+    for (start, size), copies in zip(pieces, fetched):
+        part = slice(start, start + size)
+        for copy in copies:
+            copy.wait()
+        value = act[:, part]
+        term = lax.dot_general(value, down[:, part], NT, preferred_element_type=F32)
+        hidden = term if hidden is None else hidden + term
+        scaled_b = (cot[:, part].astype(F32) * value.astype(F32)).astype(BF16)
+        term = lax.dot_general(scaled_b, up[:, part], NT, preferred_element_type=F32)
+        back = term if back is None else back + term
+    hidden, back = hidden.astype(BF16), back.astype(BF16)
+    rows = lax.dot_general(up_order, hidden, NT, preferred_element_type=F32).astype(BF16)
+    keep[0], send[0] = rows[:half], rows[half:]
+    rows = lax.dot_general(down_order, back, NT, preferred_element_type=F32).astype(BF16)
+    keep[1], send[1] = rows[:half], rows[half:]
+    written = [
+        pltpu.make_async_copy(send, send_hbm, out_sems.at[0]),
+        pltpu.make_async_copy(keep, keep_hbm, out_sems.at[1]),
+    ]
+    for copy in written:
+        copy.start()
     blocks = 3
     for first in range(0, width // EMBED_WIDTH, blocks):
         part = slice(first * EMBED_WIDTH, (first + blocks) * EMBED_WIDTH)
         mixed = jnp.dot(hidden, up[:, part], preferred_element_type=F32)
         tail = jnp.dot(back, down[:, part], preferred_element_type=F32)
         for k in range(blocks):
-            block = first + k
+            place = first + k
             mine = slice(k * EMBED_WIDTH, (k + 1) * EMBED_WIDTH)
-            cols = slice(block * EMBED_WIDTH, (block + 1) * EMBED_WIDTH)
-            bias = bias_ref[block : block + 1, :]
+            cols = slice(place * EMBED_WIDTH, (place + 1) * EMBED_WIDTH)
+            bias = bias_ref[place : place + 1, :]
             grad = cot[:, cols].astype(F32) * (1.0 + (mixed[:, mine] + bias)) + tail[:, mine]
-            store[block] = grad.astype(BF16)
-    dense_ref[...] = store[0]
+            store[place] = grad.astype(BF16)
+    written.append(pltpu.make_async_copy(store.at[0], dense_hbm, out_sems.at[2]))
+    written[-1].start()
     for shift in range(n_table):
         for slot in range(slots):
             rows = slice(slot * tokens, (slot + 1) * tokens)
-            outs[shift][rows, :] = store[feature_ref[shift * slots + slot] + 1]
-
-
-def input_call(table_index, owners, act, cot, down, up, bias, ids, lengths, n_table, slots):
+            message[shift, rows, :] = store[feature_ref[shift * slots + slot] + 1]
+        written.append(pltpu.make_async_copy(message.at[shift], outs[shift], out_sems.at[3 + shift]))
+        written[-1].start()
+    for copy in written:
+        copy.wait()
+
+
+def input_call(
+    table_index, rep_index, owners, act, cot, down, up, bias, ids, lengths, n_table, slots, up_bits, down_bits
+):
     tokens, width = act.shape
     rank = down.shape[0]
     id_rows = -(-slots * BAG // 16) * 16
-    parts = len(pieces_of(width))
+    sent = slots * tokens + id_rows
     return pl.pallas_call(
-        functools.partial(input_kernel, n_table, slots),
-        in_specs=[SMEM, SMEM, ANY, ANY, ANY, ANY, VMEM, VMEM, VMEM],
-        out_specs=[VMEM] * (3 + n_table),
+        functools.partial(input_kernel, n_table, slots, up_bits, down_bits),
+        in_specs=[SMEM, SMEM, SMEM, ANY, ANY, ANY, ANY, VMEM, VMEM, VMEM],
+        out_specs=[ANY] * (3 + n_table),
         out_shape=[
-            jax.ShapeDtypeStruct((tokens, rank), BF16),
-            jax.ShapeDtypeStruct((tokens, rank), BF16),
+            jax.ShapeDtypeStruct((2, rank // 2, tokens), BF16),
+            jax.ShapeDtypeStruct((2, rank // 2, tokens), BF16),
             jax.ShapeDtypeStruct((tokens, EMBED_WIDTH), BF16),
         ]
-        + [jax.ShapeDtypeStruct((slots * tokens + id_rows, EMBED_WIDTH), BF16)] * n_table,
+        + [jax.ShapeDtypeStruct((sent, EMBED_WIDTH), BF16)] * n_table,
         scratch_shapes=[
             pltpu.VMEM((tokens, width), BF16),
             pltpu.VMEM((tokens, width), BF16),
             pltpu.VMEM((rank, width), BF16),
             pltpu.VMEM((rank, width), BF16),
+            pltpu.VMEM((2, rank // 2, tokens), BF16),
+            pltpu.VMEM((2, rank // 2, tokens), BF16),
             pltpu.VMEM((SPARSE_FEATURES + 2, tokens, EMBED_WIDTH), BF16),
+            pltpu.VMEM((n_table, sent, EMBED_WIDTH), BF16),
             pltpu.VMEM((n_table, id_rows, EMBED_WIDTH), F32),
             pltpu.SMEM((n_table * slots,), jnp.int32),
-            pltpu.SemaphoreType.DMA((4, parts)),
+            pltpu.SemaphoreType.DMA((4, len(pieces_of(width)))),
+            pltpu.SemaphoreType.DMA((3 + n_table,)),
         ],
         compiler_params=params(60),
         cost_estimate=pl.CostEstimate(
             flops=8 * tokens * rank * width, bytes_accessed=4 * (tokens + rank) * width, transcendentals=0
         ),
-    )(table_index, owners, act, cot, down, up, bias, ids, lengths)
-
-
-def order_matrix(rep_index, rows, size, block, bits):
-    out_row = lax.broadcasted_iota(jnp.int32, (rows, size), 0)
-    in_row = lax.broadcasted_iota(jnp.int32, (rows, size), 1)
-    source = lax.rem(out_row, block)
-    position = lax.div(out_row, block)
-    for place, bit in enumerate(bits):
-        flag = lax.rem(lax.div(position, 1 << (len(bits) - 1 - place)), 2)
-        own = lax.rem(lax.div(rep_index, bit), 2)
-        source = source + jnp.where(flag == own, 0, bit) * block
-    return (source == in_row).astype(F32).astype(BF16)
+    )(table_index, rep_index, owners, act, cot, down, up, bias, ids, lengths)
 
 
 def bias_terms(value):
@@ -182,35 +200,15 @@
 
 
 def terms_kernel(
-    ride, up_bits, down_bits, rep_ref, hidden_ref, back_ref, act_hbm, cot_hbm, act_other_hbm, cot_other_hbm,
-    down_hbm, up_hbm, up_keep_ref, up_send_ref, down_keep_ref, down_send_ref, bias_ref,
-    act, cot, act_other, cot_other, down, up, sems,
+    ride, keep_ref, other_ref, act, cot, act_other, cot_other,
+    up_keep_ref, up_send_ref, down_keep_ref, down_send_ref, bias_ref,
 ):
-    tokens, width = act.shape
-    rank = down.shape[0]
-    wait = fetch(
-        (
-            (act_other_hbm, act_other), (down_hbm, down), (cot_other_hbm, cot_other), (up_hbm, up),
-            (act_hbm, act), (cot_hbm, cot),
-        ),
-        width,
-        sems,
-    )
-    half, block = rank // 2, rank >> len(up_bits)
-    up_order = order_matrix(rep_ref[0], half, rank, block, up_bits)
-    down_order = order_matrix(rep_ref[0], half, rank, block, down_bits)
-    hidden_other, back_other = factors(act_other, cot_other, down, up, width, wait)
-    hidden = jnp.concatenate([hidden_ref[...], hidden_other], axis=0)
-    back = jnp.concatenate([back_ref[...], back_other], axis=0)
-    hidden = lax.dot_general(up_order, hidden, NT, preferred_element_type=F32).astype(BF16)
-    back = lax.dot_general(down_order, back, NT, preferred_element_type=F32).astype(BF16)
-    for place in range(len(pieces_of(width))):
-        wait(4, place)
-        wait(5, place)
+    width = act.shape[1]
+    hidden = jnp.concatenate([keep_ref[0], other_ref[0]], axis=1)
+    back = jnp.concatenate([keep_ref[1], other_ref[1]], axis=1)
     blocks = 3
-    keep = half // 2
-    if width // EMBED_WIDTH < BIAS_ROWS:
-        bias_ref[...] = jnp.zeros_like(bias_ref)
+    keep = hidden.shape[0] // 2
+    bias_ref[...] = jnp.zeros_like(bias_ref)
     for first in range(0, width // EMBED_WIDTH, blocks):
         part = slice(first * EMBED_WIDTH, (first + blocks) * EMBED_WIDTH)
         values = jnp.concatenate([act[:, part], act_other[:, part]], axis=0)
@@ -231,18 +229,13 @@
         bias_ref[...] = high + low
 
 
-def terms_call(
-    rep_index, hidden, back, act, cot, act_other, cot_other, down, up, ride, up_bits, down_bits
-):
+def terms_call(keep, other, act, cot, act_other, cot_other, ride):
     tokens, width = act.shape
-    rank = down.shape[0]
-    rows = rank // 4
+    rows = keep.shape[1] // 2
     extra = extra_columns(rows) if ride else 0
-    parts = len(pieces_of(width))
-    wide = pltpu.VMEM((tokens, width), BF16)
     return pl.pallas_call(
-        functools.partial(terms_kernel, ride, up_bits, down_bits),
-        in_specs=[SMEM, VMEM, VMEM] + [ANY] * 6,
+        functools.partial(terms_kernel, ride),
+        in_specs=[VMEM] * 6,
         out_specs=[VMEM] * 5,
         out_shape=[
             jax.ShapeDtypeStruct((rows, width), F32),
@@ -251,17 +244,11 @@
             jax.ShapeDtypeStruct((rows, width), BF16),
             jax.ShapeDtypeStruct((BIAS_ROWS, EMBED_WIDTH), F32),
         ],
-        scratch_shapes=[
-            wide, wide, wide, wide,
-            pltpu.VMEM((rank, width), BF16),
-            pltpu.VMEM((rank, width), BF16),
-            pltpu.SemaphoreType.DMA((6, parts)),
-        ],
-        compiler_params=params(60),
+        compiler_params=params(16),
         cost_estimate=pl.CostEstimate(
-            flops=8 * tokens * rank * width, bytes_accessed=8 * tokens * width + 4 * rank * width, transcendentals=0
+            flops=16 * tokens * rows * width, bytes_accessed=8 * tokens * width + 12 * rows * width, transcendentals=0
         ),
-    )(rep_index, hidden, back, act, cot, act_other, cot_other, down, up)
+    )(keep, other, act, cot, act_other, cot_other)
 
 
 def halve_kernel(
@@ -366,7 +353,7 @@
         total = store[0]
         for table in range(1, n_table):
             total = total + store[table]
-    bias_out_ref[...] = total * scale
+    bias_out_ref[...] = total[: bias_out_ref.shape[0]] * scale
 
 
 def finish_call(table_index, own, bias_sum, arrived, scale, ride):
@@ -379,7 +366,7 @@
         out_shape=[
             jax.ShapeDtypeStruct((rows, columns), F32),
             jax.ShapeDtypeStruct((rows, columns), F32),
-            jax.ShapeDtypeStruct(bias_sum.shape, F32),
+            jax.ShapeDtypeStruct((columns * n_table // EMBED_WIDTH, EMBED_WIDTH), F32),
         ],
         scratch_shapes=[pltpu.VMEM((n_table,) + bias_sum.shape, F32)],
         compiler_params=params(16),
@@ -424,7 +411,7 @@
         out_specs=pl.BlockSpec((1, 1, TABLE_REACH_ROWS, EMBED_WIDTH), lambda i: (0, i, 0, 0)),
         out_shape=jax.ShapeDtypeStruct((1, slots, TABLE_REACH_ROWS, EMBED_WIDTH), F32),
         scratch_shapes=[pltpu.VMEM((n_table, id_rows, tokens), jnp.int32)],
-        compiler_params=params(32),
+        compiler_params=params(16),
         cost_estimate=pl.CostEstimate(
             flops=2 * slots * n_table * tokens * TABLE_REACH_ROWS * EMBED_WIDTH,
             bytes_accessed=4 * slots * TABLE_REACH_ROWS * EMBED_WIDTH,
@@ -457,15 +444,15 @@
 
     act_other = swap(activations, "rep", 1)
     cot_other = swap(cotangent, "rep", 1)
-    hidden, back, dense_grad, *parts = input_call(
-        table_index, feature_table_slot, activations, cotangent, down_weight, up_weight,
+    keep, send, dense_grad, *parts = input_call(
+        table_index, rep_index, feature_table_slot, activations, cotangent, down_weight, up_weight,
         bias.reshape(-1, EMBED_WIDTH), jnp.transpose(bag_ids, (1, 2, 0)), jnp.transpose(bag_lengths, (1, 0)),
-        n_table, slots,
+        n_table, slots, up_bits, down_bits,
     )
+    other = swap(send, "rep", 1)
     parts = [parts[0]] + [shifted(parts[k], k) for k in range(1, n_table)]
     up_keep, up_send, down_keep, down_send, bias_sum = terms_call(
-        rep_index, hidden, back, activations, cotangent, act_other, cot_other, down_weight, up_weight,
-        ride, up_bits, down_bits,
+        keep, other, activations, cotangent, act_other, cot_other, ride
     )
     for place, (up_bit, down_bit) in enumerate(zip(up_bits[1:], down_bits[1:])):
         up_in = swap(up_send, "rep", up_bit)
@@ -487,6 +474,7 @@
     if not ride:
         for bit in [1 << k for k in range(n_table.bit_length() - 1)]:
             bias_sum = bias_sum + swap(bias_sum, "table", bit)
+    (up_in, down_in), parts = lax.optimization_barrier(((up_in, down_in), parts))
     own, bias_sum, *sends = split_call(
         table_index, up_keep, up_in, down_keep, down_in, bias_sum, n_table, scale, ride
     )
@@ -494,7 +482,7 @@
     up_grad, down_grad, bias_grad = finish_call(table_index, own, bias_sum, arrived, scale, ride)
     parts, _ = lax.optimization_barrier((parts, own))
     row_grad = rows_call(parts, slots)
-    bias_grad = bias_grad[: width // EMBED_WIDTH].reshape(width)
+    bias_grad = bias_grad.reshape(width)
     return (dense_grad, up_grad, down_grad, bias_grad, row_grad)
 
 

time: 71.2 us -> 51.5 us (0.72)
  waiting for transfers between devices: 25.5 us -> 15 us
  Pallas kernels: 20.4 us -> 13 us
  local copies, waits for them, and re-layouts: 4.87 us -> 0.86 us
  starting transfers between devices: 18.4 us -> 21.3 us
    pallas_call x2, Pallas kernels: 14.2 us -> 6.85 us  [the longest x1 6.01 us: input_call(): pl.pallas_call(functools.partial(input_kernel, n_table, slots, up_bits, d...]
    ppermute x6 -> x7, waiting for transfers between devices: 11.9 us -> 6.03 us  [swap(): return lax.ppermute(value, axis, [(k, k ^ bit) for k in range(size)])]
    ppermute x6, waiting for transfers between devices: 13.6 us -> 8.94 us  [shifted(): lax.ppermute(value, 'table', [(k, (k + shift) % n_table) for k in range(n...]
    unnamed x18 -> x14, local copies, waits for them, and re-layouts: 4.26 us -> 0.86 us
    ppermute x6, starting transfers between devices: 11.1 us -> 13.6 us  [shifted(): lax.ppermute(value, 'table', [(k, (k + shift) % n_table) for k in range(n...]
    ppermute x6 -> x7, starting transfers between devices: 7.3 us -> 7.72 us  [swap(): return lax.ppermute(value, axis, [(k, k ^ bit) for k in range(size)])]
  transfers between devices with their start and end apart: 12 -> 13, of which waited for: 4 -> 4; matrix products, arithmetic and copies ran while one was open for 0% -> 0% of each run, Pallas kernels for 17% -> 22%
where the time goes in v3:
time: 51.5 us; the launch traced here: 50.9 us
  starting transfers between devices  21.3 us (41%)
  waiting for transfers between devices  15 us (29%)
  Pallas kernels  13 us (25%)
  local copies, waits for them, and re-layouts  0.86 us (2%)
  between operations  0.7 us (1%)
    ppermute x6, starting transfers between devices, shifted(): lax.ppermute(value, 'table', [(k, (k + shift) % n_table) for k in range(n...  13.6 us
    ppermute x6, waiting for transfers between devices, shifted(): lax.ppermute(value, 'table', [(k, (k + shift) % n_table) for k in range(n...  8.94 us
    ppermute x7, starting transfers between devices, swap(): return lax.ppermute(value, axis, [(k, k ^ bit) for k in range(size)])  7.72 us
    ppermute x7, waiting for transfers between devices, swap(): return lax.ppermute(value, axis, [(k, k ^ bit) for k in range(size)])  6.03 us
    pallas_call x1, Pallas kernels, input_call(): pl.pallas_call(functools.partial(input_kernel, n_table, slots, up_bits, d...  6.01 us
    pallas_call x1, Pallas kernels, rows_call(): pl.pallas_call(functools.partial(rows_kernel, n_table, slots), grid=(slot...  4.97 us
  transfers between devices with their start and end apart: 13, of which 4 were waited for; matrix products, arithmetic and copies ran while one was open for 0% of the time, Pallas kernels for 22%

profile of v3, /device:TPU:0, one launch (start us, length us, event | category | flops | bytes accessed | tf_op | source)
XLA Modules:
  0.0 50.9 jit_solution(5238606630226980424)
XLA Ops:
  0.6 0.5 %collective-permute-start.1 = (bf16[128,3456]{1,0:T(8,128)(2,1)}, bf16[128,3456]{1,0:T(8,128)(2,1)S(1)}, u32[]{:S(2)}, u32[]{:S(2)}) collective-permute-start(bf16[128,3456]{1,0:T(8,128)(2,1)} %act.1), channel_id=1, source_target_pairs={{0,1},{1,0},{2,3},{3,2},{4,5},{5,4},{6,7},{7,6},{8,9},{9,8},{10,11... | collective-permute-start | bytes 2654216 | tf_op jit(solution)/shard_map/ppermute | solution.py:440
  1.2 0.1 collective-permute-start.2
  1.2 6.0 %shard_map.119 = (bf16[2,128,128]{2,1,0:T(8,128)(2,1)}, bf16[2,128,128]{2,1,0:T(8,128)(2,1)}, bf16[128,128]{1,0:T(8,128)(2,1)}, bf16[928,128]{1,0:T(8,128)(2,1)}...) custom-call(s32[1]{0:T(128)} %bitcast.table_ref, s32[1]{0:T(128)} %bitcast.1.rep_ref, ...), custom_call_target="tpu_custom_call" | custom-call | flops 905969664 | bytes 5308416 | tf_op jit(solution)/shard_map/pallas_call | solution.py:145
  7.3 0.5 collective-permute-start
  7.7 1.1 %collective-permute-done.other_ref = bf16[2,128,128]{2,1,0:T(8,128)(2,1)S(1)} collective-permute-done((bf16[2,128,128]{2,1,0:T(8,128)(2,1)}, bf16[2,128,128]{2,1,0:T(8,128)(2,1)S(1)}, u32[]{:S(2)}, u32[]{:S(2)}) %collective-permute-start) | collective-permute-done | bytes 65568 | tf_op jit(solution)/shard_map/ppermute | solution.py:440
  8.9 0.0 collective-permute-done.1.act_other
  8.9 0.0 collective-permute-done.2.cot_other
  8.9 0.0 copy-start.3
  8.9 0.8 %copy-done.3 = bf16[2,128,128]{2,1,0:T(8,128)(2,1)S(1)} copy-done((bf16[2,128,128]{2,1,0:T(8,128)(2,1)S(1)}, bf16[2,128,128]{2,1,0:T(8,128)(2,1)}, u32[]{:S(2)}) %copy-start.3) | copy-done | bytes 65560
  9.7 0.8 %shard_map.120 = (f32[64,3456]{1,0:T(8,128)S(1)}, bf16[64,3584]{1,0:T(8,128)(2,1)S(1)}, f32[64,3456]{1,0:T(8,128)S(1)}, bf16[64,3456]{1,0:T(8,128)(2,1)S(1)}, f32[32,128]{1,0:T(8,128)S(1)}) custom-call(bf16[2,128,128]{2,1,0:T(8,128)(2,1)S(1)} %copy-done.3, bf16[2,128,128]{2,1,0:T(8,128)(2,1)S(1)} %collective-permute-done.other_ref, ...), custom_call_target="tpu_custom_call" | custom-call | flops 452984832 | bytes 6193152 | tf_op jit(solution)/shard_map/pallas_call | solution.py:236
  10.6 2.9 %collective-permute-start.3 = (bf16[64,3584]{1,0:T(8,128)(2,1)S(1)}, bf16[64,3584]{1,0:T(8,128)(2,1)S(1)}, u32[]{:S(2)}, u32[]{:S(2)}) collective-permute-start(bf16[64,3584]{1,0:T(8,128)(2,1)S(1)} %get-tuple-element.44), channel_id=1, source_target_pairs={{0,2},{1,3},{2,0},{3,1},{4,6},{5,7},{6,4},{7,5},{8,10},{9,11},{10,... | collective-permute-start | bytes 1376264 | tf_op jit(solution)/shard_map/ppermute | solution.py:440
  13.5 1.5 %collective-permute-start.4 = (bf16[64,3456]{1,0:T(8,128)(2,1)S(1)}, bf16[64,3456]{1,0:T(8,128)(2,1)S(1)}, u32[]{:S(2)}, u32[]{:S(2)}) collective-permute-start(bf16[64,3456]{1,0:T(8,128)(2,1)S(1)} %get-tuple-element.46), channel_id=1, source_target_pairs={{0,4},{1,5},{2,6},{3,7},{4,0},{5,1},{6,2},{7,3},{8,12},{9,13},{10,... | collective-permute-start | bytes 1327112 | tf_op jit(solution)/shard_map/ppermute | solution.py:440
  15.0 1.6 %collective-permute-start.7 = (bf16[928,128]{1,0:T(8,128)(2,1)S(1)}, bf16[928,128]{1,0:T(8,128)(2,1)S(1)}, u32[]{:S(2)}, u32[]{:S(2)}) collective-permute-start(bf16[928,128]{1,0:T(8,128)(2,1)S(1)} %copy-done.6), channel_id=1, source_target_pairs={{0,8},{8,16},{16,24},{24,0},{1,9},{9,17},{17,25},{25,1},{2,10},{10... | collective-permute-start | bytes 712712 | tf_op jit(solution)/shard_map/ppermute | solution.py:443
  16.6 2.6 %collective-permute-start.8 = (bf16[928,128]{1,0:T(8,128)(2,1)S(1)}, bf16[928,128]{1,0:T(8,128)(2,1)S(1)}, u32[]{:S(2)}, u32[]{:S(2)}) collective-permute-start(bf16[928,128]{1,0:T(8,128)(2,1)S(1)} %copy-done.5), channel_id=1, source_target_pairs={{0,16},{8,24},{16,0},{24,8},{1,17},{9,25},{17,1},{25,9},{2,18},{10... | collective-permute-start | bytes 712712 | tf_op jit(solution)/shard_map/ppermute | solution.py:443
  19.2 1.3 %collective-permute-start.9 = (bf16[928,128]{1,0:T(8,128)(2,1)S(1)}, bf16[928,128]{1,0:T(8,128)(2,1)S(1)}, u32[]{:S(2)}, u32[]{:S(2)}) collective-permute-start(bf16[928,128]{1,0:T(8,128)(2,1)S(1)} %copy-done.4), channel_id=1, source_target_pairs={{0,24},{8,0},{16,8},{24,16},{1,25},{9,1},{17,9},{25,17},{2,26},{10... | collective-permute-start | bytes 712712 | tf_op jit(solution)/shard_map/ppermute | solution.py:443
  20.5 4.9 %collective-permute-done.4.down_in_ref = bf16[64,3456]{1,0:T(8,128)(2,1)S(1)} collective-permute-done((bf16[64,3456]{1,0:T(8,128)(2,1)S(1)}, bf16[64,3456]{1,0:T(8,128)(2,1)S(1)}, u32[]{:S(2)}, u32[]{:S(2)}) %collective-permute-start.4) | collective-permute-done | bytes 442400 | tf_op jit(solution)/shard_map/ppermute | solution.py:440
  25.4 0.0 collective-permute-done.3.up_in_ref
  25.4 0.2 shard_map.121
  25.6 1.6 %collective-permute-start.5 = (bf16[32,3712]{1,0:T(8,128)(2,1)S(1)}, bf16[32,3712]{1,0:T(8,128)(2,1)S(1)}, u32[]{:S(2)}, u32[]{:S(2)}) collective-permute-start(bf16[32,3712]{1,0:T(8,128)(2,1)S(1)} %get-tuple-element.49), channel_id=1, source_target_pairs={{0,4},{1,5},{2,6},{3,7},{4,0},{5,1},{6,2},{7,3},{8,12},{9,13},{10,... | collective-permute-start | bytes 712712 | tf_op jit(solution)/shard_map/ppermute | solution.py:440
  27.2 0.6 %collective-permute-start.6 = (bf16[32,3456]{1,0:T(8,128)(2,1)S(1)}, bf16[32,3456]{1,0:T(8,128)(2,1)S(1)}, u32[]{:S(2)}, u32[]{:S(2)}) collective-permute-start(bf16[32,3456]{1,0:T(8,128)(2,1)S(1)} %get-tuple-element.50), channel_id=1, source_target_pairs={{0,2},{1,3},{2,0},{3,1},{4,6},{5,7},{6,4},{7,5},{8,10},{9,11},{10,... | collective-permute-start | bytes 663560 | tf_op jit(solution)/shard_map/ppermute | solution.py:440
  27.8 6.7 %collective-permute-done.8.refs_2_ = bf16[928,128]{1,0:T(8,128)(2,1)S(1)} collective-permute-done((bf16[928,128]{1,0:T(8,128)(2,1)S(1)}, bf16[928,128]{1,0:T(8,128)(2,1)S(1)}, u32[]{:S(2)}, u32[]{:S(2)}) %collective-permute-start.8) | collective-permute-done | bytes 237600 | tf_op jit(solution)/shard_map/ppermute | solution.py:443
  34.5 0.0 collective-permute-done.9.refs_3_
  34.5 0.0 collective-permute-done.6.down_in_ref
  34.5 0.0 collective-permute-done.5.up_in_ref
  34.5 0.4 shard_map.122
  34.8 5.6 %collective-permute-start.10 = (bf16[2,32,1024]{2,1,0:T(8,128)(2,1)S(1)}, bf16[2,32,1024]{2,1,0:T(8,128)(2,1)S(1)}, u32[]{:S(2)}, u32[]{:S(2)}) collective-permute-start(bf16[2,32,1024]{2,1,0:T(8,128)(2,1)S(1)} %get-tuple-element.61), channel_id=1, source_target_pairs={{0,8},{8,16},{16,24},{24,0},{1,9},{9,17},{17,25},{25,1},{2,10},{10... | collective-permute-start | bytes 393224 | tf_op jit(solution)/shard_map/ppermute | solution.py:443
  40.4 1.6 %collective-permute-start.11 = (bf16[2,32,1024]{2,1,0:T(8,128)(2,1)S(1)}, bf16[2,32,1024]{2,1,0:T(8,128)(2,1)S(1)}, u32[]{:S(2)}, u32[]{:S(2)}) collective-permute-start(bf16[2,32,1024]{2,1,0:T(8,128)(2,1)S(1)} %get-tuple-element.62), channel_id=1, source_target_pairs={{0,16},{8,24},{16,0},{24,8},{1,17},{9,25},{17,1},{25,9},{2,18},{10... | collective-permute-start | bytes 393224 | tf_op jit(solution)/shard_map/ppermute | solution.py:443
  42.0 0.8 %collective-permute-start.12 = (bf16[2,32,1024]{2,1,0:T(8,128)(2,1)S(1)}, bf16[2,32,1024]{2,1,0:T(8,128)(2,1)S(1)}, u32[]{:S(2)}, u32[]{:S(2)}) collective-permute-start(bf16[2,32,1024]{2,1,0:T(8,128)(2,1)S(1)} %get-tuple-element.63), channel_id=1, source_target_pairs={{0,24},{8,0},{16,8},{24,16},{1,25},{9,1},{17,9},{25,17},{2,26},{10... | collective-permute-start | bytes 393224 | tf_op jit(solution)/shard_map/ppermute | solution.py:443
  42.9 5.0 %shard_map.124 = f32[1,7,512,128]{3,2,1,0:T(8,128)} custom-call(bf16[928,128]{1,0:T(8,128)(2,1)S(1)} %copy-done.2, bf16[928,128]{1,0:T(8,128)(2,1)S(1)} %collective-permute-done.7.refs_1_, bf16[928,128]{1,0:T(8,128)(2,1)S(1)} %collective-permute-done.8.refs_2_, bf16[928,128]{1,0:T(8,128)(2,1)S(1)} %collective-permute-done.9.refs_3_), custom_call_target="tpu_custom_call" | custom-call | flops 469762048 | bytes 1835008 | tf_op jit(solution)/shard_map/pallas_call | solution.py:407
  47.9 2.3 %collective-permute-done.11.rest_1_ = bf16[2,32,1024]{2,1,0:T(8,128)(2,1)S(1)} collective-permute-done((bf16[2,32,1024]{2,1,0:T(8,128)(2,1)S(1)}, bf16[2,32,1024]{2,1,0:T(8,128)(2,1)S(1)}, u32[]{:S(2)}, u32[]{:S(2)}) %collective-permute-start.11) | collective-permute-done | bytes 131104 | tf_op jit(solution)/shard_map/ppermute | solution.py:443
  50.1 0.0 collective-permute-done.12.rest_2_
  50.1 0.7 %shard_map.123 = (f32[32,864]{1,0:T(8,128)}, f32[32,864]{1,0:T(8,128)}, f32[27,128]{1,0:T(8,128)}) custom-call(s32[1]{0:T(128)} %bitcast.table_ref, f32[2,32,864]{2,1,0:T(8,128)S(1)} %get-tuple-element.59.own_ref, f32[32,128]{1,0:T(8,128)S(1)} %get-tuple-element.60.bias_ref, bf16[2,32,1024]{2,1,0:T(8,128)(2,1)S(1)} %collective-permute-done.10.rest_0_, ...), custom_call_target="tpu_custom_call" | custom-call | tf_op jit(solution)/shard_map/pallas_call | solution.py:362
  (14 shorter events, 0.0 us)
Async XLA Ops:
  0.6 8.2 %collective-permute-start.1 = (bf16[128,3456]{1,0:T(8,128)(2,1)}, bf16[128,3456]{1,0:T(8,128)(2,1)S(1)}, u32[]{:S(2)}, u32[]{:S(2)}) collective-permute-start(bf16[128,3456]{1,0:T(8,128)(2,1)} %act.1), channel_id=1, source_target_pairs={{0,1},{1,0},{2,3},{3,2},{4,5},{5,4},{6,7},{7,6},{8,9},{9,8},{10,11... | collective-permute-start | bytes 2654216 | tf_op jit(solution)/shard_map/ppermute | solution.py:440
  1.2 7.7 %collective-permute-start.2 = (bf16[128,3456]{1,0:T(8,128)(2,1)}, bf16[128,3456]{1,0:T(8,128)(2,1)S(1)}, u32[]{:S(2)}, u32[]{:S(2)}) collective-permute-start(bf16[128,3456]{1,0:T(8,128)(2,1)} %cot.1), channel_id=1, source_target_pairs={{0,1},{1,0},{2,3},{3,2},{4,5},{5,4},{6,7},{7,6},{8,9},{9,8},{10,11... | collective-permute-start | bytes 2654216 | tf_op jit(solution)/shard_map/ppermute | solution.py:440
  1.2 7.6 %copy-start = (bf16[128,3456]{1,0:T(8,128)(2,1)S(1)}, bf16[128,3456]{1,0:T(8,128)(2,1)}, u32[]{:S(2)}) copy-start(bf16[128,3456]{1,0:T(8,128)(2,1)} %act.1) | copy-start | bytes 2654212
  1.2 7.6 %copy-start.1 = (bf16[128,3456]{1,0:T(8,128)(2,1)S(1)}, bf16[128,3456]{1,0:T(8,128)(2,1)}, u32[]{:S(2)}) copy-start(bf16[128,3456]{1,0:T(8,128)(2,1)} %cot.1) | copy-start | bytes 2654212
  7.3 1.6 %collective-permute-start = (bf16[2,128,128]{2,1,0:T(8,128)(2,1)}, bf16[2,128,128]{2,1,0:T(8,128)(2,1)S(1)}, u32[]{:S(2)}, u32[]{:S(2)}) collective-permute-start(bf16[2,128,128]{2,1,0:T(8,128)(2,1)} %get-tuple-element.42), channel_id=1, source_target_pairs={{0,1},{1,0},{2,3},{3,2},{4,5},{5,4},{6,7},{7,6},{8,9},{9,8},{10,11... | collective-permute-start | bytes 196616 | tf_op jit(solution)/shard_map/ppermute | solution.py:440
  8.9 0.8 %copy-start.3 = (bf16[2,128,128]{2,1,0:T(8,128)(2,1)S(1)}, bf16[2,128,128]{2,1,0:T(8,128)(2,1)}, u32[]{:S(2)}) copy-start(bf16[2,128,128]{2,1,0:T(8,128)(2,1)} %get-tuple-element.41.keep_ref) | copy-start | bytes 196612
  9.7 5.3 %copy-start.6 = (bf16[928,128]{1,0:T(8,128)(2,1)S(1)}, bf16[928,128]{1,0:T(8,128)(2,1)}, u32[]{:S(2)}) copy-start(bf16[928,128]{1,0:T(8,128)(2,1)} %get-tuple-element.52) | copy-start | bytes 712708
  9.7 6.9 %copy-start.5 = (bf16[928,128]{1,0:T(8,128)(2,1)S(1)}, bf16[928,128]{1,0:T(8,128)(2,1)}, u32[]{:S(2)}) copy-start(bf16[928,128]{1,0:T(8,128)(2,1)} %get-tuple-element.53) | copy-start | bytes 712708
  9.7 9.4 %copy-start.4 = (bf16[928,128]{1,0:T(8,128)(2,1)S(1)}, bf16[928,128]{1,0:T(8,128)(2,1)}, u32[]{:S(2)}) copy-start(bf16[928,128]{1,0:T(8,128)(2,1)} %get-tuple-element.54) | copy-start | bytes 712708
  10.6 14.9 %collective-permute-start.3 = (bf16[64,3584]{1,0:T(8,128)(2,1)S(1)}, bf16[64,3584]{1,0:T(8,128)(2,1)S(1)}, u32[]{:S(2)}, u32[]{:S(2)}) collective-permute-start(bf16[64,3584]{1,0:T(8,128)(2,1)S(1)} %get-tuple-element.44), channel_id=1, source_target_pairs={{0,2},{1,3},{2,0},{3,1},{4,6},{5,7},{6,4},{7,5},{8,10},{9,11},{10,... | collective-permute-start | bytes 1376264 | tf_op jit(solution)/shard_map/ppermute | solution.py:440
  13.5 11.9 %collective-permute-start.4 = (bf16[64,3456]{1,0:T(8,128)(2,1)S(1)}, bf16[64,3456]{1,0:T(8,128)(2,1)S(1)}, u32[]{:S(2)}, u32[]{:S(2)}) collective-permute-start(bf16[64,3456]{1,0:T(8,128)(2,1)S(1)} %get-tuple-element.46), channel_id=1, source_target_pairs={{0,4},{1,5},{2,6},{3,7},{4,0},{5,1},{6,2},{7,3},{8,12},{9,13},{10,... | collective-permute-start | bytes 1327112 | tf_op jit(solution)/shard_map/ppermute | solution.py:440
  15.0 12.8 %collective-permute-start.7 = (bf16[928,128]{1,0:T(8,128)(2,1)S(1)}, bf16[928,128]{1,0:T(8,128)(2,1)S(1)}, u32[]{:S(2)}, u32[]{:S(2)}) collective-permute-start(bf16[928,128]{1,0:T(8,128)(2,1)S(1)} %copy-done.6), channel_id=1, source_target_pairs={{0,8},{8,16},{16,24},{24,0},{1,9},{9,17},{17,25},{25,1},{2,10},{10... | collective-permute-start | bytes 712712 | tf_op jit(solution)/shard_map/ppermute | solution.py:443
  16.6 17.9 %collective-permute-start.8 = (bf16[928,128]{1,0:T(8,128)(2,1)S(1)}, bf16[928,128]{1,0:T(8,128)(2,1)S(1)}, u32[]{:S(2)}, u32[]{:S(2)}) collective-permute-start(bf16[928,128]{1,0:T(8,128)(2,1)S(1)} %copy-done.5), channel_id=1, source_target_pairs={{0,16},{8,24},{16,0},{24,8},{1,17},{9,25},{17,1},{25,9},{2,18},{10... | collective-permute-start | bytes 712712 | tf_op jit(solution)/shard_map/ppermute | solution.py:443
  19.2 15.3 %collective-permute-start.9 = (bf16[928,128]{1,0:T(8,128)(2,1)S(1)}, bf16[928,128]{1,0:T(8,128)(2,1)S(1)}, u32[]{:S(2)}, u32[]{:S(2)}) collective-permute-start(bf16[928,128]{1,0:T(8,128)(2,1)S(1)} %copy-done.4), channel_id=1, source_target_pairs={{0,24},{8,0},{16,8},{24,16},{1,25},{9,1},{17,9},{25,17},{2,26},{10... | collective-permute-start | bytes 712712 | tf_op jit(solution)/shard_map/ppermute | solution.py:443
  25.4 17.5 %copy-start.2 = (bf16[928,128]{1,0:T(8,128)(2,1)S(1)}, bf16[928,128]{1,0:T(8,128)(2,1)}, u32[]{:S(2)}) copy-start(bf16[928,128]{1,0:T(8,128)(2,1)} %get-tuple-element.71.refs_0_) | copy-start | bytes 712708
  25.6 8.9 %collective-permute-start.5 = (bf16[32,3712]{1,0:T(8,128)(2,1)S(1)}, bf16[32,3712]{1,0:T(8,128)(2,1)S(1)}, u32[]{:S(2)}, u32[]{:S(2)}) collective-permute-start(bf16[32,3712]{1,0:T(8,128)(2,1)S(1)} %get-tuple-element.49), channel_id=1, source_target_pairs={{0,4},{1,5},{2,6},{3,7},{4,0},{5,1},{6,2},{7,3},{8,12},{9,13},{10,... | collective-permute-start | bytes 712712 | tf_op jit(solution)/shard_map/ppermute | solution.py:440
  27.2 7.3 %collective-permute-start.6 = (bf16[32,3456]{1,0:T(8,128)(2,1)S(1)}, bf16[32,3456]{1,0:T(8,128)(2,1)S(1)}, u32[]{:S(2)}, u32[]{:S(2)}) collective-permute-start(bf16[32,3456]{1,0:T(8,128)(2,1)S(1)} %get-tuple-element.50), channel_id=1, source_target_pairs={{0,2},{1,3},{2,0},{3,1},{4,6},{5,7},{6,4},{7,5},{8,10},{9,11},{10,... | collective-permute-start | bytes 663560 | tf_op jit(solution)/shard_map/ppermute | solution.py:440
  34.8 13.0 %collective-permute-start.10 = (bf16[2,32,1024]{2,1,0:T(8,128)(2,1)S(1)}, bf16[2,32,1024]{2,1,0:T(8,128)(2,1)S(1)}, u32[]{:S(2)}, u32[]{:S(2)}) collective-permute-start(bf16[2,32,1024]{2,1,0:T(8,128)(2,1)S(1)} %get-tuple-element.61), channel_id=1, source_target_pairs={{0,8},{8,16},{16,24},{24,0},{1,9},{9,17},{17,25},{25,1},{2,10},{10... | collective-permute-start | bytes 393224 | tf_op jit(solution)/shard_map/ppermute | solution.py:443
  40.4 9.7 %collective-permute-start.11 = (bf16[2,32,1024]{2,1,0:T(8,128)(2,1)S(1)}, bf16[2,32,1024]{2,1,0:T(8,128)(2,1)S(1)}, u32[]{:S(2)}, u32[]{:S(2)}) collective-permute-start(bf16[2,32,1024]{2,1,0:T(8,128)(2,1)S(1)} %get-tuple-element.62), channel_id=1, source_target_pairs={{0,16},{8,24},{16,0},{24,8},{1,17},{9,25},{17,1},{25,9},{2,18},{10... | collective-permute-start | bytes 393224 | tf_op jit(solution)/shard_map/ppermute | solution.py:443
  42.0 8.1 %collective-permute-start.12 = (bf16[2,32,1024]{2,1,0:T(8,128)(2,1)S(1)}, bf16[2,32,1024]{2,1,0:T(8,128)(2,1)S(1)}, u32[]{:S(2)}, u32[]{:S(2)}) collective-permute-start(bf16[2,32,1024]{2,1,0:T(8,128)(2,1)S(1)} %get-tuple-element.63), channel_id=1, source_target_pairs={{0,24},{8,0},{16,8},{24,16},{1,25},{9,1},{17,9},{25,17},{2,26},{10... | collective-permute-start | bytes 393224 | tf_op jit(solution)/shard_map/ppermute | solution.py:443

commit v4 on v3

--- a/solution.py
+++ b/solution.py
@@ -450,34 +450,49 @@
         n_table, slots, up_bits, down_bits,
     )
     other = swap(send, "rep", 1)
-    parts = [parts[0]] + [shifted(parts[k], k) for k in range(1, n_table)]
-    up_keep, up_send, down_keep, down_send, bias_sum = terms_call(
-        keep, other, activations, cotangent, act_other, cot_other, ride
+    middle = n_table // 2
+    parts[middle] = shifted(parts[middle], middle)
+    near = [k for k in range(1, n_table) if k != middle]
+    terms = terms_call(keep, other, activations, cotangent, act_other, cot_other, ride)
+
+    def chain(sent, up_keep, up_send, down_keep, down_send, bias_sum):
+        sent = [shifted(value, k) for value, k in zip(sent, near)]
+        for place, (up_bit, down_bit) in enumerate(zip(up_bits[1:], down_bits[1:])):
+            up_in = swap(up_send, "rep", up_bit)
+            down_in = swap(down_send, "rep", down_bit)
+            if not ride:
+                bias_sum = bias_sum + swap(bias_sum, "rep", up_bit)
+            if place == len(far_bits) - 1:
+                break
+            if ride:
+                up_keep, up_send, down_keep, down_send, bias_sum = halve_call(
+                    up_keep, up_in, down_keep, down_in, bias_sum
+                )
+            else:
+                half = up_keep.shape[0] // 2
+                up = up_keep + up_in.astype(F32)
+                down = down_keep + down_in.astype(F32)
+                up_keep, up_send = up[:half], up[half:].astype(BF16)
+                down_keep, down_send = down[:half], down[half:].astype(BF16)
+        if not ride:
+            for bit in [1 << k for k in range(n_table.bit_length() - 1)]:
+                bias_sum = bias_sum + swap(bias_sum, "table", bit)
+        (up_in, down_in), sent = lax.optimization_barrier(((up_in, down_in), sent))
+        own, total, *sends = split_call(
+            table_index, up_keep, up_in, down_keep, down_in, bias_sum, n_table, scale, ride
+        )
+        return sent, own, total, sends
+
+    operands = ([parts[k] for k in near], *terms)
+    shapes = jax.eval_shape(chain, *operands)
+    came, own, bias_sum, sends = lax.cond(
+        feature_table_slot[0] >= 0,
+        chain,
+        lambda *_: jax.tree.map(lambda x: jnp.zeros(x.shape, x.dtype), shapes),
+        *operands,
     )
-    for place, (up_bit, down_bit) in enumerate(zip(up_bits[1:], down_bits[1:])):
-        up_in = swap(up_send, "rep", up_bit)
-        down_in = swap(down_send, "rep", down_bit)
-        if not ride:
-            bias_sum = bias_sum + swap(bias_sum, "rep", up_bit)
-        if place == len(far_bits) - 1:
-            break
-        if ride:
-            up_keep, up_send, down_keep, down_send, bias_sum = halve_call(
-                up_keep, up_in, down_keep, down_in, bias_sum
-            )
-        else:
-            half = up_keep.shape[0] // 2
-            up = up_keep + up_in.astype(F32)
-            down = down_keep + down_in.astype(F32)
-            up_keep, up_send = up[:half], up[half:].astype(BF16)
-            down_keep, down_send = down[:half], down[half:].astype(BF16)
-    if not ride:
-        for bit in [1 << k for k in range(n_table.bit_length() - 1)]:
-            bias_sum = bias_sum + swap(bias_sum, "table", bit)
-    (up_in, down_in), parts = lax.optimization_barrier(((up_in, down_in), parts))
-    own, bias_sum, *sends = split_call(
-        table_index, up_keep, up_in, down_keep, down_in, bias_sum, n_table, scale, ride
-    )
+    for value, k in zip(came, near):
+        parts[k] = value
     arrived = [shifted(value, k + 1) for k, value in enumerate(sends)]
     up_grad, down_grad, bias_grad = finish_call(table_index, own, bias_sum, arrived, scale, ride)
     parts, _ = lax.optimization_barrier((parts, own))

time: 51.5 us -> 49 us (0.951)
  starting transfers between devices: 21.3 us -> 17.7 us
  Pallas kernels: 13 us -> 14.3 us
    ppermute x7, waiting for transfers between devices: 6.03 us -> 11.1 us  [swap(): return lax.ppermute(value, axis, [(k, k ^ bit) for k in range(size)])]
    ppermute x6, waiting for transfers between devices: 8.94 us -> 3.95 us  [shifted(): lax.ppermute(value, 'table', [(k, (k + shift) % n_table) for k in range(n...]
    ppermute x7, starting transfers between devices: 7.72 us -> 5.83 us  [swap(): return lax.ppermute(value, axis, [(k, k ^ bit) for k in range(size)])]
    ppermute x6, starting transfers between devices: 13.6 us -> 11.9 us  [shifted(): lax.ppermute(value, 'table', [(k, (k + shift) % n_table) for k in range(n...]
    pallas_call x1, Pallas kernels: 4.97 us -> 6.04 us  [rows_call(): pl.pallas_call(functools.partial(rows_kernel, n_table, slots), grid=(slot...]
  transfers between devices with their start and end apart: 13 -> 13, of which waited for: 4 -> 5; matrix products, arithmetic and copies ran while one was open for 0% -> 0% of each run, Pallas kernels for 22% -> 28%
where the time goes in v4:
time: 49 us; the launch traced here: 48.7 us
  starting transfers between devices  17.7 us (36%)
  waiting for transfers between devices  15 us (31%)
  Pallas kernels  14.3 us (29%)
  local copies, waits for them, and re-layouts  0.95 us (2%)
  between operations  0.73 us (1%)
    ppermute x6, starting transfers between devices, shifted(): lax.ppermute(value, 'table', [(k, (k + shift) % n_table) for k in range(n...  11.9 us
    ppermute x7, waiting for transfers between devices, swap(): return lax.ppermute(value, axis, [(k, k ^ bit) for k in range(size)])  11.1 us
    pallas_call x1, Pallas kernels, input_call(): pl.pallas_call(functools.partial(input_kernel, n_table, slots, up_bits, d...  6.21 us
    pallas_call x1, Pallas kernels, rows_call(): pl.pallas_call(functools.partial(rows_kernel, n_table, slots), grid=(slot...  6.04 us
    ppermute x7, starting transfers between devices, swap(): return lax.ppermute(value, axis, [(k, k ^ bit) for k in range(size)])  5.83 us
    ppermute x6, waiting for transfers between devices, shifted(): lax.ppermute(value, 'table', [(k, (k + shift) % n_table) for k in range(n...  3.95 us
  transfers between devices with their start and end apart: 13, of which 5 were waited for; matrix products, arithmetic and copies ran while one was open for 0% of the time, Pallas kernels for 28%

profile of v4, /device:TPU:0, one launch (start us, length us, event | category | flops | bytes accessed | tf_op | source)
XLA Modules:
  0.0 48.7 jit_solution(11758830578077278014)
XLA Ops:
  0.6 0.5 %collective-permute-start.7 = (bf16[128,3456]{1,0:T(8,128)(2,1)}, bf16[128,3456]{1,0:T(8,128)(2,1)S(1)}, u32[]{:S(2)}, u32[]{:S(2)}) collective-permute-start(bf16[128,3456]{1,0:T(8,128)(2,1)} %act.1), channel_id=1, source_target_pairs={{0,1},{1,0},{2,3},{3,2},{4,5},{5,4},{6,7},{7,6},{8,9},{9,8},{10,11... | collective-permute-start | bytes 2654216 | tf_op jit(solution)/shard_map/ppermute | solution.py:440
  1.2 0.1 collective-permute-start.8
  1.2 6.2 %shard_map.119 = (bf16[2,128,128]{2,1,0:T(8,128)(2,1)}, bf16[2,128,128]{2,1,0:T(8,128)(2,1)}, bf16[128,128]{1,0:T(8,128)(2,1)}, bf16[928,128]{1,0:T(8,128)(2,1)}...) custom-call(s32[1]{0:T(128)} %bitcast.table_ref, s32[1]{0:T(128)} %bitcast.1.rep_ref, ...), custom_call_target="tpu_custom_call" | custom-call | flops 905969664 | bytes 5308416 | tf_op jit(solution)/shard_map/pallas_call | solution.py:145
  7.5 4.1 %collective-permute-start.12 = (bf16[928,128]{1,0:T(8,128)(2,1)}, bf16[928,128]{1,0:T(8,128)(2,1)S(1)}, u32[]{:S(2)}, u32[]{:S(2)}) collective-permute-start(bf16[928,128]{1,0:T(8,128)(2,1)} %get-tuple-element.89), channel_id=1, source_target_pairs={{0,16},{8,24},{16,0},{24,8},{1,17},{9,25},{17,1},{25,9},{2,18},{10... | collective-permute-start | bytes 712712 | tf_op jit(solution)/shard_map/ppermute | solution.py:443
  11.5 0.0 collective-permute-start.6
  11.6 1.4 %collective-permute-done.6.other_ref = bf16[2,128,128]{2,1,0:T(8,128)(2,1)S(1)} collective-permute-done((bf16[2,128,128]{2,1,0:T(8,128)(2,1)}, bf16[2,128,128]{2,1,0:T(8,128)(2,1)S(1)}, u32[]{:S(2)}, u32[]{:S(2)}) %collective-permute-start.6) | collective-permute-done | bytes 65568 | tf_op jit(solution)/shard_map/ppermute | solution.py:440
  13.0 0.0 copy-start.3
  13.0 0.8 %copy-done.3 = bf16[2,128,128]{2,1,0:T(8,128)(2,1)S(1)} copy-done((bf16[2,128,128]{2,1,0:T(8,128)(2,1)S(1)}, bf16[2,128,128]{2,1,0:T(8,128)(2,1)}, u32[]{:S(2)}) %copy-start.3) | copy-done | bytes 65560
  13.9 0.8 %shard_map.120 = (f32[64,3456]{1,0:T(8,128)S(1)}, bf16[64,3584]{1,0:T(8,128)(2,1)S(1)}, f32[64,3456]{1,0:T(8,128)S(1)}, bf16[64,3456]{1,0:T(8,128)(2,1)S(1)}, f32[32,128]{1,0:T(8,128)S(1)}) custom-call(bf16[2,128,128]{2,1,0:T(8,128)(2,1)S(1)} %copy-done.3, bf16[2,128,128]{2,1,0:T(8,128)(2,1)S(1)} %collective-permute-done.6.other_ref, ...), custom_call_target="tpu_custom_call" | custom-call | flops 452984832 | bytes 6193152 | tf_op jit(solution)/shard_map/pallas_call | solution.py:236
  14.7 0.1 copy-done.5
  14.8 21.7 %conditional.1 = (bf16[928,128]{1,0:T(8,128)(2,1)}, bf16[928,128]{1,0:T(8,128)(2,1)}, f32[2,32,864]{2,1,0:T(8,128)S(1)}, f32[32,128]{1,0:T(8,128)S(1)}, bf16[2,3...) conditional(s32[]{:T(128)} %bitcast.5, () %tuple.18, ...), branch_computations={%region_0.0_spmd, %region_1.0_spmd} | conditional | bytes 7340328 | solution.py:488
  14.8 1.5 %collective-permute-start = (bf16[64,3584]{1,0:T(8,128)(2,1)S(1)}, bf16[64,3584]{1,0:T(8,128)(2,1)S(1)}, u32[]{:S(2)}, u32[]{:S(2)}) collective-permute-start(bf16[64,3584]{1,0:T(8,128)(2,1)S(1)} %get-tuple-element.17), channel_id=1, source_target_pairs={{0,2},{1,3},{2,0},{3,1},{4,6},{5,7},{6,4},{7,5},{8,10},{9,11},{10,... | collective-permute-start | bytes 1376264 | tf_op jit(solution)/shard_map/cond/branch_1_fun/ppermute | solution.py:440
  16.3 1.5 %collective-permute-start.1 = (bf16[64,3456]{1,0:T(8,128)(2,1)S(1)}, bf16[64,3456]{1,0:T(8,128)(2,1)S(1)}, u32[]{:S(2)}, u32[]{:S(2)}) collective-permute-start(bf16[64,3456]{1,0:T(8,128)(2,1)S(1)} %get-tuple-element.19), channel_id=1, source_target_pairs={{0,4},{1,5},{2,6},{3,7},{4,0},{5,1},{6,2},{7,3},{8,12},{9,13},{10,... | collective-permute-start | bytes 1327112 | tf_op jit(solution)/shard_map/cond/branch_1_fun/ppermute | solution.py:440
  17.8 1.6 %collective-permute-start.4 = (bf16[928,128]{1,0:T(8,128)(2,1)S(1)}, bf16[928,128]{1,0:T(8,128)(2,1)}, u32[]{:S(2)}, u32[]{:S(2)}) collective-permute-start(bf16[928,128]{1,0:T(8,128)(2,1)S(1)} %get-tuple-element.23), channel_id=1, source_target_pairs={{0,8},{8,16},{16,24},{24,0},{1,9},{9,17},{17,25},{25,1},{2,10},{10... | collective-permute-start | bytes 712712 | tf_op jit(solution)/shard_map/cond/branch_1_fun/ppermute | solution.py:443
  19.4 2.2 %collective-permute-start.5 = (bf16[928,128]{1,0:T(8,128)(2,1)S(1)}, bf16[928,128]{1,0:T(8,128)(2,1)}, u32[]{:S(2)}, u32[]{:S(2)}) collective-permute-start(bf16[928,128]{1,0:T(8,128)(2,1)S(1)} %get-tuple-element.24), channel_id=1, source_target_pairs={{0,24},{8,0},{16,8},{24,16},{1,25},{9,1},{17,9},{25,17},{2,26},{10... | collective-permute-start | bytes 712712 | tf_op jit(solution)/shard_map/cond/branch_1_fun/ppermute | solution.py:443
  21.7 6.6 %collective-permute-done.1.down_in_ref = bf16[64,3456]{1,0:T(8,128)(2,1)S(1)} collective-permute-done((bf16[64,3456]{1,0:T(8,128)(2,1)S(1)}, bf16[64,3456]{1,0:T(8,128)(2,1)S(1)}, u32[]{:S(2)}, u32[]{:S(2)}) %collective-permute-start.1) | collective-permute-done | bytes 442400 | tf_op jit(solution)/shard_map/cond/branch_1_fun/ppermute | solution.py:440
  28.3 0.0 collective-permute-done.up_in_ref
  28.3 0.2 branch_1_fun.2
  28.4 1.6 %collective-permute-start.2 = (bf16[32,3712]{1,0:T(8,128)(2,1)S(1)}, bf16[32,3712]{1,0:T(8,128)(2,1)S(1)}, u32[]{:S(2)}, u32[]{:S(2)}) collective-permute-start(bf16[32,3712]{1,0:T(8,128)(2,1)S(1)} %get-tuple-element.21), channel_id=1, source_target_pairs={{0,4},{1,5},{2,6},{3,7},{4,0},{5,1},{6,2},{7,3},{8,12},{9,13},{10,... | collective-permute-start | bytes 712712 | tf_op jit(solution)/shard_map/cond/branch_1_fun/ppermute | solution.py:440
  30.0 0.6 %collective-permute-start.3 = (bf16[32,3456]{1,0:T(8,128)(2,1)S(1)}, bf16[32,3456]{1,0:T(8,128)(2,1)S(1)}, u32[]{:S(2)}, u32[]{:S(2)}) collective-permute-start(bf16[32,3456]{1,0:T(8,128)(2,1)S(1)} %get-tuple-element.22), channel_id=1, source_target_pairs={{0,2},{1,3},{2,0},{3,1},{4,6},{5,7},{6,4},{7,5},{8,10},{9,11},{10,... | collective-permute-start | bytes 663560 | tf_op jit(solution)/shard_map/cond/branch_1_fun/ppermute | solution.py:440
  30.6 0.0 collective-permute-done.4
  30.6 2.5 %collective-permute-done.5 = bf16[928,128]{1,0:T(8,128)(2,1)} collective-permute-done((bf16[928,128]{1,0:T(8,128)(2,1)S(1)}, bf16[928,128]{1,0:T(8,128)(2,1)}, u32[]{:S(2)}, u32[]{:S(2)}) %collective-permute-start.5) | collective-permute-done | bytes 237600 | tf_op jit(solution)/shard_map/cond/branch_1_fun/ppermute | solution.py:443
  33.2 3.0 %collective-permute-done.3.down_in_ref = bf16[32,3456]{1,0:T(8,128)(2,1)S(1)} collective-permute-done((bf16[32,3456]{1,0:T(8,128)(2,1)S(1)}, bf16[32,3456]{1,0:T(8,128)(2,1)S(1)}, u32[]{:S(2)}, u32[]{:S(2)}) %collective-permute-start.3) | collective-permute-done | bytes 221216 | tf_op jit(solution)/shard_map/cond/branch_1_fun/ppermute | solution.py:440
  36.2 0.4 branch_1_fun.3
  36.5 1.5 %collective-permute-start.9 = (bf16[2,32,1024]{2,1,0:T(8,128)(2,1)S(1)}, bf16[2,32,1024]{2,1,0:T(8,128)(2,1)S(1)}, u32[]{:S(2)}, u32[]{:S(2)}) collective-permute-start(bf16[2,32,1024]{2,1,0:T(8,128)(2,1)S(1)} %get-tuple-element.81), channel_id=1, source_target_pairs={{0,8},{8,16},{16,24},{24,0},{1,9},{9,17},{17,25},{25,1},{2,10},{10... | collective-permute-start | bytes 393224 | tf_op jit(solution)/shard_map/ppermute | solution.py:443
  38.1 0.4 collective-permute-start.10
  38.5 2.0 %collective-permute-start.11 = (bf16[2,32,1024]{2,1,0:T(8,128)(2,1)S(1)}, bf16[2,32,1024]{2,1,0:T(8,128)(2,1)S(1)}, u32[]{:S(2)}, u32[]{:S(2)}) collective-permute-start(bf16[2,32,1024]{2,1,0:T(8,128)(2,1)S(1)} %get-tuple-element.83), channel_id=1, source_target_pairs={{0,24},{8,0},{16,8},{24,16},{1,25},{9,1},{17,9},{25,17},{2,26},{10... | collective-permute-start | bytes 393224 | tf_op jit(solution)/shard_map/ppermute | solution.py:443
  40.5 0.0 collective-permute-done.12.refs_2_
  40.5 6.0 %shard_map.122 = f32[1,7,512,128]{3,2,1,0:T(8,128)} custom-call(bf16[928,128]{1,0:T(8,128)(2,1)S(1)} %copy-done.2, bf16[928,128]{1,0:T(8,128)(2,1)} %get-tuple-element.92.refs_1_, bf16[928,128]{1,0:T(8,128)(2,1)S(1)} %collective-permute-done.12.refs_2_, bf16[928,128]{1,0:T(8,128)(2,1)} %get-tuple-element.94.refs_3_), custom_call_target="tpu_custom_call" | custom-call | flops 469762048 | bytes 1835008 | tf_op jit(solution)/shard_map/pallas_call | solution.py:407
  46.6 1.4 %collective-permute-done.10.rest_1_ = bf16[2,32,1024]{2,1,0:T(8,128)(2,1)S(1)} collective-permute-done((bf16[2,32,1024]{2,1,0:T(8,128)(2,1)S(1)}, bf16[2,32,1024]{2,1,0:T(8,128)(2,1)S(1)}, u32[]{:S(2)}, u32[]{:S(2)}) %collective-permute-start.10) | collective-permute-done | bytes 131104 | tf_op jit(solution)/shard_map/ppermute | solution.py:443
  48.0 0.0 collective-permute-done.11.rest_2_
  48.0 0.7 %shard_map.121 = (f32[32,864]{1,0:T(8,128)}, f32[32,864]{1,0:T(8,128)}, f32[27,128]{1,0:T(8,128)}) custom-call(s32[1]{0:T(128)} %bitcast.table_ref, f32[2,32,864]{2,1,0:T(8,128)S(1)} %get-tuple-element.79.own_ref, f32[32,128]{1,0:T(8,128)S(1)} %get-tuple-element.80.bias_ref, bf16[2,32,1024]{2,1,0:T(8,128)(2,1)S(1)} %collective-permute-done.9.rest_0_, ...), custom_call_target="tpu_custom_call" | custom-call | tf_op jit(solution)/shard_map/pallas_call | solution.py:362
  (13 shorter events, 0.0 us)
Async XLA Ops:
  0.6 12.4 %collective-permute-start.7 = (bf16[128,3456]{1,0:T(8,128)(2,1)}, bf16[128,3456]{1,0:T(8,128)(2,1)S(1)}, u32[]{:S(2)}, u32[]{:S(2)}) collective-permute-start(bf16[128,3456]{1,0:T(8,128)(2,1)} %act.1), channel_id=1, source_target_pairs={{0,1},{1,0},{2,3},{3,2},{4,5},{5,4},{6,7},{7,6},{8,9},{9,8},{10,11... | collective-permute-start | bytes 2654216 | tf_op jit(solution)/shard_map/ppermute | solution.py:440
  1.2 11.9 %collective-permute-start.8 = (bf16[128,3456]{1,0:T(8,128)(2,1)}, bf16[128,3456]{1,0:T(8,128)(2,1)S(1)}, u32[]{:S(2)}, u32[]{:S(2)}) collective-permute-start(bf16[128,3456]{1,0:T(8,128)(2,1)} %cot.1), channel_id=1, source_target_pairs={{0,1},{1,0},{2,3},{3,2},{4,5},{5,4},{6,7},{7,6},{8,9},{9,8},{10,11... | collective-permute-start | bytes 2654216 | tf_op jit(solution)/shard_map/ppermute | solution.py:440
  1.2 10.3 %copy-start.4 = (s32[26]{0:T(128)S(1)}, s32[26]{0:T(128)}, u32[]{:S(2)}) copy-start(s32[26]{0:T(128)} %owner_ref.1) | copy-start | bytes 316
  1.2 11.8 %copy-start = (bf16[128,3456]{1,0:T(8,128)(2,1)S(1)}, bf16[128,3456]{1,0:T(8,128)(2,1)}, u32[]{:S(2)}) copy-start(bf16[128,3456]{1,0:T(8,128)(2,1)} %act.1) | copy-start | bytes 2654212
  1.2 11.8 %copy-start.1 = (bf16[128,3456]{1,0:T(8,128)(2,1)S(1)}, bf16[128,3456]{1,0:T(8,128)(2,1)}, u32[]{:S(2)}) copy-start(bf16[128,3456]{1,0:T(8,128)(2,1)} %cot.1) | copy-start | bytes 2654212
  7.5 33.1 %collective-permute-start.12 = (bf16[928,128]{1,0:T(8,128)(2,1)}, bf16[928,128]{1,0:T(8,128)(2,1)S(1)}, u32[]{:S(2)}, u32[]{:S(2)}) collective-permute-start(bf16[928,128]{1,0:T(8,128)(2,1)} %get-tuple-element.89), channel_id=1, source_target_pairs={{0,16},{8,24},{16,0},{24,8},{1,17},{9,25},{17,1},{25,9},{2,18},{10... | collective-permute-start | bytes 712712 | tf_op jit(solution)/shard_map/ppermute | solution.py:443
  11.5 1.5 %collective-permute-start.6 = (bf16[2,128,128]{2,1,0:T(8,128)(2,1)}, bf16[2,128,128]{2,1,0:T(8,128)(2,1)S(1)}, u32[]{:S(2)}, u32[]{:S(2)}) collective-permute-start(bf16[2,128,128]{2,1,0:T(8,128)(2,1)} %get-tuple-element.71), channel_id=1, source_target_pairs={{0,1},{1,0},{2,3},{3,2},{4,5},{5,4},{6,7},{7,6},{8,9},{9,8},{10,11... | collective-permute-start | bytes 196616 | tf_op jit(solution)/shard_map/ppermute | solution.py:440
  13.0 0.8 %copy-start.3 = (bf16[2,128,128]{2,1,0:T(8,128)(2,1)S(1)}, bf16[2,128,128]{2,1,0:T(8,128)(2,1)}, u32[]{:S(2)}) copy-start(bf16[2,128,128]{2,1,0:T(8,128)(2,1)} %get-tuple-element.70.keep_ref) | copy-start | bytes 196612
  13.9 0.9 %copy-start.5 = (bf16[928,128]{1,0:T(8,128)(2,1)S(1)}, bf16[928,128]{1,0:T(8,128)(2,1)}, u32[]{:S(2)}) copy-start(bf16[928,128]{1,0:T(8,128)(2,1)} %get-tuple-element.78) | copy-start | bytes 712708
  14.8 25.7 %copy-start.2 = (bf16[928,128]{1,0:T(8,128)(2,1)S(1)}, bf16[928,128]{1,0:T(8,128)(2,1)}, u32[]{:S(2)}) copy-start(bf16[928,128]{1,0:T(8,128)(2,1)} %get-tuple-element.91.refs_0_) | copy-start | bytes 712708
  14.8 13.5 %collective-permute-start = (bf16[64,3584]{1,0:T(8,128)(2,1)S(1)}, bf16[64,3584]{1,0:T(8,128)(2,1)S(1)}, u32[]{:S(2)}, u32[]{:S(2)}) collective-permute-start(bf16[64,3584]{1,0:T(8,128)(2,1)S(1)} %get-tuple-element.17), channel_id=1, source_target_pairs={{0,2},{1,3},{2,0},{3,1},{4,6},{5,7},{6,4},{7,5},{8,10},{9,11},{10,... | collective-permute-start | bytes 1376264 | tf_op jit(solution)/shard_map/cond/branch_1_fun/ppermute | solution.py:440
  16.3 11.9 %collective-permute-start.1 = (bf16[64,3456]{1,0:T(8,128)(2,1)S(1)}, bf16[64,3456]{1,0:T(8,128)(2,1)S(1)}, u32[]{:S(2)}, u32[]{:S(2)}) collective-permute-start(bf16[64,3456]{1,0:T(8,128)(2,1)S(1)} %get-tuple-element.19), channel_id=1, source_target_pairs={{0,4},{1,5},{2,6},{3,7},{4,0},{5,1},{6,2},{7,3},{8,12},{9,13},{10,... | collective-permute-start | bytes 1327112 | tf_op jit(solution)/shard_map/cond/branch_1_fun/ppermute | solution.py:440
  17.8 12.8 %collective-permute-start.4 = (bf16[928,128]{1,0:T(8,128)(2,1)S(1)}, bf16[928,128]{1,0:T(8,128)(2,1)}, u32[]{:S(2)}, u32[]{:S(2)}) collective-permute-start(bf16[928,128]{1,0:T(8,128)(2,1)S(1)} %get-tuple-element.23), channel_id=1, source_target_pairs={{0,8},{8,16},{16,24},{24,0},{1,9},{9,17},{17,25},{25,1},{2,10},{10... | collective-permute-start | bytes 712712 | tf_op jit(solution)/shard_map/cond/branch_1_fun/ppermute | solution.py:443
  19.4 13.7 %collective-permute-start.5 = (bf16[928,128]{1,0:T(8,128)(2,1)S(1)}, bf16[928,128]{1,0:T(8,128)(2,1)}, u32[]{:S(2)}, u32[]{:S(2)}) collective-permute-start(bf16[928,128]{1,0:T(8,128)(2,1)S(1)} %get-tuple-element.24), channel_id=1, source_target_pairs={{0,24},{8,0},{16,8},{24,16},{1,25},{9,1},{17,9},{25,17},{2,26},{10... | collective-permute-start | bytes 712712 | tf_op jit(solution)/shard_map/cond/branch_1_fun/ppermute | solution.py:443
  28.4 7.8 %collective-permute-start.2 = (bf16[32,3712]{1,0:T(8,128)(2,1)S(1)}, bf16[32,3712]{1,0:T(8,128)(2,1)S(1)}, u32[]{:S(2)}, u32[]{:S(2)}) collective-permute-start(bf16[32,3712]{1,0:T(8,128)(2,1)S(1)} %get-tuple-element.21), channel_id=1, source_target_pairs={{0,4},{1,5},{2,6},{3,7},{4,0},{5,1},{6,2},{7,3},{8,12},{9,13},{10,... | collective-permute-start | bytes 712712 | tf_op jit(solution)/shard_map/cond/branch_1_fun/ppermute | solution.py:440
  30.0 6.2 %collective-permute-start.3 = (bf16[32,3456]{1,0:T(8,128)(2,1)S(1)}, bf16[32,3456]{1,0:T(8,128)(2,1)S(1)}, u32[]{:S(2)}, u32[]{:S(2)}) collective-permute-start(bf16[32,3456]{1,0:T(8,128)(2,1)S(1)} %get-tuple-element.22), channel_id=1, source_target_pairs={{0,2},{1,3},{2,0},{3,1},{4,6},{5,7},{6,4},{7,5},{8,10},{9,11},{10,... | collective-permute-start | bytes 663560 | tf_op jit(solution)/shard_map/cond/branch_1_fun/ppermute | solution.py:440
  36.5 10.0 %collective-permute-start.9 = (bf16[2,32,1024]{2,1,0:T(8,128)(2,1)S(1)}, bf16[2,32,1024]{2,1,0:T(8,128)(2,1)S(1)}, u32[]{:S(2)}, u32[]{:S(2)}) collective-permute-start(bf16[2,32,1024]{2,1,0:T(8,128)(2,1)S(1)} %get-tuple-element.81), channel_id=1, source_target_pairs={{0,8},{8,16},{16,24},{24,0},{1,9},{9,17},{17,25},{25,1},{2,10},{10... | collective-permute-start | bytes 393224 | tf_op jit(solution)/shard_map/ppermute | solution.py:443
  38.1 9.9 %collective-permute-start.10 = (bf16[2,32,1024]{2,1,0:T(8,128)(2,1)S(1)}, bf16[2,32,1024]{2,1,0:T(8,128)(2,1)S(1)}, u32[]{:S(2)}, u32[]{:S(2)}) collective-permute-start(bf16[2,32,1024]{2,1,0:T(8,128)(2,1)S(1)} %get-tuple-element.82), channel_id=1, source_target_pairs={{0,16},{8,24},{16,0},{24,8},{1,17},{9,25},{17,1},{25,9},{2,18},{10... | collective-permute-start | bytes 393224 | tf_op jit(solution)/shard_map/ppermute | solution.py:443
  38.5 9.5 %collective-permute-start.11 = (bf16[2,32,1024]{2,1,0:T(8,128)(2,1)S(1)}, bf16[2,32,1024]{2,1,0:T(8,128)(2,1)S(1)}, u32[]{:S(2)}, u32[]{:S(2)}) collective-permute-start(bf16[2,32,1024]{2,1,0:T(8,128)(2,1)S(1)} %get-tuple-element.83), channel_id=1, source_target_pairs={{0,24},{8,0},{16,8},{24,16},{1,25},{9,1},{17,9},{25,17},{2,26},{10... | collective-permute-start | bytes 393224 | tf_op jit(solution)/shard_map/ppermute | solution.py:443

commit v5 on v3

--- a/solution.py
+++ b/solution.py
@@ -373,6 +373,132 @@
     )(table_index, own, bias_sum, *arrived)
 
 
+def put_rows(ref, high, low):
+    wide = ref.shape[1] // EMBED_WIDTH
+    first = ref.shape[0] - 8
+    ref[first:, :] = jnp.zeros((8, ref.shape[1]), BF16)
+    rows = []
+    for value in (high, low):
+        for row in range(4):
+            pieces = [
+                value[min(row * wide + k, BIAS_ROWS - 1) : min(row * wide + k, BIAS_ROWS - 1) + 1, :]
+                for k in range(wide)
+            ]
+            rows.append(jnp.concatenate(pieces, axis=1))
+    ref[first:, :] = jnp.concatenate(rows, axis=0).astype(BF16)
+
+
+def get_rows(ref, store):
+    wide = ref.shape[1] // EMBED_WIDTH
+    value = ref[ref.shape[0] - 8 :, :].astype(F32)
+    value = value[:4] + value[4:]
+    for place in range(min(4 * wide, BIAS_ROWS)):
+        row, k = divmod(place, wide)
+        store[place : place + 1, :] = value[row : row + 1, k * EMBED_WIDTH : (k + 1) * EMBED_WIDTH]
+    return store[...]
+
+
+def padded(columns):
+    return -(-columns // EMBED_WIDTH) * EMBED_WIDTH
+
+
+def first_kernel(
+    n_table, scale, table_ref, up_keep_ref, up_in_ref, down_keep_ref, down_in_ref, bias_ref,
+    keep_ref, send_ref, bias_out_ref, store,
+):
+    _, _, rows, columns = keep_ref.shape
+    width = up_keep_ref.shape[1]
+    pairs = ((up_keep_ref, up_in_ref), (down_keep_ref, down_in_ref))
+    for which, (keep, arrived) in enumerate(pairs):
+        total = (keep[...] + arrived[:, :width].astype(F32)) * scale
+        for table in range(n_table):
+            store[table, which] = total[:, table * columns : (table + 1) * columns]
+    for place in range(n_table // 2):
+        keep_ref[place] = store[table_ref[0] ^ (2 * place)]
+        for which in range(2):
+            first = (2 * place + which) * rows
+            value = store[table_ref[0] ^ (2 * place + 1), which]
+            send_ref[first : first + rows, :columns] = value.astype(BF16)
+    high, low = bias_terms(bias_ref[...] + get_bias(up_in_ref, width))
+    put_rows(send_ref, high, low)
+    bias_out_ref[...] = high + low
+
+
+def first_call(table_index, up_keep, up_in, down_keep, down_in, bias_sum, n_table, scale):
+    rows, width = up_keep.shape
+    columns = width // n_table
+    return pl.pallas_call(
+        functools.partial(first_kernel, n_table, scale),
+        in_specs=[SMEM] + [VMEM] * 5,
+        out_specs=[VMEM] * 3,
+        out_shape=[
+            jax.ShapeDtypeStruct((n_table // 2, 2, rows, columns), F32),
+            jax.ShapeDtypeStruct((n_table * rows + 8, padded(columns)), BF16),
+            jax.ShapeDtypeStruct(bias_sum.shape, F32),
+        ],
+        scratch_shapes=[pltpu.VMEM((n_table, 2, rows, columns), F32)],
+        compiler_params=params(16),
+    )(table_index, up_keep, up_in, down_keep, down_in, bias_sum)
+
+
+def next_kernel(keep_ref, in_ref, bias_ref, out_ref, send_ref, bias_out_ref, store):
+    count, _, rows, columns = keep_ref.shape
+    for place in range(count):
+        for which in range(2):
+            first = (2 * place + which) * rows
+            total = keep_ref[place, which] + in_ref[first : first + rows, :columns].astype(F32)
+            if place % 2 == 0:
+                out_ref[place // 2, which] = total
+            else:
+                first = (place - 1 + which) * rows
+                send_ref[first : first + rows, :columns] = total.astype(BF16)
+    store[...] = jnp.zeros_like(store)
+    high, low = bias_terms(bias_ref[...] + get_rows(in_ref, store))
+    put_rows(send_ref, high, low)
+    bias_out_ref[...] = high + low
+
+
+def next_call(keep, arrived, bias_sum):
+    count, _, rows, columns = keep.shape
+    return pl.pallas_call(
+        next_kernel,
+        in_specs=[VMEM] * 3,
+        out_specs=[VMEM] * 3,
+        out_shape=[
+            jax.ShapeDtypeStruct((count // 2, 2, rows, columns), F32),
+            jax.ShapeDtypeStruct((count * rows + 8, padded(columns)), BF16),
+            jax.ShapeDtypeStruct(bias_sum.shape, F32),
+        ],
+        scratch_shapes=[pltpu.VMEM(bias_sum.shape, F32)],
+        compiler_params=params(16),
+    )(keep, arrived, bias_sum)
+
+
+def last_kernel(scale, keep_ref, in_ref, bias_ref, up_ref, down_ref, bias_out_ref, store):
+    rows, columns = up_ref.shape
+    up_ref[...] = keep_ref[0, 0] + in_ref[:rows, :columns].astype(F32)
+    down_ref[...] = keep_ref[0, 1] + in_ref[rows : 2 * rows, :columns].astype(F32)
+    store[...] = jnp.zeros_like(store)
+    total = bias_ref[...] + get_rows(in_ref, store)
+    bias_out_ref[...] = total[: bias_out_ref.shape[0]] * scale
+
+
+def last_call(keep, arrived, bias_sum, n_table, scale):
+    _, _, rows, columns = keep.shape
+    return pl.pallas_call(
+        functools.partial(last_kernel, scale),
+        in_specs=[VMEM] * 3,
+        out_specs=[VMEM] * 3,
+        out_shape=[
+            jax.ShapeDtypeStruct((rows, columns), F32),
+            jax.ShapeDtypeStruct((rows, columns), F32),
+            jax.ShapeDtypeStruct((columns * n_table // EMBED_WIDTH, EMBED_WIDTH), F32),
+        ],
+        scratch_shapes=[pltpu.VMEM(bias_sum.shape, F32)],
+        compiler_params=params(16),
+    )(keep, arrived, bias_sum)
+
+
 def rows_kernel(n_table, slots, *refs):
     parts, out_ref = refs[:n_table], refs[n_table]
     id_store = refs[n_table + 1]
@@ -454,32 +580,58 @@
     up_keep, up_send, down_keep, down_send, bias_sum = terms_call(
         keep, other, activations, cotangent, act_other, cot_other, ride
     )
-    for place, (up_bit, down_bit) in enumerate(zip(up_bits[1:], down_bits[1:])):
-        up_in = swap(up_send, "rep", up_bit)
-        down_in = swap(down_send, "rep", down_bit)
+    def exchange(place, up_send, down_send, bias_sum):
+        up_in = swap(up_send, "rep", up_bits[place])
+        down_in = swap(down_send, "rep", down_bits[place])
         if not ride:
-            bias_sum = bias_sum + swap(bias_sum, "rep", up_bit)
-        if place == len(far_bits) - 1:
-            break
+            bias_sum = bias_sum + swap(bias_sum, "rep", up_bits[place])
+        return up_in, down_in, bias_sum
+
+    def halved(up_keep, up_in, down_keep, down_in, bias_sum):
         if ride:
-            up_keep, up_send, down_keep, down_send, bias_sum = halve_call(
-                up_keep, up_in, down_keep, down_in, bias_sum
+            return halve_call(up_keep, up_in, down_keep, down_in, bias_sum)
+        half = up_keep.shape[0] // 2
+        up = up_keep + up_in.astype(F32)
+        down = down_keep + down_in.astype(F32)
+        return up[:half], up[half:].astype(BF16), down[:half], down[half:].astype(BF16), bias_sum
+
+    def chain(up_keep, up_send, down_keep, down_send, bias_sum):
+        for place in range(2, len(up_bits)):
+            up_in, down_in, bias_sum = exchange(place, up_send, down_send, bias_sum)
+            if place < len(up_bits) - 1:
+                up_keep, up_send, down_keep, down_send, bias_sum = halved(
+                    up_keep, up_in, down_keep, down_in, bias_sum
+                )
+        if not ride:
+            for bit in [1 << k for k in range(n_table.bit_length() - 1)]:
+                bias_sum = bias_sum + swap(bias_sum, "table", bit)
+        if not ride:
+            return split_call(
+                table_index, up_keep, up_in, down_keep, down_in, bias_sum, n_table, scale, ride
             )
-        else:
-            half = up_keep.shape[0] // 2
-            up = up_keep + up_in.astype(F32)
-            down = down_keep + down_in.astype(F32)
-            up_keep, up_send = up[:half], up[half:].astype(BF16)
-            down_keep, down_send = down[:half], down[half:].astype(BF16)
-    if not ride:
-        for bit in [1 << k for k in range(n_table.bit_length() - 1)]:
-            bias_sum = bias_sum + swap(bias_sum, "table", bit)
-    (up_in, down_in), parts = lax.optimization_barrier(((up_in, down_in), parts))
-    own, bias_sum, *sends = split_call(
-        table_index, up_keep, up_in, down_keep, down_in, bias_sum, n_table, scale, ride
+        own, message, bias_sum = first_call(
+            table_index, up_keep, up_in, down_keep, down_in, bias_sum, n_table, scale
+        )
+        for bit in [1 << k for k in range(n_table.bit_length() - 2)]:
+            message = swap(message, "table", bit)
+            own, message, bias_sum = next_call(own, message, bias_sum)
+        return [own, bias_sum, message]
+
+    up_in, down_in, bias_sum = exchange(1, up_send, down_send, bias_sum)
+    terms = halved(up_keep, up_in, down_keep, down_in, bias_sum)
+    shapes = jax.eval_shape(chain, *terms)
+    own, bias_sum, *sends = lax.cond(
+        feature_table_slot[0] >= 0,
+        chain,
+        lambda *_: jax.tree.map(lambda x: jnp.zeros(x.shape, x.dtype), shapes),
+        *terms,
     )
-    arrived = [shifted(value, k + 1) for k, value in enumerate(sends)]
-    up_grad, down_grad, bias_grad = finish_call(table_index, own, bias_sum, arrived, scale, ride)
+    if ride:
+        message = swap(sends[0], "table", n_table // 2)
+        up_grad, down_grad, bias_grad = last_call(own, message, bias_sum, n_table, scale)
+    else:
+        arrived = [shifted(value, k + 1) for k, value in enumerate(sends)]
+        up_grad, down_grad, bias_grad = finish_call(table_index, own, bias_sum, arrived, scale, ride)
     parts, _ = lax.optimization_barrier((parts, own))
     row_grad = rows_call(parts, slots)
     bias_grad = bias_grad.reshape(width)

time: 51.5 us -> 48.8 us (0.948)
  starting transfers between devices: 21.3 us -> 16.8 us
  waiting for transfers between devices: 15 us -> 17.1 us
    ppermute x7 -> x9, waiting for transfers between devices: 6.03 us -> 17.1 us  [swap(): return lax.ppermute(value, axis, [(k, k ^ bit) for k in range(size)])]
    ppermute x6 -> x3, starting transfers between devices: 13.6 us -> 4.62 us  [shifted(): lax.ppermute(value, 'table', [(k, (k + shift) % n_table) for k in range(n...]
    ppermute x6 -> x3, waiting for transfers between devices: 8.94 us -> 0.01 us  [shifted(): lax.ppermute(value, 'table', [(k, (k + shift) % n_table) for k in range(n...]
    ppermute x7 -> x9, starting transfers between devices: 7.72 us -> 12.2 us  [swap(): return lax.ppermute(value, axis, [(k, k ^ bit) for k in range(size)])]
    pallas_call x2 -> x3, Pallas kernels: 1.07 us -> 1.09 us  [the longest x1 0.7 us: last_call(): pl.pallas_call(functools.partial(last_kernel, scale), in_specs=[VMEM] * 3...]
  transfers between devices with their start and end apart: 13 -> 12, of which waited for: 4 -> 4; matrix products, arithmetic and copies ran while one was open for 0% -> 0% of each run, Pallas kernels for 22% -> 24%
where the time goes in v5:
time: 48.8 us; the launch traced here: 48.6 us
  waiting for transfers between devices  17.1 us (35%)
  starting transfers between devices  16.8 us (34%)
  Pallas kernels  13.1 us (27%)
  local copies, waits for them, and re-layouts  0.86 us (2%)
  between operations  0.75 us (2%)
    ppermute x9, waiting for transfers between devices, swap(): return lax.ppermute(value, axis, [(k, k ^ bit) for k in range(size)])  17.1 us
    ppermute x9, starting transfers between devices, swap(): return lax.ppermute(value, axis, [(k, k ^ bit) for k in range(size)])  12.2 us
    pallas_call x1, Pallas kernels, input_call(): pl.pallas_call(functools.partial(input_kernel, n_table, slots, up_bits, d...  6 us
    pallas_call x1, Pallas kernels, rows_call(): pl.pallas_call(functools.partial(rows_kernel, n_table, slots), grid=(slot...  4.99 us
    ppermute x3, starting transfers between devices, shifted(): lax.ppermute(value, 'table', [(k, (k + shift) % n_table) for k in range(n...  4.62 us
  transfers between devices with their start and end apart: 12, of which 4 were waited for; matrix products, arithmetic and copies ran while one was open for 0% of the time, Pallas kernels for 24%

profile of v5, /device:TPU:0, one launch (start us, length us, event | category | flops | bytes accessed | tf_op | source)
XLA Modules:
  0.0 48.6 jit_solution(3786761639296928090)
XLA Ops:
  0.6 0.5 %collective-permute-start.4 = (bf16[128,3456]{1,0:T(8,128)(2,1)}, bf16[128,3456]{1,0:T(8,128)(2,1)S(1)}, u32[]{:S(2)}, u32[]{:S(2)}) collective-permute-start(bf16[128,3456]{1,0:T(8,128)(2,1)} %act.1), channel_id=1, source_target_pairs={{0,1},{1,0},{2,3},{3,2},{4,5},{5,4},{6,7},{7,6},{8,9},{9,8},{10,11... | collective-permute-start | bytes 2654216 | tf_op jit(solution)/shard_map/ppermute | solution.py:566
  1.2 0.1 collective-permute-start.5
  1.2 6.0 %shard_map.119 = (bf16[2,128,128]{2,1,0:T(8,128)(2,1)}, bf16[2,128,128]{2,1,0:T(8,128)(2,1)}, bf16[128,128]{1,0:T(8,128)(2,1)}, bf16[928,128]{1,0:T(8,128)(2,1)}...) custom-call(s32[1]{0:T(128)} %bitcast.table_ref, s32[1]{0:T(128)} %bitcast.1.rep_ref, ...), custom_call_target="tpu_custom_call" | custom-call | flops 905969664 | bytes 5308416 | tf_op jit(solution)/shard_map/pallas_call | solution.py:145
  7.2 0.5 %collective-permute-start.3 = (bf16[2,128,128]{2,1,0:T(8,128)(2,1)}, bf16[2,128,128]{2,1,0:T(8,128)(2,1)S(1)}, u32[]{:S(2)}, u32[]{:S(2)}) collective-permute-start(bf16[2,128,128]{2,1,0:T(8,128)(2,1)} %get-tuple-element.58), channel_id=1, source_target_pairs={{0,1},{1,0},{2,3},{3,2},{4,5},{5,4},{6,7},{7,6},{8,9},{9,8},{10,11... | collective-permute-start | bytes 196616 | tf_op jit(solution)/shard_map/ppermute | solution.py:566
  7.7 1.1 %collective-permute-done.3.other_ref = bf16[2,128,128]{2,1,0:T(8,128)(2,1)S(1)} collective-permute-done((bf16[2,128,128]{2,1,0:T(8,128)(2,1)}, bf16[2,128,128]{2,1,0:T(8,128)(2,1)S(1)}, u32[]{:S(2)}, u32[]{:S(2)}) %collective-permute-start.3) | collective-permute-done | bytes 65568 | tf_op jit(solution)/shard_map/ppermute | solution.py:566
  8.9 0.0 collective-permute-done.4.act_other
  8.9 0.0 collective-permute-done.5.cot_other
  8.9 0.0 copy-start.3
  8.9 0.8 %copy-done.3 = bf16[2,128,128]{2,1,0:T(8,128)(2,1)S(1)} copy-done((bf16[2,128,128]{2,1,0:T(8,128)(2,1)S(1)}, bf16[2,128,128]{2,1,0:T(8,128)(2,1)}, u32[]{:S(2)}) %copy-start.3) | copy-done | bytes 65560
  9.7 0.8 %shard_map.120 = (f32[64,3456]{1,0:T(8,128)S(1)}, bf16[64,3584]{1,0:T(8,128)(2,1)S(1)}, f32[64,3456]{1,0:T(8,128)S(1)}, bf16[64,3456]{1,0:T(8,128)(2,1)S(1)}, f32[32,128]{1,0:T(8,128)S(1)}) custom-call(bf16[2,128,128]{2,1,0:T(8,128)(2,1)S(1)} %copy-done.3, bf16[2,128,128]{2,1,0:T(8,128)(2,1)S(1)} %collective-permute-done.3.other_ref, ...), custom_call_target="tpu_custom_call" | custom-call | flops 452984832 | bytes 6193152 | tf_op jit(solution)/shard_map/pallas_call | solution.py:236
  10.6 2.9 %collective-permute-start.6 = (bf16[64,3584]{1,0:T(8,128)(2,1)S(1)}, bf16[64,3584]{1,0:T(8,128)(2,1)S(1)}, u32[]{:S(2)}, u32[]{:S(2)}) collective-permute-start(bf16[64,3584]{1,0:T(8,128)(2,1)S(1)} %get-tuple-element.60), channel_id=1, source_target_pairs={{0,2},{1,3},{2,0},{3,1},{4,6},{5,7},{6,4},{7,5},{8,10},{9,11},{10,... | collective-permute-start | bytes 1376264 | tf_op jit(solution)/shard_map/ppermute | solution.py:566
  13.5 1.5 %collective-permute-start.7 = (bf16[64,3456]{1,0:T(8,128)(2,1)S(1)}, bf16[64,3456]{1,0:T(8,128)(2,1)S(1)}, u32[]{:S(2)}, u32[]{:S(2)}) collective-permute-start(bf16[64,3456]{1,0:T(8,128)(2,1)S(1)} %get-tuple-element.62), channel_id=1, source_target_pairs={{0,4},{1,5},{2,6},{3,7},{4,0},{5,1},{6,2},{7,3},{8,12},{9,13},{10,... | collective-permute-start | bytes 1327112 | tf_op jit(solution)/shard_map/ppermute | solution.py:566
  15.0 2.6 %collective-permute-start.10 = (bf16[928,128]{1,0:T(8,128)(2,1)}, bf16[928,128]{1,0:T(8,128)(2,1)S(1)}, u32[]{:S(2)}, u32[]{:S(2)}) collective-permute-start(bf16[928,128]{1,0:T(8,128)(2,1)} %get-tuple-element.77), channel_id=1, source_target_pairs={{0,16},{8,24},{16,0},{24,8},{1,17},{9,25},{17,1},{25,9},{2,18},{10... | collective-permute-start | bytes 712712 | tf_op jit(solution)/shard_map/ppermute | solution.py:569
  17.6 1.3 %collective-permute-start.11 = (bf16[928,128]{1,0:T(8,128)(2,1)S(1)}, bf16[928,128]{1,0:T(8,128)(2,1)S(1)}, u32[]{:S(2)}, u32[]{:S(2)}) collective-permute-start(bf16[928,128]{1,0:T(8,128)(2,1)S(1)} %copy-done.6), channel_id=1, source_target_pairs={{0,24},{8,0},{16,8},{24,16},{1,25},{9,1},{17,9},{25,17},{2,26},{10... | collective-permute-start | bytes 712712 | tf_op jit(solution)/shard_map/ppermute | solution.py:569
  18.9 0.7 %collective-permute-start.9 = (bf16[928,128]{1,0:T(8,128)(2,1)S(1)}, bf16[928,128]{1,0:T(8,128)(2,1)S(1)}, u32[]{:S(2)}, u32[]{:S(2)}) collective-permute-start(bf16[928,128]{1,0:T(8,128)(2,1)S(1)} %copy-done.5), channel_id=1, source_target_pairs={{0,8},{8,16},{16,24},{24,0},{1,9},{9,17},{17,25},{25,1},{2,10},{10... | collective-permute-start | bytes 712712 | tf_op jit(solution)/shard_map/ppermute | solution.py:569
  19.7 5.8 %collective-permute-done.7.down_in_ref = bf16[64,3456]{1,0:T(8,128)(2,1)S(1)} collective-permute-done((bf16[64,3456]{1,0:T(8,128)(2,1)S(1)}, bf16[64,3456]{1,0:T(8,128)(2,1)S(1)}, u32[]{:S(2)}, u32[]{:S(2)}) %collective-permute-start.7) | collective-permute-done | bytes 442400 | tf_op jit(solution)/shard_map/ppermute | solution.py:566
  25.4 0.0 collective-permute-done.6.up_in_ref
  25.4 0.2 shard_map.121
  25.6 0.0 copy-start.2
  25.6 14.4 %conditional.1 = (f32[1,2,32,864]{3,2,1,0:T(8,128)S(1)}, f32[32,128]{1,0:T(8,128)S(1)}, bf16[72,896]{1,0:T(8,128)(2,1)S(1)}) conditional(s32[]{:T(128)} %bitcast.5, () %tuple.17, (bf16[32,3712]{1,0:T(8,128)(2,1)S(1)}, bf16[32,3456]{1,0:T(8,128)(2,1)S(1)}, s32[1]{0:T(128)}, f32[32,3456]{1,0:T(8,128)S(1)}, f32[32,3456]{1,0:T(8,128)S(1)}, ...), branch_computations={%region_0.0_spmd, %region_1.0_spmd} | conditional | bytes 2810000 | solution.py:623
  25.6 1.6 %collective-permute-start = (bf16[32,3712]{1,0:T(8,128)(2,1)S(1)}, bf16[32,3712]{1,0:T(8,128)(2,1)S(1)}, u32[]{:S(2)}, u32[]{:S(2)}) collective-permute-start(bf16[32,3712]{1,0:T(8,128)(2,1)S(1)} %get-tuple-element.14), channel_id=1, source_target_pairs={{0,4},{1,5},{2,6},{3,7},{4,0},{5,1},{6,2},{7,3},{8,12},{9,13},{10,... | collective-permute-start | bytes 712712 | tf_op jit(solution)/shard_map/cond/branch_1_fun/ppermute | solution.py:566
  27.2 0.6 %collective-permute-start.1 = (bf16[32,3456]{1,0:T(8,128)(2,1)S(1)}, bf16[32,3456]{1,0:T(8,128)(2,1)S(1)}, u32[]{:S(2)}, u32[]{:S(2)}) collective-permute-start(bf16[32,3456]{1,0:T(8,128)(2,1)S(1)} %get-tuple-element.16), channel_id=1, source_target_pairs={{0,2},{1,3},{2,0},{3,1},{4,6},{5,7},{6,4},{7,5},{8,10},{9,11},{10,... | collective-permute-start | bytes 663560 | tf_op jit(solution)/shard_map/cond/branch_1_fun/ppermute | solution.py:566
  27.8 5.4 %collective-permute-done.1.down_in_ref = bf16[32,3456]{1,0:T(8,128)(2,1)S(1)} collective-permute-done((bf16[32,3456]{1,0:T(8,128)(2,1)S(1)}, bf16[32,3456]{1,0:T(8,128)(2,1)S(1)}, u32[]{:S(2)}, u32[]{:S(2)}) %collective-permute-start.1) | collective-permute-done | bytes 221216 | tf_op jit(solution)/shard_map/cond/branch_1_fun/ppermute | solution.py:566
  33.3 0.3 branch_1_fun.2
  33.6 1.6 %collective-permute-start.2 = (bf16[136,896]{1,0:T(8,128)(2,1)S(1)}, bf16[136,896]{1,0:T(8,128)(2,1)S(1)}, u32[]{:S(2)}, u32[]{:S(2)}) collective-permute-start(bf16[136,896]{1,0:T(8,128)(2,1)S(1)} %get-tuple-element.19), channel_id=1, source_target_pairs={{0,8},{8,0},{16,24},{24,16},{1,9},{9,1},{17,25},{25,17},{2,10},{10... | collective-permute-start | bytes 731144 | tf_op jit(solution)/shard_map/cond/branch_1_fun/ppermute | solution.py:566
  35.2 4.7 %collective-permute-done.2.in_ref = bf16[136,896]{1,0:T(8,128)(2,1)S(1)} collective-permute-done((bf16[136,896]{1,0:T(8,128)(2,1)S(1)}, bf16[136,896]{1,0:T(8,128)(2,1)S(1)}, u32[]{:S(2)}, u32[]{:S(2)}) %collective-permute-start.2) | collective-permute-done | bytes 243744 | tf_op jit(solution)/shard_map/cond/branch_1_fun/ppermute | solution.py:566
  40.0 0.1 branch_1_fun.3
  40.0 2.9 %collective-permute-start.8 = (bf16[72,896]{1,0:T(8,128)(2,1)S(1)}, bf16[72,896]{1,0:T(8,128)(2,1)S(1)}, u32[]{:S(2)}, u32[]{:S(2)}) collective-permute-start(bf16[72,896]{1,0:T(8,128)(2,1)S(1)} %get-tuple-element.70), channel_id=1, source_target_pairs={{0,16},{8,24},{16,0},{24,8},{1,17},{9,25},{17,1},{25,9},{2,18},{10... | collective-permute-start | bytes 387080 | tf_op jit(solution)/shard_map/ppermute | solution.py:566
  42.9 0.0 collective-permute-done.10.refs_2_
  42.9 5.0 %shard_map.123 = f32[1,7,512,128]{3,2,1,0:T(8,128)} custom-call(bf16[928,128]{1,0:T(8,128)(2,1)S(1)} %copy-done.2, bf16[928,128]{1,0:T(8,128)(2,1)S(1)} %collective-permute-done.9.refs_1_, bf16[928,128]{1,0:T(8,128)(2,1)S(1)} %collective-permute-done.10.refs_2_, bf16[928,128]{1,0:T(8,128)(2,1)S(1)} %collective-permute-done.11.refs_3_), custom_call_target="tpu_custom_call" | custom-call | flops 469762048 | bytes 1835008 | tf_op jit(solution)/shard_map/pallas_call | solution.py:533
  47.9 0.0 collective-permute-done.8.in_ref
  47.9 0.7 %shard_map.122 = (f32[32,864]{1,0:T(8,128)}, f32[32,864]{1,0:T(8,128)}, f32[27,128]{1,0:T(8,128)}) custom-call(f32[1,2,32,864]{3,2,1,0:T(8,128)S(1)} %get-tuple-element.69.keep_ref, bf16[72,896]{1,0:T(8,128)(2,1)S(1)} %collective-permute-done.8.in_ref, f32[32,128]{1,0:T(8,128)S(1)} %get-tuple-element.71.bias_ref), custom_call_target="tpu_custom_call" | custom-call | tf_op jit(solution)/shard_map/pallas_call | solution.py:488
  (14 shorter events, 0.0 us)
Async XLA Ops:
  0.6 8.2 %collective-permute-start.4 = (bf16[128,3456]{1,0:T(8,128)(2,1)}, bf16[128,3456]{1,0:T(8,128)(2,1)S(1)}, u32[]{:S(2)}, u32[]{:S(2)}) collective-permute-start(bf16[128,3456]{1,0:T(8,128)(2,1)} %act.1), channel_id=1, source_target_pairs={{0,1},{1,0},{2,3},{3,2},{4,5},{5,4},{6,7},{7,6},{8,9},{9,8},{10,11... | collective-permute-start | bytes 2654216 | tf_op jit(solution)/shard_map/ppermute | solution.py:566
  1.2 7.7 %collective-permute-start.5 = (bf16[128,3456]{1,0:T(8,128)(2,1)}, bf16[128,3456]{1,0:T(8,128)(2,1)S(1)}, u32[]{:S(2)}, u32[]{:S(2)}) collective-permute-start(bf16[128,3456]{1,0:T(8,128)(2,1)} %cot.1), channel_id=1, source_target_pairs={{0,1},{1,0},{2,3},{3,2},{4,5},{5,4},{6,7},{7,6},{8,9},{9,8},{10,11... | collective-permute-start | bytes 2654216 | tf_op jit(solution)/shard_map/ppermute | solution.py:566
  1.2 7.6 %copy-start = (bf16[128,3456]{1,0:T(8,128)(2,1)S(1)}, bf16[128,3456]{1,0:T(8,128)(2,1)}, u32[]{:S(2)}) copy-start(bf16[128,3456]{1,0:T(8,128)(2,1)} %act.1) | copy-start | bytes 2654212
  1.2 7.6 %copy-start.1 = (bf16[128,3456]{1,0:T(8,128)(2,1)S(1)}, bf16[128,3456]{1,0:T(8,128)(2,1)}, u32[]{:S(2)}) copy-start(bf16[128,3456]{1,0:T(8,128)(2,1)} %cot.1) | copy-start | bytes 2654212
  7.2 1.6 %collective-permute-start.3 = (bf16[2,128,128]{2,1,0:T(8,128)(2,1)}, bf16[2,128,128]{2,1,0:T(8,128)(2,1)S(1)}, u32[]{:S(2)}, u32[]{:S(2)}) collective-permute-start(bf16[2,128,128]{2,1,0:T(8,128)(2,1)} %get-tuple-element.58), channel_id=1, source_target_pairs={{0,1},{1,0},{2,3},{3,2},{4,5},{5,4},{6,7},{7,6},{8,9},{9,8},{10,11... | collective-permute-start | bytes 196616 | tf_op jit(solution)/shard_map/ppermute | solution.py:566
  8.9 0.8 %copy-start.3 = (bf16[2,128,128]{2,1,0:T(8,128)(2,1)S(1)}, bf16[2,128,128]{2,1,0:T(8,128)(2,1)}, u32[]{:S(2)}) copy-start(bf16[2,128,128]{2,1,0:T(8,128)(2,1)} %get-tuple-element.57.keep_ref) | copy-start | bytes 196612
  9.7 7.9 %copy-start.6 = (bf16[928,128]{1,0:T(8,128)(2,1)S(1)}, bf16[928,128]{1,0:T(8,128)(2,1)}, u32[]{:S(2)}) copy-start(bf16[928,128]{1,0:T(8,128)(2,1)} %get-tuple-element.78) | copy-start | bytes 712708
  9.7 9.2 %copy-start.5 = (bf16[928,128]{1,0:T(8,128)(2,1)S(1)}, bf16[928,128]{1,0:T(8,128)(2,1)}, u32[]{:S(2)}) copy-start(bf16[928,128]{1,0:T(8,128)(2,1)} %get-tuple-element.76) | copy-start | bytes 712708
  9.7 9.9 %copy-start.4 = (s32[26]{0:T(128)S(1)}, s32[26]{0:T(128)}, u32[]{:S(2)}) copy-start(s32[26]{0:T(128)} %owner_ref.1) | copy-start | bytes 316
  10.6 14.9 %collective-permute-start.6 = (bf16[64,3584]{1,0:T(8,128)(2,1)S(1)}, bf16[64,3584]{1,0:T(8,128)(2,1)S(1)}, u32[]{:S(2)}, u32[]{:S(2)}) collective-permute-start(bf16[64,3584]{1,0:T(8,128)(2,1)S(1)} %get-tuple-element.60), channel_id=1, source_target_pairs={{0,2},{1,3},{2,0},{3,1},{4,6},{5,7},{6,4},{7,5},{8,10},{9,11},{10,... | collective-permute-start | bytes 1376264 | tf_op jit(solution)/shard_map/ppermute | solution.py:566
  13.5 12.0 %collective-permute-start.7 = (bf16[64,3456]{1,0:T(8,128)(2,1)S(1)}, bf16[64,3456]{1,0:T(8,128)(2,1)S(1)}, u32[]{:S(2)}, u32[]{:S(2)}) collective-permute-start(bf16[64,3456]{1,0:T(8,128)(2,1)S(1)} %get-tuple-element.62), channel_id=1, source_target_pairs={{0,4},{1,5},{2,6},{3,7},{4,0},{5,1},{6,2},{7,3},{8,12},{9,13},{10,... | collective-permute-start | bytes 1327112 | tf_op jit(solution)/shard_map/ppermute | solution.py:566
  15.0 27.9 %collective-permute-start.10 = (bf16[928,128]{1,0:T(8,128)(2,1)}, bf16[928,128]{1,0:T(8,128)(2,1)S(1)}, u32[]{:S(2)}, u32[]{:S(2)}) collective-permute-start(bf16[928,128]{1,0:T(8,128)(2,1)} %get-tuple-element.77), channel_id=1, source_target_pairs={{0,16},{8,24},{16,0},{24,8},{1,17},{9,25},{17,1},{25,9},{2,18},{10... | collective-permute-start | bytes 712712 | tf_op jit(solution)/shard_map/ppermute | solution.py:569
  17.6 25.3 %collective-permute-start.11 = (bf16[928,128]{1,0:T(8,128)(2,1)S(1)}, bf16[928,128]{1,0:T(8,128)(2,1)S(1)}, u32[]{:S(2)}, u32[]{:S(2)}) collective-permute-start(bf16[928,128]{1,0:T(8,128)(2,1)S(1)} %copy-done.6), channel_id=1, source_target_pairs={{0,24},{8,0},{16,8},{24,16},{1,25},{9,1},{17,9},{25,17},{2,26},{10... | collective-permute-start | bytes 712712 | tf_op jit(solution)/shard_map/ppermute | solution.py:569
  18.9 24.0 %collective-permute-start.9 = (bf16[928,128]{1,0:T(8,128)(2,1)S(1)}, bf16[928,128]{1,0:T(8,128)(2,1)S(1)}, u32[]{:S(2)}, u32[]{:S(2)}) collective-permute-start(bf16[928,128]{1,0:T(8,128)(2,1)S(1)} %copy-done.5), channel_id=1, source_target_pairs={{0,8},{8,16},{16,24},{24,0},{1,9},{9,17},{17,25},{25,1},{2,10},{10... | collective-permute-start | bytes 712712 | tf_op jit(solution)/shard_map/ppermute | solution.py:569
  25.6 17.3 %copy-start.2 = (bf16[928,128]{1,0:T(8,128)(2,1)S(1)}, bf16[928,128]{1,0:T(8,128)(2,1)}, u32[]{:S(2)}) copy-start(bf16[928,128]{1,0:T(8,128)(2,1)} %get-tuple-element.79.refs_0_) | copy-start | bytes 712708
  25.6 7.7 %collective-permute-start = (bf16[32,3712]{1,0:T(8,128)(2,1)S(1)}, bf16[32,3712]{1,0:T(8,128)(2,1)S(1)}, u32[]{:S(2)}, u32[]{:S(2)}) collective-permute-start(bf16[32,3712]{1,0:T(8,128)(2,1)S(1)} %get-tuple-element.14), channel_id=1, source_target_pairs={{0,4},{1,5},{2,6},{3,7},{4,0},{5,1},{6,2},{7,3},{8,12},{9,13},{10,... | collective-permute-start | bytes 712712 | tf_op jit(solution)/shard_map/cond/branch_1_fun/ppermute | solution.py:566
  27.2 6.1 %collective-permute-start.1 = (bf16[32,3456]{1,0:T(8,128)(2,1)S(1)}, bf16[32,3456]{1,0:T(8,128)(2,1)S(1)}, u32[]{:S(2)}, u32[]{:S(2)}) collective-permute-start(bf16[32,3456]{1,0:T(8,128)(2,1)S(1)} %get-tuple-element.16), channel_id=1, source_target_pairs={{0,2},{1,3},{2,0},{3,1},{4,6},{5,7},{6,4},{7,5},{8,10},{9,11},{10,... | collective-permute-start | bytes 663560 | tf_op jit(solution)/shard_map/cond/branch_1_fun/ppermute | solution.py:566
  33.6 6.4 %collective-permute-start.2 = (bf16[136,896]{1,0:T(8,128)(2,1)S(1)}, bf16[136,896]{1,0:T(8,128)(2,1)S(1)}, u32[]{:S(2)}, u32[]{:S(2)}) collective-permute-start(bf16[136,896]{1,0:T(8,128)(2,1)S(1)} %get-tuple-element.19), channel_id=1, source_target_pairs={{0,8},{8,0},{16,24},{24,16},{1,9},{9,1},{17,25},{25,17},{2,10},{10... | collective-permute-start | bytes 731144 | tf_op jit(solution)/shard_map/cond/branch_1_fun/ppermute | solution.py:566
  40.0 7.9 %collective-permute-start.8 = (bf16[72,896]{1,0:T(8,128)(2,1)S(1)}, bf16[72,896]{1,0:T(8,128)(2,1)S(1)}, u32[]{:S(2)}, u32[]{:S(2)}) collective-permute-start(bf16[72,896]{1,0:T(8,128)(2,1)S(1)} %get-tuple-element.70), channel_id=1, source_target_pairs={{0,16},{8,24},{16,0},{24,8},{1,17},{9,25},{17,1},{25,9},{2,18},{10... | collective-permute-start | bytes 387080 | tf_op jit(solution)/shard_map/ppermute | solution.py:566

commit v6 on v5

--- a/solution.py
+++ b/solution.py
@@ -49,10 +49,10 @@
 def input_kernel(
     n_table, slots, up_bits, down_bits, table_ref, rep_ref, owner_ref,
     act_hbm, cot_hbm, down_hbm, up_hbm, bias_ref, ids_ref, length_ref,
-    keep_hbm, send_hbm, dense_hbm, *rest,
+    keep, send_hbm, dense_hbm, *rest,
 ):
     outs = rest[:n_table]
-    act, cot, down, up, keep, send, store, message, id_store, feature_ref, in_sems, out_sems = rest[n_table:]
+    act, cot, down, up, send, store, message, id_store, feature_ref, in_sems, out_sems = rest[n_table:]
     tokens, width = act.shape
     rank = down.shape[0]
     half = rank // 2
@@ -105,12 +105,8 @@
     keep[0], send[0] = rows[:half], rows[half:]
     rows = lax.dot_general(down_order, back, NT, preferred_element_type=F32).astype(BF16)
     keep[1], send[1] = rows[:half], rows[half:]
-    written = [
-        pltpu.make_async_copy(send, send_hbm, out_sems.at[0]),
-        pltpu.make_async_copy(keep, keep_hbm, out_sems.at[1]),
-    ]
-    for copy in written:
-        copy.start()
+    written = [pltpu.make_async_copy(send, send_hbm, out_sems.at[0])]
+    written[0].start()
     blocks = 3
     for first in range(0, width // EMBED_WIDTH, blocks):
         part = slice(first * EMBED_WIDTH, (first + blocks) * EMBED_WIDTH)
@@ -145,9 +141,9 @@
     return pl.pallas_call(
         functools.partial(input_kernel, n_table, slots, up_bits, down_bits),
         in_specs=[SMEM, SMEM, SMEM, ANY, ANY, ANY, ANY, VMEM, VMEM, VMEM],
-        out_specs=[ANY] * (3 + n_table),
-        out_shape=[
-            jax.ShapeDtypeStruct((2, rank // 2, tokens), BF16),
+        out_specs=[VMEM] + [ANY] * (2 + n_table),
+        out_shape=[
+            pltpu.VMEM((2, rank // 2, tokens), BF16),
             jax.ShapeDtypeStruct((2, rank // 2, tokens), BF16),
             jax.ShapeDtypeStruct((tokens, EMBED_WIDTH), BF16),
         ]
@@ -157,7 +153,6 @@
             pltpu.VMEM((tokens, width), BF16),
             pltpu.VMEM((rank, width), BF16),
             pltpu.VMEM((rank, width), BF16),
-            pltpu.VMEM((2, rank // 2, tokens), BF16),
             pltpu.VMEM((2, rank // 2, tokens), BF16),
             pltpu.VMEM((SPARSE_FEATURES + 2, tokens, EMBED_WIDTH), BF16),
             pltpu.VMEM((n_table, sent, EMBED_WIDTH), BF16),
@@ -499,44 +494,50 @@
     )(keep, arrived, bias_sum)
 
 
-def rows_kernel(n_table, slots, *refs):
-    parts, out_ref = refs[:n_table], refs[n_table]
-    id_store = refs[n_table + 1]
+def rows_kernel(slots, *refs):
+    *parts, out_hbm, id_store, row_store, out, sems = refs
     tokens = (parts[0].shape[0] - id_store.shape[1]) // slots
-    slot = pl.program_id(0)
-
-    @pl.when(slot == 0)
-    def _():
-        for source in range(n_table):
-            ids = parts[source][slots * tokens :, :].astype(F32).astype(jnp.int32)
-            id_store[source] = ids + EMPTY
-
-    rows = lax.broadcasted_iota(jnp.int32, (TABLE_REACH_ROWS, tokens), 0)
-    counts, grads = [], []
-    for source in range(n_table):
-        count = jnp.zeros((TABLE_REACH_ROWS, tokens), F32)
-        for entry in range(BAG):
-            ids = id_store[source, pl.ds(slot * BAG + entry, 1), :]
-            count = count + jnp.where(ids == rows, 1.0, 0.0)
-        counts.append(count.astype(BF16))
-        grads.append(parts[source][pl.ds(pl.multiple_of(slot * tokens, tokens), tokens), :])
-    count = jnp.concatenate(counts, axis=1)
-    grad = jnp.concatenate(grads, axis=0)
-    out_ref[0, 0] = jnp.dot(count, grad, preferred_element_type=F32)
+    numbers = lax.broadcasted_iota(jnp.int32, row_store.shape, 0) - EMPTY
+    row_store[...] = numbers.astype(F32).astype(BF16)
+    for source, part in enumerate(parts):
+        id_store[source] = part[slots * tokens :, :].astype(F32)
+    copies = []
+    for slot in range(slots):
+        rows = row_store[...].reshape(TABLE_REACH_ROWS // 16, 16, tokens)
+        one, zero = jnp.ones(rows.shape, BF16), jnp.zeros(rows.shape, BF16)
+        counts = []
+        for source in range(len(parts)):
+            count = None
+            for entry in range(BAG):
+                place = slot * BAG + entry
+                ids = jnp.broadcast_to(id_store[source, place : place + 1, :], (16, tokens)).astype(BF16)
+                found = jnp.where(rows == ids[None], one, zero)
+                count = found if count is None else count + found
+            counts.append(count.reshape(TABLE_REACH_ROWS, tokens))
+        count = jnp.concatenate(counts, axis=1)
+        grad = jnp.concatenate([part[slot * tokens : (slot + 1) * tokens, :] for part in parts], axis=0)
+        out[slot] = jnp.dot(count, grad, preferred_element_type=F32)
+        copies.append(pltpu.make_async_copy(out.at[slot], out_hbm.at[0, slot], sems.at[slot]))
+        copies[-1].start()
+    for copy in copies:
+        copy.wait()
 
 
 def rows_call(parts, slots):
     n_table = len(parts)
     id_rows = -(-slots * BAG // 16) * 16
     tokens = (parts[0].shape[0] - id_rows) // slots
-    whole = pl.BlockSpec(parts[0].shape, lambda i: (0, 0))
-    return pl.pallas_call(
-        functools.partial(rows_kernel, n_table, slots),
-        grid=(slots,),
-        in_specs=[whole] * n_table,
-        out_specs=pl.BlockSpec((1, 1, TABLE_REACH_ROWS, EMBED_WIDTH), lambda i: (0, i, 0, 0)),
+    return pl.pallas_call(
+        functools.partial(rows_kernel, slots),
+        in_specs=[VMEM] * n_table,
+        out_specs=ANY,
         out_shape=jax.ShapeDtypeStruct((1, slots, TABLE_REACH_ROWS, EMBED_WIDTH), F32),
-        scratch_shapes=[pltpu.VMEM((n_table, id_rows, tokens), jnp.int32)],
+        scratch_shapes=[
+            pltpu.VMEM((n_table, id_rows, tokens), F32),
+            pltpu.VMEM((TABLE_REACH_ROWS, tokens), BF16),
+            pltpu.VMEM((slots, TABLE_REACH_ROWS, EMBED_WIDTH), F32),
+            pltpu.SemaphoreType.DMA((slots,)),
+        ],
         compiler_params=params(16),
         cost_estimate=pl.CostEstimate(
             flops=2 * slots * n_table * tokens * TABLE_REACH_ROWS * EMBED_WIDTH,

time: 48.8 us -> 47.4 us (0.971)
  Pallas kernels: 13.1 us -> 11.9 us
  local copies, waits for them, and re-layouts: 0.86 us -> 0.03 us
  waiting for transfers between devices: 17.1 us -> 17.6 us
    pallas_call x1, Pallas kernels: 4.99 us -> 3.82 us  [rows_call(): pl.pallas_call(functools.partial(rows_kernel, slots), in_specs=[VMEM] * n...]
    unnamed x14 -> x12, local copies, waits for them, and re-layouts: 0.86 us -> 0.03 us
    ppermute x9, waiting for transfers between devices: 17.1 us -> 17.6 us  [swap(): return lax.ppermute(value, axis, [(k, k ^ bit) for k in range(size)])]
  transfers between devices with their start and end apart: 12 -> 12, of which waited for: 4 -> 5; matrix products, arithmetic and copies ran while one was open for 0% -> 0% of each run, Pallas kernels for 24% -> 22%
where the time goes in v6:
time: 47.4 us; the launch traced here: 47.2 us
  waiting for transfers between devices  17.6 us (37%)
  starting transfers between devices  16.9 us (36%)
  Pallas kernels  11.9 us (25%)
  between operations  0.77 us (2%)
    ppermute x9, waiting for transfers between devices, swap(): return lax.ppermute(value, axis, [(k, k ^ bit) for k in range(size)])  17.6 us
    ppermute x9, starting transfers between devices, swap(): return lax.ppermute(value, axis, [(k, k ^ bit) for k in range(size)])  12.2 us
    pallas_call x1, Pallas kernels, input_call(): pl.pallas_call(functools.partial(input_kernel, n_table, slots, up_bits, d...  6.01 us
    ppermute x3, starting transfers between devices, shifted(): lax.ppermute(value, 'table', [(k, (k + shift) % n_table) for k in range(n...  4.61 us
    pallas_call x1, Pallas kernels, rows_call(): pl.pallas_call(functools.partial(rows_kernel, slots), in_specs=[VMEM] * n...  3.82 us
  transfers between devices with their start and end apart: 12, of which 5 were waited for; matrix products, arithmetic and copies ran while one was open for 0% of the time, Pallas kernels for 22%

profile of v6, /device:TPU:0, one launch (start us, length us, event | category | flops | bytes accessed | tf_op | source)
XLA Modules:
  0.0 47.2 jit_solution(7127035544565247948)
XLA Ops:
  0.6 0.5 %collective-permute-start.4 = (bf16[128,3456]{1,0:T(8,128)(2,1)}, bf16[128,3456]{1,0:T(8,128)(2,1)S(1)}, u32[]{:S(2)}, u32[]{:S(2)}) collective-permute-start(bf16[128,3456]{1,0:T(8,128)(2,1)} %act.1), channel_id=1, source_target_pairs={{0,1},{1,0},{2,3},{3,2},{4,5},{5,4},{6,7},{7,6},{8,9},{9,8},{10,11... | collective-permute-start | bytes 2654216 | tf_op jit(solution)/shard_map/ppermute | solution.py:567
  1.2 0.1 collective-permute-start.5
  1.2 6.0 %shard_map.119 = (bf16[2,128,128]{2,1,0:T(8,128)(2,1)S(1)}, bf16[2,128,128]{2,1,0:T(8,128)(2,1)}, bf16[128,128]{1,0:T(8,128)(2,1)}, bf16[928,128]{1,0:T(8,128)(2...) custom-call(s32[1]{0:T(128)} %bitcast.table_ref, s32[1]{0:T(128)} %bitcast.1.rep_ref, ...), custom_call_target="tpu_custom_call" | custom-call | flops 905969664 | bytes 5308416 | tf_op jit(solution)/shard_map/pallas_call | solution.py:141
  7.3 0.5 %collective-permute-start.3 = (bf16[2,128,128]{2,1,0:T(8,128)(2,1)}, bf16[2,128,128]{2,1,0:T(8,128)(2,1)S(1)}, u32[]{:S(2)}, u32[]{:S(2)}) collective-permute-start(bf16[2,128,128]{2,1,0:T(8,128)(2,1)} %get-tuple-element.58), channel_id=1, source_target_pairs={{0,1},{1,0},{2,3},{3,2},{4,5},{5,4},{6,7},{7,6},{8,9},{9,8},{10,11... | collective-permute-start | bytes 196616 | tf_op jit(solution)/shard_map/ppermute | solution.py:567
  7.7 1.1 %collective-permute-done.3.other_ref = bf16[2,128,128]{2,1,0:T(8,128)(2,1)S(1)} collective-permute-done((bf16[2,128,128]{2,1,0:T(8,128)(2,1)}, bf16[2,128,128]{2,1,0:T(8,128)(2,1)S(1)}, u32[]{:S(2)}, u32[]{:S(2)}) %collective-permute-start.3) | collective-permute-done | bytes 65568 | tf_op jit(solution)/shard_map/ppermute | solution.py:567
  8.9 0.0 collective-permute-done.4.act_other
  8.9 0.0 collective-permute-done.5.cot_other
  8.9 0.0 copy-start.3
  8.9 0.8 %shard_map.120 = (f32[64,3456]{1,0:T(8,128)S(1)}, bf16[64,3584]{1,0:T(8,128)(2,1)S(1)}, f32[64,3456]{1,0:T(8,128)S(1)}, bf16[64,3456]{1,0:T(8,128)(2,1)S(1)}, f32[32,128]{1,0:T(8,128)S(1)}) custom-call(bf16[2,128,128]{2,1,0:T(8,128)(2,1)S(1)} %get-tuple-element.57.keep_ref, bf16[2,128,128]{2,1,0:T(8,128)(2,1)S(1)} %collective-permute-done.3.other_ref, ...), custom_call_target="tpu_custom_call" | custom-call | flops 452984832 | bytes 6193152 | tf_op jit(solution)/shard_map/pallas_call | solution.py:231
  9.8 2.9 %collective-permute-start.6 = (bf16[64,3584]{1,0:T(8,128)(2,1)S(1)}, bf16[64,3584]{1,0:T(8,128)(2,1)S(1)}, u32[]{:S(2)}, u32[]{:S(2)}) collective-permute-start(bf16[64,3584]{1,0:T(8,128)(2,1)S(1)} %get-tuple-element.60), channel_id=1, source_target_pairs={{0,2},{1,3},{2,0},{3,1},{4,6},{5,7},{6,4},{7,5},{8,10},{9,11},{10,... | collective-permute-start | bytes 1376264 | tf_op jit(solution)/shard_map/ppermute | solution.py:567
  12.7 1.5 %collective-permute-start.7 = (bf16[64,3456]{1,0:T(8,128)(2,1)S(1)}, bf16[64,3456]{1,0:T(8,128)(2,1)S(1)}, u32[]{:S(2)}, u32[]{:S(2)}) collective-permute-start(bf16[64,3456]{1,0:T(8,128)(2,1)S(1)} %get-tuple-element.62), channel_id=1, source_target_pairs={{0,4},{1,5},{2,6},{3,7},{4,0},{5,1},{6,2},{7,3},{8,12},{9,13},{10,... | collective-permute-start | bytes 1327112 | tf_op jit(solution)/shard_map/ppermute | solution.py:567
  14.2 2.6 %collective-permute-start.10 = (bf16[928,128]{1,0:T(8,128)(2,1)}, bf16[928,128]{1,0:T(8,128)(2,1)S(1)}, u32[]{:S(2)}, u32[]{:S(2)}) collective-permute-start(bf16[928,128]{1,0:T(8,128)(2,1)} %get-tuple-element.77), channel_id=1, source_target_pairs={{0,16},{8,24},{16,0},{24,8},{1,17},{9,25},{17,1},{25,9},{2,18},{10... | collective-permute-start | bytes 712712 | tf_op jit(solution)/shard_map/ppermute | solution.py:570
  16.8 1.3 %collective-permute-start.11 = (bf16[928,128]{1,0:T(8,128)(2,1)S(1)}, bf16[928,128]{1,0:T(8,128)(2,1)S(1)}, u32[]{:S(2)}, u32[]{:S(2)}) collective-permute-start(bf16[928,128]{1,0:T(8,128)(2,1)S(1)} %copy-done.5), channel_id=1, source_target_pairs={{0,24},{8,0},{16,8},{24,16},{1,25},{9,1},{17,9},{25,17},{2,26},{10... | collective-permute-start | bytes 712712 | tf_op jit(solution)/shard_map/ppermute | solution.py:570
  18.1 0.7 %collective-permute-start.9 = (bf16[928,128]{1,0:T(8,128)(2,1)S(1)}, bf16[928,128]{1,0:T(8,128)(2,1)S(1)}, u32[]{:S(2)}, u32[]{:S(2)}) collective-permute-start(bf16[928,128]{1,0:T(8,128)(2,1)S(1)} %copy-done.4), channel_id=1, source_target_pairs={{0,8},{8,16},{16,24},{24,0},{1,9},{9,17},{17,25},{25,1},{2,10},{10... | collective-permute-start | bytes 712712 | tf_op jit(solution)/shard_map/ppermute | solution.py:570
  18.8 5.8 %collective-permute-done.7.down_in_ref = bf16[64,3456]{1,0:T(8,128)(2,1)S(1)} collective-permute-done((bf16[64,3456]{1,0:T(8,128)(2,1)S(1)}, bf16[64,3456]{1,0:T(8,128)(2,1)S(1)}, u32[]{:S(2)}, u32[]{:S(2)}) %collective-permute-start.7) | collective-permute-done | bytes 442400 | tf_op jit(solution)/shard_map/ppermute | solution.py:567
  24.6 0.2 shard_map.121
  24.8 0.0 copy-start.2
  24.8 14.4 %conditional.1 = (f32[1,2,32,864]{3,2,1,0:T(8,128)S(1)}, f32[32,128]{1,0:T(8,128)S(1)}, bf16[72,896]{1,0:T(8,128)(2,1)S(1)}) conditional(s32[]{:T(128)} %bitcast.5, () %tuple.17, (bf16[32,3712]{1,0:T(8,128)(2,1)S(1)}, bf16[32,3456]{1,0:T(8,128)(2,1)S(1)}, s32[1]{0:T(128)}, f32[32,3456]{1,0:T(8,128)S(1)}, f32[32,3456]{1,0:T(8,128)S(1)}, ...), branch_computations={%region_0.0_spmd, %region_1.0_spmd} | conditional | bytes 2810000 | solution.py:624
  24.8 1.6 %collective-permute-start = (bf16[32,3712]{1,0:T(8,128)(2,1)S(1)}, bf16[32,3712]{1,0:T(8,128)(2,1)S(1)}, u32[]{:S(2)}, u32[]{:S(2)}) collective-permute-start(bf16[32,3712]{1,0:T(8,128)(2,1)S(1)} %get-tuple-element.14), channel_id=1, source_target_pairs={{0,4},{1,5},{2,6},{3,7},{4,0},{5,1},{6,2},{7,3},{8,12},{9,13},{10,... | collective-permute-start | bytes 712712 | tf_op jit(solution)/shard_map/cond/branch_1_fun/ppermute | solution.py:567
  26.4 0.6 %collective-permute-start.1 = (bf16[32,3456]{1,0:T(8,128)(2,1)S(1)}, bf16[32,3456]{1,0:T(8,128)(2,1)S(1)}, u32[]{:S(2)}, u32[]{:S(2)}) collective-permute-start(bf16[32,3456]{1,0:T(8,128)(2,1)S(1)} %get-tuple-element.16), channel_id=1, source_target_pairs={{0,2},{1,3},{2,0},{3,1},{4,6},{5,7},{6,4},{7,5},{8,10},{9,11},{10,... | collective-permute-start | bytes 663560 | tf_op jit(solution)/shard_map/cond/branch_1_fun/ppermute | solution.py:567
  27.0 5.4 %collective-permute-done.1.down_in_ref = bf16[32,3456]{1,0:T(8,128)(2,1)S(1)} collective-permute-done((bf16[32,3456]{1,0:T(8,128)(2,1)S(1)}, bf16[32,3456]{1,0:T(8,128)(2,1)S(1)}, u32[]{:S(2)}, u32[]{:S(2)}) %collective-permute-start.1) | collective-permute-done | bytes 221216 | tf_op jit(solution)/shard_map/cond/branch_1_fun/ppermute | solution.py:567
  32.5 0.0 collective-permute-done.up_in_ref
  32.5 0.3 branch_1_fun.2
  32.8 1.6 %collective-permute-start.2 = (bf16[136,896]{1,0:T(8,128)(2,1)S(1)}, bf16[136,896]{1,0:T(8,128)(2,1)S(1)}, u32[]{:S(2)}, u32[]{:S(2)}) collective-permute-start(bf16[136,896]{1,0:T(8,128)(2,1)S(1)} %get-tuple-element.19), channel_id=1, source_target_pairs={{0,8},{8,0},{16,24},{24,16},{1,9},{9,1},{17,25},{25,17},{2,10},{10... | collective-permute-start | bytes 731144 | tf_op jit(solution)/shard_map/cond/branch_1_fun/ppermute | solution.py:567
  34.4 4.7 %collective-permute-done.2.in_ref = bf16[136,896]{1,0:T(8,128)(2,1)S(1)} collective-permute-done((bf16[136,896]{1,0:T(8,128)(2,1)S(1)}, bf16[136,896]{1,0:T(8,128)(2,1)S(1)}, u32[]{:S(2)}, u32[]{:S(2)}) %collective-permute-start.2) | collective-permute-done | bytes 243744 | tf_op jit(solution)/shard_map/cond/branch_1_fun/ppermute | solution.py:567
  39.2 0.1 branch_1_fun.3
  39.2 2.9 %collective-permute-start.8 = (bf16[72,896]{1,0:T(8,128)(2,1)S(1)}, bf16[72,896]{1,0:T(8,128)(2,1)S(1)}, u32[]{:S(2)}, u32[]{:S(2)}) collective-permute-start(bf16[72,896]{1,0:T(8,128)(2,1)S(1)} %get-tuple-element.70), channel_id=1, source_target_pairs={{0,16},{8,24},{16,0},{24,8},{1,17},{9,25},{17,1},{25,9},{2,18},{10... | collective-permute-start | bytes 387080 | tf_op jit(solution)/shard_map/ppermute | solution.py:567
  42.1 0.0 collective-permute-done.10.refs_2_
  42.1 0.0 collective-permute-done.11.refs_3_
  42.1 3.8 %shard_map.123 = f32[1,7,512,128]{3,2,1,0:T(8,128)} custom-call(bf16[928,128]{1,0:T(8,128)(2,1)S(1)} %copy-done.2, bf16[928,128]{1,0:T(8,128)(2,1)S(1)} %collective-permute-done.9.refs_1_, bf16[928,128]{1,0:T(8,128)(2,1)S(1)} %collective-permute-done.10.refs_2_, bf16[928,128]{1,0:T(8,128)(2,1)S(1)} %collective-permute-done.11.refs_3_), custom_call_target="tpu_custom_call" | custom-call | flops 469762048 | bytes 1835008 | tf_op jit(solution)/shard_map/pallas_call | solution.py:530
  46.0 0.6 %collective-permute-done.8.in_ref = bf16[72,896]{1,0:T(8,128)(2,1)S(1)} collective-permute-done((bf16[72,896]{1,0:T(8,128)(2,1)S(1)}, bf16[72,896]{1,0:T(8,128)(2,1)S(1)}, u32[]{:S(2)}, u32[]{:S(2)}) %collective-permute-start.8) | collective-permute-done | bytes 129056 | tf_op jit(solution)/shard_map/ppermute | solution.py:567
  46.5 0.7 %shard_map.122 = (f32[32,864]{1,0:T(8,128)}, f32[32,864]{1,0:T(8,128)}, f32[27,128]{1,0:T(8,128)}) custom-call(f32[1,2,32,864]{3,2,1,0:T(8,128)S(1)} %get-tuple-element.69.keep_ref, bf16[72,896]{1,0:T(8,128)(2,1)S(1)} %collective-permute-done.8.in_ref, f32[32,128]{1,0:T(8,128)S(1)} %get-tuple-element.71.bias_ref), custom_call_target="tpu_custom_call" | custom-call | tf_op jit(solution)/shard_map/pallas_call | solution.py:483
  (12 shorter events, 0.0 us)
Async XLA Ops:
  0.6 8.2 %collective-permute-start.4 = (bf16[128,3456]{1,0:T(8,128)(2,1)}, bf16[128,3456]{1,0:T(8,128)(2,1)S(1)}, u32[]{:S(2)}, u32[]{:S(2)}) collective-permute-start(bf16[128,3456]{1,0:T(8,128)(2,1)} %act.1), channel_id=1, source_target_pairs={{0,1},{1,0},{2,3},{3,2},{4,5},{5,4},{6,7},{7,6},{8,9},{9,8},{10,11... | collective-permute-start | bytes 2654216 | tf_op jit(solution)/shard_map/ppermute | solution.py:567
  1.2 7.7 %collective-permute-start.5 = (bf16[128,3456]{1,0:T(8,128)(2,1)}, bf16[128,3456]{1,0:T(8,128)(2,1)S(1)}, u32[]{:S(2)}, u32[]{:S(2)}) collective-permute-start(bf16[128,3456]{1,0:T(8,128)(2,1)} %cot.1), channel_id=1, source_target_pairs={{0,1},{1,0},{2,3},{3,2},{4,5},{5,4},{6,7},{7,6},{8,9},{9,8},{10,11... | collective-permute-start | bytes 2654216 | tf_op jit(solution)/shard_map/ppermute | solution.py:567
  1.2 7.6 %copy-start = (bf16[128,3456]{1,0:T(8,128)(2,1)S(1)}, bf16[128,3456]{1,0:T(8,128)(2,1)}, u32[]{:S(2)}) copy-start(bf16[128,3456]{1,0:T(8,128)(2,1)} %act.1) | copy-start | bytes 2654212
  1.2 7.6 %copy-start.1 = (bf16[128,3456]{1,0:T(8,128)(2,1)S(1)}, bf16[128,3456]{1,0:T(8,128)(2,1)}, u32[]{:S(2)}) copy-start(bf16[128,3456]{1,0:T(8,128)(2,1)} %cot.1) | copy-start | bytes 2654212
  7.3 1.6 %collective-permute-start.3 = (bf16[2,128,128]{2,1,0:T(8,128)(2,1)}, bf16[2,128,128]{2,1,0:T(8,128)(2,1)S(1)}, u32[]{:S(2)}, u32[]{:S(2)}) collective-permute-start(bf16[2,128,128]{2,1,0:T(8,128)(2,1)} %get-tuple-element.58), channel_id=1, source_target_pairs={{0,1},{1,0},{2,3},{3,2},{4,5},{5,4},{6,7},{7,6},{8,9},{9,8},{10,11... | collective-permute-start | bytes 196616 | tf_op jit(solution)/shard_map/ppermute | solution.py:567
  8.9 7.9 %copy-start.5 = (bf16[928,128]{1,0:T(8,128)(2,1)S(1)}, bf16[928,128]{1,0:T(8,128)(2,1)}, u32[]{:S(2)}) copy-start(bf16[928,128]{1,0:T(8,128)(2,1)} %get-tuple-element.78) | copy-start | bytes 712708
  8.9 9.2 %copy-start.4 = (bf16[928,128]{1,0:T(8,128)(2,1)S(1)}, bf16[928,128]{1,0:T(8,128)(2,1)}, u32[]{:S(2)}) copy-start(bf16[928,128]{1,0:T(8,128)(2,1)} %get-tuple-element.76) | copy-start | bytes 712708
  8.9 9.9 %copy-start.3 = (s32[26]{0:T(128)S(1)}, s32[26]{0:T(128)}, u32[]{:S(2)}) copy-start(s32[26]{0:T(128)} %owner_ref.1) | copy-start | bytes 316
  9.8 14.9 %collective-permute-start.6 = (bf16[64,3584]{1,0:T(8,128)(2,1)S(1)}, bf16[64,3584]{1,0:T(8,128)(2,1)S(1)}, u32[]{:S(2)}, u32[]{:S(2)}) collective-permute-start(bf16[64,3584]{1,0:T(8,128)(2,1)S(1)} %get-tuple-element.60), channel_id=1, source_target_pairs={{0,2},{1,3},{2,0},{3,1},{4,6},{5,7},{6,4},{7,5},{8,10},{9,11},{10,... | collective-permute-start | bytes 1376264 | tf_op jit(solution)/shard_map/ppermute | solution.py:567
  12.7 12.0 %collective-permute-start.7 = (bf16[64,3456]{1,0:T(8,128)(2,1)S(1)}, bf16[64,3456]{1,0:T(8,128)(2,1)S(1)}, u32[]{:S(2)}, u32[]{:S(2)}) collective-permute-start(bf16[64,3456]{1,0:T(8,128)(2,1)S(1)} %get-tuple-element.62), channel_id=1, source_target_pairs={{0,4},{1,5},{2,6},{3,7},{4,0},{5,1},{6,2},{7,3},{8,12},{9,13},{10,... | collective-permute-start | bytes 1327112 | tf_op jit(solution)/shard_map/ppermute | solution.py:567
  14.2 27.9 %collective-permute-start.10 = (bf16[928,128]{1,0:T(8,128)(2,1)}, bf16[928,128]{1,0:T(8,128)(2,1)S(1)}, u32[]{:S(2)}, u32[]{:S(2)}) collective-permute-start(bf16[928,128]{1,0:T(8,128)(2,1)} %get-tuple-element.77), channel_id=1, source_target_pairs={{0,16},{8,24},{16,0},{24,8},{1,17},{9,25},{17,1},{25,9},{2,18},{10... | collective-permute-start | bytes 712712 | tf_op jit(solution)/shard_map/ppermute | solution.py:570
  16.8 25.3 %collective-permute-start.11 = (bf16[928,128]{1,0:T(8,128)(2,1)S(1)}, bf16[928,128]{1,0:T(8,128)(2,1)S(1)}, u32[]{:S(2)}, u32[]{:S(2)}) collective-permute-start(bf16[928,128]{1,0:T(8,128)(2,1)S(1)} %copy-done.5), channel_id=1, source_target_pairs={{0,24},{8,0},{16,8},{24,16},{1,25},{9,1},{17,9},{25,17},{2,26},{10... | collective-permute-start | bytes 712712 | tf_op jit(solution)/shard_map/ppermute | solution.py:570
  18.1 24.0 %collective-permute-start.9 = (bf16[928,128]{1,0:T(8,128)(2,1)S(1)}, bf16[928,128]{1,0:T(8,128)(2,1)S(1)}, u32[]{:S(2)}, u32[]{:S(2)}) collective-permute-start(bf16[928,128]{1,0:T(8,128)(2,1)S(1)} %copy-done.4), channel_id=1, source_target_pairs={{0,8},{8,16},{16,24},{24,0},{1,9},{9,17},{17,25},{25,1},{2,10},{10... | collective-permute-start | bytes 712712 | tf_op jit(solution)/shard_map/ppermute | solution.py:570
  24.8 17.4 %copy-start.2 = (bf16[928,128]{1,0:T(8,128)(2,1)S(1)}, bf16[928,128]{1,0:T(8,128)(2,1)}, u32[]{:S(2)}) copy-start(bf16[928,128]{1,0:T(8,128)(2,1)} %get-tuple-element.79.refs_0_) | copy-start | bytes 712708
  24.8 7.6 %collective-permute-start = (bf16[32,3712]{1,0:T(8,128)(2,1)S(1)}, bf16[32,3712]{1,0:T(8,128)(2,1)S(1)}, u32[]{:S(2)}, u32[]{:S(2)}) collective-permute-start(bf16[32,3712]{1,0:T(8,128)(2,1)S(1)} %get-tuple-element.14), channel_id=1, source_target_pairs={{0,4},{1,5},{2,6},{3,7},{4,0},{5,1},{6,2},{7,3},{8,12},{9,13},{10,... | collective-permute-start | bytes 712712 | tf_op jit(solution)/shard_map/cond/branch_1_fun/ppermute | solution.py:567
  26.4 6.1 %collective-permute-start.1 = (bf16[32,3456]{1,0:T(8,128)(2,1)S(1)}, bf16[32,3456]{1,0:T(8,128)(2,1)S(1)}, u32[]{:S(2)}, u32[]{:S(2)}) collective-permute-start(bf16[32,3456]{1,0:T(8,128)(2,1)S(1)} %get-tuple-element.16), channel_id=1, source_target_pairs={{0,2},{1,3},{2,0},{3,1},{4,6},{5,7},{6,4},{7,5},{8,10},{9,11},{10,... | collective-permute-start | bytes 663560 | tf_op jit(solution)/shard_map/cond/branch_1_fun/ppermute | solution.py:567
  32.8 6.4 %collective-permute-start.2 = (bf16[136,896]{1,0:T(8,128)(2,1)S(1)}, bf16[136,896]{1,0:T(8,128)(2,1)S(1)}, u32[]{:S(2)}, u32[]{:S(2)}) collective-permute-start(bf16[136,896]{1,0:T(8,128)(2,1)S(1)} %get-tuple-element.19), channel_id=1, source_target_pairs={{0,8},{8,0},{16,24},{24,16},{1,9},{9,1},{17,25},{25,17},{2,10},{10... | collective-permute-start | bytes 731144 | tf_op jit(solution)/shard_map/cond/branch_1_fun/ppermute | solution.py:567
  39.2 7.3 %collective-permute-start.8 = (bf16[72,896]{1,0:T(8,128)(2,1)S(1)}, bf16[72,896]{1,0:T(8,128)(2,1)S(1)}, u32[]{:S(2)}, u32[]{:S(2)}) collective-permute-start(bf16[72,896]{1,0:T(8,128)(2,1)S(1)} %get-tuple-element.70), channel_id=1, source_target_pairs={{0,16},{8,24},{16,0},{24,8},{1,17},{9,25},{17,1},{25,9},{2,18},{10... | collective-permute-start | bytes 387080 | tf_op jit(solution)/shard_map/ppermute | solution.py:567

commit v7 on v6

--- a/solution.py
+++ b/solution.py
@@ -35,24 +35,24 @@
 
 
 def order_matrix(rep_index, size, block, bits):
-    out_row = lax.broadcasted_iota(jnp.int32, (size, size), 0)
+    out_row = lax.broadcasted_iota(jnp.int32, (size, 1), 0)
     in_row = lax.broadcasted_iota(jnp.int32, (size, size), 1)
-    source = lax.rem(out_row, block)
-    position = lax.div(out_row, block)
+    source = out_row & (block - 1)
     for place, bit in enumerate(bits):
-        flag = lax.rem(lax.div(position, 1 << (len(bits) - 1 - place)), 2)
-        own = lax.rem(lax.div(rep_index, bit), 2)
-        source = source + jnp.where(flag == own, 0, bit) * block
+        unit = size >> (place + 1)
+        flag = (out_row >> (unit.bit_length() - 1)) & 1
+        own = (rep_index >> (bit.bit_length() - 1)) & 1
+        source = source + (flag ^ own) * (bit * block)
     return (source == in_row).astype(F32).astype(BF16)
 
 
 def input_kernel(
     n_table, slots, up_bits, down_bits, table_ref, rep_ref, owner_ref,
     act_hbm, cot_hbm, down_hbm, up_hbm, bias_ref, ids_ref, length_ref,
-    keep, send_hbm, dense_hbm, *rest,
+    keep, send, dense_ref, *rest,
 ):
     outs = rest[:n_table]
-    act, cot, down, up, send, store, message, id_store, feature_ref, in_sems, out_sems = rest[n_table:]
+    act, cot, down, up, store, id_store, feature_ref, in_sems = rest[n_table:]
     tokens, width = act.shape
     rank = down.shape[0]
     half = rank // 2
@@ -75,20 +75,22 @@
     for place in range(n_table * slots):
         feature_ref[place] = SPARSE_FEATURES
     for feature in range(SPARSE_FEATURES):
-        slot = owner_ref[feature]
-        shift = lax.rem(lax.div(slot, slots) + n_table - table_ref[0], n_table)
-        feature_ref[shift * slots + lax.rem(slot, slots)] = feature
+        feature_ref[owner_ref[feature]] = feature
+    firsts = []
+    for shift in range(n_table):
+        owner = table_ref[0] + shift
+        firsts.append(jnp.where(owner >= n_table, owner - n_table, owner) * slots)
     store[SPARSE_FEATURES + 1] = jnp.zeros(store.shape[1:], BF16)
     id_store[...] = jnp.full(id_store.shape, EMPTY, F32)
     entries = lax.broadcasted_iota(jnp.int32, (BAG, tokens), 0)
     for shift in range(n_table):
         for slot in range(slots):
-            feature = feature_ref[shift * slots + slot]
+            feature = feature_ref[firsts[shift] + slot]
             at = jnp.minimum(feature, SPARSE_FEATURES - 1)
             length = jnp.where(feature < SPARSE_FEATURES, length_ref[pl.ds(at, 1), :], 0)
             ids = jnp.where(entries < length, ids_ref[at] - EMPTY, EMPTY)
             id_store[shift, slot * BAG : (slot + 1) * BAG, :] = ids.astype(F32)
-        message[shift, slots * tokens :, :] = id_store[shift].astype(BF16)
+        outs[shift][slots * tokens :, :] = id_store[shift].astype(BF16)
     hidden = back = None
     for (start, size), copies in zip(pieces, fetched):
         part = slice(start, start + size)
@@ -105,8 +107,6 @@
     keep[0], send[0] = rows[:half], rows[half:]
     rows = lax.dot_general(down_order, back, NT, preferred_element_type=F32).astype(BF16)
     keep[1], send[1] = rows[:half], rows[half:]
-    written = [pltpu.make_async_copy(send, send_hbm, out_sems.at[0])]
-    written[0].start()
     blocks = 3
     for first in range(0, width // EMBED_WIDTH, blocks):
         part = slice(first * EMBED_WIDTH, (first + blocks) * EMBED_WIDTH)
@@ -119,16 +119,11 @@
             bias = bias_ref[place : place + 1, :]
             grad = cot[:, cols].astype(F32) * (1.0 + (mixed[:, mine] + bias)) + tail[:, mine]
             store[place] = grad.astype(BF16)
-    written.append(pltpu.make_async_copy(store.at[0], dense_hbm, out_sems.at[2]))
-    written[-1].start()
+    dense_ref[...] = store[0]
     for shift in range(n_table):
         for slot in range(slots):
             rows = slice(slot * tokens, (slot + 1) * tokens)
-            message[shift, rows, :] = store[feature_ref[shift * slots + slot] + 1]
-        written.append(pltpu.make_async_copy(message.at[shift], outs[shift], out_sems.at[3 + shift]))
-        written[-1].start()
-    for copy in written:
-        copy.wait()
+            outs[shift][rows, :] = store[feature_ref[firsts[shift] + slot] + 1]
 
 
 def input_call(
@@ -141,27 +136,24 @@
     return pl.pallas_call(
         functools.partial(input_kernel, n_table, slots, up_bits, down_bits),
         in_specs=[SMEM, SMEM, SMEM, ANY, ANY, ANY, ANY, VMEM, VMEM, VMEM],
-        out_specs=[VMEM] + [ANY] * (2 + n_table),
+        out_specs=[VMEM] * (3 + n_table),
         out_shape=[
             pltpu.VMEM((2, rank // 2, tokens), BF16),
-            jax.ShapeDtypeStruct((2, rank // 2, tokens), BF16),
+            pltpu.VMEM((2, rank // 2, tokens), BF16),
             jax.ShapeDtypeStruct((tokens, EMBED_WIDTH), BF16),
         ]
-        + [jax.ShapeDtypeStruct((sent, EMBED_WIDTH), BF16)] * n_table,
+        + [pltpu.VMEM((sent, EMBED_WIDTH), BF16)] * n_table,
         scratch_shapes=[
             pltpu.VMEM((tokens, width), BF16),
             pltpu.VMEM((tokens, width), BF16),
             pltpu.VMEM((rank, width), BF16),
             pltpu.VMEM((rank, width), BF16),
-            pltpu.VMEM((2, rank // 2, tokens), BF16),
             pltpu.VMEM((SPARSE_FEATURES + 2, tokens, EMBED_WIDTH), BF16),
-            pltpu.VMEM((n_table, sent, EMBED_WIDTH), BF16),
             pltpu.VMEM((n_table, id_rows, EMBED_WIDTH), F32),
             pltpu.SMEM((n_table * slots,), jnp.int32),
             pltpu.SemaphoreType.DMA((4, len(pieces_of(width)))),
-            pltpu.SemaphoreType.DMA((3 + n_table,)),
-        ],
-        compiler_params=params(60),
+        ],
+        compiler_params=params(58),
         cost_estimate=pl.CostEstimate(
             flops=8 * tokens * rank * width, bytes_accessed=4 * (tokens + rank) * width, transcendentals=0
         ),

time: 47.4 us -> 46.2 us (0.975)
  Pallas kernels: 11.9 us -> 11 us
    pallas_call x1, Pallas kernels: 6.01 us -> 5.08 us  [input_call(): pl.pallas_call(functools.partial(input_kernel, n_table, slots, up_bits, d...]
  transfers between devices with their start and end apart: 12 -> 12, of which waited for: 5 -> 5; matrix products, arithmetic and copies ran while one was open for 0% -> 0% of each run, Pallas kernels for 22% -> 21%
where the time goes in v7:
time: 46.2 us; the launch traced here: 46 us
  waiting for transfers between devices  17.2 us (37%)
  starting transfers between devices  17 us (37%)
  Pallas kernels  11 us (24%)
  between operations  0.74 us (2%)
    ppermute x9, waiting for transfers between devices, swap(): return lax.ppermute(value, axis, [(k, k ^ bit) for k in range(size)])  17.2 us
    ppermute x9, starting transfers between devices, swap(): return lax.ppermute(value, axis, [(k, k ^ bit) for k in range(size)])  12.4 us
    pallas_call x1, Pallas kernels, input_call(): pl.pallas_call(functools.partial(input_kernel, n_table, slots, up_bits, d...  5.08 us
    ppermute x3, starting transfers between devices, shifted(): lax.ppermute(value, 'table', [(k, (k + shift) % n_table) for k in range(n...  4.62 us
    pallas_call x1, Pallas kernels, rows_call(): pl.pallas_call(functools.partial(rows_kernel, slots), in_specs=[VMEM] * n...  3.82 us
  transfers between devices with their start and end apart: 12, of which 5 were waited for; matrix products, arithmetic and copies ran while one was open for 0% of the time, Pallas kernels for 21%

profile of v7, /device:TPU:0, one launch (start us, length us, event | category | flops | bytes accessed | tf_op | source)
XLA Modules:
  0.0 46.0 jit_solution(7518514780663563771)
XLA Ops:
  0.6 0.5 %collective-permute-start.4 = (bf16[128,3456]{1,0:T(8,128)(2,1)}, bf16[128,3456]{1,0:T(8,128)(2,1)S(1)}, u32[]{:S(2)}, u32[]{:S(2)}) collective-permute-start(bf16[128,3456]{1,0:T(8,128)(2,1)} %act.1), channel_id=1, source_target_pairs={{0,1},{1,0},{2,3},{3,2},{4,5},{5,4},{6,7},{7,6},{8,9},{9,8},{10,11... | collective-permute-start | bytes 2654216 | tf_op jit(solution)/shard_map/ppermute | solution.py:559
  1.2 0.1 collective-permute-start.5
  1.2 5.1 %shard_map.119 = (bf16[2,128,128]{2,1,0:T(8,128)(2,1)S(1)}, bf16[2,128,128]{2,1,0:T(8,128)(2,1)S(1)}, bf16[128,128]{1,0:T(8,128)(2,1)}, bf16[928,128]{1,0:T(8,12...) custom-call(s32[1]{0:T(128)} %bitcast.table_ref, ...), custom_call_target="tpu_custom_call" | custom-call | flops 905969664 | bytes 5308416 | tf_op jit(solution)/shard_map/pallas_call | solution.py:136
  6.3 0.5 %collective-permute-start.3 = (bf16[2,128,128]{2,1,0:T(8,128)(2,1)S(1)}, bf16[2,128,128]{2,1,0:T(8,128)(2,1)S(1)}, u32[]{:S(2)}, u32[]{:S(2)}) collective-permute-start(bf16[2,128,128]{2,1,0:T(8,128)(2,1)S(1)} %get-tuple-element.58), channel_id=1, source_target_pairs={{0,1},{1,0},{2,3},{3,2},{4,5},{5,4},{6,7},{7,6},{8,9},{9,8},{10,11... | collective-permute-start | bytes 196616 | tf_op jit(solution)/shard_map/ppermute | solution.py:559
  6.8 0.9 %collective-permute-done.3.other_ref = bf16[2,128,128]{2,1,0:T(8,128)(2,1)S(1)} collective-permute-done((bf16[2,128,128]{2,1,0:T(8,128)(2,1)S(1)}, bf16[2,128,128]{2,1,0:T(8,128)(2,1)S(1)}, u32[]{:S(2)}, u32[]{:S(2)}) %collective-permute-start.3) | collective-permute-done | bytes 65568 | tf_op jit(solution)/shard_map/ppermute | solution.py:559
  7.7 0.0 collective-permute-done.4.act_other
  7.7 0.0 copy-start.2
  7.8 0.8 %shard_map.120 = (f32[64,3456]{1,0:T(8,128)S(1)}, bf16[64,3584]{1,0:T(8,128)(2,1)S(1)}, f32[64,3456]{1,0:T(8,128)S(1)}, bf16[64,3456]{1,0:T(8,128)(2,1)S(1)}, f32[32,128]{1,0:T(8,128)S(1)}) custom-call(bf16[2,128,128]{2,1,0:T(8,128)(2,1)S(1)} %get-tuple-element.57.keep_ref, bf16[2,128,128]{2,1,0:T(8,128)(2,1)S(1)} %collective-permute-done.3.other_ref, ...), custom_call_target="tpu_custom_call" | custom-call | flops 452984832 | bytes 6193152 | tf_op jit(solution)/shard_map/pallas_call | solution.py:223
  8.6 2.9 %collective-permute-start.6 = (bf16[64,3584]{1,0:T(8,128)(2,1)S(1)}, bf16[64,3584]{1,0:T(8,128)(2,1)S(1)}, u32[]{:S(2)}, u32[]{:S(2)}) collective-permute-start(bf16[64,3584]{1,0:T(8,128)(2,1)S(1)} %get-tuple-element.60), channel_id=1, source_target_pairs={{0,2},{1,3},{2,0},{3,1},{4,6},{5,7},{6,4},{7,5},{8,10},{9,11},{10,... | collective-permute-start | bytes 1376264 | tf_op jit(solution)/shard_map/ppermute | solution.py:559
  11.5 1.5 %collective-permute-start.7 = (bf16[64,3456]{1,0:T(8,128)(2,1)S(1)}, bf16[64,3456]{1,0:T(8,128)(2,1)S(1)}, u32[]{:S(2)}, u32[]{:S(2)}) collective-permute-start(bf16[64,3456]{1,0:T(8,128)(2,1)S(1)} %get-tuple-element.62), channel_id=1, source_target_pairs={{0,4},{1,5},{2,6},{3,7},{4,0},{5,1},{6,2},{7,3},{8,12},{9,13},{10,... | collective-permute-start | bytes 1327112 | tf_op jit(solution)/shard_map/ppermute | solution.py:559
  13.0 2.6 %collective-permute-start.10 = (bf16[928,128]{1,0:T(8,128)(2,1)S(1)}, bf16[928,128]{1,0:T(8,128)(2,1)S(1)}, u32[]{:S(2)}, u32[]{:S(2)}) collective-permute-start(bf16[928,128]{1,0:T(8,128)(2,1)S(1)} %get-tuple-element.77), channel_id=1, source_target_pairs={{0,16},{8,24},{16,0},{24,8},{1,17},{9,25},{17,1},{25,9},{2,18},{10... | collective-permute-start | bytes 712712 | tf_op jit(solution)/shard_map/ppermute | solution.py:562
  15.6 1.3 %collective-permute-start.11 = (bf16[928,128]{1,0:T(8,128)(2,1)S(1)}, bf16[928,128]{1,0:T(8,128)(2,1)S(1)}, u32[]{:S(2)}, u32[]{:S(2)}) collective-permute-start(bf16[928,128]{1,0:T(8,128)(2,1)S(1)} %get-tuple-element.78), channel_id=1, source_target_pairs={{0,24},{8,0},{16,8},{24,16},{1,25},{9,1},{17,9},{25,17},{2,26},{10... | collective-permute-start | bytes 712712 | tf_op jit(solution)/shard_map/ppermute | solution.py:562
  17.0 0.7 %collective-permute-start.9 = (bf16[928,128]{1,0:T(8,128)(2,1)S(1)}, bf16[928,128]{1,0:T(8,128)(2,1)S(1)}, u32[]{:S(2)}, u32[]{:S(2)}) collective-permute-start(bf16[928,128]{1,0:T(8,128)(2,1)S(1)} %get-tuple-element.76), channel_id=1, source_target_pairs={{0,8},{8,16},{16,24},{24,0},{1,9},{9,17},{17,25},{25,1},{2,10},{10... | collective-permute-start | bytes 712712 | tf_op jit(solution)/shard_map/ppermute | solution.py:562
  17.7 5.8 %collective-permute-done.7.down_in_ref = bf16[64,3456]{1,0:T(8,128)(2,1)S(1)} collective-permute-done((bf16[64,3456]{1,0:T(8,128)(2,1)S(1)}, bf16[64,3456]{1,0:T(8,128)(2,1)S(1)}, u32[]{:S(2)}, u32[]{:S(2)}) %collective-permute-start.7) | collective-permute-done | bytes 442400 | tf_op jit(solution)/shard_map/ppermute | solution.py:559
  23.5 0.0 collective-permute-done.6.up_in_ref
  23.5 0.2 shard_map.121
  23.6 14.3 %conditional.1 = (f32[1,2,32,864]{3,2,1,0:T(8,128)S(1)}, f32[32,128]{1,0:T(8,128)S(1)}, bf16[72,896]{1,0:T(8,128)(2,1)S(1)}) conditional(s32[]{:T(128)} %bitcast.5, () %tuple.17, (bf16[32,3712]{1,0:T(8,128)(2,1)S(1)}, bf16[32,3456]{1,0:T(8,128)(2,1)S(1)}, s32[1]{0:T(128)}, f32[32,3456]{1,0:T(8,128)S(1)}, f32[32,3456]{1,0:T(8,128)S(1)}, ...), branch_computations={%region_0.0_spmd, %region_1.0_spmd} | conditional | bytes 2810000 | solution.py:616
  23.6 1.6 %collective-permute-start = (bf16[32,3712]{1,0:T(8,128)(2,1)S(1)}, bf16[32,3712]{1,0:T(8,128)(2,1)S(1)}, u32[]{:S(2)}, u32[]{:S(2)}) collective-permute-start(bf16[32,3712]{1,0:T(8,128)(2,1)S(1)} %get-tuple-element.14), channel_id=1, source_target_pairs={{0,4},{1,5},{2,6},{3,7},{4,0},{5,1},{6,2},{7,3},{8,12},{9,13},{10,... | collective-permute-start | bytes 712712 | tf_op jit(solution)/shard_map/cond/branch_1_fun/ppermute | solution.py:559
  25.2 0.6 %collective-permute-start.1 = (bf16[32,3456]{1,0:T(8,128)(2,1)S(1)}, bf16[32,3456]{1,0:T(8,128)(2,1)S(1)}, u32[]{:S(2)}, u32[]{:S(2)}) collective-permute-start(bf16[32,3456]{1,0:T(8,128)(2,1)S(1)} %get-tuple-element.16), channel_id=1, source_target_pairs={{0,2},{1,3},{2,0},{3,1},{4,6},{5,7},{6,4},{7,5},{8,10},{9,11},{10,... | collective-permute-start | bytes 663560 | tf_op jit(solution)/shard_map/cond/branch_1_fun/ppermute | solution.py:559
  25.9 5.4 %collective-permute-done.1.down_in_ref = bf16[32,3456]{1,0:T(8,128)(2,1)S(1)} collective-permute-done((bf16[32,3456]{1,0:T(8,128)(2,1)S(1)}, bf16[32,3456]{1,0:T(8,128)(2,1)S(1)}, u32[]{:S(2)}, u32[]{:S(2)}) %collective-permute-start.1) | collective-permute-done | bytes 221216 | tf_op jit(solution)/shard_map/cond/branch_1_fun/ppermute | solution.py:559
  31.3 0.0 collective-permute-done.up_in_ref
  31.3 0.3 branch_1_fun.2
  31.6 1.6 %collective-permute-start.2 = (bf16[136,896]{1,0:T(8,128)(2,1)S(1)}, bf16[136,896]{1,0:T(8,128)(2,1)S(1)}, u32[]{:S(2)}, u32[]{:S(2)}) collective-permute-start(bf16[136,896]{1,0:T(8,128)(2,1)S(1)} %get-tuple-element.19), channel_id=1, source_target_pairs={{0,8},{8,0},{16,24},{24,16},{1,9},{9,1},{17,25},{25,17},{2,10},{10... | collective-permute-start | bytes 731144 | tf_op jit(solution)/shard_map/cond/branch_1_fun/ppermute | solution.py:559
  33.3 4.6 %collective-permute-done.2.in_ref = bf16[136,896]{1,0:T(8,128)(2,1)S(1)} collective-permute-done((bf16[136,896]{1,0:T(8,128)(2,1)S(1)}, bf16[136,896]{1,0:T(8,128)(2,1)S(1)}, u32[]{:S(2)}, u32[]{:S(2)}) %collective-permute-start.2) | collective-permute-done | bytes 243744 | tf_op jit(solution)/shard_map/cond/branch_1_fun/ppermute | solution.py:559
  37.9 0.1 branch_1_fun.3
  38.0 3.0 %collective-permute-start.8 = (bf16[72,896]{1,0:T(8,128)(2,1)S(1)}, bf16[72,896]{1,0:T(8,128)(2,1)S(1)}, u32[]{:S(2)}, u32[]{:S(2)}) collective-permute-start(bf16[72,896]{1,0:T(8,128)(2,1)S(1)} %get-tuple-element.70), channel_id=1, source_target_pairs={{0,16},{8,24},{16,0},{24,8},{1,17},{9,25},{17,1},{25,9},{2,18},{10... | collective-permute-start | bytes 387080 | tf_op jit(solution)/shard_map/ppermute | solution.py:559
  41.0 0.0 collective-permute-done.10.refs_2_
  41.0 0.0 collective-permute-done.11.refs_3_
  41.0 0.0 collective-permute-done.9.refs_1_
  41.0 3.8 %shard_map.123 = f32[1,7,512,128]{3,2,1,0:T(8,128)} custom-call(bf16[928,128]{1,0:T(8,128)(2,1)S(1)} %get-tuple-element.79.refs_0_, bf16[928,128]{1,0:T(8,128)(2,1)S(1)} %collective-permute-done.9.refs_1_, bf16[928,128]{1,0:T(8,128)(2,1)S(1)} %collective-permute-done.10.refs_2_, bf16[928,128]{1,0:T(8,128)(2,1)S(1)} %collective-permute-done.11.refs_3_), custom_call_target="tpu_custom_call" | custom-call | flops 469762048 | bytes 1835008 | tf_op jit(solution)/shard_map/pallas_call | solution.py:522
  44.8 0.5 %collective-permute-done.8.in_ref = bf16[72,896]{1,0:T(8,128)(2,1)S(1)} collective-permute-done((bf16[72,896]{1,0:T(8,128)(2,1)S(1)}, bf16[72,896]{1,0:T(8,128)(2,1)S(1)}, u32[]{:S(2)}, u32[]{:S(2)}) %collective-permute-start.8) | collective-permute-done | bytes 129056 | tf_op jit(solution)/shard_map/ppermute | solution.py:559
  45.3 0.7 %shard_map.122 = (f32[32,864]{1,0:T(8,128)}, f32[32,864]{1,0:T(8,128)}, f32[27,128]{1,0:T(8,128)}) custom-call(f32[1,2,32,864]{3,2,1,0:T(8,128)S(1)} %get-tuple-element.69.keep_ref, bf16[72,896]{1,0:T(8,128)(2,1)S(1)} %collective-permute-done.8.in_ref, f32[32,128]{1,0:T(8,128)S(1)} %get-tuple-element.71.bias_ref), custom_call_target="tpu_custom_call" | custom-call | tf_op jit(solution)/shard_map/pallas_call | solution.py:475
  (6 shorter events, 0.0 us)
Async XLA Ops:
  0.6 7.1 %collective-permute-start.4 = (bf16[128,3456]{1,0:T(8,128)(2,1)}, bf16[128,3456]{1,0:T(8,128)(2,1)S(1)}, u32[]{:S(2)}, u32[]{:S(2)}) collective-permute-start(bf16[128,3456]{1,0:T(8,128)(2,1)} %act.1), channel_id=1, source_target_pairs={{0,1},{1,0},{2,3},{3,2},{4,5},{5,4},{6,7},{7,6},{8,9},{9,8},{10,11... | collective-permute-start | bytes 2654216 | tf_op jit(solution)/shard_map/ppermute | solution.py:559
  1.2 6.6 %collective-permute-start.5 = (bf16[128,3456]{1,0:T(8,128)(2,1)}, bf16[128,3456]{1,0:T(8,128)(2,1)S(1)}, u32[]{:S(2)}, u32[]{:S(2)}) collective-permute-start(bf16[128,3456]{1,0:T(8,128)(2,1)} %cot.1), channel_id=1, source_target_pairs={{0,1},{1,0},{2,3},{3,2},{4,5},{5,4},{6,7},{7,6},{8,9},{9,8},{10,11... | collective-permute-start | bytes 2654216 | tf_op jit(solution)/shard_map/ppermute | solution.py:559
  1.2 6.5 %copy-start = (bf16[128,3456]{1,0:T(8,128)(2,1)S(1)}, bf16[128,3456]{1,0:T(8,128)(2,1)}, u32[]{:S(2)}) copy-start(bf16[128,3456]{1,0:T(8,128)(2,1)} %act.1) | copy-start | bytes 2654212
  1.2 6.5 %copy-start.1 = (bf16[128,3456]{1,0:T(8,128)(2,1)S(1)}, bf16[128,3456]{1,0:T(8,128)(2,1)}, u32[]{:S(2)}) copy-start(bf16[128,3456]{1,0:T(8,128)(2,1)} %cot.1) | copy-start | bytes 2654212
  6.3 1.4 %collective-permute-start.3 = (bf16[2,128,128]{2,1,0:T(8,128)(2,1)S(1)}, bf16[2,128,128]{2,1,0:T(8,128)(2,1)S(1)}, u32[]{:S(2)}, u32[]{:S(2)}) collective-permute-start(bf16[2,128,128]{2,1,0:T(8,128)(2,1)S(1)} %get-tuple-element.58), channel_id=1, source_target_pairs={{0,1},{1,0},{2,3},{3,2},{4,5},{5,4},{6,7},{7,6},{8,9},{9,8},{10,11... | collective-permute-start | bytes 196616 | tf_op jit(solution)/shard_map/ppermute | solution.py:559
  7.7 9.9 %copy-start.2 = (s32[26]{0:T(128)S(1)}, s32[26]{0:T(128)}, u32[]{:S(2)}) copy-start(s32[26]{0:T(128)} %owner_ref.1) | copy-start | bytes 316
  8.6 14.9 %collective-permute-start.6 = (bf16[64,3584]{1,0:T(8,128)(2,1)S(1)}, bf16[64,3584]{1,0:T(8,128)(2,1)S(1)}, u32[]{:S(2)}, u32[]{:S(2)}) collective-permute-start(bf16[64,3584]{1,0:T(8,128)(2,1)S(1)} %get-tuple-element.60), channel_id=1, source_target_pairs={{0,2},{1,3},{2,0},{3,1},{4,6},{5,7},{6,4},{7,5},{8,10},{9,11},{10,... | collective-permute-start | bytes 1376264 | tf_op jit(solution)/shard_map/ppermute | solution.py:559
  11.5 11.9 %collective-permute-start.7 = (bf16[64,3456]{1,0:T(8,128)(2,1)S(1)}, bf16[64,3456]{1,0:T(8,128)(2,1)S(1)}, u32[]{:S(2)}, u32[]{:S(2)}) collective-permute-start(bf16[64,3456]{1,0:T(8,128)(2,1)S(1)} %get-tuple-element.62), channel_id=1, source_target_pairs={{0,4},{1,5},{2,6},{3,7},{4,0},{5,1},{6,2},{7,3},{8,12},{9,13},{10,... | collective-permute-start | bytes 1327112 | tf_op jit(solution)/shard_map/ppermute | solution.py:559
  13.0 27.9 %collective-permute-start.10 = (bf16[928,128]{1,0:T(8,128)(2,1)S(1)}, bf16[928,128]{1,0:T(8,128)(2,1)S(1)}, u32[]{:S(2)}, u32[]{:S(2)}) collective-permute-start(bf16[928,128]{1,0:T(8,128)(2,1)S(1)} %get-tuple-element.77), channel_id=1, source_target_pairs={{0,16},{8,24},{16,0},{24,8},{1,17},{9,25},{17,1},{25,9},{2,18},{10... | collective-permute-start | bytes 712712 | tf_op jit(solution)/shard_map/ppermute | solution.py:562
  15.6 25.3 %collective-permute-start.11 = (bf16[928,128]{1,0:T(8,128)(2,1)S(1)}, bf16[928,128]{1,0:T(8,128)(2,1)S(1)}, u32[]{:S(2)}, u32[]{:S(2)}) collective-permute-start(bf16[928,128]{1,0:T(8,128)(2,1)S(1)} %get-tuple-element.78), channel_id=1, source_target_pairs={{0,24},{8,0},{16,8},{24,16},{1,25},{9,1},{17,9},{25,17},{2,26},{10... | collective-permute-start | bytes 712712 | tf_op jit(solution)/shard_map/ppermute | solution.py:562
  17.0 24.0 %collective-permute-start.9 = (bf16[928,128]{1,0:T(8,128)(2,1)S(1)}, bf16[928,128]{1,0:T(8,128)(2,1)S(1)}, u32[]{:S(2)}, u32[]{:S(2)}) collective-permute-start(bf16[928,128]{1,0:T(8,128)(2,1)S(1)} %get-tuple-element.76), channel_id=1, source_target_pairs={{0,8},{8,16},{16,24},{24,0},{1,9},{9,17},{17,25},{25,1},{2,10},{10... | collective-permute-start | bytes 712712 | tf_op jit(solution)/shard_map/ppermute | solution.py:562
  23.6 7.7 %collective-permute-start = (bf16[32,3712]{1,0:T(8,128)(2,1)S(1)}, bf16[32,3712]{1,0:T(8,128)(2,1)S(1)}, u32[]{:S(2)}, u32[]{:S(2)}) collective-permute-start(bf16[32,3712]{1,0:T(8,128)(2,1)S(1)} %get-tuple-element.14), channel_id=1, source_target_pairs={{0,4},{1,5},{2,6},{3,7},{4,0},{5,1},{6,2},{7,3},{8,12},{9,13},{10,... | collective-permute-start | bytes 712712 | tf_op jit(solution)/shard_map/cond/branch_1_fun/ppermute | solution.py:559
  25.2 6.1 %collective-permute-start.1 = (bf16[32,3456]{1,0:T(8,128)(2,1)S(1)}, bf16[32,3456]{1,0:T(8,128)(2,1)S(1)}, u32[]{:S(2)}, u32[]{:S(2)}) collective-permute-start(bf16[32,3456]{1,0:T(8,128)(2,1)S(1)} %get-tuple-element.16), channel_id=1, source_target_pairs={{0,2},{1,3},{2,0},{3,1},{4,6},{5,7},{6,4},{7,5},{8,10},{9,11},{10,... | collective-permute-start | bytes 663560 | tf_op jit(solution)/shard_map/cond/branch_1_fun/ppermute | solution.py:559
  31.6 6.2 %collective-permute-start.2 = (bf16[136,896]{1,0:T(8,128)(2,1)S(1)}, bf16[136,896]{1,0:T(8,128)(2,1)S(1)}, u32[]{:S(2)}, u32[]{:S(2)}) collective-permute-start(bf16[136,896]{1,0:T(8,128)(2,1)S(1)} %get-tuple-element.19), channel_id=1, source_target_pairs={{0,8},{8,0},{16,24},{24,16},{1,9},{9,1},{17,25},{25,17},{2,10},{10... | collective-permute-start | bytes 731144 | tf_op jit(solution)/shard_map/cond/branch_1_fun/ppermute | solution.py:559
  38.0 7.3 %collective-permute-start.8 = (bf16[72,896]{1,0:T(8,128)(2,1)S(1)}, bf16[72,896]{1,0:T(8,128)(2,1)S(1)}, u32[]{:S(2)}, u32[]{:S(2)}) collective-permute-start(bf16[72,896]{1,0:T(8,128)(2,1)S(1)} %get-tuple-element.70), channel_id=1, source_target_pairs={{0,16},{8,24},{16,0},{24,8},{1,17},{9,25},{17,1},{25,9},{2,18},{10... | collective-permute-start | bytes 387080 | tf_op jit(solution)/shard_map/ppermute | solution.py:559

commit v8 on v7

--- a/solution.py
+++ b/solution.py
@@ -49,10 +49,10 @@
 def input_kernel(
     n_table, slots, up_bits, down_bits, table_ref, rep_ref, owner_ref,
     act_hbm, cot_hbm, down_hbm, up_hbm, bias_ref, ids_ref, length_ref,
-    keep, send, dense_ref, *rest,
+    act, cot, keep, send, dense_ref, *rest,
 ):
     outs = rest[:n_table]
-    act, cot, down, up, store, id_store, feature_ref, in_sems = rest[n_table:]
+    down, up, store, id_store, feature_ref, in_sems = rest[n_table:]
     tokens, width = act.shape
     rank = down.shape[0]
     half = rank // 2
@@ -136,16 +136,16 @@
     return pl.pallas_call(
         functools.partial(input_kernel, n_table, slots, up_bits, down_bits),
         in_specs=[SMEM, SMEM, SMEM, ANY, ANY, ANY, ANY, VMEM, VMEM, VMEM],
-        out_specs=[VMEM] * (3 + n_table),
-        out_shape=[
+        out_specs=[VMEM] * (5 + n_table),
+        out_shape=[
+            pltpu.VMEM((tokens, width), BF16),
+            pltpu.VMEM((tokens, width), BF16),
             pltpu.VMEM((2, rank // 2, tokens), BF16),
             pltpu.VMEM((2, rank // 2, tokens), BF16),
             jax.ShapeDtypeStruct((tokens, EMBED_WIDTH), BF16),
         ]
         + [pltpu.VMEM((sent, EMBED_WIDTH), BF16)] * n_table,
         scratch_shapes=[
-            pltpu.VMEM((tokens, width), BF16),
-            pltpu.VMEM((tokens, width), BF16),
             pltpu.VMEM((rank, width), BF16),
             pltpu.VMEM((rank, width), BF16),
             pltpu.VMEM((SPARSE_FEATURES + 2, tokens, EMBED_WIDTH), BF16),
@@ -153,7 +153,7 @@
             pltpu.SMEM((n_table * slots,), jnp.int32),
             pltpu.SemaphoreType.DMA((4, len(pieces_of(width)))),
         ],
-        compiler_params=params(58),
+        compiler_params=params(57),
         cost_estimate=pl.CostEstimate(
             flops=8 * tokens * rank * width, bytes_accessed=4 * (tokens + rank) * width, transcendentals=0
         ),
@@ -563,7 +563,7 @@
 
     act_other = swap(activations, "rep", 1)
     cot_other = swap(cotangent, "rep", 1)
-    keep, send, dense_grad, *parts = input_call(
+    act, cot, keep, send, dense_grad, *parts = input_call(
         table_index, rep_index, feature_table_slot, activations, cotangent, down_weight, up_weight,
         bias.reshape(-1, EMBED_WIDTH), jnp.transpose(bag_ids, (1, 2, 0)), jnp.transpose(bag_lengths, (1, 0)),
         n_table, slots, up_bits, down_bits,
@@ -571,7 +571,7 @@
     other = swap(send, "rep", 1)
     parts = [parts[0]] + [shifted(parts[k], k) for k in range(1, n_table)]
     up_keep, up_send, down_keep, down_send, bias_sum = terms_call(
-        keep, other, activations, cotangent, act_other, cot_other, ride
+        keep, other, act, cot, act_other, cot_other, ride
     )
     def exchange(place, up_send, down_send, bias_sum):
         up_in = swap(up_send, "rep", up_bits[place])

time: 46.2 us -> 46 us (level)
  transfers between devices with their start and end apart: 12 -> 12, of which waited for: 5 -> 5; matrix products, arithmetic and copies ran while one was open for 0% -> 0% of each run, Pallas kernels for 21% -> 20%
where the time goes in v8:
time: 46 us; the launch traced here: 45.8 us
  waiting for transfers between devices  17.2 us (37%)
  starting transfers between devices  17 us (37%)
  Pallas kernels  10.9 us (24%)
  between operations  0.72 us (2%)
    ppermute x9, waiting for transfers between devices, swap(): return lax.ppermute(value, axis, [(k, k ^ bit) for k in range(size)])  17.2 us
    ppermute x9, starting transfers between devices, swap(): return lax.ppermute(value, axis, [(k, k ^ bit) for k in range(size)])  12.4 us
    pallas_call x1, Pallas kernels, input_call(): pl.pallas_call(functools.partial(input_kernel, n_table, slots, up_bits, d...  4.96 us
    ppermute x3, starting transfers between devices, shifted(): lax.ppermute(value, 'table', [(k, (k + shift) % n_table) for k in range(n...  4.61 us
    pallas_call x1, Pallas kernels, rows_call(): pl.pallas_call(functools.partial(rows_kernel, slots), in_specs=[VMEM] * n...  3.82 us
  transfers between devices with their start and end apart: 12, of which 5 were waited for; matrix products, arithmetic and copies ran while one was open for 0% of the time, Pallas kernels for 20%

profile of v8, /device:TPU:0, one launch (start us, length us, event | category | flops | bytes accessed | tf_op | source)
XLA Modules:
  0.0 45.8 jit_solution(13649587346722478867)
XLA Ops:
  0.6 0.5 %collective-permute-start.4 = (bf16[128,3456]{1,0:T(8,128)(2,1)}, bf16[128,3456]{1,0:T(8,128)(2,1)S(1)}, u32[]{:S(2)}, u32[]{:S(2)}) collective-permute-start(bf16[128,3456]{1,0:T(8,128)(2,1)} %act_hbm.1), channel_id=1, source_target_pairs={{0,1},{1,0},{2,3},{3,2},{4,5},{5,4},{6,7},{7,6},{8,9},{9,8},{10,11... | collective-permute-start | bytes 2654216 | tf_op jit(solution)/shard_map/ppermute | solution.py:559
  1.2 0.1 collective-permute-start.5
  1.2 5.0 %shard_map.119 = (bf16[128,3456]{1,0:T(8,128)(2,1)S(1)}, bf16[128,3456]{1,0:T(8,128)(2,1)S(1)}, bf16[2,128,128]{2,1,0:T(8,128)(2,1)S(1)}, bf16[2,128,128]{2,1,0:...) custom-call(s32[1]{0:T(128)} %bitcast.table_ref, ...), custom_call_target="tpu_custom_call" | custom-call | flops 905969664 | bytes 5308416 | tf_op jit(solution)/shard_map/pallas_call | solution.py:136
  6.2 0.5 %collective-permute-start.3 = (bf16[2,128,128]{2,1,0:T(8,128)(2,1)S(1)}, bf16[2,128,128]{2,1,0:T(8,128)(2,1)S(1)}, u32[]{:S(2)}, u32[]{:S(2)}) collective-permute-start(bf16[2,128,128]{2,1,0:T(8,128)(2,1)S(1)} %get-tuple-element.60), channel_id=1, source_target_pairs={{0,1},{1,0},{2,3},{3,2},{4,5},{5,4},{6,7},{7,6},{8,9},{9,8},{10,11... | collective-permute-start | bytes 196616 | tf_op jit(solution)/shard_map/ppermute | solution.py:559
  6.7 0.9 %collective-permute-done.3.other_ref = bf16[2,128,128]{2,1,0:T(8,128)(2,1)S(1)} collective-permute-done((bf16[2,128,128]{2,1,0:T(8,128)(2,1)S(1)}, bf16[2,128,128]{2,1,0:T(8,128)(2,1)S(1)}, u32[]{:S(2)}, u32[]{:S(2)}) %collective-permute-start.3) | collective-permute-done | bytes 65568 | tf_op jit(solution)/shard_map/ppermute | solution.py:559
  7.6 0.0 collective-permute-done.4.act_other
  7.6 0.0 collective-permute-done.5.cot_other
  7.6 0.8 %shard_map.120 = (f32[64,3456]{1,0:T(8,128)S(1)}, bf16[64,3584]{1,0:T(8,128)(2,1)S(1)}, f32[64,3456]{1,0:T(8,128)S(1)}, bf16[64,3456]{1,0:T(8,128)(2,1)S(1)}, f32[32,128]{1,0:T(8,128)S(1)}) custom-call(bf16[2,128,128]{2,1,0:T(8,128)(2,1)S(1)} %get-tuple-element.59.keep_ref, bf16[2,128,128]{2,1,0:T(8,128)(2,1)S(1)} %collective-permute-done.3.other_ref, ...), custom_call_target="tpu_custom_call" | custom-call | flops 452984832 | bytes 6193152 | tf_op jit(solution)/shard_map/pallas_call | solution.py:223
  8.4 2.9 %collective-permute-start.6 = (bf16[64,3584]{1,0:T(8,128)(2,1)S(1)}, bf16[64,3584]{1,0:T(8,128)(2,1)S(1)}, u32[]{:S(2)}, u32[]{:S(2)}) collective-permute-start(bf16[64,3584]{1,0:T(8,128)(2,1)S(1)} %get-tuple-element.64), channel_id=1, source_target_pairs={{0,2},{1,3},{2,0},{3,1},{4,6},{5,7},{6,4},{7,5},{8,10},{9,11},{10,... | collective-permute-start | bytes 1376264 | tf_op jit(solution)/shard_map/ppermute | solution.py:559
  11.4 1.5 %collective-permute-start.7 = (bf16[64,3456]{1,0:T(8,128)(2,1)S(1)}, bf16[64,3456]{1,0:T(8,128)(2,1)S(1)}, u32[]{:S(2)}, u32[]{:S(2)}) collective-permute-start(bf16[64,3456]{1,0:T(8,128)(2,1)S(1)} %get-tuple-element.66), channel_id=1, source_target_pairs={{0,4},{1,5},{2,6},{3,7},{4,0},{5,1},{6,2},{7,3},{8,12},{9,13},{10,... | collective-permute-start | bytes 1327112 | tf_op jit(solution)/shard_map/ppermute | solution.py:559
  12.9 2.6 %collective-permute-start.10 = (bf16[928,128]{1,0:T(8,128)(2,1)S(1)}, bf16[928,128]{1,0:T(8,128)(2,1)S(1)}, u32[]{:S(2)}, u32[]{:S(2)}) collective-permute-start(bf16[928,128]{1,0:T(8,128)(2,1)S(1)} %get-tuple-element.81), channel_id=1, source_target_pairs={{0,16},{8,24},{16,0},{24,8},{1,17},{9,25},{17,1},{25,9},{2,18},{10... | collective-permute-start | bytes 712712 | tf_op jit(solution)/shard_map/ppermute | solution.py:562
  15.5 1.3 %collective-permute-start.11 = (bf16[928,128]{1,0:T(8,128)(2,1)S(1)}, bf16[928,128]{1,0:T(8,128)(2,1)S(1)}, u32[]{:S(2)}, u32[]{:S(2)}) collective-permute-start(bf16[928,128]{1,0:T(8,128)(2,1)S(1)} %get-tuple-element.82), channel_id=1, source_target_pairs={{0,24},{8,0},{16,8},{24,16},{1,25},{9,1},{17,9},{25,17},{2,26},{10... | collective-permute-start | bytes 712712 | tf_op jit(solution)/shard_map/ppermute | solution.py:562
  16.8 0.7 %collective-permute-start.9 = (bf16[928,128]{1,0:T(8,128)(2,1)S(1)}, bf16[928,128]{1,0:T(8,128)(2,1)S(1)}, u32[]{:S(2)}, u32[]{:S(2)}) collective-permute-start(bf16[928,128]{1,0:T(8,128)(2,1)S(1)} %get-tuple-element.80), channel_id=1, source_target_pairs={{0,8},{8,16},{16,24},{24,0},{1,9},{9,17},{17,25},{25,1},{2,10},{10... | collective-permute-start | bytes 712712 | tf_op jit(solution)/shard_map/ppermute | solution.py:562
  17.5 5.8 %collective-permute-done.7.down_in_ref = bf16[64,3456]{1,0:T(8,128)(2,1)S(1)} collective-permute-done((bf16[64,3456]{1,0:T(8,128)(2,1)S(1)}, bf16[64,3456]{1,0:T(8,128)(2,1)S(1)}, u32[]{:S(2)}, u32[]{:S(2)}) %collective-permute-start.7) | collective-permute-done | bytes 442400 | tf_op jit(solution)/shard_map/ppermute | solution.py:559
  23.3 0.0 collective-permute-done.6.up_in_ref
  23.3 0.2 shard_map.121
  23.5 14.3 %conditional.1 = (f32[1,2,32,864]{3,2,1,0:T(8,128)S(1)}, f32[32,128]{1,0:T(8,128)S(1)}, bf16[72,896]{1,0:T(8,128)(2,1)S(1)}) conditional(s32[]{:T(128)} %bitcast.5, () %tuple.17, (bf16[32,3712]{1,0:T(8,128)(2,1)S(1)}, bf16[32,3456]{1,0:T(8,128)(2,1)S(1)}, s32[1]{0:T(128)}, f32[32,3456]{1,0:T(8,128)S(1)}, f32[32,3456]{1,0:T(8,128)S(1)}, ...), branch_computations={%region_0.0_spmd, %region_1.0_spmd} | conditional | bytes 2810000 | solution.py:616
  23.5 1.6 %collective-permute-start = (bf16[32,3712]{1,0:T(8,128)(2,1)S(1)}, bf16[32,3712]{1,0:T(8,128)(2,1)S(1)}, u32[]{:S(2)}, u32[]{:S(2)}) collective-permute-start(bf16[32,3712]{1,0:T(8,128)(2,1)S(1)} %get-tuple-element.14), channel_id=1, source_target_pairs={{0,4},{1,5},{2,6},{3,7},{4,0},{5,1},{6,2},{7,3},{8,12},{9,13},{10,... | collective-permute-start | bytes 712712 | tf_op jit(solution)/shard_map/cond/branch_1_fun/ppermute | solution.py:559
  25.1 0.6 %collective-permute-start.1 = (bf16[32,3456]{1,0:T(8,128)(2,1)S(1)}, bf16[32,3456]{1,0:T(8,128)(2,1)S(1)}, u32[]{:S(2)}, u32[]{:S(2)}) collective-permute-start(bf16[32,3456]{1,0:T(8,128)(2,1)S(1)} %get-tuple-element.16), channel_id=1, source_target_pairs={{0,2},{1,3},{2,0},{3,1},{4,6},{5,7},{6,4},{7,5},{8,10},{9,11},{10,... | collective-permute-start | bytes 663560 | tf_op jit(solution)/shard_map/cond/branch_1_fun/ppermute | solution.py:559
  25.7 5.4 %collective-permute-done.1.down_in_ref = bf16[32,3456]{1,0:T(8,128)(2,1)S(1)} collective-permute-done((bf16[32,3456]{1,0:T(8,128)(2,1)S(1)}, bf16[32,3456]{1,0:T(8,128)(2,1)S(1)}, u32[]{:S(2)}, u32[]{:S(2)}) %collective-permute-start.1) | collective-permute-done | bytes 221216 | tf_op jit(solution)/shard_map/cond/branch_1_fun/ppermute | solution.py:559
  31.1 0.0 collective-permute-done.up_in_ref
  31.1 0.3 branch_1_fun.2
  31.5 1.6 %collective-permute-start.2 = (bf16[136,896]{1,0:T(8,128)(2,1)S(1)}, bf16[136,896]{1,0:T(8,128)(2,1)S(1)}, u32[]{:S(2)}, u32[]{:S(2)}) collective-permute-start(bf16[136,896]{1,0:T(8,128)(2,1)S(1)} %get-tuple-element.19), channel_id=1, source_target_pairs={{0,8},{8,0},{16,24},{24,16},{1,9},{9,1},{17,25},{25,17},{2,10},{10... | collective-permute-start | bytes 731144 | tf_op jit(solution)/shard_map/cond/branch_1_fun/ppermute | solution.py:559
  33.1 4.6 %collective-permute-done.2.in_ref = bf16[136,896]{1,0:T(8,128)(2,1)S(1)} collective-permute-done((bf16[136,896]{1,0:T(8,128)(2,1)S(1)}, bf16[136,896]{1,0:T(8,128)(2,1)S(1)}, u32[]{:S(2)}, u32[]{:S(2)}) %collective-permute-start.2) | collective-permute-done | bytes 243744 | tf_op jit(solution)/shard_map/cond/branch_1_fun/ppermute | solution.py:559
  37.7 0.1 branch_1_fun.3
  37.8 3.0 %collective-permute-start.8 = (bf16[72,896]{1,0:T(8,128)(2,1)S(1)}, bf16[72,896]{1,0:T(8,128)(2,1)S(1)}, u32[]{:S(2)}, u32[]{:S(2)}) collective-permute-start(bf16[72,896]{1,0:T(8,128)(2,1)S(1)} %get-tuple-element.74), channel_id=1, source_target_pairs={{0,16},{8,24},{16,0},{24,8},{1,17},{9,25},{17,1},{25,9},{2,18},{10... | collective-permute-start | bytes 387080 | tf_op jit(solution)/shard_map/ppermute | solution.py:559
  40.8 0.0 collective-permute-done.10.refs_2_
  40.8 0.0 collective-permute-done.11.refs_3_
  40.8 0.0 collective-permute-done.9.refs_1_
  40.8 3.8 %shard_map.123 = f32[1,7,512,128]{3,2,1,0:T(8,128)} custom-call(bf16[928,128]{1,0:T(8,128)(2,1)S(1)} %get-tuple-element.83.refs_0_, bf16[928,128]{1,0:T(8,128)(2,1)S(1)} %collective-permute-done.9.refs_1_, bf16[928,128]{1,0:T(8,128)(2,1)S(1)} %collective-permute-done.10.refs_2_, bf16[928,128]{1,0:T(8,128)(2,1)S(1)} %collective-permute-done.11.refs_3_), custom_call_target="tpu_custom_call" | custom-call | flops 469762048 | bytes 1835008 | tf_op jit(solution)/shard_map/pallas_call | solution.py:522
  44.6 0.5 %collective-permute-done.8.in_ref = bf16[72,896]{1,0:T(8,128)(2,1)S(1)} collective-permute-done((bf16[72,896]{1,0:T(8,128)(2,1)S(1)}, bf16[72,896]{1,0:T(8,128)(2,1)S(1)}, u32[]{:S(2)}, u32[]{:S(2)}) %collective-permute-start.8) | collective-permute-done | bytes 129056 | tf_op jit(solution)/shard_map/ppermute | solution.py:559
  45.1 0.7 %shard_map.122 = (f32[32,864]{1,0:T(8,128)}, f32[32,864]{1,0:T(8,128)}, f32[27,128]{1,0:T(8,128)}) custom-call(f32[1,2,32,864]{3,2,1,0:T(8,128)S(1)} %get-tuple-element.73.keep_ref, bf16[72,896]{1,0:T(8,128)(2,1)S(1)} %collective-permute-done.8.in_ref, f32[32,128]{1,0:T(8,128)S(1)} %get-tuple-element.75.bias_ref), custom_call_target="tpu_custom_call" | custom-call | tf_op jit(solution)/shard_map/pallas_call | solution.py:475
  (2 shorter events, 0.0 us)
Async XLA Ops:
  0.6 7.0 %collective-permute-start.4 = (bf16[128,3456]{1,0:T(8,128)(2,1)}, bf16[128,3456]{1,0:T(8,128)(2,1)S(1)}, u32[]{:S(2)}, u32[]{:S(2)}) collective-permute-start(bf16[128,3456]{1,0:T(8,128)(2,1)} %act_hbm.1), channel_id=1, source_target_pairs={{0,1},{1,0},{2,3},{3,2},{4,5},{5,4},{6,7},{7,6},{8,9},{9,8},{10,11... | collective-permute-start | bytes 2654216 | tf_op jit(solution)/shard_map/ppermute | solution.py:559
  1.2 6.4 %collective-permute-start.5 = (bf16[128,3456]{1,0:T(8,128)(2,1)}, bf16[128,3456]{1,0:T(8,128)(2,1)S(1)}, u32[]{:S(2)}, u32[]{:S(2)}) collective-permute-start(bf16[128,3456]{1,0:T(8,128)(2,1)} %cot_hbm.1), channel_id=1, source_target_pairs={{0,1},{1,0},{2,3},{3,2},{4,5},{5,4},{6,7},{7,6},{8,9},{9,8},{10,11... | collective-permute-start | bytes 2654216 | tf_op jit(solution)/shard_map/ppermute | solution.py:559
  6.2 1.4 %collective-permute-start.3 = (bf16[2,128,128]{2,1,0:T(8,128)(2,1)S(1)}, bf16[2,128,128]{2,1,0:T(8,128)(2,1)S(1)}, u32[]{:S(2)}, u32[]{:S(2)}) collective-permute-start(bf16[2,128,128]{2,1,0:T(8,128)(2,1)S(1)} %get-tuple-element.60), channel_id=1, source_target_pairs={{0,1},{1,0},{2,3},{3,2},{4,5},{5,4},{6,7},{7,6},{8,9},{9,8},{10,11... | collective-permute-start | bytes 196616 | tf_op jit(solution)/shard_map/ppermute | solution.py:559
  7.6 9.9 %copy-start = (s32[26]{0:T(128)S(1)}, s32[26]{0:T(128)}, u32[]{:S(2)}) copy-start(s32[26]{0:T(128)} %owner_ref.1) | copy-start | bytes 316
  8.4 14.9 %collective-permute-start.6 = (bf16[64,3584]{1,0:T(8,128)(2,1)S(1)}, bf16[64,3584]{1,0:T(8,128)(2,1)S(1)}, u32[]{:S(2)}, u32[]{:S(2)}) collective-permute-start(bf16[64,3584]{1,0:T(8,128)(2,1)S(1)} %get-tuple-element.64), channel_id=1, source_target_pairs={{0,2},{1,3},{2,0},{3,1},{4,6},{5,7},{6,4},{7,5},{8,10},{9,11},{10,... | collective-permute-start | bytes 1376264 | tf_op jit(solution)/shard_map/ppermute | solution.py:559
  11.4 11.9 %collective-permute-start.7 = (bf16[64,3456]{1,0:T(8,128)(2,1)S(1)}, bf16[64,3456]{1,0:T(8,128)(2,1)S(1)}, u32[]{:S(2)}, u32[]{:S(2)}) collective-permute-start(bf16[64,3456]{1,0:T(8,128)(2,1)S(1)} %get-tuple-element.66), channel_id=1, source_target_pairs={{0,4},{1,5},{2,6},{3,7},{4,0},{5,1},{6,2},{7,3},{8,12},{9,13},{10,... | collective-permute-start | bytes 1327112 | tf_op jit(solution)/shard_map/ppermute | solution.py:559
  12.9 27.9 %collective-permute-start.10 = (bf16[928,128]{1,0:T(8,128)(2,1)S(1)}, bf16[928,128]{1,0:T(8,128)(2,1)S(1)}, u32[]{:S(2)}, u32[]{:S(2)}) collective-permute-start(bf16[928,128]{1,0:T(8,128)(2,1)S(1)} %get-tuple-element.81), channel_id=1, source_target_pairs={{0,16},{8,24},{16,0},{24,8},{1,17},{9,25},{17,1},{25,9},{2,18},{10... | collective-permute-start | bytes 712712 | tf_op jit(solution)/shard_map/ppermute | solution.py:562
  15.5 25.3 %collective-permute-start.11 = (bf16[928,128]{1,0:T(8,128)(2,1)S(1)}, bf16[928,128]{1,0:T(8,128)(2,1)S(1)}, u32[]{:S(2)}, u32[]{:S(2)}) collective-permute-start(bf16[928,128]{1,0:T(8,128)(2,1)S(1)} %get-tuple-element.82), channel_id=1, source_target_pairs={{0,24},{8,0},{16,8},{24,16},{1,25},{9,1},{17,9},{25,17},{2,26},{10... | collective-permute-start | bytes 712712 | tf_op jit(solution)/shard_map/ppermute | solution.py:562
  16.8 24.0 %collective-permute-start.9 = (bf16[928,128]{1,0:T(8,128)(2,1)S(1)}, bf16[928,128]{1,0:T(8,128)(2,1)S(1)}, u32[]{:S(2)}, u32[]{:S(2)}) collective-permute-start(bf16[928,128]{1,0:T(8,128)(2,1)S(1)} %get-tuple-element.80), channel_id=1, source_target_pairs={{0,8},{8,16},{16,24},{24,0},{1,9},{9,17},{17,25},{25,1},{2,10},{10... | collective-permute-start | bytes 712712 | tf_op jit(solution)/shard_map/ppermute | solution.py:562
  23.5 7.7 %collective-permute-start = (bf16[32,3712]{1,0:T(8,128)(2,1)S(1)}, bf16[32,3712]{1,0:T(8,128)(2,1)S(1)}, u32[]{:S(2)}, u32[]{:S(2)}) collective-permute-start(bf16[32,3712]{1,0:T(8,128)(2,1)S(1)} %get-tuple-element.14), channel_id=1, source_target_pairs={{0,4},{1,5},{2,6},{3,7},{4,0},{5,1},{6,2},{7,3},{8,12},{9,13},{10,... | collective-permute-start | bytes 712712 | tf_op jit(solution)/shard_map/cond/branch_1_fun/ppermute | solution.py:559
  25.1 6.1 %collective-permute-start.1 = (bf16[32,3456]{1,0:T(8,128)(2,1)S(1)}, bf16[32,3456]{1,0:T(8,128)(2,1)S(1)}, u32[]{:S(2)}, u32[]{:S(2)}) collective-permute-start(bf16[32,3456]{1,0:T(8,128)(2,1)S(1)} %get-tuple-element.16), channel_id=1, source_target_pairs={{0,2},{1,3},{2,0},{3,1},{4,6},{5,7},{6,4},{7,5},{8,10},{9,11},{10,... | collective-permute-start | bytes 663560 | tf_op jit(solution)/shard_map/cond/branch_1_fun/ppermute | solution.py:559
  31.5 6.2 %collective-permute-start.2 = (bf16[136,896]{1,0:T(8,128)(2,1)S(1)}, bf16[136,896]{1,0:T(8,128)(2,1)S(1)}, u32[]{:S(2)}, u32[]{:S(2)}) collective-permute-start(bf16[136,896]{1,0:T(8,128)(2,1)S(1)} %get-tuple-element.19), channel_id=1, source_target_pairs={{0,8},{8,0},{16,24},{24,16},{1,9},{9,1},{17,25},{25,17},{2,10},{10... | collective-permute-start | bytes 731144 | tf_op jit(solution)/shard_map/cond/branch_1_fun/ppermute | solution.py:559
  37.8 7.3 %collective-permute-start.8 = (bf16[72,896]{1,0:T(8,128)(2,1)S(1)}, bf16[72,896]{1,0:T(8,128)(2,1)S(1)}, u32[]{:S(2)}, u32[]{:S(2)}) collective-permute-start(bf16[72,896]{1,0:T(8,128)(2,1)S(1)} %get-tuple-element.74), channel_id=1, source_target_pairs={{0,16},{8,24},{16,0},{24,8},{1,17},{9,25},{17,1},{25,9},{2,18},{10... | collective-permute-start | bytes 387080 | tf_op jit(solution)/shard_map/ppermute | solution.py:559

commit v9 on v8

--- a/solution.py
+++ b/solution.py
@@ -14,6 +14,7 @@
 TABLE_REACH_ROWS = 512
 EMPTY = TABLE_REACH_ROWS // 2
 BIAS_ROWS = 32
+MESSAGE_ROWS = 16
 F32 = jnp.float32
 BF16 = jnp.bfloat16
 MIB = 1024 * 1024
@@ -362,23 +363,20 @@
 
 def put_rows(ref, high, low):
     wide = ref.shape[1] // EMBED_WIDTH
-    first = ref.shape[0] - 8
-    ref[first:, :] = jnp.zeros((8, ref.shape[1]), BF16)
     rows = []
     for value in (high, low):
         for row in range(4):
-            pieces = [
-                value[min(row * wide + k, BIAS_ROWS - 1) : min(row * wide + k, BIAS_ROWS - 1) + 1, :]
-                for k in range(wide)
-            ]
-            rows.append(jnp.concatenate(pieces, axis=1))
+            places = [min(row * wide + k, BIAS_ROWS - 1) for k in range(wide)]
+            rows.append(jnp.concatenate([value[place : place + 1, :] for place in places], axis=1))
+    rows.append(jnp.zeros((MESSAGE_ROWS - 8, ref.shape[1]), F32))
+    first = ref.shape[0] - MESSAGE_ROWS
     ref[first:, :] = jnp.concatenate(rows, axis=0).astype(BF16)
 
 
 def get_rows(ref, store):
     wide = ref.shape[1] // EMBED_WIDTH
-    value = ref[ref.shape[0] - 8 :, :].astype(F32)
-    value = value[:4] + value[4:]
+    value = ref[ref.shape[0] - MESSAGE_ROWS :, :].astype(F32)
+    value = value[:4] + value[4:8]
     for place in range(min(4 * wide, BIAS_ROWS)):
         row, k = divmod(place, wide)
         store[place : place + 1, :] = value[row : row + 1, k * EMBED_WIDTH : (k + 1) * EMBED_WIDTH]
@@ -420,7 +418,7 @@
         out_specs=[VMEM] * 3,
         out_shape=[
             jax.ShapeDtypeStruct((n_table // 2, 2, rows, columns), F32),
-            jax.ShapeDtypeStruct((n_table * rows + 8, padded(columns)), BF16),
+            jax.ShapeDtypeStruct((n_table * rows + MESSAGE_ROWS, padded(columns)), BF16),
             jax.ShapeDtypeStruct(bias_sum.shape, F32),
         ],
         scratch_shapes=[pltpu.VMEM((n_table, 2, rows, columns), F32)],
@@ -453,7 +451,7 @@
         out_specs=[VMEM] * 3,
         out_shape=[
             jax.ShapeDtypeStruct((count // 2, 2, rows, columns), F32),
-            jax.ShapeDtypeStruct((count * rows + 8, padded(columns)), BF16),
+            jax.ShapeDtypeStruct((count * rows + MESSAGE_ROWS, padded(columns)), BF16),
             jax.ShapeDtypeStruct(bias_sum.shape, F32),
         ],
         scratch_shapes=[pltpu.VMEM(bias_sum.shape, F32)],

time: 46 us -> 46.5 us (1.011)
  waiting for transfers between devices: 17.2 us -> 17.8 us
    ppermute x9, waiting for transfers between devices: 17.2 us -> 17.8 us  [swap(): return lax.ppermute(value, axis, [(k, k ^ bit) for k in range(size)])]
where the time goes in v9:
time: 46.5 us; the launch traced here: 46.3 us
  waiting for transfers between devices  17.8 us (38%)
  starting transfers between devices  16.9 us (36%)
  Pallas kernels  10.9 us (23%)
  between operations  0.72 us (2%)
    ppermute x9, waiting for transfers between devices, swap(): return lax.ppermute(value, axis, [(k, k ^ bit) for k in range(size)])  17.8 us
    ppermute x9, starting transfers between devices, swap(): return lax.ppermute(value, axis, [(k, k ^ bit) for k in range(size)])  12.3 us
    pallas_call x1, Pallas kernels, input_call(): pl.pallas_call(functools.partial(input_kernel, n_table, slots, up_bits, d...  4.96 us
    ppermute x3, starting transfers between devices, shifted(): lax.ppermute(value, 'table', [(k, (k + shift) % n_table) for k in range(n...  4.61 us
    pallas_call x1, Pallas kernels, rows_call(): pl.pallas_call(functools.partial(rows_kernel, slots), in_specs=[VMEM] * n...  3.82 us
  transfers between devices with their start and end apart: 12, of which 5 were waited for; matrix products, arithmetic and copies ran while one was open for 0% of the time, Pallas kernels for 20%

profile of v9, /device:TPU:0, one launch (start us, length us, event | category | flops | bytes accessed | tf_op | source)
XLA Modules:
  0.0 46.3 jit_solution(1605375771733966288)
XLA Ops:
  0.6 0.5 %collective-permute-start.4 = (bf16[128,3456]{1,0:T(8,128)(2,1)}, bf16[128,3456]{1,0:T(8,128)(2,1)S(1)}, u32[]{:S(2)}, u32[]{:S(2)}) collective-permute-start(bf16[128,3456]{1,0:T(8,128)(2,1)} %act_hbm.1), channel_id=1, source_target_pairs={{0,1},{1,0},{2,3},{3,2},{4,5},{5,4},{6,7},{7,6},{8,9},{9,8},{10,11... | collective-permute-start | bytes 2654216 | tf_op jit(solution)/shard_map/ppermute | solution.py:557
  1.2 0.1 collective-permute-start.5
  1.2 5.0 %shard_map.119 = (bf16[128,3456]{1,0:T(8,128)(2,1)S(1)}, bf16[128,3456]{1,0:T(8,128)(2,1)S(1)}, bf16[2,128,128]{2,1,0:T(8,128)(2,1)S(1)}, bf16[2,128,128]{2,1,0:...) custom-call(s32[1]{0:T(128)} %bitcast.table_ref, ...), custom_call_target="tpu_custom_call" | custom-call | flops 905969664 | bytes 5308416 | tf_op jit(solution)/shard_map/pallas_call | solution.py:137
  6.2 0.5 %collective-permute-start.3 = (bf16[2,128,128]{2,1,0:T(8,128)(2,1)S(1)}, bf16[2,128,128]{2,1,0:T(8,128)(2,1)S(1)}, u32[]{:S(2)}, u32[]{:S(2)}) collective-permute-start(bf16[2,128,128]{2,1,0:T(8,128)(2,1)S(1)} %get-tuple-element.60), channel_id=1, source_target_pairs={{0,1},{1,0},{2,3},{3,2},{4,5},{5,4},{6,7},{7,6},{8,9},{9,8},{10,11... | collective-permute-start | bytes 196616 | tf_op jit(solution)/shard_map/ppermute | solution.py:557
  6.7 0.9 %collective-permute-done.3.other_ref = bf16[2,128,128]{2,1,0:T(8,128)(2,1)S(1)} collective-permute-done((bf16[2,128,128]{2,1,0:T(8,128)(2,1)S(1)}, bf16[2,128,128]{2,1,0:T(8,128)(2,1)S(1)}, u32[]{:S(2)}, u32[]{:S(2)}) %collective-permute-start.3) | collective-permute-done | bytes 65568 | tf_op jit(solution)/shard_map/ppermute | solution.py:557
  7.6 0.0 collective-permute-done.4.act_other
  7.6 0.0 collective-permute-done.5.cot_other
  7.6 0.8 %shard_map.120 = (f32[64,3456]{1,0:T(8,128)S(1)}, bf16[64,3584]{1,0:T(8,128)(2,1)S(1)}, f32[64,3456]{1,0:T(8,128)S(1)}, bf16[64,3456]{1,0:T(8,128)(2,1)S(1)}, f32[32,128]{1,0:T(8,128)S(1)}) custom-call(bf16[2,128,128]{2,1,0:T(8,128)(2,1)S(1)} %get-tuple-element.59.keep_ref, bf16[2,128,128]{2,1,0:T(8,128)(2,1)S(1)} %collective-permute-done.3.other_ref, ...), custom_call_target="tpu_custom_call" | custom-call | flops 452984832 | bytes 6193152 | tf_op jit(solution)/shard_map/pallas_call | solution.py:224
  8.4 2.9 %collective-permute-start.6 = (bf16[64,3584]{1,0:T(8,128)(2,1)S(1)}, bf16[64,3584]{1,0:T(8,128)(2,1)S(1)}, u32[]{:S(2)}, u32[]{:S(2)}) collective-permute-start(bf16[64,3584]{1,0:T(8,128)(2,1)S(1)} %get-tuple-element.64), channel_id=1, source_target_pairs={{0,2},{1,3},{2,0},{3,1},{4,6},{5,7},{6,4},{7,5},{8,10},{9,11},{10,... | collective-permute-start | bytes 1376264 | tf_op jit(solution)/shard_map/ppermute | solution.py:557
  11.4 1.5 %collective-permute-start.7 = (bf16[64,3456]{1,0:T(8,128)(2,1)S(1)}, bf16[64,3456]{1,0:T(8,128)(2,1)S(1)}, u32[]{:S(2)}, u32[]{:S(2)}) collective-permute-start(bf16[64,3456]{1,0:T(8,128)(2,1)S(1)} %get-tuple-element.66), channel_id=1, source_target_pairs={{0,4},{1,5},{2,6},{3,7},{4,0},{5,1},{6,2},{7,3},{8,12},{9,13},{10,... | collective-permute-start | bytes 1327112 | tf_op jit(solution)/shard_map/ppermute | solution.py:557
  12.9 2.6 %collective-permute-start.10 = (bf16[928,128]{1,0:T(8,128)(2,1)S(1)}, bf16[928,128]{1,0:T(8,128)(2,1)S(1)}, u32[]{:S(2)}, u32[]{:S(2)}) collective-permute-start(bf16[928,128]{1,0:T(8,128)(2,1)S(1)} %get-tuple-element.81), channel_id=1, source_target_pairs={{0,16},{8,24},{16,0},{24,8},{1,17},{9,25},{17,1},{25,9},{2,18},{10... | collective-permute-start | bytes 712712 | tf_op jit(solution)/shard_map/ppermute | solution.py:560
  15.5 1.3 %collective-permute-start.11 = (bf16[928,128]{1,0:T(8,128)(2,1)S(1)}, bf16[928,128]{1,0:T(8,128)(2,1)S(1)}, u32[]{:S(2)}, u32[]{:S(2)}) collective-permute-start(bf16[928,128]{1,0:T(8,128)(2,1)S(1)} %get-tuple-element.82), channel_id=1, source_target_pairs={{0,24},{8,0},{16,8},{24,16},{1,25},{9,1},{17,9},{25,17},{2,26},{10... | collective-permute-start | bytes 712712 | tf_op jit(solution)/shard_map/ppermute | solution.py:560
  16.8 0.7 %collective-permute-start.9 = (bf16[928,128]{1,0:T(8,128)(2,1)S(1)}, bf16[928,128]{1,0:T(8,128)(2,1)S(1)}, u32[]{:S(2)}, u32[]{:S(2)}) collective-permute-start(bf16[928,128]{1,0:T(8,128)(2,1)S(1)} %get-tuple-element.80), channel_id=1, source_target_pairs={{0,8},{8,16},{16,24},{24,0},{1,9},{9,17},{17,25},{25,1},{2,10},{10... | collective-permute-start | bytes 712712 | tf_op jit(solution)/shard_map/ppermute | solution.py:560
  17.5 5.8 %collective-permute-done.7.down_in_ref = bf16[64,3456]{1,0:T(8,128)(2,1)S(1)} collective-permute-done((bf16[64,3456]{1,0:T(8,128)(2,1)S(1)}, bf16[64,3456]{1,0:T(8,128)(2,1)S(1)}, u32[]{:S(2)}, u32[]{:S(2)}) %collective-permute-start.7) | collective-permute-done | bytes 442400 | tf_op jit(solution)/shard_map/ppermute | solution.py:557
  23.3 0.0 collective-permute-done.6.up_in_ref
  23.3 0.2 shard_map.121
  23.5 14.6 %conditional.1 = (f32[1,2,32,864]{3,2,1,0:T(8,128)S(1)}, f32[32,128]{1,0:T(8,128)S(1)}, bf16[80,896]{1,0:T(8,128)(2,1)S(1)}) conditional(s32[]{:T(128)} %bitcast.5, () %tuple.17, (bf16[32,3712]{1,0:T(8,128)(2,1)S(1)}, bf16[32,3456]{1,0:T(8,128)(2,1)S(1)}, s32[1]{0:T(128)}, f32[32,3456]{1,0:T(8,128)S(1)}, f32[32,3456]{1,0:T(8,128)S(1)}, ...), branch_computations={%region_0.0_spmd, %region_1.0_spmd} | conditional | bytes 2867344 | solution.py:614
  23.5 1.6 %collective-permute-start = (bf16[32,3712]{1,0:T(8,128)(2,1)S(1)}, bf16[32,3712]{1,0:T(8,128)(2,1)S(1)}, u32[]{:S(2)}, u32[]{:S(2)}) collective-permute-start(bf16[32,3712]{1,0:T(8,128)(2,1)S(1)} %get-tuple-element.14), channel_id=1, source_target_pairs={{0,4},{1,5},{2,6},{3,7},{4,0},{5,1},{6,2},{7,3},{8,12},{9,13},{10,... | collective-permute-start | bytes 712712 | tf_op jit(solution)/shard_map/cond/branch_1_fun/ppermute | solution.py:557
  25.1 0.6 %collective-permute-start.1 = (bf16[32,3456]{1,0:T(8,128)(2,1)S(1)}, bf16[32,3456]{1,0:T(8,128)(2,1)S(1)}, u32[]{:S(2)}, u32[]{:S(2)}) collective-permute-start(bf16[32,3456]{1,0:T(8,128)(2,1)S(1)} %get-tuple-element.16), channel_id=1, source_target_pairs={{0,2},{1,3},{2,0},{3,1},{4,6},{5,7},{6,4},{7,5},{8,10},{9,11},{10,... | collective-permute-start | bytes 663560 | tf_op jit(solution)/shard_map/cond/branch_1_fun/ppermute | solution.py:557
  25.7 5.4 %collective-permute-done.1.down_in_ref = bf16[32,3456]{1,0:T(8,128)(2,1)S(1)} collective-permute-done((bf16[32,3456]{1,0:T(8,128)(2,1)S(1)}, bf16[32,3456]{1,0:T(8,128)(2,1)S(1)}, u32[]{:S(2)}, u32[]{:S(2)}) %collective-permute-start.1) | collective-permute-done | bytes 221216 | tf_op jit(solution)/shard_map/cond/branch_1_fun/ppermute | solution.py:557
  31.1 0.0 collective-permute-done.up_in_ref
  31.1 0.3 branch_1_fun.2
  31.5 1.6 %collective-permute-start.2 = (bf16[144,896]{1,0:T(8,128)(2,1)S(1)}, bf16[144,896]{1,0:T(8,128)(2,1)S(1)}, u32[]{:S(2)}, u32[]{:S(2)}) collective-permute-start(bf16[144,896]{1,0:T(8,128)(2,1)S(1)} %get-tuple-element.19), channel_id=1, source_target_pairs={{0,8},{8,0},{16,24},{24,16},{1,9},{9,1},{17,25},{25,17},{2,10},{10... | collective-permute-start | bytes 774152 | tf_op jit(solution)/shard_map/cond/branch_1_fun/ppermute | solution.py:557
  33.1 4.8 %collective-permute-done.2.in_ref = bf16[144,896]{1,0:T(8,128)(2,1)S(1)} collective-permute-done((bf16[144,896]{1,0:T(8,128)(2,1)S(1)}, bf16[144,896]{1,0:T(8,128)(2,1)S(1)}, u32[]{:S(2)}, u32[]{:S(2)}) %collective-permute-start.2) | collective-permute-done | bytes 258080 | tf_op jit(solution)/shard_map/cond/branch_1_fun/ppermute | solution.py:557
  37.9 0.1 branch_1_fun.3
  38.0 2.9 %collective-permute-start.8 = (bf16[80,896]{1,0:T(8,128)(2,1)S(1)}, bf16[80,896]{1,0:T(8,128)(2,1)S(1)}, u32[]{:S(2)}, u32[]{:S(2)}) collective-permute-start(bf16[80,896]{1,0:T(8,128)(2,1)S(1)} %get-tuple-element.74), channel_id=1, source_target_pairs={{0,16},{8,24},{16,0},{24,8},{1,17},{9,25},{17,1},{25,9},{2,18},{10... | collective-permute-start | bytes 430088 | tf_op jit(solution)/shard_map/ppermute | solution.py:557
  40.9 0.0 collective-permute-done.10.refs_2_
  41.0 0.0 collective-permute-done.11.refs_3_
  41.0 0.0 collective-permute-done.9.refs_1_
  41.0 3.8 %shard_map.123 = f32[1,7,512,128]{3,2,1,0:T(8,128)} custom-call(bf16[928,128]{1,0:T(8,128)(2,1)S(1)} %get-tuple-element.83.refs_0_, bf16[928,128]{1,0:T(8,128)(2,1)S(1)} %collective-permute-done.9.refs_1_, bf16[928,128]{1,0:T(8,128)(2,1)S(1)} %collective-permute-done.10.refs_2_, bf16[928,128]{1,0:T(8,128)(2,1)S(1)} %collective-permute-done.11.refs_3_), custom_call_target="tpu_custom_call" | custom-call | flops 469762048 | bytes 1835008 | tf_op jit(solution)/shard_map/pallas_call | solution.py:520
  44.8 0.8 %collective-permute-done.8.in_ref = bf16[80,896]{1,0:T(8,128)(2,1)S(1)} collective-permute-done((bf16[80,896]{1,0:T(8,128)(2,1)S(1)}, bf16[80,896]{1,0:T(8,128)(2,1)S(1)}, u32[]{:S(2)}, u32[]{:S(2)}) %collective-permute-start.8) | collective-permute-done | bytes 143392 | tf_op jit(solution)/shard_map/ppermute | solution.py:557
  45.6 0.7 %shard_map.122 = (f32[32,864]{1,0:T(8,128)}, f32[32,864]{1,0:T(8,128)}, f32[27,128]{1,0:T(8,128)}) custom-call(f32[1,2,32,864]{3,2,1,0:T(8,128)S(1)} %get-tuple-element.73.keep_ref, bf16[80,896]{1,0:T(8,128)(2,1)S(1)} %collective-permute-done.8.in_ref, f32[32,128]{1,0:T(8,128)S(1)} %get-tuple-element.75.bias_ref), custom_call_target="tpu_custom_call" | custom-call | tf_op jit(solution)/shard_map/pallas_call | solution.py:473
  (2 shorter events, 0.0 us)
Async XLA Ops:
  0.6 7.0 %collective-permute-start.4 = (bf16[128,3456]{1,0:T(8,128)(2,1)}, bf16[128,3456]{1,0:T(8,128)(2,1)S(1)}, u32[]{:S(2)}, u32[]{:S(2)}) collective-permute-start(bf16[128,3456]{1,0:T(8,128)(2,1)} %act_hbm.1), channel_id=1, source_target_pairs={{0,1},{1,0},{2,3},{3,2},{4,5},{5,4},{6,7},{7,6},{8,9},{9,8},{10,11... | collective-permute-start | bytes 2654216 | tf_op jit(solution)/shard_map/ppermute | solution.py:557
  1.2 6.4 %collective-permute-start.5 = (bf16[128,3456]{1,0:T(8,128)(2,1)}, bf16[128,3456]{1,0:T(8,128)(2,1)S(1)}, u32[]{:S(2)}, u32[]{:S(2)}) collective-permute-start(bf16[128,3456]{1,0:T(8,128)(2,1)} %cot_hbm.1), channel_id=1, source_target_pairs={{0,1},{1,0},{2,3},{3,2},{4,5},{5,4},{6,7},{7,6},{8,9},{9,8},{10,11... | collective-permute-start | bytes 2654216 | tf_op jit(solution)/shard_map/ppermute | solution.py:557
  6.2 1.4 %collective-permute-start.3 = (bf16[2,128,128]{2,1,0:T(8,128)(2,1)S(1)}, bf16[2,128,128]{2,1,0:T(8,128)(2,1)S(1)}, u32[]{:S(2)}, u32[]{:S(2)}) collective-permute-start(bf16[2,128,128]{2,1,0:T(8,128)(2,1)S(1)} %get-tuple-element.60), channel_id=1, source_target_pairs={{0,1},{1,0},{2,3},{3,2},{4,5},{5,4},{6,7},{7,6},{8,9},{9,8},{10,11... | collective-permute-start | bytes 196616 | tf_op jit(solution)/shard_map/ppermute | solution.py:557
  7.6 9.9 %copy-start = (s32[26]{0:T(128)S(1)}, s32[26]{0:T(128)}, u32[]{:S(2)}) copy-start(s32[26]{0:T(128)} %owner_ref.1) | copy-start | bytes 316
  8.4 14.9 %collective-permute-start.6 = (bf16[64,3584]{1,0:T(8,128)(2,1)S(1)}, bf16[64,3584]{1,0:T(8,128)(2,1)S(1)}, u32[]{:S(2)}, u32[]{:S(2)}) collective-permute-start(bf16[64,3584]{1,0:T(8,128)(2,1)S(1)} %get-tuple-element.64), channel_id=1, source_target_pairs={{0,2},{1,3},{2,0},{3,1},{4,6},{5,7},{6,4},{7,5},{8,10},{9,11},{10,... | collective-permute-start | bytes 1376264 | tf_op jit(solution)/shard_map/ppermute | solution.py:557
  11.4 11.9 %collective-permute-start.7 = (bf16[64,3456]{1,0:T(8,128)(2,1)S(1)}, bf16[64,3456]{1,0:T(8,128)(2,1)S(1)}, u32[]{:S(2)}, u32[]{:S(2)}) collective-permute-start(bf16[64,3456]{1,0:T(8,128)(2,1)S(1)} %get-tuple-element.66), channel_id=1, source_target_pairs={{0,4},{1,5},{2,6},{3,7},{4,0},{5,1},{6,2},{7,3},{8,12},{9,13},{10,... | collective-permute-start | bytes 1327112 | tf_op jit(solution)/shard_map/ppermute | solution.py:557
  12.9 28.1 %collective-permute-start.10 = (bf16[928,128]{1,0:T(8,128)(2,1)S(1)}, bf16[928,128]{1,0:T(8,128)(2,1)S(1)}, u32[]{:S(2)}, u32[]{:S(2)}) collective-permute-start(bf16[928,128]{1,0:T(8,128)(2,1)S(1)} %get-tuple-element.81), channel_id=1, source_target_pairs={{0,16},{8,24},{16,0},{24,8},{1,17},{9,25},{17,1},{25,9},{2,18},{10... | collective-permute-start | bytes 712712 | tf_op jit(solution)/shard_map/ppermute | solution.py:560
  15.5 25.5 %collective-permute-start.11 = (bf16[928,128]{1,0:T(8,128)(2,1)S(1)}, bf16[928,128]{1,0:T(8,128)(2,1)S(1)}, u32[]{:S(2)}, u32[]{:S(2)}) collective-permute-start(bf16[928,128]{1,0:T(8,128)(2,1)S(1)} %get-tuple-element.82), channel_id=1, source_target_pairs={{0,24},{8,0},{16,8},{24,16},{1,25},{9,1},{17,9},{25,17},{2,26},{10... | collective-permute-start | bytes 712712 | tf_op jit(solution)/shard_map/ppermute | solution.py:560
  16.8 24.1 %collective-permute-start.9 = (bf16[928,128]{1,0:T(8,128)(2,1)S(1)}, bf16[928,128]{1,0:T(8,128)(2,1)S(1)}, u32[]{:S(2)}, u32[]{:S(2)}) collective-permute-start(bf16[928,128]{1,0:T(8,128)(2,1)S(1)} %get-tuple-element.80), channel_id=1, source_target_pairs={{0,8},{8,16},{16,24},{24,0},{1,9},{9,17},{17,25},{25,1},{2,10},{10... | collective-permute-start | bytes 712712 | tf_op jit(solution)/shard_map/ppermute | solution.py:560
  23.5 7.7 %collective-permute-start = (bf16[32,3712]{1,0:T(8,128)(2,1)S(1)}, bf16[32,3712]{1,0:T(8,128)(2,1)S(1)}, u32[]{:S(2)}, u32[]{:S(2)}) collective-permute-start(bf16[32,3712]{1,0:T(8,128)(2,1)S(1)} %get-tuple-element.14), channel_id=1, source_target_pairs={{0,4},{1,5},{2,6},{3,7},{4,0},{5,1},{6,2},{7,3},{8,12},{9,13},{10,... | collective-permute-start | bytes 712712 | tf_op jit(solution)/shard_map/cond/branch_1_fun/ppermute | solution.py:557
  25.1 6.1 %collective-permute-start.1 = (bf16[32,3456]{1,0:T(8,128)(2,1)S(1)}, bf16[32,3456]{1,0:T(8,128)(2,1)S(1)}, u32[]{:S(2)}, u32[]{:S(2)}) collective-permute-start(bf16[32,3456]{1,0:T(8,128)(2,1)S(1)} %get-tuple-element.16), channel_id=1, source_target_pairs={{0,2},{1,3},{2,0},{3,1},{4,6},{5,7},{6,4},{7,5},{8,10},{9,11},{10,... | collective-permute-start | bytes 663560 | tf_op jit(solution)/shard_map/cond/branch_1_fun/ppermute | solution.py:557
  31.5 6.5 %collective-permute-start.2 = (bf16[144,896]{1,0:T(8,128)(2,1)S(1)}, bf16[144,896]{1,0:T(8,128)(2,1)S(1)}, u32[]{:S(2)}, u32[]{:S(2)}) collective-permute-start(bf16[144,896]{1,0:T(8,128)(2,1)S(1)} %get-tuple-element.19), channel_id=1, source_target_pairs={{0,8},{8,0},{16,24},{24,16},{1,9},{9,1},{17,25},{25,17},{2,10},{10... | collective-permute-start | bytes 774152 | tf_op jit(solution)/shard_map/cond/branch_1_fun/ppermute | solution.py:557
  38.0 7.6 %collective-permute-start.8 = (bf16[80,896]{1,0:T(8,128)(2,1)S(1)}, bf16[80,896]{1,0:T(8,128)(2,1)S(1)}, u32[]{:S(2)}, u32[]{:S(2)}) collective-permute-start(bf16[80,896]{1,0:T(8,128)(2,1)S(1)} %get-tuple-element.74), channel_id=1, source_target_pairs={{0,16},{8,24},{16,0},{24,8},{1,17},{9,25},{17,1},{25,9},{2,18},{10... | collective-permute-start | bytes 430088 | tf_op jit(solution)/shard_map/ppermute | solution.py:557

commit v10 on v9

--- a/solution.py
+++ b/solution.py
@@ -14,7 +14,6 @@
 TABLE_REACH_ROWS = 512
 EMPTY = TABLE_REACH_ROWS // 2
 BIAS_ROWS = 32
-MESSAGE_ROWS = 16
 F32 = jnp.float32
 BF16 = jnp.bfloat16
 MIB = 1024 * 1024
@@ -361,28 +360,6 @@
     )(table_index, own, bias_sum, *arrived)
 
 
-def put_rows(ref, high, low):
-    wide = ref.shape[1] // EMBED_WIDTH
-    rows = []
-    for value in (high, low):
-        for row in range(4):
-            places = [min(row * wide + k, BIAS_ROWS - 1) for k in range(wide)]
-            rows.append(jnp.concatenate([value[place : place + 1, :] for place in places], axis=1))
-    rows.append(jnp.zeros((MESSAGE_ROWS - 8, ref.shape[1]), F32))
-    first = ref.shape[0] - MESSAGE_ROWS
-    ref[first:, :] = jnp.concatenate(rows, axis=0).astype(BF16)
-
-
-def get_rows(ref, store):
-    wide = ref.shape[1] // EMBED_WIDTH
-    value = ref[ref.shape[0] - MESSAGE_ROWS :, :].astype(F32)
-    value = value[:4] + value[4:8]
-    for place in range(min(4 * wide, BIAS_ROWS)):
-        row, k = divmod(place, wide)
-        store[place : place + 1, :] = value[row : row + 1, k * EMBED_WIDTH : (k + 1) * EMBED_WIDTH]
-    return store[...]
-
-
 def padded(columns):
     return -(-columns // EMBED_WIDTH) * EMBED_WIDTH
 
@@ -401,12 +378,16 @@
     for place in range(n_table // 2):
         keep_ref[place] = store[table_ref[0] ^ (2 * place)]
         for which in range(2):
-            first = (2 * place + which) * rows
+            first = place * padded(columns)
             value = store[table_ref[0] ^ (2 * place + 1), which]
-            send_ref[first : first + rows, :columns] = value.astype(BF16)
+            send_ref[which * rows : (which + 1) * rows, first : first + columns] = value.astype(BF16)
     high, low = bias_terms(bias_ref[...] + get_bias(up_in_ref, width))
-    put_rows(send_ref, high, low)
+    put_bias(send_ref, n_table // 2 * padded(columns), high, low)
     bias_out_ref[...] = high + low
+
+
+def message_shape(tables, rows, columns):
+    return (2 * rows, tables * padded(columns) + extra_columns(2 * rows))
 
 
 def first_call(table_index, up_keep, up_in, down_keep, down_in, bias_sum, n_table, scale):
@@ -418,7 +399,7 @@
         out_specs=[VMEM] * 3,
         out_shape=[
             jax.ShapeDtypeStruct((n_table // 2, 2, rows, columns), F32),
-            jax.ShapeDtypeStruct((n_table * rows + MESSAGE_ROWS, padded(columns)), BF16),
+            jax.ShapeDtypeStruct(message_shape(n_table // 2, rows, columns), BF16),
             jax.ShapeDtypeStruct(bias_sum.shape, F32),
         ],
         scratch_shapes=[pltpu.VMEM((n_table, 2, rows, columns), F32)],
@@ -426,20 +407,20 @@
     )(table_index, up_keep, up_in, down_keep, down_in, bias_sum)
 
 
-def next_kernel(keep_ref, in_ref, bias_ref, out_ref, send_ref, bias_out_ref, store):
+def next_kernel(keep_ref, in_ref, bias_ref, out_ref, send_ref, bias_out_ref):
     count, _, rows, columns = keep_ref.shape
     for place in range(count):
         for which in range(2):
-            first = (2 * place + which) * rows
-            total = keep_ref[place, which] + in_ref[first : first + rows, :columns].astype(F32)
+            part = slice(which * rows, (which + 1) * rows)
+            first = place * padded(columns)
+            total = keep_ref[place, which] + in_ref[part, first : first + columns].astype(F32)
             if place % 2 == 0:
                 out_ref[place // 2, which] = total
             else:
-                first = (place - 1 + which) * rows
-                send_ref[first : first + rows, :columns] = total.astype(BF16)
-    store[...] = jnp.zeros_like(store)
-    high, low = bias_terms(bias_ref[...] + get_rows(in_ref, store))
-    put_rows(send_ref, high, low)
+                first = place // 2 * padded(columns)
+                send_ref[part, first : first + columns] = total.astype(BF16)
+    high, low = bias_terms(bias_ref[...] + get_bias(in_ref, count * padded(columns)))
+    put_bias(send_ref, count // 2 * padded(columns), high, low)
     bias_out_ref[...] = high + low
 
 
@@ -451,20 +432,18 @@
         out_specs=[VMEM] * 3,
         out_shape=[
             jax.ShapeDtypeStruct((count // 2, 2, rows, columns), F32),
-            jax.ShapeDtypeStruct((count * rows + MESSAGE_ROWS, padded(columns)), BF16),
+            jax.ShapeDtypeStruct(message_shape(count // 2, rows, columns), BF16),
             jax.ShapeDtypeStruct(bias_sum.shape, F32),
         ],
-        scratch_shapes=[pltpu.VMEM(bias_sum.shape, F32)],
         compiler_params=params(16),
     )(keep, arrived, bias_sum)
 
 
-def last_kernel(scale, keep_ref, in_ref, bias_ref, up_ref, down_ref, bias_out_ref, store):
+def last_kernel(scale, keep_ref, in_ref, bias_ref, up_ref, down_ref, bias_out_ref):
     rows, columns = up_ref.shape
     up_ref[...] = keep_ref[0, 0] + in_ref[:rows, :columns].astype(F32)
     down_ref[...] = keep_ref[0, 1] + in_ref[rows : 2 * rows, :columns].astype(F32)
-    store[...] = jnp.zeros_like(store)
-    total = bias_ref[...] + get_rows(in_ref, store)
+    total = bias_ref[...] + get_bias(in_ref, padded(columns))
     bias_out_ref[...] = total[: bias_out_ref.shape[0]] * scale
 
 
@@ -479,7 +458,6 @@
             jax.ShapeDtypeStruct((rows, columns), F32),
             jax.ShapeDtypeStruct((columns * n_table // EMBED_WIDTH, EMBED_WIDTH), F32),
         ],
-        scratch_shapes=[pltpu.VMEM(bias_sum.shape, F32)],
         compiler_params=params(16),
     )(keep, arrived, bias_sum)
 

time: 46.5 us -> 46.1 us (level)
  waiting for transfers between devices: 17.8 us -> 17.3 us
    ppermute x9, waiting for transfers between devices: 17.8 us -> 17.2 us  [swap(): return lax.ppermute(value, axis, [(k, k ^ bit) for k in range(size)])]
where the time goes in v10:
time: 46.1 us; the launch traced here: 45.9 us
  waiting for transfers between devices  17.3 us (38%)
  starting transfers between devices  17 us (37%)
  Pallas kernels  10.8 us (23%)
  between operations  0.72 us (2%)
    ppermute x9, waiting for transfers between devices, swap(): return lax.ppermute(value, axis, [(k, k ^ bit) for k in range(size)])  17.2 us
    ppermute x9, starting transfers between devices, swap(): return lax.ppermute(value, axis, [(k, k ^ bit) for k in range(size)])  12.4 us
    pallas_call x1, Pallas kernels, input_call(): pl.pallas_call(functools.partial(input_kernel, n_table, slots, up_bits, d...  4.96 us
    ppermute x3, starting transfers between devices, shifted(): lax.ppermute(value, 'table', [(k, (k + shift) % n_table) for k in range(n...  4.61 us
    pallas_call x1, Pallas kernels, rows_call(): pl.pallas_call(functools.partial(rows_kernel, slots), in_specs=[VMEM] * n...  3.82 us
  transfers between devices with their start and end apart: 12, of which 5 were waited for; matrix products, arithmetic and copies ran while one was open for 0% of the time, Pallas kernels for 20%

profile of v10, /device:TPU:0, one launch (start us, length us, event | category | flops | bytes accessed | tf_op | source)
XLA Modules:
  0.0 45.9 jit_solution(3822091603958521439)
XLA Ops:
  0.6 0.5 %collective-permute-start.4 = (bf16[128,3456]{1,0:T(8,128)(2,1)}, bf16[128,3456]{1,0:T(8,128)(2,1)S(1)}, u32[]{:S(2)}, u32[]{:S(2)}) collective-permute-start(bf16[128,3456]{1,0:T(8,128)(2,1)} %act_hbm.1), channel_id=1, source_target_pairs={{0,1},{1,0},{2,3},{3,2},{4,5},{5,4},{6,7},{7,6},{8,9},{9,8},{10,11... | collective-permute-start | bytes 2654216 | tf_op jit(solution)/shard_map/ppermute | solution.py:535
  1.2 0.1 collective-permute-start.5
  1.2 5.0 %shard_map.119 = (bf16[128,3456]{1,0:T(8,128)(2,1)S(1)}, bf16[128,3456]{1,0:T(8,128)(2,1)S(1)}, bf16[2,128,128]{2,1,0:T(8,128)(2,1)S(1)}, bf16[2,128,128]{2,1,0:...) custom-call(s32[1]{0:T(128)} %bitcast.table_ref, ...), custom_call_target="tpu_custom_call" | custom-call | flops 905969664 | bytes 5308416 | tf_op jit(solution)/shard_map/pallas_call | solution.py:136
  6.2 0.5 %collective-permute-start.3 = (bf16[2,128,128]{2,1,0:T(8,128)(2,1)S(1)}, bf16[2,128,128]{2,1,0:T(8,128)(2,1)S(1)}, u32[]{:S(2)}, u32[]{:S(2)}) collective-permute-start(bf16[2,128,128]{2,1,0:T(8,128)(2,1)S(1)} %get-tuple-element.60), channel_id=1, source_target_pairs={{0,1},{1,0},{2,3},{3,2},{4,5},{5,4},{6,7},{7,6},{8,9},{9,8},{10,11... | collective-permute-start | bytes 196616 | tf_op jit(solution)/shard_map/ppermute | solution.py:535
  6.7 0.9 %collective-permute-done.3.other_ref = bf16[2,128,128]{2,1,0:T(8,128)(2,1)S(1)} collective-permute-done((bf16[2,128,128]{2,1,0:T(8,128)(2,1)S(1)}, bf16[2,128,128]{2,1,0:T(8,128)(2,1)S(1)}, u32[]{:S(2)}, u32[]{:S(2)}) %collective-permute-start.3) | collective-permute-done | bytes 65568 | tf_op jit(solution)/shard_map/ppermute | solution.py:535
  7.6 0.0 collective-permute-done.4.act_other
  7.6 0.0 collective-permute-done.5.cot_other
  7.6 0.8 %shard_map.120 = (f32[64,3456]{1,0:T(8,128)S(1)}, bf16[64,3584]{1,0:T(8,128)(2,1)S(1)}, f32[64,3456]{1,0:T(8,128)S(1)}, bf16[64,3456]{1,0:T(8,128)(2,1)S(1)}, f32[32,128]{1,0:T(8,128)S(1)}) custom-call(bf16[2,128,128]{2,1,0:T(8,128)(2,1)S(1)} %get-tuple-element.59.keep_ref, bf16[2,128,128]{2,1,0:T(8,128)(2,1)S(1)} %collective-permute-done.3.other_ref, ...), custom_call_target="tpu_custom_call" | custom-call | flops 452984832 | bytes 6193152 | tf_op jit(solution)/shard_map/pallas_call | solution.py:223
  8.5 2.9 %collective-permute-start.6 = (bf16[64,3584]{1,0:T(8,128)(2,1)S(1)}, bf16[64,3584]{1,0:T(8,128)(2,1)S(1)}, u32[]{:S(2)}, u32[]{:S(2)}) collective-permute-start(bf16[64,3584]{1,0:T(8,128)(2,1)S(1)} %get-tuple-element.64), channel_id=1, source_target_pairs={{0,2},{1,3},{2,0},{3,1},{4,6},{5,7},{6,4},{7,5},{8,10},{9,11},{10,... | collective-permute-start | bytes 1376264 | tf_op jit(solution)/shard_map/ppermute | solution.py:535
  11.4 1.5 %collective-permute-start.7 = (bf16[64,3456]{1,0:T(8,128)(2,1)S(1)}, bf16[64,3456]{1,0:T(8,128)(2,1)S(1)}, u32[]{:S(2)}, u32[]{:S(2)}) collective-permute-start(bf16[64,3456]{1,0:T(8,128)(2,1)S(1)} %get-tuple-element.66), channel_id=1, source_target_pairs={{0,4},{1,5},{2,6},{3,7},{4,0},{5,1},{6,2},{7,3},{8,12},{9,13},{10,... | collective-permute-start | bytes 1327112 | tf_op jit(solution)/shard_map/ppermute | solution.py:535
  12.9 2.6 %collective-permute-start.10 = (bf16[928,128]{1,0:T(8,128)(2,1)S(1)}, bf16[928,128]{1,0:T(8,128)(2,1)S(1)}, u32[]{:S(2)}, u32[]{:S(2)}) collective-permute-start(bf16[928,128]{1,0:T(8,128)(2,1)S(1)} %get-tuple-element.81), channel_id=1, source_target_pairs={{0,16},{8,24},{16,0},{24,8},{1,17},{9,25},{17,1},{25,9},{2,18},{10... | collective-permute-start | bytes 712712 | tf_op jit(solution)/shard_map/ppermute | solution.py:538
  15.5 1.3 %collective-permute-start.11 = (bf16[928,128]{1,0:T(8,128)(2,1)S(1)}, bf16[928,128]{1,0:T(8,128)(2,1)S(1)}, u32[]{:S(2)}, u32[]{:S(2)}) collective-permute-start(bf16[928,128]{1,0:T(8,128)(2,1)S(1)} %get-tuple-element.82), channel_id=1, source_target_pairs={{0,24},{8,0},{16,8},{24,16},{1,25},{9,1},{17,9},{25,17},{2,26},{10... | collective-permute-start | bytes 712712 | tf_op jit(solution)/shard_map/ppermute | solution.py:538
  16.8 0.7 %collective-permute-start.9 = (bf16[928,128]{1,0:T(8,128)(2,1)S(1)}, bf16[928,128]{1,0:T(8,128)(2,1)S(1)}, u32[]{:S(2)}, u32[]{:S(2)}) collective-permute-start(bf16[928,128]{1,0:T(8,128)(2,1)S(1)} %get-tuple-element.80), channel_id=1, source_target_pairs={{0,8},{8,16},{16,24},{24,0},{1,9},{9,17},{17,25},{25,1},{2,10},{10... | collective-permute-start | bytes 712712 | tf_op jit(solution)/shard_map/ppermute | solution.py:538
  17.5 5.8 %collective-permute-done.7.down_in_ref = bf16[64,3456]{1,0:T(8,128)(2,1)S(1)} collective-permute-done((bf16[64,3456]{1,0:T(8,128)(2,1)S(1)}, bf16[64,3456]{1,0:T(8,128)(2,1)S(1)}, u32[]{:S(2)}, u32[]{:S(2)}) %collective-permute-start.7) | collective-permute-done | bytes 442400 | tf_op jit(solution)/shard_map/ppermute | solution.py:535
  23.3 0.0 collective-permute-done.6.up_in_ref
  23.3 0.2 shard_map.121
  23.5 14.3 %conditional.1 = (f32[1,2,32,864]{3,2,1,0:T(8,128)S(1)}, f32[32,128]{1,0:T(8,128)S(1)}, bf16[64,1024]{1,0:T(8,128)(2,1)S(1)}) conditional(s32[]{:T(128)} %bitcast.5, () %tuple.17, (bf16[32,3712]{1,0:T(8,128)(2,1)S(1)}, bf16[32,3456]{1,0:T(8,128)(2,1)S(1)}, s32[1]{0:T(128)}, f32[32,3456]{1,0:T(8,128)S(1)}, f32[32,3456]{1,0:T(8,128)S(1)}, ...), branch_computations={%region_0.0_spmd, %region_1.0_spmd} | conditional | bytes 2818192 | solution.py:592
  23.5 1.6 %collective-permute-start = (bf16[32,3712]{1,0:T(8,128)(2,1)S(1)}, bf16[32,3712]{1,0:T(8,128)(2,1)S(1)}, u32[]{:S(2)}, u32[]{:S(2)}) collective-permute-start(bf16[32,3712]{1,0:T(8,128)(2,1)S(1)} %get-tuple-element.14), channel_id=1, source_target_pairs={{0,4},{1,5},{2,6},{3,7},{4,0},{5,1},{6,2},{7,3},{8,12},{9,13},{10,... | collective-permute-start | bytes 712712 | tf_op jit(solution)/shard_map/cond/branch_1_fun/ppermute | solution.py:535
  25.1 0.6 %collective-permute-start.1 = (bf16[32,3456]{1,0:T(8,128)(2,1)S(1)}, bf16[32,3456]{1,0:T(8,128)(2,1)S(1)}, u32[]{:S(2)}, u32[]{:S(2)}) collective-permute-start(bf16[32,3456]{1,0:T(8,128)(2,1)S(1)} %get-tuple-element.16), channel_id=1, source_target_pairs={{0,2},{1,3},{2,0},{3,1},{4,6},{5,7},{6,4},{7,5},{8,10},{9,11},{10,... | collective-permute-start | bytes 663560 | tf_op jit(solution)/shard_map/cond/branch_1_fun/ppermute | solution.py:535
  25.7 5.4 %collective-permute-done.1.down_in_ref = bf16[32,3456]{1,0:T(8,128)(2,1)S(1)} collective-permute-done((bf16[32,3456]{1,0:T(8,128)(2,1)S(1)}, bf16[32,3456]{1,0:T(8,128)(2,1)S(1)}, u32[]{:S(2)}, u32[]{:S(2)}) %collective-permute-start.1) | collective-permute-done | bytes 221216 | tf_op jit(solution)/shard_map/cond/branch_1_fun/ppermute | solution.py:535
  31.1 0.0 collective-permute-done.up_in_ref
  31.1 0.3 branch_1_fun.2
  31.5 1.6 %collective-permute-start.2 = (bf16[64,1920]{1,0:T(8,128)(2,1)S(1)}, bf16[64,1920]{1,0:T(8,128)(2,1)S(1)}, u32[]{:S(2)}, u32[]{:S(2)}) collective-permute-start(bf16[64,1920]{1,0:T(8,128)(2,1)S(1)} %get-tuple-element.19), channel_id=1, source_target_pairs={{0,8},{8,0},{16,24},{24,16},{1,9},{9,1},{17,25},{25,17},{2,10},{10... | collective-permute-start | bytes 737288 | tf_op jit(solution)/shard_map/cond/branch_1_fun/ppermute | solution.py:535
  33.1 4.6 %collective-permute-done.2.in_ref = bf16[64,1920]{1,0:T(8,128)(2,1)S(1)} collective-permute-done((bf16[64,1920]{1,0:T(8,128)(2,1)S(1)}, bf16[64,1920]{1,0:T(8,128)(2,1)S(1)}, u32[]{:S(2)}, u32[]{:S(2)}) %collective-permute-start.2) | collective-permute-done | bytes 245792 | tf_op jit(solution)/shard_map/cond/branch_1_fun/ppermute | solution.py:535
  37.7 0.1 branch_1_fun.3
  37.8 3.0 %collective-permute-start.8 = (bf16[64,1024]{1,0:T(8,128)(2,1)S(1)}, bf16[64,1024]{1,0:T(8,128)(2,1)S(1)}, u32[]{:S(2)}, u32[]{:S(2)}) collective-permute-start(bf16[64,1024]{1,0:T(8,128)(2,1)S(1)} %get-tuple-element.74), channel_id=1, source_target_pairs={{0,16},{8,24},{16,0},{24,8},{1,17},{9,25},{17,1},{25,9},{2,18},{10... | collective-permute-start | bytes 393224 | tf_op jit(solution)/shard_map/ppermute | solution.py:535
  40.8 0.0 collective-permute-done.10.refs_2_
  40.8 0.0 collective-permute-done.11.refs_3_
  40.8 0.0 collective-permute-done.9.refs_1_
  40.8 3.8 %shard_map.123 = f32[1,7,512,128]{3,2,1,0:T(8,128)} custom-call(bf16[928,128]{1,0:T(8,128)(2,1)S(1)} %get-tuple-element.83.refs_0_, bf16[928,128]{1,0:T(8,128)(2,1)S(1)} %collective-permute-done.9.refs_1_, bf16[928,128]{1,0:T(8,128)(2,1)S(1)} %collective-permute-done.10.refs_2_, bf16[928,128]{1,0:T(8,128)(2,1)S(1)} %collective-permute-done.11.refs_3_), custom_call_target="tpu_custom_call" | custom-call | flops 469762048 | bytes 1835008 | tf_op jit(solution)/shard_map/pallas_call | solution.py:498
  44.7 0.5 %collective-permute-done.8.in_ref = bf16[64,1024]{1,0:T(8,128)(2,1)S(1)} collective-permute-done((bf16[64,1024]{1,0:T(8,128)(2,1)S(1)}, bf16[64,1024]{1,0:T(8,128)(2,1)S(1)}, u32[]{:S(2)}, u32[]{:S(2)}) %collective-permute-start.8) | collective-permute-done | bytes 131104 | tf_op jit(solution)/shard_map/ppermute | solution.py:535
  45.2 0.7 %shard_map.122 = (f32[32,864]{1,0:T(8,128)}, f32[32,864]{1,0:T(8,128)}, f32[27,128]{1,0:T(8,128)}) custom-call(f32[1,2,32,864]{3,2,1,0:T(8,128)S(1)} %get-tuple-element.73.keep_ref, bf16[64,1024]{1,0:T(8,128)(2,1)S(1)} %collective-permute-done.8.in_ref, f32[32,128]{1,0:T(8,128)S(1)} %get-tuple-element.75.bias_ref), custom_call_target="tpu_custom_call" | custom-call | tf_op jit(solution)/shard_map/pallas_call | solution.py:452
  (2 shorter events, 0.0 us)
Async XLA Ops:
  0.6 7.0 %collective-permute-start.4 = (bf16[128,3456]{1,0:T(8,128)(2,1)}, bf16[128,3456]{1,0:T(8,128)(2,1)S(1)}, u32[]{:S(2)}, u32[]{:S(2)}) collective-permute-start(bf16[128,3456]{1,0:T(8,128)(2,1)} %act_hbm.1), channel_id=1, source_target_pairs={{0,1},{1,0},{2,3},{3,2},{4,5},{5,4},{6,7},{7,6},{8,9},{9,8},{10,11... | collective-permute-start | bytes 2654216 | tf_op jit(solution)/shard_map/ppermute | solution.py:535
  1.2 6.5 %collective-permute-start.5 = (bf16[128,3456]{1,0:T(8,128)(2,1)}, bf16[128,3456]{1,0:T(8,128)(2,1)S(1)}, u32[]{:S(2)}, u32[]{:S(2)}) collective-permute-start(bf16[128,3456]{1,0:T(8,128)(2,1)} %cot_hbm.1), channel_id=1, source_target_pairs={{0,1},{1,0},{2,3},{3,2},{4,5},{5,4},{6,7},{7,6},{8,9},{9,8},{10,11... | collective-permute-start | bytes 2654216 | tf_op jit(solution)/shard_map/ppermute | solution.py:535
  6.2 1.4 %collective-permute-start.3 = (bf16[2,128,128]{2,1,0:T(8,128)(2,1)S(1)}, bf16[2,128,128]{2,1,0:T(8,128)(2,1)S(1)}, u32[]{:S(2)}, u32[]{:S(2)}) collective-permute-start(bf16[2,128,128]{2,1,0:T(8,128)(2,1)S(1)} %get-tuple-element.60), channel_id=1, source_target_pairs={{0,1},{1,0},{2,3},{3,2},{4,5},{5,4},{6,7},{7,6},{8,9},{9,8},{10,11... | collective-permute-start | bytes 196616 | tf_op jit(solution)/shard_map/ppermute | solution.py:535
  7.6 9.9 %copy-start = (s32[26]{0:T(128)S(1)}, s32[26]{0:T(128)}, u32[]{:S(2)}) copy-start(s32[26]{0:T(128)} %owner_ref.1) | copy-start | bytes 316
  8.5 14.9 %collective-permute-start.6 = (bf16[64,3584]{1,0:T(8,128)(2,1)S(1)}, bf16[64,3584]{1,0:T(8,128)(2,1)S(1)}, u32[]{:S(2)}, u32[]{:S(2)}) collective-permute-start(bf16[64,3584]{1,0:T(8,128)(2,1)S(1)} %get-tuple-element.64), channel_id=1, source_target_pairs={{0,2},{1,3},{2,0},{3,1},{4,6},{5,7},{6,4},{7,5},{8,10},{9,11},{10,... | collective-permute-start | bytes 1376264 | tf_op jit(solution)/shard_map/ppermute | solution.py:535
  11.4 11.9 %collective-permute-start.7 = (bf16[64,3456]{1,0:T(8,128)(2,1)S(1)}, bf16[64,3456]{1,0:T(8,128)(2,1)S(1)}, u32[]{:S(2)}, u32[]{:S(2)}) collective-permute-start(bf16[64,3456]{1,0:T(8,128)(2,1)S(1)} %get-tuple-element.66), channel_id=1, source_target_pairs={{0,4},{1,5},{2,6},{3,7},{4,0},{5,1},{6,2},{7,3},{8,12},{9,13},{10,... | collective-permute-start | bytes 1327112 | tf_op jit(solution)/shard_map/ppermute | solution.py:535
  12.9 27.9 %collective-permute-start.10 = (bf16[928,128]{1,0:T(8,128)(2,1)S(1)}, bf16[928,128]{1,0:T(8,128)(2,1)S(1)}, u32[]{:S(2)}, u32[]{:S(2)}) collective-permute-start(bf16[928,128]{1,0:T(8,128)(2,1)S(1)} %get-tuple-element.81), channel_id=1, source_target_pairs={{0,16},{8,24},{16,0},{24,8},{1,17},{9,25},{17,1},{25,9},{2,18},{10... | collective-permute-start | bytes 712712 | tf_op jit(solution)/shard_map/ppermute | solution.py:538
  15.5 25.4 %collective-permute-start.11 = (bf16[928,128]{1,0:T(8,128)(2,1)S(1)}, bf16[928,128]{1,0:T(8,128)(2,1)S(1)}, u32[]{:S(2)}, u32[]{:S(2)}) collective-permute-start(bf16[928,128]{1,0:T(8,128)(2,1)S(1)} %get-tuple-element.82), channel_id=1, source_target_pairs={{0,24},{8,0},{16,8},{24,16},{1,25},{9,1},{17,9},{25,17},{2,26},{10... | collective-permute-start | bytes 712712 | tf_op jit(solution)/shard_map/ppermute | solution.py:538
  16.8 24.0 %collective-permute-start.9 = (bf16[928,128]{1,0:T(8,128)(2,1)S(1)}, bf16[928,128]{1,0:T(8,128)(2,1)S(1)}, u32[]{:S(2)}, u32[]{:S(2)}) collective-permute-start(bf16[928,128]{1,0:T(8,128)(2,1)S(1)} %get-tuple-element.80), channel_id=1, source_target_pairs={{0,8},{8,16},{16,24},{24,0},{1,9},{9,17},{17,25},{25,1},{2,10},{10... | collective-permute-start | bytes 712712 | tf_op jit(solution)/shard_map/ppermute | solution.py:538
  23.5 7.6 %collective-permute-start = (bf16[32,3712]{1,0:T(8,128)(2,1)S(1)}, bf16[32,3712]{1,0:T(8,128)(2,1)S(1)}, u32[]{:S(2)}, u32[]{:S(2)}) collective-permute-start(bf16[32,3712]{1,0:T(8,128)(2,1)S(1)} %get-tuple-element.14), channel_id=1, source_target_pairs={{0,4},{1,5},{2,6},{3,7},{4,0},{5,1},{6,2},{7,3},{8,12},{9,13},{10,... | collective-permute-start | bytes 712712 | tf_op jit(solution)/shard_map/cond/branch_1_fun/ppermute | solution.py:535
  25.1 6.1 %collective-permute-start.1 = (bf16[32,3456]{1,0:T(8,128)(2,1)S(1)}, bf16[32,3456]{1,0:T(8,128)(2,1)S(1)}, u32[]{:S(2)}, u32[]{:S(2)}) collective-permute-start(bf16[32,3456]{1,0:T(8,128)(2,1)S(1)} %get-tuple-element.16), channel_id=1, source_target_pairs={{0,2},{1,3},{2,0},{3,1},{4,6},{5,7},{6,4},{7,5},{8,10},{9,11},{10,... | collective-permute-start | bytes 663560 | tf_op jit(solution)/shard_map/cond/branch_1_fun/ppermute | solution.py:535
  31.5 6.3 %collective-permute-start.2 = (bf16[64,1920]{1,0:T(8,128)(2,1)S(1)}, bf16[64,1920]{1,0:T(8,128)(2,1)S(1)}, u32[]{:S(2)}, u32[]{:S(2)}) collective-permute-start(bf16[64,1920]{1,0:T(8,128)(2,1)S(1)} %get-tuple-element.19), channel_id=1, source_target_pairs={{0,8},{8,0},{16,24},{24,16},{1,9},{9,1},{17,25},{25,17},{2,10},{10... | collective-permute-start | bytes 737288 | tf_op jit(solution)/shard_map/cond/branch_1_fun/ppermute | solution.py:535
  37.8 7.4 %collective-permute-start.8 = (bf16[64,1024]{1,0:T(8,128)(2,1)S(1)}, bf16[64,1024]{1,0:T(8,128)(2,1)S(1)}, u32[]{:S(2)}, u32[]{:S(2)}) collective-permute-start(bf16[64,1024]{1,0:T(8,128)(2,1)S(1)} %get-tuple-element.74), channel_id=1, source_target_pairs={{0,16},{8,24},{16,0},{24,8},{1,17},{9,25},{17,1},{25,9},{2,18},{10... | collective-permute-start | bytes 393224 | tf_op jit(solution)/shard_map/ppermute | solution.py:535

commit v11 on v10

--- a/solution.py
+++ b/solution.py
@@ -48,11 +48,11 @@
 
 def input_kernel(
     n_table, slots, up_bits, down_bits, table_ref, rep_ref, owner_ref,
-    act_hbm, cot_hbm, down_hbm, up_hbm, bias_ref, ids_ref, length_ref,
+    act_hbm, cot_hbm, down_hbm, up_hbm, bias_hbm, ids_hbm, length_hbm,
     act, cot, keep, send, dense_ref, *rest,
 ):
     outs = rest[:n_table]
-    down, up, store, id_store, feature_ref, in_sems = rest[n_table:]
+    down, up, bias_ref, ids_ref, length_ref, store, id_store, feature_ref, in_sems, small_sems = rest[n_table:]
     tokens, width = act.shape
     rank = down.shape[0]
     half = rank // 2
@@ -69,9 +69,30 @@
         )
         for copy in fetched[-1]:
             copy.start()
+    small = [
+        pltpu.make_async_copy(source, target, small_sems.at[which])
+        for which, (source, target) in enumerate(
+            ((bias_hbm, bias_ref), (ids_hbm, ids_ref), (length_hbm, length_ref))
+        )
+    ]
+    for copy in small:
+        copy.start()
     block = rank >> len(up_bits)
     up_order = order_matrix(rep_ref[0], rank, block, up_bits)
     down_order = order_matrix(rep_ref[0], rank, block, down_bits)
+    hidden = back = None
+    for (start, size), copies in zip(pieces, fetched):
+        part = slice(start, start + size)
+        for copy in copies:
+            copy.wait()
+        value = act[:, part]
+        term = lax.dot_general(value, down[:, part], NT, preferred_element_type=F32)
+        hidden = term if hidden is None else hidden + term
+        scaled_b = (cot[:, part].astype(F32) * value.astype(F32)).astype(BF16)
+        term = lax.dot_general(scaled_b, up[:, part], NT, preferred_element_type=F32)
+        back = term if back is None else back + term
+    for copy in small:
+        copy.wait()
     for place in range(n_table * slots):
         feature_ref[place] = SPARSE_FEATURES
     for feature in range(SPARSE_FEATURES):
@@ -91,17 +112,6 @@
             ids = jnp.where(entries < length, ids_ref[at] - EMPTY, EMPTY)
             id_store[shift, slot * BAG : (slot + 1) * BAG, :] = ids.astype(F32)
         outs[shift][slots * tokens :, :] = id_store[shift].astype(BF16)
-    hidden = back = None
-    for (start, size), copies in zip(pieces, fetched):
-        part = slice(start, start + size)
-        for copy in copies:
-            copy.wait()
-        value = act[:, part]
-        term = lax.dot_general(value, down[:, part], NT, preferred_element_type=F32)
-        hidden = term if hidden is None else hidden + term
-        scaled_b = (cot[:, part].astype(F32) * value.astype(F32)).astype(BF16)
-        term = lax.dot_general(scaled_b, up[:, part], NT, preferred_element_type=F32)
-        back = term if back is None else back + term
     hidden, back = hidden.astype(BF16), back.astype(BF16)
     rows = lax.dot_general(up_order, hidden, NT, preferred_element_type=F32).astype(BF16)
     keep[0], send[0] = rows[:half], rows[half:]
@@ -135,7 +145,7 @@
     sent = slots * tokens + id_rows
     return pl.pallas_call(
         functools.partial(input_kernel, n_table, slots, up_bits, down_bits),
-        in_specs=[SMEM, SMEM, SMEM, ANY, ANY, ANY, ANY, VMEM, VMEM, VMEM],
+        in_specs=[SMEM, SMEM, SMEM, ANY, ANY, ANY, ANY, ANY, ANY, ANY],
         out_specs=[VMEM] * (5 + n_table),
         out_shape=[
             pltpu.VMEM((tokens, width), BF16),
@@ -148,10 +158,14 @@
         scratch_shapes=[
             pltpu.VMEM((rank, width), BF16),
             pltpu.VMEM((rank, width), BF16),
+            pltpu.VMEM(bias.shape, F32),
+            pltpu.VMEM(ids.shape, jnp.int32),
+            pltpu.VMEM(lengths.shape, jnp.int32),
             pltpu.VMEM((SPARSE_FEATURES + 2, tokens, EMBED_WIDTH), BF16),
             pltpu.VMEM((n_table, id_rows, EMBED_WIDTH), F32),
             pltpu.SMEM((n_table * slots,), jnp.int32),
             pltpu.SemaphoreType.DMA((4, len(pieces_of(width)))),
+            pltpu.SemaphoreType.DMA((3,)),
         ],
         compiler_params=params(57),
         cost_estimate=pl.CostEstimate(

time: 46.1 us -> 46 us (level)
  no operation moved by 1% of the time
where the time goes in v11:
time: 46 us; the launch traced here: 45.8 us
  waiting for transfers between devices  17.2 us (37%)
  starting transfers between devices  17 us (37%)
  Pallas kernels  10.8 us (23%)
  between operations  0.72 us (2%)
    ppermute x9, waiting for transfers between devices, swap(): return lax.ppermute(value, axis, [(k, k ^ bit) for k in range(size)])  17.2 us
    ppermute x9, starting transfers between devices, swap(): return lax.ppermute(value, axis, [(k, k ^ bit) for k in range(size)])  12.4 us
    pallas_call x1, Pallas kernels, input_call(): pl.pallas_call(functools.partial(input_kernel, n_table, slots, up_bits, d...  4.91 us
    ppermute x3, starting transfers between devices, shifted(): lax.ppermute(value, 'table', [(k, (k + shift) % n_table) for k in range(n...  4.61 us
    pallas_call x1, Pallas kernels, rows_call(): pl.pallas_call(functools.partial(rows_kernel, slots), in_specs=[VMEM] * n...  3.82 us
  transfers between devices with their start and end apart: 12, of which 5 were waited for; matrix products, arithmetic and copies ran while one was open for 0% of the time, Pallas kernels for 20%

profile of v11, /device:TPU:0, one launch (start us, length us, event | category | flops | bytes accessed | tf_op | source)
XLA Modules:
  0.0 45.8 jit_solution(15063963164100936742)
XLA Ops:
  0.6 0.5 %collective-permute-start.4 = (bf16[128,3456]{1,0:T(8,128)(2,1)}, bf16[128,3456]{1,0:T(8,128)(2,1)S(1)}, u32[]{:S(2)}, u32[]{:S(2)}) collective-permute-start(bf16[128,3456]{1,0:T(8,128)(2,1)} %act_hbm.1), channel_id=1, source_target_pairs={{0,1},{1,0},{2,3},{3,2},{4,5},{5,4},{6,7},{7,6},{8,9},{9,8},{10,11... | collective-permute-start | bytes 2654216 | tf_op jit(solution)/shard_map/ppermute | solution.py:549
  1.2 0.1 collective-permute-start.5
  1.2 4.9 %shard_map.119 = (bf16[128,3456]{1,0:T(8,128)(2,1)S(1)}, bf16[128,3456]{1,0:T(8,128)(2,1)S(1)}, bf16[2,128,128]{2,1,0:T(8,128)(2,1)S(1)}, bf16[2,128,128]{2,1,0:...) custom-call(s32[1]{0:T(128)} %bitcast.table_ref, ...), custom_call_target="tpu_custom_call" | custom-call | flops 905969664 | bytes 5308416 | tf_op jit(solution)/shard_map/pallas_call | solution.py:146
  6.1 0.5 %collective-permute-start.3 = (bf16[2,128,128]{2,1,0:T(8,128)(2,1)S(1)}, bf16[2,128,128]{2,1,0:T(8,128)(2,1)S(1)}, u32[]{:S(2)}, u32[]{:S(2)}) collective-permute-start(bf16[2,128,128]{2,1,0:T(8,128)(2,1)S(1)} %get-tuple-element.60), channel_id=1, source_target_pairs={{0,1},{1,0},{2,3},{3,2},{4,5},{5,4},{6,7},{7,6},{8,9},{9,8},{10,11... | collective-permute-start | bytes 196616 | tf_op jit(solution)/shard_map/ppermute | solution.py:549
  6.6 0.9 %collective-permute-done.3.other_ref = bf16[2,128,128]{2,1,0:T(8,128)(2,1)S(1)} collective-permute-done((bf16[2,128,128]{2,1,0:T(8,128)(2,1)S(1)}, bf16[2,128,128]{2,1,0:T(8,128)(2,1)S(1)}, u32[]{:S(2)}, u32[]{:S(2)}) %collective-permute-start.3) | collective-permute-done | bytes 65568 | tf_op jit(solution)/shard_map/ppermute | solution.py:549
  7.5 0.0 collective-permute-done.4.act_other
  7.5 0.0 collective-permute-done.5.cot_other
  7.6 0.8 %shard_map.120 = (f32[64,3456]{1,0:T(8,128)S(1)}, bf16[64,3584]{1,0:T(8,128)(2,1)S(1)}, f32[64,3456]{1,0:T(8,128)S(1)}, bf16[64,3456]{1,0:T(8,128)(2,1)S(1)}, f32[32,128]{1,0:T(8,128)S(1)}) custom-call(bf16[2,128,128]{2,1,0:T(8,128)(2,1)S(1)} %get-tuple-element.59.keep_ref, bf16[2,128,128]{2,1,0:T(8,128)(2,1)S(1)} %collective-permute-done.3.other_ref, ...), custom_call_target="tpu_custom_call" | custom-call | flops 452984832 | bytes 6193152 | tf_op jit(solution)/shard_map/pallas_call | solution.py:237
  8.4 2.9 %collective-permute-start.6 = (bf16[64,3584]{1,0:T(8,128)(2,1)S(1)}, bf16[64,3584]{1,0:T(8,128)(2,1)S(1)}, u32[]{:S(2)}, u32[]{:S(2)}) collective-permute-start(bf16[64,3584]{1,0:T(8,128)(2,1)S(1)} %get-tuple-element.64), channel_id=1, source_target_pairs={{0,2},{1,3},{2,0},{3,1},{4,6},{5,7},{6,4},{7,5},{8,10},{9,11},{10,... | collective-permute-start | bytes 1376264 | tf_op jit(solution)/shard_map/ppermute | solution.py:549
  11.3 1.5 %collective-permute-start.7 = (bf16[64,3456]{1,0:T(8,128)(2,1)S(1)}, bf16[64,3456]{1,0:T(8,128)(2,1)S(1)}, u32[]{:S(2)}, u32[]{:S(2)}) collective-permute-start(bf16[64,3456]{1,0:T(8,128)(2,1)S(1)} %get-tuple-element.66), channel_id=1, source_target_pairs={{0,4},{1,5},{2,6},{3,7},{4,0},{5,1},{6,2},{7,3},{8,12},{9,13},{10,... | collective-permute-start | bytes 1327112 | tf_op jit(solution)/shard_map/ppermute | solution.py:549
  12.8 2.6 %collective-permute-start.10 = (bf16[928,128]{1,0:T(8,128)(2,1)S(1)}, bf16[928,128]{1,0:T(8,128)(2,1)S(1)}, u32[]{:S(2)}, u32[]{:S(2)}) collective-permute-start(bf16[928,128]{1,0:T(8,128)(2,1)S(1)} %get-tuple-element.81), channel_id=1, source_target_pairs={{0,16},{8,24},{16,0},{24,8},{1,17},{9,25},{17,1},{25,9},{2,18},{10... | collective-permute-start | bytes 712712 | tf_op jit(solution)/shard_map/ppermute | solution.py:552
  15.4 1.3 %collective-permute-start.11 = (bf16[928,128]{1,0:T(8,128)(2,1)S(1)}, bf16[928,128]{1,0:T(8,128)(2,1)S(1)}, u32[]{:S(2)}, u32[]{:S(2)}) collective-permute-start(bf16[928,128]{1,0:T(8,128)(2,1)S(1)} %get-tuple-element.82), channel_id=1, source_target_pairs={{0,24},{8,0},{16,8},{24,16},{1,25},{9,1},{17,9},{25,17},{2,26},{10... | collective-permute-start | bytes 712712 | tf_op jit(solution)/shard_map/ppermute | solution.py:552
  16.8 0.7 %collective-permute-start.9 = (bf16[928,128]{1,0:T(8,128)(2,1)S(1)}, bf16[928,128]{1,0:T(8,128)(2,1)S(1)}, u32[]{:S(2)}, u32[]{:S(2)}) collective-permute-start(bf16[928,128]{1,0:T(8,128)(2,1)S(1)} %get-tuple-element.80), channel_id=1, source_target_pairs={{0,8},{8,16},{16,24},{24,0},{1,9},{9,17},{17,25},{25,1},{2,10},{10... | collective-permute-start | bytes 712712 | tf_op jit(solution)/shard_map/ppermute | solution.py:552
  17.5 5.8 %collective-permute-done.7.down_in_ref = bf16[64,3456]{1,0:T(8,128)(2,1)S(1)} collective-permute-done((bf16[64,3456]{1,0:T(8,128)(2,1)S(1)}, bf16[64,3456]{1,0:T(8,128)(2,1)S(1)}, u32[]{:S(2)}, u32[]{:S(2)}) %collective-permute-start.7) | collective-permute-done | bytes 442400 | tf_op jit(solution)/shard_map/ppermute | solution.py:549
  23.3 0.0 collective-permute-done.6.up_in_ref
  23.3 0.2 shard_map.121
  23.4 14.3 %conditional.1 = (f32[1,2,32,864]{3,2,1,0:T(8,128)S(1)}, f32[32,128]{1,0:T(8,128)S(1)}, bf16[64,1024]{1,0:T(8,128)(2,1)S(1)}) conditional(s32[]{:T(128)} %bitcast.5, () %tuple.17, (bf16[32,3712]{1,0:T(8,128)(2,1)S(1)}, bf16[32,3456]{1,0:T(8,128)(2,1)S(1)}, s32[1]{0:T(128)}, f32[32,3456]{1,0:T(8,128)S(1)}, f32[32,3456]{1,0:T(8,128)S(1)}, ...), branch_computations={%region_0.0_spmd, %region_1.0_spmd} | conditional | bytes 2818192 | solution.py:606
  23.4 1.6 %collective-permute-start = (bf16[32,3712]{1,0:T(8,128)(2,1)S(1)}, bf16[32,3712]{1,0:T(8,128)(2,1)S(1)}, u32[]{:S(2)}, u32[]{:S(2)}) collective-permute-start(bf16[32,3712]{1,0:T(8,128)(2,1)S(1)} %get-tuple-element.14), channel_id=1, source_target_pairs={{0,4},{1,5},{2,6},{3,7},{4,0},{5,1},{6,2},{7,3},{8,12},{9,13},{10,... | collective-permute-start | bytes 712712 | tf_op jit(solution)/shard_map/cond/branch_1_fun/ppermute | solution.py:549
  25.0 0.6 %collective-permute-start.1 = (bf16[32,3456]{1,0:T(8,128)(2,1)S(1)}, bf16[32,3456]{1,0:T(8,128)(2,1)S(1)}, u32[]{:S(2)}, u32[]{:S(2)}) collective-permute-start(bf16[32,3456]{1,0:T(8,128)(2,1)S(1)} %get-tuple-element.16), channel_id=1, source_target_pairs={{0,2},{1,3},{2,0},{3,1},{4,6},{5,7},{6,4},{7,5},{8,10},{9,11},{10,... | collective-permute-start | bytes 663560 | tf_op jit(solution)/shard_map/cond/branch_1_fun/ppermute | solution.py:549
  25.6 5.4 %collective-permute-done.1.down_in_ref = bf16[32,3456]{1,0:T(8,128)(2,1)S(1)} collective-permute-done((bf16[32,3456]{1,0:T(8,128)(2,1)S(1)}, bf16[32,3456]{1,0:T(8,128)(2,1)S(1)}, u32[]{:S(2)}, u32[]{:S(2)}) %collective-permute-start.1) | collective-permute-done | bytes 221216 | tf_op jit(solution)/shard_map/cond/branch_1_fun/ppermute | solution.py:549
  31.1 0.0 collective-permute-done.up_in_ref
  31.1 0.3 branch_1_fun.2
  31.4 1.6 %collective-permute-start.2 = (bf16[64,1920]{1,0:T(8,128)(2,1)S(1)}, bf16[64,1920]{1,0:T(8,128)(2,1)S(1)}, u32[]{:S(2)}, u32[]{:S(2)}) collective-permute-start(bf16[64,1920]{1,0:T(8,128)(2,1)S(1)} %get-tuple-element.19), channel_id=1, source_target_pairs={{0,8},{8,0},{16,24},{24,16},{1,9},{9,1},{17,25},{25,17},{2,10},{10... | collective-permute-start | bytes 737288 | tf_op jit(solution)/shard_map/cond/branch_1_fun/ppermute | solution.py:549
  33.1 4.6 %collective-permute-done.2.in_ref = bf16[64,1920]{1,0:T(8,128)(2,1)S(1)} collective-permute-done((bf16[64,1920]{1,0:T(8,128)(2,1)S(1)}, bf16[64,1920]{1,0:T(8,128)(2,1)S(1)}, u32[]{:S(2)}, u32[]{:S(2)}) %collective-permute-start.2) | collective-permute-done | bytes 245792 | tf_op jit(solution)/shard_map/cond/branch_1_fun/ppermute | solution.py:549
  37.7 0.1 branch_1_fun.3
  37.7 3.0 %collective-permute-start.8 = (bf16[64,1024]{1,0:T(8,128)(2,1)S(1)}, bf16[64,1024]{1,0:T(8,128)(2,1)S(1)}, u32[]{:S(2)}, u32[]{:S(2)}) collective-permute-start(bf16[64,1024]{1,0:T(8,128)(2,1)S(1)} %get-tuple-element.74), channel_id=1, source_target_pairs={{0,16},{8,24},{16,0},{24,8},{1,17},{9,25},{17,1},{25,9},{2,18},{10... | collective-permute-start | bytes 393224 | tf_op jit(solution)/shard_map/ppermute | solution.py:549
  40.8 0.0 collective-permute-done.10.refs_2_
  40.8 0.0 collective-permute-done.11.refs_3_
  40.8 0.0 collective-permute-done.9.refs_1_
  40.8 3.8 %shard_map.123 = f32[1,7,512,128]{3,2,1,0:T(8,128)} custom-call(bf16[928,128]{1,0:T(8,128)(2,1)S(1)} %get-tuple-element.83.refs_0_, bf16[928,128]{1,0:T(8,128)(2,1)S(1)} %collective-permute-done.9.refs_1_, bf16[928,128]{1,0:T(8,128)(2,1)S(1)} %collective-permute-done.10.refs_2_, bf16[928,128]{1,0:T(8,128)(2,1)S(1)} %collective-permute-done.11.refs_3_), custom_call_target="tpu_custom_call" | custom-call | flops 469762048 | bytes 1835008 | tf_op jit(solution)/shard_map/pallas_call | solution.py:512
  44.6 0.5 %collective-permute-done.8.in_ref = bf16[64,1024]{1,0:T(8,128)(2,1)S(1)} collective-permute-done((bf16[64,1024]{1,0:T(8,128)(2,1)S(1)}, bf16[64,1024]{1,0:T(8,128)(2,1)S(1)}, u32[]{:S(2)}, u32[]{:S(2)}) %collective-permute-start.8) | collective-permute-done | bytes 131104 | tf_op jit(solution)/shard_map/ppermute | solution.py:549
  45.1 0.7 %shard_map.122 = (f32[32,864]{1,0:T(8,128)}, f32[32,864]{1,0:T(8,128)}, f32[27,128]{1,0:T(8,128)}) custom-call(f32[1,2,32,864]{3,2,1,0:T(8,128)S(1)} %get-tuple-element.73.keep_ref, bf16[64,1024]{1,0:T(8,128)(2,1)S(1)} %collective-permute-done.8.in_ref, f32[32,128]{1,0:T(8,128)S(1)} %get-tuple-element.75.bias_ref), custom_call_target="tpu_custom_call" | custom-call | tf_op jit(solution)/shard_map/pallas_call | solution.py:466
  (2 shorter events, 0.0 us)
Async XLA Ops:
  0.6 6.9 %collective-permute-start.4 = (bf16[128,3456]{1,0:T(8,128)(2,1)}, bf16[128,3456]{1,0:T(8,128)(2,1)S(1)}, u32[]{:S(2)}, u32[]{:S(2)}) collective-permute-start(bf16[128,3456]{1,0:T(8,128)(2,1)} %act_hbm.1), channel_id=1, source_target_pairs={{0,1},{1,0},{2,3},{3,2},{4,5},{5,4},{6,7},{7,6},{8,9},{9,8},{10,11... | collective-permute-start | bytes 2654216 | tf_op jit(solution)/shard_map/ppermute | solution.py:549
  1.2 6.4 %collective-permute-start.5 = (bf16[128,3456]{1,0:T(8,128)(2,1)}, bf16[128,3456]{1,0:T(8,128)(2,1)S(1)}, u32[]{:S(2)}, u32[]{:S(2)}) collective-permute-start(bf16[128,3456]{1,0:T(8,128)(2,1)} %cot_hbm.1), channel_id=1, source_target_pairs={{0,1},{1,0},{2,3},{3,2},{4,5},{5,4},{6,7},{7,6},{8,9},{9,8},{10,11... | collective-permute-start | bytes 2654216 | tf_op jit(solution)/shard_map/ppermute | solution.py:549
  6.1 1.4 %collective-permute-start.3 = (bf16[2,128,128]{2,1,0:T(8,128)(2,1)S(1)}, bf16[2,128,128]{2,1,0:T(8,128)(2,1)S(1)}, u32[]{:S(2)}, u32[]{:S(2)}) collective-permute-start(bf16[2,128,128]{2,1,0:T(8,128)(2,1)S(1)} %get-tuple-element.60), channel_id=1, source_target_pairs={{0,1},{1,0},{2,3},{3,2},{4,5},{5,4},{6,7},{7,6},{8,9},{9,8},{10,11... | collective-permute-start | bytes 196616 | tf_op jit(solution)/shard_map/ppermute | solution.py:549
  7.6 9.9 %copy-start = (s32[26]{0:T(128)S(1)}, s32[26]{0:T(128)}, u32[]{:S(2)}) copy-start(s32[26]{0:T(128)} %owner_ref.1) | copy-start | bytes 316
  8.4 14.9 %collective-permute-start.6 = (bf16[64,3584]{1,0:T(8,128)(2,1)S(1)}, bf16[64,3584]{1,0:T(8,128)(2,1)S(1)}, u32[]{:S(2)}, u32[]{:S(2)}) collective-permute-start(bf16[64,3584]{1,0:T(8,128)(2,1)S(1)} %get-tuple-element.64), channel_id=1, source_target_pairs={{0,2},{1,3},{2,0},{3,1},{4,6},{5,7},{6,4},{7,5},{8,10},{9,11},{10,... | collective-permute-start | bytes 1376264 | tf_op jit(solution)/shard_map/ppermute | solution.py:549
  11.3 11.9 %collective-permute-start.7 = (bf16[64,3456]{1,0:T(8,128)(2,1)S(1)}, bf16[64,3456]{1,0:T(8,128)(2,1)S(1)}, u32[]{:S(2)}, u32[]{:S(2)}) collective-permute-start(bf16[64,3456]{1,0:T(8,128)(2,1)S(1)} %get-tuple-element.66), channel_id=1, source_target_pairs={{0,4},{1,5},{2,6},{3,7},{4,0},{5,1},{6,2},{7,3},{8,12},{9,13},{10,... | collective-permute-start | bytes 1327112 | tf_op jit(solution)/shard_map/ppermute | solution.py:549
  12.8 27.9 %collective-permute-start.10 = (bf16[928,128]{1,0:T(8,128)(2,1)S(1)}, bf16[928,128]{1,0:T(8,128)(2,1)S(1)}, u32[]{:S(2)}, u32[]{:S(2)}) collective-permute-start(bf16[928,128]{1,0:T(8,128)(2,1)S(1)} %get-tuple-element.81), channel_id=1, source_target_pairs={{0,16},{8,24},{16,0},{24,8},{1,17},{9,25},{17,1},{25,9},{2,18},{10... | collective-permute-start | bytes 712712 | tf_op jit(solution)/shard_map/ppermute | solution.py:552
  15.4 25.4 %collective-permute-start.11 = (bf16[928,128]{1,0:T(8,128)(2,1)S(1)}, bf16[928,128]{1,0:T(8,128)(2,1)S(1)}, u32[]{:S(2)}, u32[]{:S(2)}) collective-permute-start(bf16[928,128]{1,0:T(8,128)(2,1)S(1)} %get-tuple-element.82), channel_id=1, source_target_pairs={{0,24},{8,0},{16,8},{24,16},{1,25},{9,1},{17,9},{25,17},{2,26},{10... | collective-permute-start | bytes 712712 | tf_op jit(solution)/shard_map/ppermute | solution.py:552
  16.8 24.0 %collective-permute-start.9 = (bf16[928,128]{1,0:T(8,128)(2,1)S(1)}, bf16[928,128]{1,0:T(8,128)(2,1)S(1)}, u32[]{:S(2)}, u32[]{:S(2)}) collective-permute-start(bf16[928,128]{1,0:T(8,128)(2,1)S(1)} %get-tuple-element.80), channel_id=1, source_target_pairs={{0,8},{8,16},{16,24},{24,0},{1,9},{9,17},{17,25},{25,1},{2,10},{10... | collective-permute-start | bytes 712712 | tf_op jit(solution)/shard_map/ppermute | solution.py:552
  23.4 7.6 %collective-permute-start = (bf16[32,3712]{1,0:T(8,128)(2,1)S(1)}, bf16[32,3712]{1,0:T(8,128)(2,1)S(1)}, u32[]{:S(2)}, u32[]{:S(2)}) collective-permute-start(bf16[32,3712]{1,0:T(8,128)(2,1)S(1)} %get-tuple-element.14), channel_id=1, source_target_pairs={{0,4},{1,5},{2,6},{3,7},{4,0},{5,1},{6,2},{7,3},{8,12},{9,13},{10,... | collective-permute-start | bytes 712712 | tf_op jit(solution)/shard_map/cond/branch_1_fun/ppermute | solution.py:549
  25.0 6.1 %collective-permute-start.1 = (bf16[32,3456]{1,0:T(8,128)(2,1)S(1)}, bf16[32,3456]{1,0:T(8,128)(2,1)S(1)}, u32[]{:S(2)}, u32[]{:S(2)}) collective-permute-start(bf16[32,3456]{1,0:T(8,128)(2,1)S(1)} %get-tuple-element.16), channel_id=1, source_target_pairs={{0,2},{1,3},{2,0},{3,1},{4,6},{5,7},{6,4},{7,5},{8,10},{9,11},{10,... | collective-permute-start | bytes 663560 | tf_op jit(solution)/shard_map/cond/branch_1_fun/ppermute | solution.py:549
  31.4 6.3 %collective-permute-start.2 = (bf16[64,1920]{1,0:T(8,128)(2,1)S(1)}, bf16[64,1920]{1,0:T(8,128)(2,1)S(1)}, u32[]{:S(2)}, u32[]{:S(2)}) collective-permute-start(bf16[64,1920]{1,0:T(8,128)(2,1)S(1)} %get-tuple-element.19), channel_id=1, source_target_pairs={{0,8},{8,0},{16,24},{24,16},{1,9},{9,1},{17,25},{25,17},{2,10},{10... | collective-permute-start | bytes 737288 | tf_op jit(solution)/shard_map/cond/branch_1_fun/ppermute | solution.py:549
  37.7 7.4 %collective-permute-start.8 = (bf16[64,1024]{1,0:T(8,128)(2,1)S(1)}, bf16[64,1024]{1,0:T(8,128)(2,1)S(1)}, u32[]{:S(2)}, u32[]{:S(2)}) collective-permute-start(bf16[64,1024]{1,0:T(8,128)(2,1)S(1)} %get-tuple-element.74), channel_id=1, source_target_pairs={{0,16},{8,24},{16,0},{24,8},{1,17},{9,25},{17,1},{25,9},{2,18},{10... | collective-permute-start | bytes 393224 | tf_op jit(solution)/shard_map/ppermute | solution.py:549
